TPU v7x, 512 devices: a whole 4x4x16 slice. The times are simulated.
512 devices in a mesh: dp: 64 (over z_lo, x, core), code: 8 (over z_hi, y).
Axes of the slice: x: 4, y: 4, z: 16 (z_hi: 2, z_lo: 8; z = z_hi * 8 + z_lo), core: 2. Of those that a mesh axis runs over, the one named last changes fastest.
Arguments:
- latents: bfloat16 [24576, 256], P('dp'), may hold values from -6 to 6
- codebook: bfloat16 [32768, 256], P('code'), may hold values from -6 to 6
Outputs:
- targets: float32 [32768, 256], P(('code', 'dp'))
- reconstruction: float32 [24576, 256], P('dp')
All inputs are finite; a program needn't handle non-finite values.
Results may differ from a plain program's by a relative error of at most 0.0022.
Values sent between devices are 32-bit elements; how exact they have to be, the bound alone decides.
No kernel may reach another device: no remote copies, remote signals or barrier semaphores. Data moves between devices by JAX's collectives and lax.ppermute only.
A program may use at most 64 MiB of HBM per device.

v0:
```python
import jax
import jax.numpy as jnp
from jax import lax
from jax.sharding import PartitionSpec as P

ITERS = 3


SHARP = 48.0
EPSILON = 1e-06


def scaled(values):
    floats = values.astype(jnp.float32)
    return lax.rsqrt(jnp.mean(floats * floats, axis=-1) + EPSILON)


def per_device(latents, codebook):
    token_count = latents.shape[0]
    code_count = codebook.shape[0]
    width = latents.shape[1]
    total_tokens = token_count * lax.axis_size("dp")
    total_codes = code_count * lax.axis_size("code")
    row_norm = scaled(latents)
    code_norm = scaled(codebook)
    inner = jnp.dot(latents, codebook.T, preferred_element_type=jnp.float32)
    stored_tile = jnp.exp(inner * (SHARP / width) * row_norm[:, None] * code_norm[None, :])

    def fetch_tile():
        return stored_tile

    col_scale = jnp.ones((code_count,), jnp.float32)
    row_scale = jnp.ones((token_count,), jnp.float32)
    for sweep_index in range(ITERS):
        kernel_now = fetch_tile()
        row_part = jnp.sum(kernel_now * col_scale[None, :], axis=1)
        row_scale = 1.0 / lax.psum(row_part, "code")
        col_part = jnp.sum(kernel_now * row_scale[:, None], axis=0)
        col_scale = total_tokens / total_codes / lax.psum(col_part, "dp")
    plan = (row_scale[:, None] * fetch_tile() * col_scale[None, :]).astype(jnp.bfloat16)
    mass = jnp.sum(plan.astype(jnp.float32), axis=1)
    numer = jnp.dot(plan, codebook, preferred_element_type=jnp.float32)
    total_numer, total_mass = lax.psum((numer, mass), "code")
    rebuilt = total_numer / total_mass[:, None]
    summed = lax.psum_scatter(
        lax.dot_general(
            plan, latents, (((0,), (0,)), ((), ())), preferred_element_type=jnp.float32
        ),
        "dp",
        scatter_dimension=0,
        tiled=True,
    )
    targets = summed * (total_codes / total_tokens)
    return (targets, rebuilt)


def solution(mesh):
    placed = (P("dp", None), P("code", None))
    return jax.shard_map(
        per_device,
        mesh=mesh,
        in_specs=placed,
        out_specs=(P(("code", "dp"), None), P("dp", None)),
        check_vma=False,
    )
```

profile of v0, /device:TPU:24, one launch (start us, length us, event | category | flops | bytes accessed | tf_op | source)
XLA Modules:
  0.0 1862.8 jit_solution(5005039438245175391)
XLA Ops:
  8.0 0.0 all-reduce.2.cloned.1.call-start
  8.0 1.1 multiply_reduce_fusion.6
  9.1 2.2 multiply_reduce_fusion.5
  11.4 5.8 fusion
  17.1 36.0 %psum.56 = f32[384]{0:T(512)S(1)} all-reduce(f32[384]{0:T(512)S(1)} %get-tuple-element.4), channel_id=1, replica_groups=mesh['dp'=64,'code'=8] {'code'}, use_global_device_ids=true, to_apply=%region_3.0 | all-reduce | flops 384 | bytes 3072 | tf_op jit(solution)/shard_map/psum | solution.py:37
  53.1 3.6 multiply_reduce_fusion.3
  56.8 425.2 %psum.57 = f32[4096]{0:T(1024)S(1)} all-reduce(f32[4096]{0:T(1024)S(1)} %multiply_reduce_fusion.3), channel_id=1, replica_groups=mesh['dp'=64,'code'=8] {'dp'}, use_global_device_ids=true, to_apply=%region_5.0 | all-reduce | flops 4096 | bytes 32768 | tf_op jit(solution)/shard_map/psum | solution.py:39
  482.0 3.3 multiply_reduce_fusion.2
  485.3 35.4 %psum.58 = f32[384]{0:T(512)S(1)} all-reduce(f32[384]{0:T(512)S(1)} %multiply_reduce_fusion.2), channel_id=1, replica_groups=mesh['dp'=64,'code'=8] {'code'}, use_global_device_ids=true, to_apply=%region_7.0 | all-reduce | flops 384 | bytes 3072 | tf_op jit(solution)/shard_map/psum | solution.py:37
  520.7 3.6 multiply_reduce_fusion.1
  524.3 418.7 %psum.59 = f32[4096]{0:T(1024)S(1)} all-reduce(f32[4096]{0:T(1024)S(1)} %multiply_reduce_fusion.1), channel_id=1, replica_groups=mesh['dp'=64,'code'=8] {'dp'}, use_global_device_ids=true, to_apply=%region_9.0 | all-reduce | flops 4096 | bytes 32768 | tf_op jit(solution)/shard_map/psum | solution.py:39
  943.1 3.3 multiply_reduce_fusion
  946.4 33.4 %psum.60 = f32[384]{0:T(512)S(1)} all-reduce(f32[384]{0:T(512)S(1)} %multiply_reduce_fusion), channel_id=1, replica_groups=mesh['dp'=64,'code'=8] {'code'}, use_global_device_ids=true, to_apply=%region_11.0 | all-reduce | flops 384 | bytes 3072 | tf_op jit(solution)/shard_map/psum | solution.py:37
  979.8 3.6 multiply_reduce_fusion.4
  983.5 418.7 %psum.61 = f32[4096]{0:T(1024)S(1)} all-reduce(f32[4096]{0:T(1024)S(1)} %multiply_reduce_fusion.4), channel_id=1, replica_groups=mesh['dp'=64,'code'=8] {'dp'}, use_global_device_ids=true, to_apply=%region_13.0 | all-reduce | flops 4096 | bytes 32768 | tf_op jit(solution)/shard_map/psum | solution.py:39
  1402.2 0.0 copy-start
  1402.2 0.0 copy-start.1
  1402.3 3.8 convert_reduce_fusion
  1406.1 0.0 copy-done
  1406.1 1.8 fusion.2
  1407.9 0.0 all-reduce.2.cloned.1.call-update
  1407.9 0.0 reduce-scatter.2.cloned.1.call-start
  1407.9 0.0 copy-done.1
  1407.9 3.2 fusion.1
  1411.2 0.0 reduce-scatter.2.cloned.1.call-update
  1411.2 35.4 %psum.63 = f32[384]{0:T(512)S(1)} all-reduce(f32[384]{0:T(512)S(1)} %get-tuple-element.2), channel_id=1, replica_groups=mesh['dp'=64,'code'=8] {'code'}, use_global_device_ids=true, to_apply=%region_17.0 | all-reduce | flops 384 | bytes 3072 | tf_op jit(solution)/shard_map/psum | solution.py:43
  1446.6 111.8 %all-reduce.2.cloned.1.call-done = f32[384,256]{1,0:T(8,128)} async-done(((f32[384,256]{1,0:T(8,128)}), f32[384,256]{1,0:T(8,128)}) %all-reduce.2.cloned.1.call-update) | async-done | bytes 393232 | tf_op jit(solution)/shard_map/psum | solution.py:43
  1558.4 1.9 broadcast_divide_fusion
  1560.3 293.6 %reduce-scatter.2.cloned.1.call-done = f32[64,256]{1,0:T(8,128)} async-done(((f32[4096,256]{1,0:T(8,128)}), f32[64,256]{1,0:T(8,128)}) %reduce-scatter.2.cloned.1.call-update) | async-done | bytes 65552 | tf_op jit(solution)/shard_map/reduce_scatter | solution.py:45
  1853.9 1.5 broadcast_multiply_fusion
  (8 shorter events, 0.1 us)
Async XLA Ops:
  8.0 1550.4 %all-reduce.2.cloned.1.call-start = ((), (), s32[]{:S(2)}) async-start(), calls=%async_computation.2 | async-start | bytes 786432 | tf_op jit(solution)/shard_map/psum | solution.py:43
  1402.2 3.9 copy-start
  1402.2 5.7 copy-start.1
  1407.9 446.0 %reduce-scatter.2.cloned.1.call-start = ((), (), s32[]{:S(2)}) async-start(), calls=%async_computation.1 | async-start | bytes 4259840 | tf_op jit(solution)/shard_map/reduce_scatter | solution.py:45
Sparse Core Ops, SparseCore 0:
  1408.0 150.3 all-reduce.1
Sparse Core Ops, SparseCore 1:
  1411.3 442.5 reduce-scatter.1
where the time goes:
time: 1860 us
  blocking collectives  1400 us (75%)
  waiting for transfers between devices  405 us (22%)
  other arithmetic  28.1 us (2%)
    psum x3, blocking collectives, per_device(): col_scale = total_tokens / total_codes / lax.psum(col_part, 'dp')  1260 us
    reduce_scatter x1, waiting for transfers between devices, per_device(): lax.psum_scatter(lax.dot_general(plan, latents, (((0,), (0,)), ((), ())),...  294 us
    psum x1, waiting for transfers between devices, per_device(): total_numer, total_mass = lax.psum((numer, mass), 'code')  112 us
    psum x3, blocking collectives, per_device(): row_scale = 1.0 / lax.psum(row_part, 'code')  105 us
  transfers between devices with their start and end apart: 2, of which 2 were waited for; matrix products, arithmetic and copies ran while one was open for 0% of the time, Pallas kernels for 0%

commit v1 on v0

v1 whole, which is shorter than its diff:
```python
import jax
import jax.numpy as jnp
from jax import lax
from jax.sharding import Mesh, PartitionSpec as P

ITERS = 3
SHARP = 48.0
EPSILON = 1e-06

AXES = ("z", "x", "c", "h", "y")
Z, X, C, H, Y = 8, 4, 2, 2, 4


def scaled(values):
    floats = values.astype(jnp.float32)
    return lax.rsqrt(jnp.mean(floats * floats, axis=-1) + EPSILON)


def exchange(blocks, axes):
    return lax.all_to_all(blocks, axes, 0, 0, tiled=True)


def spread(block, axes, count):
    return exchange(jnp.broadcast_to(block[None], (count,) + block.shape), axes)


def per_device(latents, codebook):
    token_count, width = latents.shape
    code_count = codebook.shape[0]
    total_tokens = token_count * Z * X * C
    total_codes = code_count * H * Y
    share = code_count // (Z * X * C)
    codebook = codebook.reshape(Z, X, C, share, width).transpose(2, 1, 0, 3, 4).reshape(code_count, width)
    row_norm = scaled(latents)
    code_norm = scaled(codebook)
    inner = jnp.dot(latents, codebook.T, preferred_element_type=jnp.float32)
    tile = jnp.exp(inner * (SHARP / width) * row_norm[:, None] * code_norm[None, :])

    def rows(col_scale):
        part = jnp.sum(tile * col_scale[None, :], axis=1)
        return 1.0 / jnp.sum(spread(part, ("h", "y"), H * Y), axis=0)

    def columns(row_scale):
        part = jnp.sum(tile * row_scale[:, None], axis=0).reshape(C * X, Z * share)
        part = jnp.sum(exchange(part, ("c", "x")), axis=0)
        total = jnp.sum(spread(part, ("z",), Z), axis=0)
        mine = total_tokens / total_codes / total
        return mine, spread(mine, ("c", "x"), C * X).reshape(code_count)

    col_scale = jnp.ones((code_count,), jnp.float32)
    for sweep_index in range(ITERS):
        row_scale = rows(col_scale)
        mine, col_scale = columns(row_scale)

    weighted = (row_scale[:, None] * tile).astype(jnp.bfloat16)
    summed = lax.dot_general(weighted, latents, (((0,), (0,)), ((), ())), preferred_element_type=jnp.float32)
    summed = jnp.sum(exchange(summed.reshape(C, code_count // C, width), "c"), axis=0)
    summed = jnp.sum(exchange(summed.reshape(X, Z * share, width), "x"), axis=0)
    summed = jnp.sum(exchange(summed.reshape(Z, share, width), "z"), axis=0)
    own = lax.dynamic_slice(mine, (lax.axis_index("z") * share,), (share,))
    targets = summed * (own * (total_codes / total_tokens))[:, None]

    plan = (row_scale[:, None] * tile * col_scale[None, :]).astype(jnp.bfloat16)
    mass = jnp.sum(plan.astype(jnp.float32), axis=1)
    numer = jnp.dot(plan, codebook, preferred_element_type=jnp.float32)
    group = token_count // Y
    packed = jnp.concatenate(
        [
            numer.reshape(Y, group, width),
            jnp.pad(mass.reshape(Y, 1, group), ((0, 0), (0, 7), (0, width - group))),
        ],
        axis=1,
    )
    packed = jnp.sum(exchange(packed, "y"), axis=0)
    packed = packed + lax.ppermute(packed, "h", [(0, 1), (1, 0)])
    part = packed[:group] / packed[group, :group][:, None]
    rebuilt = spread(part, ("y",), Y).reshape(token_count, width)
    return (targets, rebuilt)


def solution(mesh):
    fine = Mesh(mesh.devices.reshape(Z, X, C, H, Y), AXES)
    return jax.shard_map(
        per_device,
        mesh=fine,
        in_specs=(P(("z", "x", "c"), None), P(("h", "y"), None)),
        out_specs=(P(("h", "y", "z", "x", "c"), None), P(("z", "x", "c"), None)),
        check_vma=False,
    )
```

time: 1860 us -> 286 us (0.15)
  blocking collectives: 1400 us -> 146 us
  waiting for transfers between devices: 405 us -> 57.6 us
  starting transfers between devices: 0.08 us -> 30.6 us
    psum x7 -> x0, blocking collectives: 1400 us -> none  [the longest x3 1260 us: per_device(): col_scale = total_tokens / total_codes / lax.psum(col_part, 'dp')]
    reduce_scatter x1 -> x0, waiting for transfers between devices: 294 us -> none  [per_device(): lax.psum_scatter(lax.dot_general(plan, latents, (((0,), (0,)), ((), ())),...]
    all_to_all x0 -> x11, blocking collectives: none -> 146 us  [exchange(): return lax.all_to_all(blocks, axes, 0, 0, tiled=True)]
    psum x1 -> x0, waiting for transfers between devices: 112 us -> none  [per_device(): total_numer, total_mass = lax.psum((numer, mass), 'code')]
    all_to_all x0 -> x6, waiting for transfers between devices: none -> 44.8 us  [exchange(): return lax.all_to_all(blocks, axes, 0, 0, tiled=True)]
    all_to_all x0 -> x6, starting transfers between devices: none -> 28.1 us  [exchange(): return lax.all_to_all(blocks, axes, 0, 0, tiled=True)]
  transfers between devices with their start and end apart: 2 -> 7, of which waited for: 2 -> 5; matrix products, arithmetic and copies ran while one was open for 0% -> 7% of each run, Pallas kernels for 0% -> 0%
where the time goes in v1:
time: 286 us; the launch traced here: 284 us
  blocking collectives  146 us (51%)
  waiting for transfers between devices  57.6 us (20%)
  other arithmetic  31.5 us (11%)
  starting transfers between devices  30.6 us (11%)
  matrix products  12.9 us (5%)
  local copies, waits for them, and re-layouts  4.17 us (1%)
    all_to_all x11, blocking collectives, exchange(): return lax.all_to_all(blocks, axes, 0, 0, tiled=True)  146 us
    all_to_all x6, waiting for transfers between devices, exchange(): return lax.all_to_all(blocks, axes, 0, 0, tiled=True)  44.8 us
    all_to_all x6, starting transfers between devices, exchange(): return lax.all_to_all(blocks, axes, 0, 0, tiled=True)  28.1 us
    ppermute x1, waiting for transfers between devices, per_device(): packed = packed + lax.ppermute(packed, 'h', [(0, 1), (1, 0)])  12.8 us
    reduce_sum x3, other arithmetic, columns(): part = jnp.sum(tile * row_scale[:, None], axis=0).reshape(C * X, Z * share)  10.9 us
    reduce_sum x2, other arithmetic, rows(): part = jnp.sum(tile * col_scale[None, :], axis=1)  6.68 us
    dot_general x1, matrix products, per_device(): lax.dot_general(weighted, latents, (((0,), (0,)), ((), ())), preferred_el...  6.26 us
  transfers between devices with their start and end apart: 7, of which 5 were waited for; matrix products, arithmetic and copies ran while one was open for 7% of the time, Pallas kernels for 0%

profile of v1, /device:TPU:24, one launch (start us, length us, event | category | flops | bytes accessed | tf_op | source)
XLA Modules:
  0.0 283.7 jit_solution(16402045053250783221)
XLA Ops:
  0.6 1.8 copy.22
  2.4 3.0 %multiply_reduce_fusion.5 = f32[2,4,8,64]{3,0,1,2:T(2,128)S(1)} fusion(bf16[2,4,8,64,256]{4,3,0,1,2:T(8,128)(2,1)} %bitcast.28), kind=kLoop, calls=%fused_computation.9 | loop fusion | flops 3141632 | bytes 2113536 | tf_op jit(solution)/shard_map/reduce_sum | solution.py:16
  5.4 0.1 rsqrt.19
  5.5 0.1 multiply_reduce_fusion.6
  5.7 4.0 %fusion.4 = (f32[384]{0:T(512)S(1)}, f32[384,4096]{1,0:T(8,128)}) fusion(f32[4096]{0:T(1024)S(1)} %rsqrt.19, f32[384]{0:T(512)S(1)} %rsqrt_multiply_fusion, bf16[384,256]{1,0:T(8,128)(2,1)S(1)} %copy-done.1, bf16[4096,256]{1,0:T(8,128)(2,1)S(1)} %bitcast.30), kind=kOutput, calls=%fused_computation.29 | convolution fusion | flops 810024576 | bytes 8604672 | tf_op jit(solution)/shard_map/dot_general | solution.py:36
  9.7 30.6 %all_to_all.106 = f32[8,1,384]{2,1,0:T(1,128)S(1)} all-to-all(f32[8,1,384]{2,1,0:T(1,128)S(1)} %broadcast_in_dim.20), channel_id=1, replica_groups=mesh['z'=8,'x'=4,'c'=2,'h'=2,'y'=4] {'h','y'}, dimensions={0} | all-to-all | bytes 24576 | tf_op jit(solution)/shard_map/all_to_all | solution.py:20
  40.3 3.6 %multiply_reduce_fusion.3 = f32[4096]{0:T(1024)S(1)} fusion(f32[384,4096]{1,0:T(8,128)} %get-tuple-element.5, f32[384]{0:T(512)S(1)} %broadcast_divide_fusion.5), kind=kLoop, calls=%fused_computation.5 | loop fusion | flops 3141632 | bytes 6309376 | tf_op jit(solution)/shard_map/reduce_sum | solution.py:44
  44.0 9.4 %all_to_all.107 = f32[8,1,512]{2,1,0:T(1,128)S(1)} all-to-all(f32[8,1,512]{2,1,0:T(1,128)S(1)} %bitcast.34), channel_id=1, replica_groups=mesh['z'=8,'x'=4,'c'=2,'h'=2,'y'=4] {'c','x'}, dimensions={0} | all-to-all | bytes 32768 | tf_op jit(solution)/shard_map/all_to_all | solution.py:20
  53.4 15.3 %all_to_all.108 = f32[8,1,512]{2,1,0:T(1,128)S(1)} all-to-all(f32[8,1,512]{2,1,0:T(1,128)S(1)} %broadcast_in_dim.21), channel_id=1, replica_groups=mesh['z'=8,'x'=4,'c'=2,'h'=2,'y'=4] {'z'}, dimensions={0} | all-to-all | bytes 32768 | tf_op jit(solution)/shard_map/all_to_all | solution.py:20
  68.8 7.6 %all_to_all.109 = f32[8,1,512]{2,1,0:T(1,128)S(1)} all-to-all(f32[8,1,512]{2,1,0:T(1,128)S(1)} %broadcast_in_dim.22), channel_id=1, replica_groups=mesh['z'=8,'x'=4,'c'=2,'h'=2,'y'=4] {'c','x'}, dimensions={0} | all-to-all | bytes 32768 | tf_op jit(solution)/shard_map/all_to_all | solution.py:20
  76.5 3.3 %multiply_reduce_fusion.2 = f32[384]{0:T(512)S(1)} fusion(f32[384,4096]{1,0:T(8,128)} %get-tuple-element.5, f32[4096]{0:T(1024)S(1)} %bitcast.35), kind=kLoop, calls=%fused_computation.4 | loop fusion | flops 3145344 | bytes 6309376 | tf_op jit(solution)/shard_map/reduce_sum | solution.py:40
  79.8 17.3 %all_to_all.110 = f32[8,1,384]{2,1,0:T(1,128)S(1)} all-to-all(f32[8,1,384]{2,1,0:T(1,128)S(1)} %broadcast_in_dim.23), channel_id=1, replica_groups=mesh['z'=8,'x'=4,'c'=2,'h'=2,'y'=4] {'h','y'}, dimensions={0} | all-to-all | bytes 24576 | tf_op jit(solution)/shard_map/all_to_all | solution.py:20
  97.1 3.6 %multiply_reduce_fusion.1 = f32[4096]{0:T(1024)S(1)} fusion(f32[384,4096]{1,0:T(8,128)} %get-tuple-element.5, f32[384]{0:T(512)S(1)} %broadcast_divide_fusion.4), kind=kLoop, calls=%fused_computation.3 | loop fusion | flops 3141632 | bytes 6309376 | tf_op jit(solution)/shard_map/reduce_sum | solution.py:44
  100.8 7.6 %all_to_all.111 = f32[8,1,512]{2,1,0:T(1,128)S(1)} all-to-all(f32[8,1,512]{2,1,0:T(1,128)S(1)} %bitcast.36), channel_id=1, replica_groups=mesh['z'=8,'x'=4,'c'=2,'h'=2,'y'=4] {'c','x'}, dimensions={0} | all-to-all | bytes 32768 | tf_op jit(solution)/shard_map/all_to_all | solution.py:20
  108.5 12.9 %all_to_all.112 = f32[8,1,512]{2,1,0:T(1,128)S(1)} all-to-all(f32[8,1,512]{2,1,0:T(1,128)S(1)} %broadcast_in_dim.24), channel_id=1, replica_groups=mesh['z'=8,'x'=4,'c'=2,'h'=2,'y'=4] {'z'}, dimensions={0} | all-to-all | bytes 32768 | tf_op jit(solution)/shard_map/all_to_all | solution.py:20
  121.4 7.6 %all_to_all.113 = f32[8,1,512]{2,1,0:T(1,128)S(1)} all-to-all(f32[8,1,512]{2,1,0:T(1,128)S(1)} %broadcast_in_dim.25), channel_id=1, replica_groups=mesh['z'=8,'x'=4,'c'=2,'h'=2,'y'=4] {'c','x'}, dimensions={0} | all-to-all | bytes 32768 | tf_op jit(solution)/shard_map/all_to_all | solution.py:20
  129.0 3.3 %multiply_reduce_fusion = f32[384]{0:T(512)S(1)} fusion(f32[384,4096]{1,0:T(8,128)} %get-tuple-element.5, f32[4096]{0:T(1024)S(1)} %bitcast.37), kind=kLoop, calls=%fused_computation.2 | loop fusion | flops 3145344 | bytes 6309376 | tf_op jit(solution)/shard_map/reduce_sum | solution.py:40
  132.4 17.3 %all_to_all.114 = f32[8,1,384]{2,1,0:T(1,128)S(1)} all-to-all(f32[8,1,384]{2,1,0:T(1,128)S(1)} %broadcast_in_dim.26), channel_id=1, replica_groups=mesh['z'=8,'x'=4,'c'=2,'h'=2,'y'=4] {'h','y'}, dimensions={0} | all-to-all | bytes 24576 | tf_op jit(solution)/shard_map/all_to_all | solution.py:20
  149.7 3.6 %multiply_reduce_fusion.4 = f32[4096]{0:T(1024)S(1)} fusion(f32[384,4096]{1,0:T(8,128)} %get-tuple-element.5, f32[384]{0:T(512)S(1)} %broadcast_divide_fusion.3), kind=kLoop, calls=%fused_computation.7 | loop fusion | flops 3141632 | bytes 6309376 | tf_op jit(solution)/shard_map/reduce_sum | solution.py:44
  153.3 7.6 %all_to_all.115 = f32[8,1,512]{2,1,0:T(1,128)S(1)} all-to-all(f32[8,1,512]{2,1,0:T(1,128)S(1)} %bitcast.38), channel_id=1, replica_groups=mesh['z'=8,'x'=4,'c'=2,'h'=2,'y'=4] {'c','x'}, dimensions={0} | all-to-all | bytes 32768 | tf_op jit(solution)/shard_map/all_to_all | solution.py:20
  161.0 12.9 %all_to_all.116 = f32[8,1,512]{2,1,0:T(1,128)S(1)} all-to-all(f32[8,1,512]{2,1,0:T(1,128)S(1)} %broadcast_in_dim.27), channel_id=1, replica_groups=mesh['z'=8,'x'=4,'c'=2,'h'=2,'y'=4] {'z'}, dimensions={0} | all-to-all | bytes 32768 | tf_op jit(solution)/shard_map/all_to_all | solution.py:20
  174.0 0.6 broadcast_in_dim.28
  174.6 3.3 %all-to-all-start.14 = ((f32[8,1,512]{2,1,0:T(1,128)}), f32[8,1,512]{2,1,0:T(1,128)S(1)}, u32[]{:S(2)}, u32[]{:S(2)}) async-start(f32[8,1,512]{2,1,0:T(1,128)} %broadcast_in_dim.28), calls=%async_computation.14 | async-start | bytes 32768 | tf_op jit(solution)/shard_map/all_to_all | solution.py:20
  177.9 6.3 %fusion = f32[4096,256]{1,0:T(8,128)} fusion(bf16[384,256]{1,0:T(8,128)(2,1)S(1)} %copy-done.1, f32[384,4096]{1,0:T(8,128)} %get-tuple-element.5, f32[384]{0:T(512)S(1)} %broadcast_divide_fusion.3), kind=kOutput, calls=%fused_computation.10 | convolution fusion | flops 808452096 | bytes 10683904 | tf_op jit(solution)/shard_map/dot_general | solution.py:56
  184.2 0.0 all-to-all-done.14
  184.2 5.6 %all-to-all-start.9 = ((f32[2,2048,256]{2,1,0:T(8,128)}), f32[2,2048,256]{2,1,0:T(8,128)}, u32[]{:S(2)}, u32[]{:S(2)}) async-start(f32[2,2048,256]{2,1,0:T(8,128)} %bitcast.26), calls=%async_computation.9 | async-start | bytes 8388608 | tf_op jit(solution)/shard_map/all_to_all | solution.py:20
  189.8 3.7 %convert_reduce_fusion = (f32[384]{0:T(512)S(1)}, bf16[384,4096]{1,0:T(8,128)(2,1)S(1)}) fusion(f32[4096]{0:T(1024)S(1)} %bitcast.33, f32[384,4096]{1,0:T(8,128)} %get-tuple-element.5, f32[384]{0:T(512)S(1)} %broadcast_divide_fusion.3), kind=kLoop, calls=%fused_computation | loop fusion | flops 7863936 | bytes 9456640 | tf_op jit(solution)/shard_map/reduce_sum | solution.py:64
  193.5 0.1 reshape.144
  193.6 2.6 fusion.5
  196.1 0.8 select_maximum_fusion
  196.9 0.0 all-to-all-done.9
  196.9 5.5 %all-to-all-start.15 = ((f32[4,104,256]{2,1,0:T(8,128)}), f32[4,104,256]{2,1,0:T(8,128)S(1)}, u32[]{:S(2)}, u32[]{:S(2)}) async-start(f32[4,104,256]{2,1,0:T(8,128)} %select_maximum_fusion), calls=%async_computation.15 | async-start | bytes 851968 | tf_op jit(solution)/shard_map/all_to_all | solution.py:20
  202.4 4.1 %reduce_sum.212 = f32[2048,256]{1,0:T(8,128)} reduce(f32[2,2048,256]{2,1,0:T(8,128)} %all-to-all-done.9, f32[]{:T(128)} %constant.13.clone.1), dimensions={0}, to_apply=%region_14.0 | reduce | flops 524288 | bytes 6291460 | tf_op jit(solution)/shard_map/reduce_sum | solution.py:57
  206.5 3.2 %all-to-all-done.15 = f32[4,104,256]{2,1,0:T(8,128)S(1)} async-done(((f32[4,104,256]{2,1,0:T(8,128)}), f32[4,104,256]{2,1,0:T(8,128)S(1)}, u32[]{:S(2)}, u32[]{:S(2)}) %all-to-all-start.15) | async-done | bytes 426016 | tf_op jit(solution)/shard_map/all_to_all | solution.py:20
  209.7 4.7 %all-to-all-start.10 = ((f32[4,512,256]{2,1,0:T(8,128)}), f32[4,512,256]{2,1,0:T(8,128)S(1)}, u32[]{:S(2)}, u32[]{:S(2)}) async-start(f32[4,512,256]{2,1,0:T(8,128)} %bitcast.9), calls=%async_computation.10 | async-start | bytes 4194304 | tf_op jit(solution)/shard_map/all_to_all | solution.py:20
  214.4 2.5 collective-permute-start
  216.9 12.8 %collective-permute-done = f32[104,256]{1,0:T(8,128)S(1)} collective-permute-done((f32[104,256]{1,0:T(8,128)S(1)}, f32[104,256]{1,0:T(8,128)S(1)}, u32[]{:S(2)}, u32[]{:S(2)}) %collective-permute-start) | collective-permute-done | bytes 106528 | tf_op jit(solution)/shard_map/ppermute | solution.py:75
  229.8 0.1 slice_divide_fusion
  229.9 10.7 %all-to-all-done.10 = f32[4,512,256]{2,1,0:T(8,128)S(1)} async-done(((f32[4,512,256]{2,1,0:T(8,128)}), f32[4,512,256]{2,1,0:T(8,128)S(1)}, u32[]{:S(2)}, u32[]{:S(2)}) %all-to-all-start.10) | async-done | bytes 2097184 | tf_op jit(solution)/shard_map/all_to_all | solution.py:20
  240.6 0.8 broadcast_in_dim.29
  241.4 5.5 %all-to-all-start.16 = ((f32[4,96,256]{2,1,0:T(8,128)}), f32[4,96,256]{2,1,0:T(8,128)S(1)}, u32[]{:S(2)}, u32[]{:S(2)}) async-start(f32[4,96,256]{2,1,0:T(8,128)} %broadcast_in_dim.29), calls=%async_computation.16 | async-start | bytes 786432 | tf_op jit(solution)/shard_map/all_to_all | solution.py:20
  246.9 1.0 reduce_sum.213
  247.8 4.4 %all-to-all-done.16 = f32[4,96,256]{2,1,0:T(8,128)S(1)} async-done(((f32[4,96,256]{2,1,0:T(8,128)}), f32[4,96,256]{2,1,0:T(8,128)S(1)}, u32[]{:S(2)}, u32[]{:S(2)}) %all-to-all-start.16) | async-done | bytes 393248 | tf_op jit(solution)/shard_map/all_to_all | solution.py:20
  252.2 3.5 %all-to-all-start.11 = ((f32[8,64,256]{2,1,0:T(8,128)}), f32[8,64,256]{2,1,0:T(8,128)S(1)}, u32[]{:S(2)}, u32[]{:S(2)}) async-start(f32[8,64,256]{2,1,0:T(8,128)} %bitcast.10), calls=%async_computation.11 | async-start | bytes 1048576 | tf_op jit(solution)/shard_map/all_to_all | solution.py:20
  255.7 0.1 dynamic-slice_multiply_fusion
  255.8 26.5 %all-to-all-done.11 = f32[8,64,256]{2,1,0:T(8,128)S(1)} async-done(((f32[8,64,256]{2,1,0:T(8,128)}), f32[8,64,256]{2,1,0:T(8,128)S(1)}, u32[]{:S(2)}, u32[]{:S(2)}) %all-to-all-start.11) | async-done | bytes 524320 | tf_op jit(solution)/shard_map/all_to_all | solution.py:20
  282.3 0.7 broadcast_multiply_fusion
  283.0 0.7 copy.48
  (33 shorter events, 0.5 us)
Async XLA Ops:
  0.6 4.9 %copy-start.1 = (bf16[384,256]{1,0:T(8,128)(2,1)S(1)}, bf16[384,256]{1,0:T(8,128)(2,1)}, u32[]{:S(2)}) copy-start(bf16[384,256]{1,0:T(8,128)(2,1)} %param.2) | copy-start | bytes 589828
  2.4 7.3 %copy-start = (bf16[2,4,8,64,256]{4,3,2,1,0:T(8,128)(2,1)}, bf16[2,4,8,64,256]{4,3,2,1,0:T(8,128)(2,1)S(1)}, u32[]{:S(2)}) copy-start(bf16[2,4,8,64,256]{4,3,2,1,0:T(8,128)(2,1)S(1)} %copy.22) | copy-start | bytes 6291460
  174.6 9.6 %all-to-all-start.14 = ((f32[8,1,512]{2,1,0:T(1,128)}), f32[8,1,512]{2,1,0:T(1,128)S(1)}, u32[]{:S(2)}, u32[]{:S(2)}) async-start(f32[8,1,512]{2,1,0:T(1,128)} %broadcast_in_dim.28), calls=%async_computation.14 | async-start | bytes 32768 | tf_op jit(solution)/shard_map/all_to_all | solution.py:20
  184.2 12.7 %all-to-all-start.9 = ((f32[2,2048,256]{2,1,0:T(8,128)}), f32[2,2048,256]{2,1,0:T(8,128)}, u32[]{:S(2)}, u32[]{:S(2)}) async-start(f32[2,2048,256]{2,1,0:T(8,128)} %bitcast.26), calls=%async_computation.9 | async-start | bytes 8388608 | tf_op jit(solution)/shard_map/all_to_all | solution.py:20
  196.9 12.8 %all-to-all-start.15 = ((f32[4,104,256]{2,1,0:T(8,128)}), f32[4,104,256]{2,1,0:T(8,128)S(1)}, u32[]{:S(2)}, u32[]{:S(2)}) async-start(f32[4,104,256]{2,1,0:T(8,128)} %select_maximum_fusion), calls=%async_computation.15 | async-start | bytes 851968 | tf_op jit(solution)/shard_map/all_to_all | solution.py:20
  209.7 30.9 %all-to-all-start.10 = ((f32[4,512,256]{2,1,0:T(8,128)}), f32[4,512,256]{2,1,0:T(8,128)S(1)}, u32[]{:S(2)}, u32[]{:S(2)}) async-start(f32[4,512,256]{2,1,0:T(8,128)} %bitcast.9), calls=%async_computation.10 | async-start | bytes 4194304 | tf_op jit(solution)/shard_map/all_to_all | solution.py:20
  214.4 15.3 %collective-permute-start = (f32[104,256]{1,0:T(8,128)S(1)}, f32[104,256]{1,0:T(8,128)S(1)}, u32[]{:S(2)}, u32[]{:S(2)}) collective-permute-start(f32[104,256]{1,0:T(8,128)S(1)} %reduce_sum.219), channel_id=1, source_target_pairs={{0,4},{4,0},{1,5},{5,1},{2,6},{6,2},{3,7},{7,3},{8,12},{12,8},{9,1... | collective-permute-start | bytes 319496 | tf_op jit(solution)/shard_map/ppermute | solution.py:75
  241.4 10.8 %all-to-all-start.16 = ((f32[4,96,256]{2,1,0:T(8,128)}), f32[4,96,256]{2,1,0:T(8,128)S(1)}, u32[]{:S(2)}, u32[]{:S(2)}) async-start(f32[4,96,256]{2,1,0:T(8,128)} %broadcast_in_dim.29), calls=%async_computation.16 | async-start | bytes 786432 | tf_op jit(solution)/shard_map/all_to_all | solution.py:20
  252.2 30.1 %all-to-all-start.11 = ((f32[8,64,256]{2,1,0:T(8,128)}), f32[8,64,256]{2,1,0:T(8,128)S(1)}, u32[]{:S(2)}, u32[]{:S(2)}) async-start(f32[8,64,256]{2,1,0:T(8,128)} %bitcast.10), calls=%async_computation.11 | async-start | bytes 1048576 | tf_op jit(solution)/shard_map/all_to_all | solution.py:20

commit v2 on v1

v2 whole, which is shorter than its diff:
```python
import functools

import jax
import jax.numpy as jnp
from jax import lax
from jax.experimental import pallas as pl
from jax.experimental.pallas import tpu as pltpu
from jax.sharding import Mesh, PartitionSpec as P

ITERS = 3
SHARP = 48.0
EPSILON = 1e-06

AXES = ("z", "x", "c", "h", "y")
Z, X, C, H, Y = 8, 4, 2, 2, 4
BLOCKS = C * X
LANES = 128
PAD = 8


def exchange(blocks, axes):
    return lax.all_to_all(blocks, axes, 0, 0, tiled=True)


def spread(block, axes, count):
    return exchange(jnp.broadcast_to(block[None], (count,) + block.shape), axes)


def params():
    return pltpu.CompilerParams(vmem_limit_bytes=24 << 20)


def column_of(row):
    return jnp.broadcast_to(row, (LANES, row.shape[1])).T


def row_of(partial):
    return jnp.sum(partial.T, axis=0, keepdims=True)


def fold(product):
    total = product[:, :LANES]
    for start in range(LANES, product.shape[1], LANES):
        total = total + product[:, start : start + LANES]
    return total


def widen(column, width):
    return jnp.concatenate([column] * (width // LANES), axis=1)


def place(b):
    return (b % X) * C + b // X


def setup_kernel(latents_ref, codes_ref, tile_ref, rows_ref, scale_ref, total_ref):
    step = pl.program_id(0)
    latents = latents_ref[...]
    width = latents.shape[1]

    @pl.when(step == 0)
    def _():
        floats = latents.astype(jnp.float32)
        mean = jnp.sum(floats * floats, axis=1, keepdims=True) * (1.0 / width)
        scale_ref[...] = jnp.broadcast_to(lax.rsqrt(mean + EPSILON) * (SHARP / width), scale_ref.shape)
        total_ref[...] = jnp.zeros_like(total_ref)

    codes = codes_ref[...].reshape(-1, width)
    count = codes.shape[0]
    floats = codes.astype(jnp.float32)
    squares = floats * floats
    high = squares.astype(jnp.bfloat16)
    low = (squares - high.astype(jnp.float32)).astype(jnp.bfloat16)
    ones = jnp.ones((8, width), jnp.bfloat16)
    across = (((1,), (1,)), ((), ()))
    dot = functools.partial(lax.dot_general, dimension_numbers=across, preferred_element_type=jnp.float32)
    sums = dot(ones, high) + dot(ones, low)
    code_norm = lax.rsqrt(sums[:1] * (1.0 / width) + EPSILON)
    inner = dot(latents, codes)
    tile = jnp.exp(inner * widen(scale_ref[...], count) * code_norm)
    tile_ref[...] = tile
    total_ref[...] += fold(tile)

    @pl.when(step == pl.num_programs(0) - 1)
    def _():
        rows_ref[...] = jnp.broadcast_to(row_of(total_ref[...])[None], rows_ref.shape)


def rows_kernel(columns_ref, tile_ref, rows_ref, total_ref):
    step = pl.program_id(0)

    @pl.when(step == 0)
    def _():
        total_ref[...] = jnp.zeros_like(total_ref)

    total_ref[...] += fold(tile_ref[...] * columns_ref[...])

    @pl.when(step == pl.num_programs(0) - 1)
    def _():
        rows_ref[...] = jnp.broadcast_to(row_of(total_ref[...])[None], rows_ref.shape)


def row_scale_of(parts_ref):
    return column_of(1.0 / jnp.sum(parts_ref[...], axis=0))


def columns_kernel(parts_ref, tile_ref, columns_ref, scale_ref):
    @pl.when(pl.program_id(0) == 0)
    def _():
        scale_ref[...] = row_scale_of(parts_ref)

    tile = tile_ref[...]
    columns_ref[...] = jnp.sum(tile * widen(scale_ref[...], tile.shape[1]), axis=0, keepdims=True)


def targets_kernel(half_ref, parts_ref, latents_ref, tile_ref, *refs):
    added_ref, out_ref, scale_ref = refs if len(refs) == 3 else (None,) + refs

    @pl.when(pl.program_id(0) == 0)
    def _():
        scale_ref[...] = row_scale_of(parts_ref)

    tile = tile_ref[...]
    weighted = (tile * widen(scale_ref[...], tile.shape[1])).astype(jnp.bfloat16)
    summed = lax.dot_general(
        weighted, latents_ref[...], (((0,), (0,)), ((), ())), preferred_element_type=jnp.float32
    )
    out_ref[...] = summed if added_ref is None else summed + added_ref[...]


def final_kernel(parts_ref, columns_ref, codes_ref, tile_ref, out_ref, scale_ref, numer_ref, mass_ref):
    step = pl.program_id(0)

    @pl.when(step == 0)
    def _():
        scale_ref[...] = row_scale_of(parts_ref)
        numer_ref[...] = jnp.zeros_like(numer_ref)
        mass_ref[...] = jnp.zeros_like(mass_ref)

    tile = tile_ref[...]
    plan = (widen(scale_ref[...], tile.shape[1]) * tile * columns_ref[...]).astype(jnp.bfloat16)
    mass_ref[...] += fold(plan.astype(jnp.float32))
    codes = codes_ref[...].reshape(tile.shape[1], -1)
    numer_ref[...] += jnp.dot(plan, codes, preferred_element_type=jnp.float32)

    @pl.when(step == pl.num_programs(0) - 1)
    def _():
        tokens, width = numer_ref.shape
        group = tokens // Y
        mass = row_of(mass_ref[...])
        mass = jnp.concatenate([mass, jnp.zeros((1, 2 * width - tokens), jnp.float32)], axis=1)
        extra = jnp.concatenate(
            [mass[:, :width], mass[:, width:], jnp.zeros((PAD - 2, width), jnp.float32)], axis=0
        )
        for y in range(Y):
            out_ref[y, :group, :] = numer_ref[y * group : (y + 1) * group, :]
            out_ref[y, group:, :] = extra


def f32(*shape):
    return jax.ShapeDtypeStruct(shape, jnp.float32)


def whole(*shape):
    return pl.BlockSpec(shape, lambda *_: (0,) * len(shape))


def cost(flops, moved, exps=0):
    return pl.CostEstimate(flops=flops, bytes_accessed=moved, transcendentals=exps)


def per_device(latents, codebook):
    token_count, width = latents.shape
    code_count = codebook.shape[0]
    total_tokens = token_count * Z * X * C
    total_codes = code_count * H * Y
    share = code_count // (Z * X * C)
    block = code_count // BLOCKS
    size = token_count * code_count

    codes = codebook.reshape(Z, X * C, share, width)
    codes_spec = pl.BlockSpec((Z, None, share, width), lambda b: (0, place(b), 0, 0))
    latents_spec = whole(token_count, width)
    tile_spec = pl.BlockSpec((token_count, block), lambda b: (0, b))
    rows_spec = whole(H * Y, 1, token_count)
    columns_spec = pl.BlockSpec((None, 1, block), lambda b: (b, 0, 0))
    per_token = pltpu.VMEM((token_count, LANES), jnp.float32)
    rows_shape = f32(H * Y, 1, token_count)
    columns_shape = f32(BLOCKS, 1, block)

    tile, part = pl.pallas_call(
        setup_kernel,
        grid=(BLOCKS,),
        in_specs=[latents_spec, codes_spec],
        out_specs=[tile_spec, rows_spec],
        out_shape=[f32(token_count, code_count), rows_shape],
        scratch_shapes=[per_token, per_token],
        compiler_params=params(),
        cost_estimate=cost(2 * size * width, 4 * size, size),
        name="setup",
    )(latents, codes)

    def rows(columns):
        return pl.pallas_call(
            rows_kernel,
            grid=(BLOCKS,),
            in_specs=[columns_spec, tile_spec],
            out_specs=rows_spec,
            out_shape=rows_shape,
            scratch_shapes=[per_token],
            compiler_params=params(),
            cost_estimate=cost(2 * size, 4 * size),
            name="rows",
        )(columns, tile)

    def columns(parts):
        return pl.pallas_call(
            columns_kernel,
            grid=(BLOCKS,),
            in_specs=[rows_spec, tile_spec],
            out_specs=columns_spec,
            out_shape=columns_shape,
            scratch_shapes=[per_token],
            compiler_params=params(),
            cost_estimate=cost(2 * size, 4 * size),
            name="columns",
        )(parts, tile)

    def targets_part(half, parts, added=None):
        spec = pl.BlockSpec((block, width), lambda i, half: (i, 0))
        more, more_specs = ((), ()) if added is None else ((added,), (spec,))
        return pl.pallas_call(
            targets_kernel,
            grid_spec=pltpu.PrefetchScalarGridSpec(
                num_scalar_prefetch=1,
                grid=(X,),
                in_specs=[
                    rows_spec,
                    latents_spec,
                    pl.BlockSpec((token_count, block), lambda i, half: (0, half[0] * X + i)),
                    *more_specs,
                ],
                out_specs=spec,
                scratch_shapes=[per_token],
            ),
            out_shape=f32(X * block, width),
            compiler_params=params(),
            cost_estimate=cost(size * width, 4 * size),
            name="targets" if added is None else "targets_added",
        )(half, parts, latents, tile, *more)

    for sweep_index in range(ITERS):
        parts = exchange(part, ("h", "y"))
        sums = jnp.sum(exchange(columns(parts), ("c", "x")), axis=0)
        total = jnp.sum(spread(sums, "z", Z), axis=0)
        mine = total_tokens / total_codes / total
        col_scale = spread(mine, ("c", "x"), BLOCKS)
        if sweep_index < ITERS - 1:
            part = rows(col_scale)

    core = lax.axis_index("c").reshape(1)
    sent = targets_part(1 - core, parts)
    summed = targets_part(core, parts, lax.ppermute(sent, "c", [(0, 1), (1, 0)]))
    summed = jnp.sum(exchange(summed.reshape(X, block, width), "x"), axis=0)
    summed = jnp.sum(exchange(summed.reshape(Z, share, width), "z"), axis=0)
    own = lax.dynamic_slice(mine, (0, lax.axis_index("z") * share), (1, share))[0]
    targets = summed * (own * (total_codes / total_tokens))[:, None]

    group = token_count // Y
    packed = pl.pallas_call(
        final_kernel,
        grid=(BLOCKS,),
        in_specs=[rows_spec, columns_spec, codes_spec, tile_spec],
        out_specs=whole(Y, group + PAD, width),
        out_shape=f32(Y, group + PAD, width),
        scratch_shapes=[per_token, pltpu.VMEM((token_count, width), jnp.float32), per_token],
        compiler_params=params(),
        cost_estimate=cost(2 * size * width, 4 * size),
        name="final",
    )(parts, col_scale, codes, tile)
    packed = jnp.sum(exchange(packed, "y"), axis=0)
    packed = packed + lax.ppermute(packed, "h", [(0, 1), (1, 0)])
    mass = packed[group : group + 2].reshape(2 * width)[:token_count]
    rebuilt = spread(packed[:group], "y", Y).reshape(token_count, width) / mass[:, None]
    return (targets, rebuilt)


def solution(mesh):
    fine = Mesh(mesh.devices.reshape(Z, X, C, H, Y), AXES)
    return jax.shard_map(
        per_device,
        mesh=fine,
        in_specs=(P(("z", "x", "c"), None), P(("h", "y"), None)),
        out_specs=(P(("h", "y", "z", "x", "c"), None), P(("z", "x", "c"), None)),
        check_vma=False,
    )
```

time: 286 us -> 278 us (0.972)
  other arithmetic: 31.5 us -> 2.89 us
  Pallas kernels: 0 us -> 23.5 us
  local copies, waits for them, and re-layouts: 4.17 us -> 17.3 us
  matrix products: 12.9 us -> 0 us
  waiting for transfers between devices: 57.6 us -> 67 us
  blocking collectives: 146 us -> 137 us
  starting transfers between devices: 30.6 us -> 27.2 us
    reduce_sum x19 -> x7, other arithmetic: 29.7 us -> 1.13 us  [the longest x1 0.95 us: per_device(): summed = jnp.sum(exchange(summed.reshape(X, block, width), 'x'), axis=0)]
    pallas_call x0 -> x9, Pallas kernels: none -> 23.5 us  [the longest x2 7.71 us: targets_part(): pl.pallas_call(targets_kernel, grid_spec=pltpu.PrefetchScalarGridSpec(num...]
    unnamed x5 -> x24, local copies, waits for them, and re-layouts: 0.75 us -> 16.5 us
    dot_general x3 -> x0, matrix products: 12.9 us -> none  [the longest x1 6.26 us: per_device(): lax.dot_general(weighted, latents, (((0,), (0,)), ((), ())), preferred_el...]
    all_to_all x11, blocking collectives: 146 us -> 137 us  [exchange(): return lax.all_to_all(blocks, axes, 0, 0, tiled=True)]
    all_to_all x6 -> x5, waiting for transfers between devices: 44.8 us -> 54.1 us  [exchange(): return lax.all_to_all(blocks, axes, 0, 0, tiled=True)]
    all_to_all x6 -> x5, starting transfers between devices: 28.1 us -> 22.7 us  [exchange(): return lax.all_to_all(blocks, axes, 0, 0, tiled=True)]
  transfers between devices with their start and end apart: 7 -> 7, of which waited for: 5 -> 5; matrix products, arithmetic and copies ran while one was open for 7% -> 1% of each run, Pallas kernels for 0% -> 4%
where the time goes in v2:
time: 278 us; the launch traced here: 275 us
  blocking collectives  137 us (49%)
  waiting for transfers between devices  67 us (24%)
  starting transfers between devices  27.2 us (10%)
  Pallas kernels  23.5 us (8%)
  local copies, waits for them, and re-layouts  17.3 us (6%)
  other arithmetic  2.89 us (1%)
    all_to_all x11, blocking collectives, exchange(): return lax.all_to_all(blocks, axes, 0, 0, tiled=True)  137 us
    all_to_all x5, waiting for transfers between devices, exchange(): return lax.all_to_all(blocks, axes, 0, 0, tiled=True)  54.1 us
    all_to_all x5, starting transfers between devices, exchange(): return lax.all_to_all(blocks, axes, 0, 0, tiled=True)  22.7 us
    unnamed x24, local copies, waits for them, and re-layouts  16.5 us
    ppermute x1, waiting for transfers between devices, per_device(): packed = packed + lax.ppermute(packed, 'h', [(0, 1), (1, 0)])  12.9 us
    pallas_call x2, Pallas kernels, targets_part(): pl.pallas_call(targets_kernel, grid_spec=pltpu.PrefetchScalarGridSpec(num...  7.71 us
  transfers between devices with their start and end apart: 7, of which 5 were waited for; matrix products, arithmetic and copies ran while one was open for 1% of the time, Pallas kernels for 4%

profile of v2, /device:TPU:24, one launch (start us, length us, event | category | flops | bytes accessed | tf_op | source)
XLA Modules:
  0.0 275.5 jit_solution(12553068311921888600)
XLA Ops:
  0.6 0.0 copy-start.7
  0.6 1.6 copy-done.7
  2.2 0.9 copy-done.9
  3.2 5.1 %setup.1 = (f32[384,4096]{1,0:T(8,128)S(1)}, f32[8,1,384]{2,1,0:T(1,128)S(1)}) custom-call(bf16[384,256]{1,0:T(8,128)(2,1)S(1)} %copy-done.9, bf16[8,8,64,256]{3,2,1,0:T(8,128)(2,1)S(1)} %bitcast.10), custom_call_target="tpu_custom_call" | custom-call | flops 805306368 | bytes 6291456 | tf_op jit(solution)/shard_map/setup/pallas_call | solution.py:191
  8.3 30.6 %all_to_all.80.parts_ref = f32[8,1,384]{2,1,0:T(1,128)S(1)} all-to-all(f32[8,1,384]{2,1,0:T(1,128)S(1)} %get-tuple-element.4), channel_id=1, replica_groups=mesh['z'=8,'x'=4,'c'=2,'h'=2,'y'=4] {'h','y'}, dimensions={0} | all-to-all | bytes 24576 | tf_op jit(solution)/shard_map/all_to_all | solution.py:22
  38.8 1.2 columns.3
  40.1 9.4 %all_to_all.81 = f32[8,1,512]{2,1,0:T(1,128)S(1)} all-to-all(f32[8,1,512]{2,1,0:T(1,128)S(1)} %columns.3), channel_id=1, replica_groups=mesh['z'=8,'x'=4,'c'=2,'h'=2,'y'=4] {'c','x'}, dimensions={0} | all-to-all | bytes 32768 | tf_op jit(solution)/shard_map/all_to_all | solution.py:22
  49.5 15.3 %all_to_all.82 = f32[8,1,512]{2,1,0:T(1,128)S(1)} all-to-all(f32[8,1,512]{2,1,0:T(1,128)S(1)} %broadcast_in_dim.14), channel_id=1, replica_groups=mesh['z'=8,'x'=4,'c'=2,'h'=2,'y'=4] {'z'}, dimensions={0} | all-to-all | bytes 32768 | tf_op jit(solution)/shard_map/all_to_all | solution.py:22
  64.9 7.6 %all_to_all.83.columns_ref = f32[8,1,512]{2,1,0:T(1,128)S(1)} all-to-all(f32[8,1,512]{2,1,0:T(1,128)S(1)} %broadcast_in_dim.15), channel_id=1, replica_groups=mesh['z'=8,'x'=4,'c'=2,'h'=2,'y'=4] {'c','x'}, dimensions={0} | all-to-all | bytes 32768 | tf_op jit(solution)/shard_map/all_to_all | solution.py:22
  72.5 2.8 %copy-done.1 = f32[384,4096]{1,0:T(8,128)S(1)} copy-done((f32[384,4096]{1,0:T(8,128)S(1)}, f32[384,4096]{1,0:T(8,128)}, u32[]{:S(2)}) %copy-start.1) | copy-done | bytes 6291480
  75.3 1.2 rows.2
  76.5 17.3 %all_to_all.84.parts_ref = f32[8,1,384]{2,1,0:T(1,128)S(1)} all-to-all(f32[8,1,384]{2,1,0:T(1,128)S(1)} %rows.2), channel_id=1, replica_groups=mesh['z'=8,'x'=4,'c'=2,'h'=2,'y'=4] {'h','y'}, dimensions={0} | all-to-all | bytes 24576 | tf_op jit(solution)/shard_map/all_to_all | solution.py:22
  93.8 1.2 columns.4
  95.0 7.6 %all_to_all.85 = f32[8,1,512]{2,1,0:T(1,128)S(1)} all-to-all(f32[8,1,512]{2,1,0:T(1,128)S(1)} %columns.4), channel_id=1, replica_groups=mesh['z'=8,'x'=4,'c'=2,'h'=2,'y'=4] {'c','x'}, dimensions={0} | all-to-all | bytes 32768 | tf_op jit(solution)/shard_map/all_to_all | solution.py:22
  102.7 12.9 %all_to_all.86 = f32[8,1,512]{2,1,0:T(1,128)S(1)} all-to-all(f32[8,1,512]{2,1,0:T(1,128)S(1)} %broadcast_in_dim.16), channel_id=1, replica_groups=mesh['z'=8,'x'=4,'c'=2,'h'=2,'y'=4] {'z'}, dimensions={0} | all-to-all | bytes 32768 | tf_op jit(solution)/shard_map/all_to_all | solution.py:22
  115.6 7.6 %all_to_all.87.columns_ref = f32[8,1,512]{2,1,0:T(1,128)S(1)} all-to-all(f32[8,1,512]{2,1,0:T(1,128)S(1)} %broadcast_in_dim.17), channel_id=1, replica_groups=mesh['z'=8,'x'=4,'c'=2,'h'=2,'y'=4] {'c','x'}, dimensions={0} | all-to-all | bytes 32768 | tf_op jit(solution)/shard_map/all_to_all | solution.py:22
  123.3 2.8 %copy-done.2 = f32[384,4096]{1,0:T(8,128)S(1)} copy-done((f32[384,4096]{1,0:T(8,128)S(1)}, f32[384,4096]{1,0:T(8,128)}, u32[]{:S(2)}) %copy-start.2) | copy-done | bytes 6291480
  126.1 1.8 rows.3
  127.8 5.3 %all-to-all-start.8 = ((f32[8,1,384]{2,1,0:T(1,128)}), f32[8,1,384]{2,1,0:T(1,128)S(1)}, u32[]{:S(2)}, u32[]{:S(2)}) async-start(f32[8,1,384]{2,1,0:T(1,128)} %rows.3), calls=%async_computation.8 | async-start | bytes 24576 | tf_op jit(solution)/shard_map/all_to_all | solution.py:22
  133.2 12.9 %all-to-all-done.8.parts_ref = f32[8,1,384]{2,1,0:T(1,128)S(1)} async-done(((f32[8,1,384]{2,1,0:T(1,128)}), f32[8,1,384]{2,1,0:T(1,128)S(1)}, u32[]{:S(2)}, u32[]{:S(2)}) %all-to-all-start.8) | async-done | bytes 12320 | tf_op jit(solution)/shard_map/all_to_all | solution.py:22
  146.0 2.8 %copy-done.3 = f32[384,4096]{1,0:T(8,128)S(1)} copy-done((f32[384,4096]{1,0:T(8,128)S(1)}, f32[384,4096]{1,0:T(8,128)}, u32[]{:S(2)}) %copy-start.3) | copy-done | bytes 6291480
  148.8 3.0 %targets.1 = f32[2048,256]{1,0:T(8,128)} custom-call(s32[1]{0:T(128)S(6)} %sub.3.half_ref, f32[8,1,384]{2,1,0:T(1,128)S(1)} %all-to-all-done.8.parts_ref, bf16[384,256]{1,0:T(8,128)(2,1)S(1)} %copy-done.10, f32[384,4096]{1,0:T(8,128)S(1)} %copy-done.3), custom_call_target="tpu_custom_call" | custom-call | flops 402653184 | bytes 6291456 | tf_op jit(solution)/shard_map/targets/pallas_call | solution.py:232
  151.9 2.0 collective-permute-start
  153.9 1.2 columns.5
  155.2 7.7 %all_to_all.88 = f32[8,1,512]{2,1,0:T(1,128)S(1)} all-to-all(f32[8,1,512]{2,1,0:T(1,128)S(1)} %columns.5), channel_id=1, replica_groups=mesh['z'=8,'x'=4,'c'=2,'h'=2,'y'=4] {'c','x'}, dimensions={0} | all-to-all | bytes 32768 | tf_op jit(solution)/shard_map/all_to_all | solution.py:22
  162.9 12.9 %all_to_all.89 = f32[8,1,512]{2,1,0:T(1,128)S(1)} all-to-all(f32[8,1,512]{2,1,0:T(1,128)S(1)} %broadcast_in_dim.18), channel_id=1, replica_groups=mesh['z'=8,'x'=4,'c'=2,'h'=2,'y'=4] {'z'}, dimensions={0} | all-to-all | bytes 32768 | tf_op jit(solution)/shard_map/all_to_all | solution.py:22
  175.8 7.6 %all_to_all.90.columns_ref = f32[8,1,512]{2,1,0:T(1,128)S(1)} all-to-all(f32[8,1,512]{2,1,0:T(1,128)S(1)} %broadcast_in_dim.19), channel_id=1, replica_groups=mesh['z'=8,'x'=4,'c'=2,'h'=2,'y'=4] {'c','x'}, dimensions={0} | all-to-all | bytes 32768 | tf_op jit(solution)/shard_map/all_to_all | solution.py:22
  183.5 0.0 copy-done.8
  183.5 2.8 %copy-done.5 = f32[384,4096]{1,0:T(8,128)S(1)} copy-done((f32[384,4096]{1,0:T(8,128)S(1)}, f32[384,4096]{1,0:T(8,128)}, u32[]{:S(2)}) %copy-start.5) | copy-done | bytes 6291480
  186.3 4.1 %final.1 = f32[4,104,256]{2,1,0:T(8,128)} custom-call(f32[8,1,384]{2,1,0:T(1,128)S(1)} %all-to-all-done.8.parts_ref, f32[8,1,512]{2,1,0:T(1,128)S(1)} %all_to_all.90.columns_ref, bf16[8,8,64,256]{3,2,1,0:T(8,128)(2,1)S(1)} %bitcast.11, f32[384,4096]{1,0:T(8,128)S(1)} %copy-done.5), custom_call_target="tpu_custom_call" | custom-call | flops 805306368 | bytes 6291456 | tf_op jit(solution)/shard_map/final/pallas_call | solution.py:270
  190.4 5.5 %all-to-all-start.14 = ((f32[4,104,256]{2,1,0:T(8,128)}), f32[4,104,256]{2,1,0:T(8,128)S(1)}, u32[]{:S(2)}, u32[]{:S(2)}) async-start(f32[4,104,256]{2,1,0:T(8,128)} %final.1), calls=%async_computation.14 | async-start | bytes 851968 | tf_op jit(solution)/shard_map/all_to_all | solution.py:22
  195.9 0.0 collective-permute-done.refs_0_
  195.9 2.8 %copy-done.6 = f32[384,4096]{1,0:T(8,128)S(1)} copy-done((f32[384,4096]{1,0:T(8,128)S(1)}, f32[384,4096]{1,0:T(8,128)}, u32[]{:S(2)}) %copy-start.6) | copy-done | bytes 6291480
  198.7 4.7 %targets_added.1 = f32[2048,256]{1,0:T(8,128)} custom-call(s32[1]{0:T(128)} %bitcast.half_ref, f32[8,1,384]{2,1,0:T(1,128)S(1)} %all-to-all-done.8.parts_ref, bf16[384,256]{1,0:T(8,128)(2,1)S(1)} %copy-done.10, f32[384,4096]{1,0:T(8,128)S(1)} %copy-done.6, f32[2048,256]{1,0:T(8,128)} %collective-permute-done.refs_0_), custom_call_target="tpu_custom_call" | custom-call | flops 402653184 | bytes 6291456 | tf_op jit(solution)/shard_map/targets_added/pallas_call | solution.py:232
  203.4 0.0 all-to-all-done.14
  203.4 3.6 %all-to-all-start.9 = ((f32[4,512,256]{2,1,0:T(8,128)}), f32[4,512,256]{2,1,0:T(8,128)S(1)}, u32[]{:S(2)}, u32[]{:S(2)}) async-start(f32[4,512,256]{2,1,0:T(8,128)} %bitcast.2), calls=%async_computation.9 | async-start | bytes 4194304 | tf_op jit(solution)/shard_map/all_to_all | solution.py:22
  207.0 2.5 collective-permute-start.1
  209.5 12.9 %collective-permute-done.1 = f32[104,256]{1,0:T(8,128)S(1)} collective-permute-done((f32[104,256]{1,0:T(8,128)S(1)}, f32[104,256]{1,0:T(8,128)S(1)}, u32[]{:S(2)}, u32[]{:S(2)}) %collective-permute-start.1) | collective-permute-done | bytes 106528 | tf_op jit(solution)/shard_map/ppermute | solution.py:282
  222.5 11.1 %all-to-all-done.9 = f32[4,512,256]{2,1,0:T(8,128)S(1)} async-done(((f32[4,512,256]{2,1,0:T(8,128)}), f32[4,512,256]{2,1,0:T(8,128)S(1)}, u32[]{:S(2)}, u32[]{:S(2)}) %all-to-all-start.9) | async-done | bytes 2097184 | tf_op jit(solution)/shard_map/all_to_all | solution.py:22
  233.6 0.8 broadcast_in_dim.20
  234.4 4.8 %all-to-all-start.15 = ((f32[4,96,256]{2,1,0:T(8,128)}), f32[4,96,256]{2,1,0:T(8,128)S(1)}, u32[]{:S(2)}, u32[]{:S(2)}) async-start(f32[4,96,256]{2,1,0:T(8,128)} %broadcast_in_dim.20), calls=%async_computation.15 | async-start | bytes 786432 | tf_op jit(solution)/shard_map/all_to_all | solution.py:22
  239.2 1.0 reduce_sum.85
  240.1 4.4 %all-to-all-done.15 = f32[4,96,256]{2,1,0:T(8,128)S(1)} async-done(((f32[4,96,256]{2,1,0:T(8,128)}), f32[4,96,256]{2,1,0:T(8,128)S(1)}, u32[]{:S(2)}, u32[]{:S(2)}) %all-to-all-start.15) | async-done | bytes 393248 | tf_op jit(solution)/shard_map/all_to_all | solution.py:22
  244.5 3.5 %all-to-all-start.10 = ((f32[8,64,256]{2,1,0:T(8,128)}), f32[8,64,256]{2,1,0:T(8,128)S(1)}, u32[]{:S(2)}, u32[]{:S(2)}) async-start(f32[8,64,256]{2,1,0:T(8,128)} %bitcast.3), calls=%async_computation.10 | async-start | bytes 1048576 | tf_op jit(solution)/shard_map/all_to_all | solution.py:22
  248.0 0.1 dynamic-slice_multiply_fusion
  248.1 0.9 bitcast_divide_fusion
  248.9 25.8 %all-to-all-done.10 = f32[8,64,256]{2,1,0:T(8,128)S(1)} async-done(((f32[8,64,256]{2,1,0:T(8,128)}), f32[8,64,256]{2,1,0:T(8,128)S(1)}, u32[]{:S(2)}, u32[]{:S(2)}) %all-to-all-start.10) | async-done | bytes 524320 | tf_op jit(solution)/shard_map/all_to_all | solution.py:22
  274.7 0.7 broadcast_multiply_fusion
  (34 shorter events, 0.4 us)
Async XLA Ops:
  0.6 1.6 copy-start.7
  2.2 0.9 copy-start.9
  8.2 31.8 %copy-start = (f32[384,4096]{1,0:T(8,128)}, f32[384,4096]{1,0:T(8,128)S(1)}, u32[]{:S(2)}) copy-start(f32[384,4096]{1,0:T(8,128)S(1)} %get-tuple-element.5.tile_ref) | copy-start | bytes 18874372
  72.5 2.8 %copy-start.1 = (f32[384,4096]{1,0:T(8,128)S(1)}, f32[384,4096]{1,0:T(8,128)}, u32[]{:S(2)}) copy-start(f32[384,4096]{1,0:T(8,128)} %copy-done) | copy-start | bytes 18874372
  123.3 2.8 %copy-start.2 = (f32[384,4096]{1,0:T(8,128)S(1)}, f32[384,4096]{1,0:T(8,128)}, u32[]{:S(2)}) copy-start(f32[384,4096]{1,0:T(8,128)} %copy-done) | copy-start | bytes 18874372
  126.1 20.0 %copy-start.10 = (bf16[384,256]{1,0:T(8,128)(2,1)S(1)}, bf16[384,256]{1,0:T(8,128)(2,1)}, u32[]{:S(2)}) copy-start(bf16[384,256]{1,0:T(8,128)(2,1)} %latents_ref.5) | copy-start | bytes 589828
  127.8 18.2 %all-to-all-start.8 = ((f32[8,1,384]{2,1,0:T(1,128)}), f32[8,1,384]{2,1,0:T(1,128)S(1)}, u32[]{:S(2)}, u32[]{:S(2)}) async-start(f32[8,1,384]{2,1,0:T(1,128)} %rows.3), calls=%async_computation.8 | async-start | bytes 24576 | tf_op jit(solution)/shard_map/all_to_all | solution.py:22
  146.0 2.8 %copy-start.3 = (f32[384,4096]{1,0:T(8,128)S(1)}, f32[384,4096]{1,0:T(8,128)}, u32[]{:S(2)}) copy-start(f32[384,4096]{1,0:T(8,128)} %copy-done) | copy-start | bytes 18874372
  148.8 5.1 %copy-start.4 = (f32[384,4096]{1,0:T(8,128)S(1)}, f32[384,4096]{1,0:T(8,128)}, u32[]{:S(2)}) copy-start(f32[384,4096]{1,0:T(8,128)} %copy-done) | copy-start | bytes 18874372
  151.9 31.6 %copy-start.8 = (bf16[4096,256]{1,0:T(8,128)(2,1)S(1)}, bf16[4096,256]{1,0:T(8,128)(2,1)}, u32[]{:S(2)}) copy-start(bf16[4096,256]{1,0:T(8,128)(2,1)} %param.3) | copy-start | bytes 6291460
  151.9 44.1 %collective-permute-start = (f32[2048,256]{1,0:T(8,128)}, f32[2048,256]{1,0:T(8,128)}, u32[]{:S(2)}, u32[]{:S(2)}) collective-permute-start(f32[2048,256]{1,0:T(8,128)} %targets.1), channel_id=1, source_target_pairs={{0,8},{8,0},{1,9},{9,1},{2,10},{10,2},{3,11},{11,3},{4,12},{12,4},... | collective-permute-start | bytes 6291464 | tf_op jit(solution)/shard_map/ppermute | solution.py:263
  183.5 2.8 %copy-start.5 = (f32[384,4096]{1,0:T(8,128)S(1)}, f32[384,4096]{1,0:T(8,128)}, u32[]{:S(2)}) copy-start(f32[384,4096]{1,0:T(8,128)} %copy-done) | copy-start | bytes 18874372
  190.4 13.0 %all-to-all-start.14 = ((f32[4,104,256]{2,1,0:T(8,128)}), f32[4,104,256]{2,1,0:T(8,128)S(1)}, u32[]{:S(2)}, u32[]{:S(2)}) async-start(f32[4,104,256]{2,1,0:T(8,128)} %final.1), calls=%async_computation.14 | async-start | bytes 851968 | tf_op jit(solution)/shard_map/all_to_all | solution.py:22
  195.9 2.8 %copy-start.6 = (f32[384,4096]{1,0:T(8,128)S(1)}, f32[384,4096]{1,0:T(8,128)}, u32[]{:S(2)}) copy-start(f32[384,4096]{1,0:T(8,128)} %copy-done) | copy-start | bytes 18874372
  203.4 30.2 %all-to-all-start.9 = ((f32[4,512,256]{2,1,0:T(8,128)}), f32[4,512,256]{2,1,0:T(8,128)S(1)}, u32[]{:S(2)}, u32[]{:S(2)}) async-start(f32[4,512,256]{2,1,0:T(8,128)} %bitcast.2), calls=%async_computation.9 | async-start | bytes 4194304 | tf_op jit(solution)/shard_map/all_to_all | solution.py:22
  207.0 15.4 %collective-permute-start.1 = (f32[104,256]{1,0:T(8,128)S(1)}, f32[104,256]{1,0:T(8,128)S(1)}, u32[]{:S(2)}, u32[]{:S(2)}) collective-permute-start(f32[104,256]{1,0:T(8,128)S(1)} %reduce_sum.89), channel_id=1, source_target_pairs={{0,4},{4,0},{1,5},{5,1},{2,6},{6,2},{3,7},{7,3},{8,12},{12,8},{9,1... | collective-permute-start | bytes 319496 | tf_op jit(solution)/shard_map/ppermute | solution.py:282
  234.4 10.1 %all-to-all-start.15 = ((f32[4,96,256]{2,1,0:T(8,128)}), f32[4,96,256]{2,1,0:T(8,128)S(1)}, u32[]{:S(2)}, u32[]{:S(2)}) async-start(f32[4,96,256]{2,1,0:T(8,128)} %broadcast_in_dim.20), calls=%async_computation.15 | async-start | bytes 786432 | tf_op jit(solution)/shard_map/all_to_all | solution.py:22
  244.5 30.2 %all-to-all-start.10 = ((f32[8,64,256]{2,1,0:T(8,128)}), f32[8,64,256]{2,1,0:T(8,128)S(1)}, u32[]{:S(2)}, u32[]{:S(2)}) async-start(f32[8,64,256]{2,1,0:T(8,128)} %bitcast.3), calls=%async_computation.10 | async-start | bytes 1048576 | tf_op jit(solution)/shard_map/all_to_all | solution.py:22

commit v3 on v2

--- a/solution.py
+++ b/solution.py
@@ -22,12 +22,8 @@
     return lax.all_to_all(blocks, axes, 0, 0, tiled=True)
 
 
-def spread(block, axes, count):
-    return exchange(jnp.broadcast_to(block[None], (count,) + block.shape), axes)
-
-
-def params():
-    return pltpu.CompilerParams(vmem_limit_bytes=24 << 20)
+def params(mib=8):
+    return pltpu.CompilerParams(vmem_limit_bytes=mib << 20)
 
 
 def column_of(row):
@@ -53,7 +49,7 @@
     return (b % X) * C + b // X
 
 
-def setup_kernel(latents_ref, codes_ref, tile_ref, rows_ref, scale_ref, total_ref):
+def setup_kernel(where_ref, latents_ref, codes_ref, tile_ref, rows_ref, scale_ref, total_ref):
     step = pl.program_id(0)
     latents = latents_ref[...]
     width = latents.shape[1]
@@ -113,19 +109,79 @@
     columns_ref[...] = jnp.sum(tile * widen(scale_ref[...], tile.shape[1]), axis=0, keepdims=True)
 
 
-def targets_kernel(half_ref, parts_ref, latents_ref, tile_ref, *refs):
-    added_ref, out_ref, scale_ref = refs if len(refs) == 3 else (None,) + refs
-
+def targets_part(parts_ref, latents_ref, tile_ref, scale_ref):
     @pl.when(pl.program_id(0) == 0)
     def _():
         scale_ref[...] = row_scale_of(parts_ref)
 
     tile = tile_ref[...]
     weighted = (tile * widen(scale_ref[...], tile.shape[1])).astype(jnp.bfloat16)
-    summed = lax.dot_general(
-        weighted, latents_ref[...], (((0,), (0,)), ((), ())), preferred_element_type=jnp.float32
+    return lax.dot_general(
+        latents_ref[...], weighted, (((0,), (0,)), ((), ())), preferred_element_type=jnp.float32
     )
-    out_ref[...] = summed if added_ref is None else summed + added_ref[...]
+
+
+def targets_sent_kernel(where_ref, parts_ref, latents_ref, tile_ref, after_ref, out_ref, scale_ref):
+    del where_ref, after_ref
+    out_ref[...] = targets_part(parts_ref, latents_ref, tile_ref, scale_ref)
+
+
+def targets_kept_kernel(
+    where_ref, parts_ref, latents_ref, tile_ref, after_ref, added_ref, one_ref, two_ref, own_one_ref, own_two_ref, scale_ref
+):
+    del where_ref, after_ref
+    slot = pl.program_id(0)
+    summed = targets_part(parts_ref, latents_ref, tile_ref, scale_ref) + added_ref[...]
+    upper, lower = jnp.split(summed, 2, axis=0)
+
+    def put(ref, index, value, when):
+        @pl.when(slot == when)
+        def _():
+            ref[index] = value
+
+    put(own_one_ref, 0, upper, 0)
+    put(one_ref, 0, upper, 1)
+    put(one_ref, 1, upper, 2)
+    put(own_one_ref, 1, upper, 3)
+    put(own_two_ref, 0, lower, 0)
+    put(own_two_ref, 1, lower, 1)
+    put(two_ref, 1, lower, 2)
+    put(two_ref, 0, lower, 3)
+
+
+def sum_kernel(parts_ref, *refs):
+    out_ref = refs[-1]
+    out_ref[...] = jnp.broadcast_to(jnp.sum(parts_ref[...], axis=0, keepdims=True), out_ref.shape)
+
+
+def inverse_kernel(factor, parts_ref, *refs):
+    out_ref = refs[-1]
+    out_ref[...] = jnp.broadcast_to(factor / jnp.sum(parts_ref[...], axis=0, keepdims=True), out_ref.shape)
+
+
+def add_kernel(kept_ref, came_ref, after_ref, out_ref):
+    del after_ref
+    out_ref[...] = kept_ref[...] + came_ref[...]
+
+
+def join_kernel(kept_ref, came_ref, spread_ref, mass_ref):
+    total = kept_ref[...] + came_ref[...]
+    group = spread_ref.shape[1]
+    spread_ref[...] = jnp.broadcast_to(total[None, :group], spread_ref.shape)
+    mass_ref[...] = total[group:]
+
+
+def turn_kernel(where_ref, own_one_ref, one_ref, more_one_ref, own_two_ref, two_ref, more_two_ref, after_ref, *refs):
+    del after_ref
+    send_ref, keep_ref, turned_ref = refs
+    upper = own_one_ref[0] + one_ref[0] + more_one_ref[...]
+    lower = own_two_ref[0] + two_ref[0] + more_two_ref[...]
+    turned_ref[...] = jnp.concatenate([upper, lower], axis=0).T
+    share = send_ref.shape[1]
+    for i, slot in enumerate((0, 4, 2, 6)):
+        for ref, s in ((keep_ref, slot), (send_ref, slot + 1)):
+            start = pl.multiple_of((where_ref[2] ^ s) * share, share)
+            ref[i] = turned_ref[pl.ds(start, share), :]
 
 
 def final_kernel(parts_ref, columns_ref, codes_ref, tile_ref, out_ref, scale_ref, numer_ref, mass_ref):
@@ -181,24 +237,27 @@
     codes = codebook.reshape(Z, X * C, share, width)
     codes_spec = pl.BlockSpec((Z, None, share, width), lambda b: (0, place(b), 0, 0))
     latents_spec = whole(token_count, width)
-    tile_spec = pl.BlockSpec((token_count, block), lambda b: (0, b))
+    tile_spec = pl.BlockSpec((None, token_count, block), lambda b: (b, 0, 0))
     rows_spec = whole(H * Y, 1, token_count)
     columns_spec = pl.BlockSpec((None, 1, block), lambda b: (b, 0, 0))
     per_token = pltpu.VMEM((token_count, LANES), jnp.float32)
     rows_shape = f32(H * Y, 1, token_count)
     columns_shape = f32(BLOCKS, 1, block)
 
+    core, x, z = (lax.axis_index(axis) for axis in ("c", "x", "z"))
+    where = jnp.stack([core, x, z, 1 - core, z * share])
+
     tile, part = pl.pallas_call(
         setup_kernel,
         grid=(BLOCKS,),
-        in_specs=[latents_spec, codes_spec],
+        in_specs=[pl.BlockSpec(memory_space=pltpu.SMEM), latents_spec, codes_spec],
         out_specs=[tile_spec, rows_spec],
-        out_shape=[f32(token_count, code_count), rows_shape],
+        out_shape=[f32(BLOCKS, token_count, block), rows_shape],
         scratch_shapes=[per_token, per_token],
-        compiler_params=params(),
+        compiler_params=params(16),
         cost_estimate=cost(2 * size * width, 4 * size, size),
         name="setup",
-    )(latents, codes)
+    )(where, latents, codes)
 
     def rows(columns):
         return pl.pallas_call(
@@ -226,45 +285,91 @@
             name="columns",
         )(parts, tile)
 
-    def targets_part(half, parts, added=None):
-        spec = pl.BlockSpec((block, width), lambda i, half: (i, 0))
-        more, more_specs = ((), ()) if added is None else ((added,), (spec,))
-        return pl.pallas_call(
-            targets_kernel,
-            grid_spec=pltpu.PrefetchScalarGridSpec(
-                num_scalar_prefetch=1,
-                grid=(X,),
-                in_specs=[
-                    rows_spec,
-                    latents_spec,
-                    pl.BlockSpec((token_count, block), lambda i, half: (0, half[0] * X + i)),
-                    *more_specs,
-                ],
-                out_specs=spec,
-                scratch_shapes=[per_token],
-            ),
-            out_shape=f32(X * block, width),
+    anywhere = pl.BlockSpec(memory_space=pl.ANY)
+
+    def targets_spec(kept):
+        spec = pl.BlockSpec((None, width, block), lambda i, where: (i, 0, 0))
+        halves = whole(2, width // 2, block)
+        return pltpu.PrefetchScalarGridSpec(
+            num_scalar_prefetch=1,
+            grid=(X,),
+            in_specs=[
+                rows_spec,
+                latents_spec,
+                pl.BlockSpec((None, token_count, block), lambda i, where: (where[0 if kept else 3] * X + (where[1] ^ i), 0, 0)),
+                anywhere,
+                *([spec] if kept else []),
+            ],
+            out_specs=[halves] * 4 if kept else spec,
+            scratch_shapes=[per_token],
+        )
+
+    def targets_sent(where, parts, after):
+        return pl.pallas_call(
+            targets_sent_kernel,
+            grid_spec=targets_spec(False),
+            out_shape=f32(X, width, block),
             compiler_params=params(),
             cost_estimate=cost(size * width, 4 * size),
-            name="targets" if added is None else "targets_added",
-        )(half, parts, latents, tile, *more)
+            name="targets_sent",
+        )(where, parts, latents, tile, after)
+
+    def targets_kept(where, parts, after, added):
+        return pl.pallas_call(
+            targets_kept_kernel,
+            grid_spec=targets_spec(True),
+            out_shape=[f32(2, width // 2, block)] * 4,
+            compiler_params=params(16),
+            cost_estimate=cost(size * width, 4 * size),
+            name="targets_kept",
+        )(where, parts, latents, tile, after, added)
+
+    def small(kernel, name, count, parts, *after):
+        return pl.pallas_call(
+            kernel,
+            in_specs=[pl.BlockSpec(memory_space=pltpu.VMEM)] + [anywhere] * len(after),
+            out_specs=pl.BlockSpec(memory_space=pltpu.VMEM),
+            out_shape=f32(count, 1, block),
+            compiler_params=params(),
+            cost_estimate=cost(parts.size, 4 * parts.size),
+            name=name,
+        )(parts, *after)
+
+    inverse = functools.partial(inverse_kernel, total_tokens / total_codes)
+    def swap(value, axis, count, bits):
+        return lax.ppermute(value, axis, [(i, i ^ bits) for i in range(count)])
+
+    def add(kept, came, after):
+        return pl.pallas_call(
+            add_kernel,
+            in_specs=[pl.BlockSpec(memory_space=pltpu.VMEM)] * 2 + [anywhere],
+            out_specs=pl.BlockSpec(memory_space=pltpu.VMEM),
+            out_shape=f32(*kept.shape),
+            compiler_params=params(),
+            cost_estimate=cost(kept.size, 12 * kept.size),
+            name="add",
+        )(kept, came, after)
 
     for sweep_index in range(ITERS):
+        last = sweep_index == ITERS - 1
         parts = exchange(part, ("h", "y"))
-        sums = jnp.sum(exchange(columns(parts), ("c", "x")), axis=0)
-        total = jnp.sum(spread(sums, "z", Z), axis=0)
-        mine = total_tokens / total_codes / total
-        col_scale = spread(mine, ("c", "x"), BLOCKS)
-        if sweep_index < ITERS - 1:
+        column_sums = columns(parts)
+        if last:
+            sent = targets_sent(where, parts, column_sums)
+        after = (sent,) if last else ()
+        sums = small(sum_kernel, "sums", Z, exchange(column_sums, ("c", "x")), *after)
+        if last:
+            kept = targets_kept(where, parts, sums, swap(sent, "c", C, 1))
+        after = (kept[0],) if last else ()
+        mine = small(inverse, "inverse", BLOCKS, exchange(sums, "z"), *after)
+        col_scale = exchange(mine, ("c", "x"))
+        if not last:
             part = rows(col_scale)
 
-    core = lax.axis_index("c").reshape(1)
-    sent = targets_part(1 - core, parts)
-    summed = targets_part(core, parts, lax.ppermute(sent, "c", [(0, 1), (1, 0)]))
-    summed = jnp.sum(exchange(summed.reshape(X, block, width), "x"), axis=0)
-    summed = jnp.sum(exchange(summed.reshape(Z, share, width), "z"), axis=0)
-    own = lax.dynamic_slice(mine, (0, lax.axis_index("z") * share), (1, share))[0]
-    targets = summed * (own * (total_codes / total_tokens))[:, None]
+    one, two, own_one, own_two = kept
+    one, two = swap(one, "x", X, 1), swap(two, "x", X, 3)
+    more_one = swap(own_one[1] + one[1], "x", X, 3)
+    more_two = swap(own_two[1] + two[1], "x", X, 1)
 
     group = token_count // Y
     packed = pl.pallas_call(
@@ -274,14 +379,38 @@
         out_specs=whole(Y, group + PAD, width),
         out_shape=f32(Y, group + PAD, width),
         scratch_shapes=[per_token, pltpu.VMEM((token_count, width), jnp.float32), per_token],
-        compiler_params=params(),
-        cost_estimate=cost(2 * size * width, 4 * size),
+        compiler_params=params(16),
+        cost_estimate=cost(20 * size * width, 4 * size),
         name="final",
     )(parts, col_scale, codes, tile)
     packed = jnp.sum(exchange(packed, "y"), axis=0)
-    packed = packed + lax.ppermute(packed, "h", [(0, 1), (1, 0)])
-    mass = packed[group : group + 2].reshape(2 * width)[:token_count]
-    rebuilt = spread(packed[:group], "y", Y).reshape(token_count, width) / mass[:, None]
+    vmem = pl.BlockSpec(memory_space=pltpu.VMEM)
+    away, near = pl.pallas_call(
+        turn_kernel,
+        in_specs=[pl.BlockSpec(memory_space=pltpu.SMEM)] + [vmem] * 6 + [anywhere],
+        out_specs=[vmem] * 2,
+        out_shape=[f32(Z // 2, share, width)] * 2,
+        scratch_shapes=[pltpu.VMEM((block, width), jnp.float32)],
+        compiler_params=params(16),
+        cost_estimate=cost(3 * block * width, 12 * block * width),
+        name="turn",
+    )(where, own_one, one, more_one, own_two, two, more_two, packed)
+    numer, mass = pl.pallas_call(
+        join_kernel,
+        in_specs=[vmem] * 2,
+        out_specs=[vmem] * 2,
+        out_shape=[f32(Y, group, width), f32(PAD, width)],
+        compiler_params=params(),
+        cost_estimate=cost(20000 * token_count * width, 8 * token_count * width),
+        name="join",
+    )(packed, swap(packed, "h", H, 1))
+    near = near + swap(away, "z", Z, 1)
+    near = add(near[:2], swap(near[2:], "z", Z, 2), mass)
+    summed = near[0] + swap(near[1], "z", Z, 4)
+    own = lax.dynamic_slice(mine, (0, 0, where[4]), (1, 1, share)).reshape(share)
+    targets = summed * (own * (total_codes / total_tokens))[:, None]
+    mass = mass[:2].reshape(2 * width)[:token_count]
+    rebuilt = exchange(numer, "y").reshape(token_count, width) / mass[:, None]
     return (targets, rebuilt)
 
 

time: 278 us -> 246 us (0.88)
  waiting for transfers between devices: 67 us -> 21.9 us
  starting transfers between devices: 27.2 us -> 50.1 us
  local copies, waits for them, and re-layouts: 17.3 us -> 9.79 us
  blocking collectives: 137 us -> 133 us
    all_to_all x5 -> x4, waiting for transfers between devices: 54.1 us -> 4.97 us  [exchange(): return lax.all_to_all(blocks, axes, 0, 0, tiled=True)]
    ppermute x2 -> x9, starting transfers between devices: 4.52 us -> 31.8 us  [swap(): return lax.ppermute(value, axis, [(i, i ^ bits) for i in range(count)])]
    unnamed x24 -> x16, local copies, waits for them, and re-layouts: 16.5 us -> 9.68 us
    all_to_all x5 -> x4, starting transfers between devices: 22.7 us -> 18.3 us  [exchange(): return lax.all_to_all(blocks, axes, 0, 0, tiled=True)]
    ppermute x2 -> x9, waiting for transfers between devices: 12.9 us -> 17 us  [swap(): return lax.ppermute(value, axis, [(i, i ^ bits) for i in range(count)])]
    all_to_all x11 -> x10, blocking collectives: 137 us -> 133 us  [exchange(): return lax.all_to_all(blocks, axes, 0, 0, tiled=True)]
    pallas_call x3 -> x12, Pallas kernels: 12.8 us -> 14.3 us  [the longest x1 5.23 us: per_device(): pl.pallas_call(setup_kernel, grid=(BLOCKS,), in_specs=[pl.BlockSpec(memor...]
  transfers between devices with their start and end apart: 7 -> 13, of which waited for: 5 -> 7; matrix products, arithmetic and copies ran while one was open for 1% -> 1% of each run, Pallas kernels for 4% -> 4%
where the time goes in v3:
time: 246 us; the launch traced here: 242 us
  blocking collectives  133 us (54%)
  starting transfers between devices  50.1 us (20%)
  Pallas kernels  22.1 us (9%)
  waiting for transfers between devices  21.9 us (9%)
  local copies, waits for them, and re-layouts  9.79 us (4%)
  other arithmetic  3.47 us (1%)
    all_to_all x10, blocking collectives, exchange(): return lax.all_to_all(blocks, axes, 0, 0, tiled=True)  133 us
    ppermute x9, starting transfers between devices, swap(): return lax.ppermute(value, axis, [(i, i ^ bits) for i in range(count)])  31.8 us
    all_to_all x4, starting transfers between devices, exchange(): return lax.all_to_all(blocks, axes, 0, 0, tiled=True)  18.3 us
    ppermute x9, waiting for transfers between devices, swap(): return lax.ppermute(value, axis, [(i, i ^ bits) for i in range(count)])  17 us
    unnamed x16, local copies, waits for them, and re-layouts  9.68 us
    pallas_call x1, Pallas kernels, per_device(): pl.pallas_call(setup_kernel, grid=(BLOCKS,), in_specs=[pl.BlockSpec(memor...  5.23 us
    all_to_all x4, waiting for transfers between devices, exchange(): return lax.all_to_all(blocks, axes, 0, 0, tiled=True)  4.97 us
  transfers between devices with their start and end apart: 13, of which 7 were waited for; matrix products, arithmetic and copies ran while one was open for 1% of the time, Pallas kernels for 4%

profile of v3, /device:TPU:24, one launch (start us, length us, event | category | flops | bytes accessed | tf_op | source)
XLA Modules:
  0.0 241.7 jit_solution(1724390371190772736)
XLA Ops:
  0.7 0.9 copy-done.3
  1.7 1.6 copy-done.5
  3.2 5.2 %setup.1 = (f32[8,384,512]{2,1,0:T(8,128)S(1)}, f32[8,1,384]{2,1,0:T(1,128)S(1)}) custom-call(s32[5]{0:T(128)S(1)} %stack.23.where_ref, bf16[384,256]{1,0:T(8,128)(2,1)S(1)} %copy-done.3, bf16[8,8,64,256]{3,2,1,0:T(8,128)(2,1)S(1)} %bitcast.26), custom_call_target="tpu_custom_call" | custom-call | flops 805306368 | bytes 6291456 | tf_op jit(solution)/shard_map/setup/pallas_call | solution.py:250
  8.5 30.6 %all_to_all.70.parts_ref = f32[8,1,384]{2,1,0:T(1,128)S(1)} all-to-all(f32[8,1,384]{2,1,0:T(1,128)S(1)} %get-tuple-element.12), channel_id=1, replica_groups=mesh['z'=8,'x'=4,'c'=2,'h'=2,'y'=4] {'h','y'}, dimensions={0} | all-to-all | bytes 24576 | tf_op jit(solution)/shard_map/all_to_all | solution.py:22
  39.1 0.8 columns.3
  39.9 9.4 %all_to_all.71.parts_ref = f32[8,1,512]{2,1,0:T(1,128)S(1)} all-to-all(f32[8,1,512]{2,1,0:T(1,128)S(1)} %columns.3), channel_id=1, replica_groups=mesh['z'=8,'x'=4,'c'=2,'h'=2,'y'=4] {'c','x'}, dimensions={0} | all-to-all | bytes 32768 | tf_op jit(solution)/shard_map/all_to_all | solution.py:22
  49.3 15.3 %all_to_all.72.parts_ref = f32[8,1,512]{2,1,0:T(1,128)S(1)} all-to-all(f32[8,1,512]{2,1,0:T(1,128)S(1)} %sums.3), channel_id=1, replica_groups=mesh['z'=8,'x'=4,'c'=2,'h'=2,'y'=4] {'z'}, dimensions={0} | all-to-all | bytes 32768 | tf_op jit(solution)/shard_map/all_to_all | solution.py:22
  64.7 7.6 %all_to_all.73.columns_ref = f32[8,1,512]{2,1,0:T(1,128)S(1)} all-to-all(f32[8,1,512]{2,1,0:T(1,128)S(1)} %inverse.3), channel_id=1, replica_groups=mesh['z'=8,'x'=4,'c'=2,'h'=2,'y'=4] {'c','x'}, dimensions={0} | all-to-all | bytes 32768 | tf_op jit(solution)/shard_map/all_to_all | solution.py:22
  72.3 0.8 rows.2
  73.1 17.3 %all_to_all.74.parts_ref = f32[8,1,384]{2,1,0:T(1,128)S(1)} all-to-all(f32[8,1,384]{2,1,0:T(1,128)S(1)} %rows.2), channel_id=1, replica_groups=mesh['z'=8,'x'=4,'c'=2,'h'=2,'y'=4] {'h','y'}, dimensions={0} | all-to-all | bytes 24576 | tf_op jit(solution)/shard_map/all_to_all | solution.py:22
  90.4 0.8 columns.4
  91.2 7.6 %all_to_all.75.parts_ref = f32[8,1,512]{2,1,0:T(1,128)S(1)} all-to-all(f32[8,1,512]{2,1,0:T(1,128)S(1)} %columns.4), channel_id=1, replica_groups=mesh['z'=8,'x'=4,'c'=2,'h'=2,'y'=4] {'c','x'}, dimensions={0} | all-to-all | bytes 32768 | tf_op jit(solution)/shard_map/all_to_all | solution.py:22
  98.9 12.9 %all_to_all.76.parts_ref = f32[8,1,512]{2,1,0:T(1,128)S(1)} all-to-all(f32[8,1,512]{2,1,0:T(1,128)S(1)} %sums.4), channel_id=1, replica_groups=mesh['z'=8,'x'=4,'c'=2,'h'=2,'y'=4] {'z'}, dimensions={0} | all-to-all | bytes 32768 | tf_op jit(solution)/shard_map/all_to_all | solution.py:22
  111.8 7.6 %all_to_all.77.columns_ref = f32[8,1,512]{2,1,0:T(1,128)S(1)} all-to-all(f32[8,1,512]{2,1,0:T(1,128)S(1)} %inverse.4), channel_id=1, replica_groups=mesh['z'=8,'x'=4,'c'=2,'h'=2,'y'=4] {'c','x'}, dimensions={0} | all-to-all | bytes 32768 | tf_op jit(solution)/shard_map/all_to_all | solution.py:22
  119.5 0.8 rows.3
  120.3 17.3 %all_to_all.78.parts_ref = f32[8,1,384]{2,1,0:T(1,128)S(1)} all-to-all(f32[8,1,384]{2,1,0:T(1,128)S(1)} %rows.3), channel_id=1, replica_groups=mesh['z'=8,'x'=4,'c'=2,'h'=2,'y'=4] {'h','y'}, dimensions={0} | all-to-all | bytes 24576 | tf_op jit(solution)/shard_map/all_to_all | solution.py:22
  137.5 0.8 columns.5.after_ref
  138.4 2.1 targets_sent.1.refs_0_
  140.5 2.1 collective-permute-start
  142.6 7.7 %all_to_all.79.parts_ref = f32[8,1,512]{2,1,0:T(1,128)S(1)} all-to-all(f32[8,1,512]{2,1,0:T(1,128)S(1)} %columns.5.after_ref), channel_id=1, replica_groups=mesh['z'=8,'x'=4,'c'=2,'h'=2,'y'=4] {'c','x'}, dimensions={0} | all-to-all | bytes 32768 | tf_op jit(solution)/shard_map/all_to_all | solution.py:22
  150.9 3.3 %all-to-all-start.10 = ((f32[8,1,512]{2,1,0:T(1,128)}), f32[8,1,512]{2,1,0:T(1,128)S(1)}, u32[]{:S(2)}, u32[]{:S(2)}) async-start(f32[8,1,512]{2,1,0:T(1,128)} %sums.5.after_ref), calls=%async_computation.10 | async-start | bytes 32768 | tf_op jit(solution)/shard_map/all_to_all | solution.py:22
  154.3 2.8 %copy-done.1 = f32[8,384,512]{2,1,0:T(8,128)S(1)} copy-done((f32[8,384,512]{2,1,0:T(8,128)S(1)}, f32[8,384,512]{2,1,0:T(8,128)}, u32[]{:S(2)}) %copy-start.1) | copy-done | bytes 6291480
  157.0 4.1 %targets_kept.1 = (f32[2,128,512]{2,1,0:T(8,128)S(1)}, f32[2,128,512]{2,1,0:T(8,128)S(1)}, f32[2,128,512]{2,1,0:T(8,128)S(1)}, f32[2,128,512]{2,1,0:T(8,128)S(1)}) custom-call(s32[5]{0:T(128)S(1)} %stack.23.where_ref, f32[8,1,384]{2,1,0:T(1,128)S(1)} %all_to_all.78.parts_ref, bf16[384,256]{1,0:T(8,128)(2,1)S(1)} %copy-done.4, f32[8,384,512]{2,1,0:T(8,128)S(1)} %copy-done.1, ...), custom_call_target="tpu_custom_call" | custom-call | flops 402653184 | bytes 6291456 | tf_op jit(solution)/shard_map/targets_kept/pallas_call | solution.py:318
  161.1 3.6 %all-to-all-done.10.parts_ref = f32[8,1,512]{2,1,0:T(1,128)S(1)} async-done(((f32[8,1,512]{2,1,0:T(1,128)}), f32[8,1,512]{2,1,0:T(1,128)S(1)}, u32[]{:S(2)}, u32[]{:S(2)}) %all-to-all-start.10) | async-done | bytes 16416 | tf_op jit(solution)/shard_map/all_to_all | solution.py:22
  165.3 3.3 %all-to-all-start.11 = ((f32[8,1,512]{2,1,0:T(1,128)}), f32[8,1,512]{2,1,0:T(1,128)S(1)}, u32[]{:S(2)}, u32[]{:S(2)}) async-start(f32[8,1,512]{2,1,0:T(1,128)} %inverse.5), calls=%async_computation.11 | async-start | bytes 32768 | tf_op jit(solution)/shard_map/all_to_all | solution.py:22
  168.7 3.8 %collective-permute-start.1 = (f32[2,128,512]{2,1,0:T(8,128)S(1)}, f32[2,128,512]{2,1,0:T(8,128)S(1)}, u32[]{:S(2)}, u32[]{:S(2)}) collective-permute-start(f32[2,128,512]{2,1,0:T(8,128)S(1)} %get-tuple-element.15.refs_0_), channel_id=1, source_target_pairs={{0,16},{16,0},{32,48},{48,32},{1,17},{17,1},{33,49},{49,33},{2,18}... | collective-permute-start | bytes 1572872 | tf_op jit(solution)/shard_map/ppermute | solution.py:340
  172.5 4.0 %collective-permute-start.3 = (f32[2,128,512]{2,1,0:T(8,128)S(1)}, f32[2,128,512]{2,1,0:T(8,128)S(1)}, u32[]{:S(2)}, u32[]{:S(2)}) collective-permute-start(f32[2,128,512]{2,1,0:T(8,128)S(1)} %get-tuple-element.17), channel_id=1, source_target_pairs={{0,48},{16,32},{32,16},{48,0},{1,49},{17,33},{33,17},{49,1},{2,50}... | collective-permute-start | bytes 1572872 | tf_op jit(solution)/shard_map/ppermute | solution.py:340
  176.5 2.8 %copy-done.2 = f32[8,384,512]{2,1,0:T(8,128)S(1)} copy-done((f32[8,384,512]{2,1,0:T(8,128)S(1)}, f32[8,384,512]{2,1,0:T(8,128)}, u32[]{:S(2)}) %copy-start.2) | copy-done | bytes 6291480
  179.3 1.6 copy-done.6
  180.9 3.7 %final.1 = f32[4,104,256]{2,1,0:T(8,128)} custom-call(f32[8,1,384]{2,1,0:T(1,128)S(1)} %all_to_all.78.parts_ref, f32[8,1,512]{2,1,0:T(1,128)S(1)} %all-to-all-done.11.columns_ref, bf16[8,8,64,256]{3,2,1,0:T(8,128)(2,1)S(1)} %bitcast.27, f32[8,384,512]{2,1,0:T(8,128)S(1)} %copy-done.2), custom_call_target="tpu_custom_call" | custom-call | flops 8053063680 | bytes 6291456 | tf_op jit(solution)/shard_map/final/pallas_call | solution.py:375
  184.6 6.1 %all-to-all-start.12 = ((f32[4,104,256]{2,1,0:T(8,128)}), f32[4,104,256]{2,1,0:T(8,128)}, u32[]{:S(2)}, u32[]{:S(2)}) async-start(f32[4,104,256]{2,1,0:T(8,128)} %final.1), calls=%async_computation.12 | async-start | bytes 851968 | tf_op jit(solution)/shard_map/all_to_all | solution.py:22
  190.7 3.1 %collective-permute-start.2 = (f32[128,512]{1,0:T(8,128)S(1)}, f32[128,512]{1,0:T(8,128)S(1)}, u32[]{:S(2)}, u32[]{:S(2)}) collective-permute-start(f32[128,512]{1,0:T(8,128)S(1)} %fusion.1), channel_id=1, source_target_pairs={{0,48},{16,32},{32,16},{48,0},{1,49},{17,33},{33,17},{49,1},{2,50}... | collective-permute-start | bytes 786440 | tf_op jit(solution)/shard_map/ppermute | solution.py:340
  193.9 1.9 collective-permute-start.4
  195.8 1.4 all-to-all-done.12
  197.2 1.0 reduce_sum.9.after_ref.kept_ref
  198.2 2.5 %collective-permute-start.7 = (f32[104,256]{1,0:T(8,128)S(1)}, f32[104,256]{1,0:T(8,128)S(1)}, u32[]{:S(2)}, u32[]{:S(2)}) collective-permute-start(f32[104,256]{1,0:T(8,128)S(1)} %reduce_sum.9.after_ref.kept_ref), channel_id=1, source_target_pairs={{0,4},{4,0},{1,5},{5,1},{2,6},{6,2},{3,7},{7,3},{8,12},{12,8},{9,1... | collective-permute-start | bytes 319496 | tf_op jit(solution)/shard_map/ppermute | solution.py:340
  201.4 1.6 collective-permute-done.4.more_two_ref
  203.0 0.8 turn.1
  203.8 2.4 %collective-permute-start.5 = (f32[4,64,256]{2,1,0:T(8,128)S(1)}, f32[4,64,256]{2,1,0:T(8,128)S(1)}, u32[]{:S(2)}, u32[]{:S(2)}) collective-permute-start(f32[4,64,256]{2,1,0:T(8,128)S(1)} %get-tuple-element.19), channel_id=1, source_target_pairs={{0,64},{64,0},{128,192},{192,128},{256,320},{320,256},{384,448},{4... | collective-permute-start | bytes 786440 | tf_op jit(solution)/shard_map/ppermute | solution.py:340
  206.2 0.7 multiply_bitcast_fusion
  207.0 9.8 %collective-permute-done.7.came_ref = f32[104,256]{1,0:T(8,128)S(1)} collective-permute-done((f32[104,256]{1,0:T(8,128)S(1)}, f32[104,256]{1,0:T(8,128)S(1)}, u32[]{:S(2)}, u32[]{:S(2)}) %collective-permute-start.7) | collective-permute-done | bytes 106528 | tf_op jit(solution)/shard_map/ppermute | solution.py:340
  216.8 0.8 join.1
  217.5 5.5 %all-to-all-start.13 = ((f32[4,96,256]{2,1,0:T(8,128)}), f32[4,96,256]{2,1,0:T(8,128)S(1)}, u32[]{:S(2)}, u32[]{:S(2)}) async-start(f32[4,96,256]{2,1,0:T(8,128)} %get-tuple-element.21), calls=%async_computation.13 | async-start | bytes 786432 | tf_op jit(solution)/shard_map/all_to_all | solution.py:22
  223.1 4.5 %collective-permute-start.6 = (f32[2,64,256]{2,1,0:T(8,128)S(1)}, f32[2,64,256]{2,1,0:T(8,128)S(1)}, u32[]{:S(2)}, u32[]{:S(2)}) collective-permute-start(f32[2,64,256]{2,1,0:T(8,128)S(1)} %get-tuple-element.22), channel_id=1, source_target_pairs={{0,128},{64,192},{128,0},{192,64},{256,384},{320,448},{384,256},{4... | collective-permute-start | bytes 393224 | tf_op jit(solution)/shard_map/ppermute | solution.py:340
  227.6 3.3 %collective-permute-done.6.came_ref = f32[2,64,256]{2,1,0:T(8,128)S(1)} collective-permute-done((f32[2,64,256]{2,1,0:T(8,128)S(1)}, f32[2,64,256]{2,1,0:T(8,128)S(1)}, u32[]{:S(2)}, u32[]{:S(2)}) %collective-permute-start.6) | collective-permute-done | bytes 131104 | tf_op jit(solution)/shard_map/ppermute | solution.py:340
  230.9 7.5 %collective-permute-start.8 = (f32[64,256]{1,0:T(8,128)S(1)}, f32[64,256]{1,0:T(8,128)S(1)}, u32[]{:S(2)}, u32[]{:S(2)}) collective-permute-start(f32[64,256]{1,0:T(8,128)S(1)} %slice_bitcast_fusion), channel_id=1, source_target_pairs={{0,256},{64,320},{128,384},{192,448},{256,0},{320,64},{384,128},{4... | collective-permute-start | bytes 196616 | tf_op jit(solution)/shard_map/ppermute | solution.py:340
  238.5 0.9 bitcast_divide_fusion
  239.4 1.6 collective-permute-done.8
  (32 shorter events, 3.0 us)
Async XLA Ops:
  0.7 0.9 copy-start.3
  1.6 1.6 copy-start.5
  8.5 129.9 %copy-start = (f32[8,384,512]{2,1,0:T(8,128)}, f32[8,384,512]{2,1,0:T(8,128)S(1)}, u32[]{:S(2)}) copy-start(f32[8,384,512]{2,1,0:T(8,128)S(1)} %get-tuple-element.13.tile_ref) | copy-start | bytes 18874372
  140.5 13.8 %copy-start.4 = (bf16[384,256]{1,0:T(8,128)(2,1)S(1)}, bf16[384,256]{1,0:T(8,128)(2,1)}, u32[]{:S(2)}) copy-start(bf16[384,256]{1,0:T(8,128)(2,1)} %latents_ref.5) | copy-start | bytes 589828
  140.5 13.7 %collective-permute-start = (f32[4,256,512]{2,1,0:T(8,128)S(1)}, f32[4,256,512]{2,1,0:T(8,128)}, u32[]{:S(2)}, u32[]{:S(2)}) collective-permute-start(f32[4,256,512]{2,1,0:T(8,128)S(1)} %targets_sent.1.refs_0_), channel_id=1, source_target_pairs={{0,8},{8,0},{1,9},{9,1},{2,10},{10,2},{3,11},{11,3},{4,12},{12,4},... | collective-permute-start | bytes 6291464 | tf_op jit(solution)/shard_map/ppermute | solution.py:340
  150.9 13.8 %all-to-all-start.10 = ((f32[8,1,512]{2,1,0:T(1,128)}), f32[8,1,512]{2,1,0:T(1,128)S(1)}, u32[]{:S(2)}, u32[]{:S(2)}) async-start(f32[8,1,512]{2,1,0:T(1,128)} %sums.5.after_ref), calls=%async_computation.10 | async-start | bytes 32768 | tf_op jit(solution)/shard_map/all_to_all | solution.py:22
  154.3 2.8 %copy-start.1 = (f32[8,384,512]{2,1,0:T(8,128)S(1)}, f32[8,384,512]{2,1,0:T(8,128)}, u32[]{:S(2)}) copy-start(f32[8,384,512]{2,1,0:T(8,128)} %copy-done) | copy-start | bytes 18874372
  165.3 11.2 %all-to-all-start.11 = ((f32[8,1,512]{2,1,0:T(1,128)}), f32[8,1,512]{2,1,0:T(1,128)S(1)}, u32[]{:S(2)}, u32[]{:S(2)}) async-start(f32[8,1,512]{2,1,0:T(1,128)} %inverse.5), calls=%async_computation.11 | async-start | bytes 32768 | tf_op jit(solution)/shard_map/all_to_all | solution.py:22
  168.7 22.0 %collective-permute-start.1 = (f32[2,128,512]{2,1,0:T(8,128)S(1)}, f32[2,128,512]{2,1,0:T(8,128)S(1)}, u32[]{:S(2)}, u32[]{:S(2)}) collective-permute-start(f32[2,128,512]{2,1,0:T(8,128)S(1)} %get-tuple-element.15.refs_0_), channel_id=1, source_target_pairs={{0,16},{16,0},{32,48},{48,32},{1,17},{17,1},{33,49},{49,33},{2,18}... | collective-permute-start | bytes 1572872 | tf_op jit(solution)/shard_map/ppermute | solution.py:340
  172.5 21.3 %collective-permute-start.3 = (f32[2,128,512]{2,1,0:T(8,128)S(1)}, f32[2,128,512]{2,1,0:T(8,128)S(1)}, u32[]{:S(2)}, u32[]{:S(2)}) collective-permute-start(f32[2,128,512]{2,1,0:T(8,128)S(1)} %get-tuple-element.17), channel_id=1, source_target_pairs={{0,48},{16,32},{32,16},{48,0},{1,49},{17,33},{33,17},{49,1},{2,50}... | collective-permute-start | bytes 1572872 | tf_op jit(solution)/shard_map/ppermute | solution.py:340
  176.5 2.8 %copy-start.2 = (f32[8,384,512]{2,1,0:T(8,128)S(1)}, f32[8,384,512]{2,1,0:T(8,128)}, u32[]{:S(2)}) copy-start(f32[8,384,512]{2,1,0:T(8,128)} %copy-done) | copy-start | bytes 18874372
  179.3 1.6 copy-start.6
  184.6 12.6 %all-to-all-start.12 = ((f32[4,104,256]{2,1,0:T(8,128)}), f32[4,104,256]{2,1,0:T(8,128)}, u32[]{:S(2)}, u32[]{:S(2)}) async-start(f32[4,104,256]{2,1,0:T(8,128)} %final.1), calls=%async_computation.12 | async-start | bytes 851968 | tf_op jit(solution)/shard_map/all_to_all | solution.py:22
  190.7 10.6 %collective-permute-start.2 = (f32[128,512]{1,0:T(8,128)S(1)}, f32[128,512]{1,0:T(8,128)S(1)}, u32[]{:S(2)}, u32[]{:S(2)}) collective-permute-start(f32[128,512]{1,0:T(8,128)S(1)} %fusion.1), channel_id=1, source_target_pairs={{0,48},{16,32},{32,16},{48,0},{1,49},{17,33},{33,17},{49,1},{2,50}... | collective-permute-start | bytes 786440 | tf_op jit(solution)/shard_map/ppermute | solution.py:340
  193.9 9.1 %collective-permute-start.4 = (f32[128,512]{1,0:T(8,128)S(1)}, f32[128,512]{1,0:T(8,128)S(1)}, u32[]{:S(2)}, u32[]{:S(2)}) collective-permute-start(f32[128,512]{1,0:T(8,128)S(1)} %fusion), channel_id=1, source_target_pairs={{0,16},{16,0},{32,48},{48,32},{1,17},{17,1},{33,49},{49,33},{2,18}... | collective-permute-start | bytes 786440 | tf_op jit(solution)/shard_map/ppermute | solution.py:340
  198.2 18.5 %collective-permute-start.7 = (f32[104,256]{1,0:T(8,128)S(1)}, f32[104,256]{1,0:T(8,128)S(1)}, u32[]{:S(2)}, u32[]{:S(2)}) collective-permute-start(f32[104,256]{1,0:T(8,128)S(1)} %reduce_sum.9.after_ref.kept_ref), channel_id=1, source_target_pairs={{0,4},{4,0},{1,5},{5,1},{2,6},{6,2},{3,7},{7,3},{8,12},{12,8},{9,1... | collective-permute-start | bytes 319496 | tf_op jit(solution)/shard_map/ppermute | solution.py:340
  203.8 19.3 %collective-permute-start.5 = (f32[4,64,256]{2,1,0:T(8,128)S(1)}, f32[4,64,256]{2,1,0:T(8,128)S(1)}, u32[]{:S(2)}, u32[]{:S(2)}) collective-permute-start(f32[4,64,256]{2,1,0:T(8,128)S(1)} %get-tuple-element.19), channel_id=1, source_target_pairs={{0,64},{64,0},{128,192},{192,128},{256,320},{320,256},{384,448},{4... | collective-permute-start | bytes 786440 | tf_op jit(solution)/shard_map/ppermute | solution.py:340
  217.5 20.9 %all-to-all-start.13 = ((f32[4,96,256]{2,1,0:T(8,128)}), f32[4,96,256]{2,1,0:T(8,128)S(1)}, u32[]{:S(2)}, u32[]{:S(2)}) async-start(f32[4,96,256]{2,1,0:T(8,128)} %get-tuple-element.21), calls=%async_computation.13 | async-start | bytes 786432 | tf_op jit(solution)/shard_map/all_to_all | solution.py:22
  223.1 7.8 %collective-permute-start.6 = (f32[2,64,256]{2,1,0:T(8,128)S(1)}, f32[2,64,256]{2,1,0:T(8,128)S(1)}, u32[]{:S(2)}, u32[]{:S(2)}) collective-permute-start(f32[2,64,256]{2,1,0:T(8,128)S(1)} %get-tuple-element.22), channel_id=1, source_target_pairs={{0,128},{64,192},{128,0},{192,64},{256,384},{320,448},{384,256},{4... | collective-permute-start | bytes 393224 | tf_op jit(solution)/shard_map/ppermute | solution.py:340
  230.9 10.1 %collective-permute-start.8 = (f32[64,256]{1,0:T(8,128)S(1)}, f32[64,256]{1,0:T(8,128)S(1)}, u32[]{:S(2)}, u32[]{:S(2)}) collective-permute-start(f32[64,256]{1,0:T(8,128)S(1)} %slice_bitcast_fusion), channel_id=1, source_target_pairs={{0,256},{64,320},{128,384},{192,448},{256,0},{320,64},{384,128},{4... | collective-permute-start | bytes 196616 | tf_op jit(solution)/shard_map/ppermute | solution.py:340

commit v4 on v3

v4 whole, which is shorter than its diff:
```python
import functools

import jax
import jax.numpy as jnp
from jax import lax
from jax.experimental import pallas as pl
from jax.experimental.pallas import tpu as pltpu
from jax.sharding import Mesh, PartitionSpec as P

ITERS = 3
SHARP = 48.0
EPSILON = 1e-06

AXES = ("z", "x", "c", "h", "y")
Z, X, C, H, Y = 8, 4, 2, 2, 4
BLOCKS = C * X
LANES = 128
PAD = 8


def exchange(blocks, axes):
    return lax.all_to_all(blocks, axes, 0, 0, tiled=True)


FETCHES = 55_500_000
FETCHES_BESIDE_TILE = 40_000_000


def params(limit=8 << 20):
    return pltpu.CompilerParams(vmem_limit_bytes=limit)


def column_of(row):
    return jnp.broadcast_to(row, (LANES, row.shape[1])).T


def row_of(partial):
    return jnp.sum(partial.T, axis=0, keepdims=True)


def fold(product):
    total = product[:, :LANES]
    for start in range(LANES, product.shape[1], LANES):
        total = total + product[:, start : start + LANES]
    return total


def widen(column, width):
    return jnp.concatenate([column] * (width // LANES), axis=1)


def place(b):
    return (b % X) * C + b // X


def fetch(pairs, sems):
    copies = [pltpu.make_async_copy(source, target, sems.at[i]) for i, (source, target) in enumerate(pairs)]
    for copy in copies:
        copy.start()
    return copies


def setup_kernel(where_ref, latents_ref, codes_ref, tile_ref, rows_ref, far_ref, tokens_ref, held_ref, sems):
    del where_ref
    pairs = [(codes_ref.at[:, place(b)], held_ref.at[b]) for b in range(BLOCKS)]
    *copies, first = fetch(pairs + [(latents_ref, tokens_ref)], sems)
    first.wait()
    saves = []
    latents = tokens_ref[...]
    width = latents.shape[1]
    floats = latents.astype(jnp.float32)
    mean = jnp.sum(floats * floats, axis=1, keepdims=True) * (1.0 / width)
    scale = jnp.broadcast_to(lax.rsqrt(mean + EPSILON) * (SHARP / width), (latents.shape[0], LANES))
    total = jnp.zeros(scale.shape, jnp.float32)
    across = (((1,), (1,)), ((), ()))
    for b in range(BLOCKS):
        copies[b].wait()
        codes = held_ref[b].reshape(-1, width)
        floats = codes.astype(jnp.float32)
        code_norm = lax.rsqrt(row_of(fold(floats * floats)) * (1.0 / width) + EPSILON)
        inner = lax.dot_general(latents, codes, across, preferred_element_type=jnp.float32)
        tile = jnp.exp(inner * widen(scale, codes.shape[0]) * code_norm)
        tile_ref[b] = tile
        saves.append(pltpu.make_async_copy(tile_ref.at[b], far_ref.at[b], sems.at[BLOCKS + 1 + b]))
        saves[b].start()
        total += fold(tile)
    rows_ref[...] = jnp.broadcast_to(row_of(total)[None], rows_ref.shape)
    for save in saves:
        save.wait()


def rows_kernel(columns_ref, tile_ref, rows_ref, total_ref):
    step = pl.program_id(0)

    @pl.when(step == 0)
    def _():
        total_ref[...] = jnp.zeros_like(total_ref)

    total_ref[...] += fold(tile_ref[...] * columns_ref[...])

    @pl.when(step == pl.num_programs(0) - 1)
    def _():
        rows_ref[...] = jnp.broadcast_to(row_of(total_ref[...])[None], rows_ref.shape)


def row_scale_of(parts_ref):
    return column_of(1.0 / jnp.sum(parts_ref[...], axis=0))


def columns_kernel(parts_ref, tile_ref, columns_ref, scale_ref):
    @pl.when(pl.program_id(0) == 0)
    def _():
        scale_ref[...] = row_scale_of(parts_ref)

    tile = tile_ref[...]
    columns_ref[...] = jnp.sum(tile * widen(scale_ref[...], tile.shape[1]), axis=0, keepdims=True)


def targets_part(tile, scale, latents):
    weighted = (tile * widen(scale, tile.shape[1])).astype(jnp.bfloat16)
    return lax.dot_general(latents, weighted, (((0,), (0,)), ((), ())), preferred_element_type=jnp.float32)


def targets_sent_kernel(where_ref, parts_ref, latents_ref, tile_ref, after_ref, out_ref, tiles_ref, sems):
    del after_ref
    pairs = [(tile_ref.at[where_ref[3] * X + (where_ref[1] ^ s)], tiles_ref.at[s]) for s in range(X)]
    copies = fetch(pairs, sems)
    scale = row_scale_of(parts_ref)
    latents = latents_ref[...]
    for s in range(X):
        copies[s].wait()
        out_ref[s] = targets_part(tiles_ref[s], scale, latents)


def targets_kept_kernel(
    where_ref, parts_ref, latents_ref, tile_ref, added_ref, after_ref,
    one_ref, two_ref, own_one_ref, own_two_ref, tiles_ref, more_ref, sems,
):
    del after_ref
    pairs = [(tile_ref.at[where_ref[0] * X + (where_ref[1] ^ s)], tiles_ref.at[s]) for s in range(X)]
    pairs += [(added_ref.at[s], more_ref.at[s]) for s in range(X)]
    copies = fetch([pairs[i] for s in range(X) for i in (s, s + X)], sems)
    scale = row_scale_of(parts_ref)
    latents = latents_ref[...]
    for s in range(X):
        copies[2 * s].wait()
        summed = targets_part(tiles_ref[s], scale, latents)
        copies[2 * s + 1].wait()
        summed += more_ref[s]
        upper, lower = jnp.split(summed, 2, axis=0)
        ref, index = ((own_one_ref, 0), (one_ref, 0), (one_ref, 1), (own_one_ref, 1))[s]
        ref[index] = upper
        ref, index = ((own_two_ref, 0), (own_two_ref, 1), (two_ref, 1), (two_ref, 0))[s]
        ref[index] = lower


def sum_kernel(parts_ref, *refs):
    out_ref = refs[-1]
    out_ref[...] = jnp.broadcast_to(jnp.sum(parts_ref[...], axis=0, keepdims=True), out_ref.shape)


def inverse_kernel(factor, parts_ref, *refs):
    out_ref = refs[-1]
    out_ref[...] = jnp.broadcast_to(factor / jnp.sum(parts_ref[...], axis=0, keepdims=True), out_ref.shape)


def add_kernel(kept_ref, came_ref, after_ref, out_ref):
    del after_ref
    out_ref[...] = kept_ref[...] + came_ref[...]


def join_kernel(kept_ref, came_ref, spread_ref, mass_ref):
    total = kept_ref[...] + came_ref[...]
    group = spread_ref.shape[1]
    spread_ref[...] = jnp.broadcast_to(total[None, :group], spread_ref.shape)
    mass_ref[...] = total[group:]


def turn_kernel(where_ref, own_one_ref, one_ref, more_one_ref, own_two_ref, two_ref, more_two_ref, after_ref, *refs):
    del after_ref
    send_ref, keep_ref, turned_ref = refs
    upper = own_one_ref[0] + one_ref[0] + more_one_ref[...]
    lower = own_two_ref[0] + two_ref[0] + more_two_ref[...]
    turned_ref[...] = jnp.concatenate([upper, lower], axis=0).T
    share = send_ref.shape[1]
    for i, slot in enumerate((0, 4, 2, 6)):
        for ref, s in ((keep_ref, slot), (send_ref, slot + 1)):
            start = pl.multiple_of((where_ref[2] ^ s) * share, share)
            ref[i] = turned_ref[pl.ds(start, share), :]


def final_kernel(
    parts_ref, columns_ref, codes_ref, tile_ref, out_ref, held_ref, tiles_ref, numer_ref, sems
):
    pairs = [
        pair
        for b in range(BLOCKS)
        for pair in ((tile_ref.at[b], tiles_ref.at[b]), (codes_ref.at[:, place(b)], held_ref.at[b]))
    ]
    copies = fetch(pairs, sems)
    tokens, width = numer_ref.shape
    scale = row_scale_of(parts_ref)
    total = jnp.zeros(scale.shape, jnp.float32)
    for b in range(BLOCKS):
        copies[2 * b].wait()
        tile = tiles_ref[b]
        plan = (widen(scale, tile.shape[1]) * tile * columns_ref[b]).astype(jnp.bfloat16)
        total += fold(plan.astype(jnp.float32))
        copies[2 * b + 1].wait()
        part = jnp.dot(plan, held_ref[b].reshape(-1, width), preferred_element_type=jnp.float32)
        numer_ref[...] = part if b == 0 else numer_ref[...] + part
    group = tokens // Y
    mass = row_of(total)
    mass = jnp.concatenate([mass, jnp.zeros((1, 2 * width - tokens), jnp.float32)], axis=1)
    extra = jnp.concatenate(
        [mass[:, :width], mass[:, width:], jnp.zeros((PAD - 2, width), jnp.float32)], axis=0
    )
    for y in range(Y):
        out_ref[y, :group, :] = numer_ref[y * group : (y + 1) * group, :]
        out_ref[y, group:, :] = extra


def f32(*shape):
    return jax.ShapeDtypeStruct(shape, jnp.float32)


def whole(*shape):
    return pl.BlockSpec(shape, lambda *_: (0,) * len(shape))


def cost(flops, moved, exps=0):
    return pl.CostEstimate(flops=flops, bytes_accessed=moved, transcendentals=exps)


def per_device(latents, codebook):
    token_count, width = latents.shape
    code_count = codebook.shape[0]
    total_tokens = token_count * Z * X * C
    total_codes = code_count * H * Y
    share = code_count // (Z * X * C)
    block = code_count // BLOCKS
    size = token_count * code_count

    codes = codebook.reshape(Z, X * C, share, width)
    tile_spec = pl.BlockSpec((None, token_count, block), lambda b: (b, 0, 0))
    rows_spec = whole(H * Y, 1, token_count)
    columns_spec = pl.BlockSpec((None, 1, block), lambda b: (b, 0, 0))
    vmem = pl.BlockSpec(memory_space=pltpu.VMEM)
    smem = pl.BlockSpec(memory_space=pltpu.SMEM)
    hbm = pl.BlockSpec(memory_space=pltpu.HBM)
    anywhere = pl.BlockSpec(memory_space=pl.ANY)
    per_token = pltpu.VMEM((token_count, LANES), jnp.float32)
    held = pltpu.VMEM((BLOCKS, Z, share, width), jnp.bfloat16)
    tiles = functools.partial(pltpu.VMEM, dtype=jnp.float32)
    rows_shape = f32(H * Y, 1, token_count)
    columns_shape = f32(BLOCKS, 1, block)

    core, x, z = (lax.axis_index(axis) for axis in ("c", "x", "z"))
    where = jnp.stack([core, x, z, 1 - core, z * share])

    tile, part, far = pl.pallas_call(
        setup_kernel,
        in_specs=[smem, hbm, hbm],
        out_specs=[vmem, vmem, hbm],
        out_shape=[f32(BLOCKS, token_count, block), rows_shape, f32(BLOCKS, token_count, block)],
        scratch_shapes=[
            pltpu.VMEM((token_count, width), jnp.bfloat16),
            held,
            pltpu.SemaphoreType.DMA((2 * BLOCKS + 1,)),
        ],
        compiler_params=params(FETCHES_BESIDE_TILE),
        cost_estimate=cost(2 * size * width, 4 * size, size),
        name="setup",
    )(where, latents, codes)

    def rows(columns):
        return pl.pallas_call(
            rows_kernel,
            grid=(BLOCKS,),
            in_specs=[columns_spec, tile_spec],
            out_specs=rows_spec,
            out_shape=rows_shape,
            scratch_shapes=[per_token],
            compiler_params=params(),
            cost_estimate=cost(2 * size, 4 * size),
            name="rows",
        )(columns, tile)

    def columns(parts):
        return pl.pallas_call(
            columns_kernel,
            grid=(BLOCKS,),
            in_specs=[rows_spec, tile_spec],
            out_specs=columns_spec,
            out_shape=columns_shape,
            scratch_shapes=[per_token],
            compiler_params=params(),
            cost_estimate=cost(2 * size, 4 * size),
            name="columns",
        )(parts, tile)

    def targets_sent(parts, after):
        return pl.pallas_call(
            targets_sent_kernel,
            in_specs=[smem, vmem, vmem, hbm, anywhere],
            out_specs=vmem,
            out_shape=f32(X, width, block),
            scratch_shapes=[tiles((X, token_count, block)), pltpu.SemaphoreType.DMA((X,))],
            compiler_params=params(FETCHES),
            cost_estimate=cost(size * width, 4 * size),
            name="targets_sent",
        )(where, parts, latents, far, after)

    def targets_kept(parts, added, after):
        return pl.pallas_call(
            targets_kept_kernel,
            in_specs=[smem, vmem, vmem, hbm, hbm, anywhere],
            out_specs=[vmem] * 4,
            out_shape=[f32(2, width // 2, block)] * 4,
            scratch_shapes=[
                tiles((X, token_count, block)),
                tiles((X, width, block)),
                pltpu.SemaphoreType.DMA((2 * X,)),
            ],
            compiler_params=params(FETCHES),
            cost_estimate=cost(size * width, 4 * size),
            name="targets_kept",
        )(where, parts, latents, far, added, after)

    def small(kernel, name, count, weight, parts, *after):
        return pl.pallas_call(
            kernel,
            in_specs=[vmem] + [anywhere] * len(after),
            out_specs=vmem,
            out_shape=f32(count, 1, block),
            compiler_params=params(),
            cost_estimate=cost(weight * parts.size, 4 * parts.size),
            name=name,
        )(parts, *after)

    inverse = functools.partial(inverse_kernel, total_tokens / total_codes)
    def swap(value, axis, count, bits):
        return lax.ppermute(value, axis, [(i, i ^ bits) for i in range(count)])

    def add(kept, came, after):
        return pl.pallas_call(
            add_kernel,
            in_specs=[vmem] * 2 + [anywhere],
            out_specs=vmem,
            out_shape=f32(*kept.shape),
            compiler_params=params(),
            cost_estimate=cost(kept.size, 12 * kept.size),
            name="add",
        )(kept, came, after)

    for sweep_index in range(ITERS):
        last = sweep_index == ITERS - 1
        parts = exchange(part, ("h", "y"))
        column_sums = columns(parts)
        if last:
            sent = targets_sent(parts, column_sums)
        sums = small(sum_kernel, "sums", Z, 20_000_000 if last else 1, exchange(column_sums, ("c", "x")))
        if last:
            kept = targets_kept(parts, swap(sent, "c", C, 1), sums)
        after = (kept[0],) if last else ()
        mine = small(inverse, "inverse", BLOCKS, 1, exchange(sums, "z"), *after)
        col_scale = exchange(mine, ("c", "x"))
        if not last:
            part = rows(col_scale)

    one, two, own_one, own_two = kept
    one, two = swap(one, "x", X, 1), swap(two, "x", X, 3)
    more_one = swap(own_one[1] + one[1], "x", X, 3)
    more_two = swap(own_two[1] + two[1], "x", X, 1)

    group = token_count // Y
    packed = pl.pallas_call(
        final_kernel,
        in_specs=[vmem, vmem, hbm, hbm],
        out_specs=vmem,
        out_shape=f32(Y, group + PAD, width),
        scratch_shapes=[
            held,
            tiles((BLOCKS, token_count, block)),
            tiles((token_count, width)),
            pltpu.SemaphoreType.DMA((2 * BLOCKS,)),
        ],
        compiler_params=params(FETCHES),
        cost_estimate=cost(13 * size * width, 4 * size),
        name="final",
    )(parts, col_scale, codes, far)
    packed = jnp.sum(exchange(packed, "y"), axis=0)
    away, near = pl.pallas_call(
        turn_kernel,
        in_specs=[smem] + [vmem] * 6 + [anywhere],
        out_specs=[vmem] * 2,
        out_shape=[f32(Z // 2, share, width)] * 2,
        scratch_shapes=[pltpu.VMEM((block, width), jnp.float32)],
        compiler_params=params(16 << 20),
        cost_estimate=cost(3 * block * width, 12 * block * width),
        name="turn",
    )(where, own_one, one, more_one, own_two, two, more_two, packed)
    numer, mass = pl.pallas_call(
        join_kernel,
        in_specs=[vmem] * 2,
        out_specs=[vmem] * 2,
        out_shape=[f32(Y, group, width), f32(PAD, width)],
        compiler_params=params(),
        cost_estimate=cost(20000 * token_count * width, 8 * token_count * width),
        name="join",
    )(packed, swap(packed, "h", H, 1))
    near = near + swap(away, "z", Z, 1)
    near = add(near[:2], swap(near[2:], "z", Z, 2), mass)
    summed = near[0] + swap(near[1], "z", Z, 4)
    own = lax.dynamic_slice(mine, (0, 0, where[4]), (1, 1, share)).reshape(share)
    targets = summed * (own * (total_codes / total_tokens))[:, None]
    mass = mass[:2].reshape(2 * width)[:token_count]
    rebuilt = exchange(numer, "y").reshape(token_count, width) / mass[:, None]
    return (targets, rebuilt)


def solution(mesh):
    fine = Mesh(mesh.devices.reshape(Z, X, C, H, Y), AXES)
    return jax.shard_map(
        per_device,
        mesh=fine,
        in_specs=(P(("z", "x", "c"), None), P(("h", "y"), None)),
        out_specs=(P(("h", "y", "z", "x", "c"), None), P(("z", "x", "c"), None)),
        check_vma=False,
    )
```

time: 246 us -> 248 us (level)
  starting transfers between devices: 50.1 us -> 65.5 us
  local copies, waits for them, and re-layouts: 9.79 us -> 2.65 us
  blocking collectives: 133 us -> 126 us
  Pallas kernels: 22.1 us -> 28.3 us
  waiting for transfers between devices: 21.9 us -> 16.9 us
    ppermute x9, starting transfers between devices: 31.8 us -> 42.6 us  [swap(): return lax.ppermute(value, axis, [(i, i ^ bits) for i in range(count)])]
    all_to_all x10 -> x9, blocking collectives: 133 us -> 126 us  [exchange(): return lax.all_to_all(blocks, axes, 0, 0, tiled=True)]
    unnamed x16 -> x14, local copies, waits for them, and re-layouts: 9.68 us -> 2.54 us
    all_to_all x4 -> x5, starting transfers between devices: 18.3 us -> 22.9 us  [exchange(): return lax.all_to_all(blocks, axes, 0, 0, tiled=True)]
    pallas_call x12, Pallas kernels: 17.2 us -> 21.6 us  [the longest x1 5.69 us: per_device(): pl.pallas_call(final_kernel, in_specs=[vmem, vmem, hbm, hbm], out_specs=v...]
    ppermute x9, waiting for transfers between devices: 17 us -> 13.2 us  [swap(): return lax.ppermute(value, axis, [(i, i ^ bits) for i in range(count)])]
    all_to_all x4 -> x5, waiting for transfers between devices: 4.97 us -> 3.69 us  [exchange(): return lax.all_to_all(blocks, axes, 0, 0, tiled=True)]
  transfers between devices with their start and end apart: 13 -> 14, of which waited for: 7 -> 8; matrix products, arithmetic and copies ran while one was open for 1% -> 1% of each run, Pallas kernels for 4% -> 7%
where the time goes in v4:
time: 248 us; the launch traced here: 244 us
  blocking collectives  126 us (51%)
  starting transfers between devices  65.5 us (26%)
  Pallas kernels  28.3 us (11%)
  waiting for transfers between devices  16.9 us (7%)
  other arithmetic  3.47 us (1%)
  local copies, waits for them, and re-layouts  2.65 us (1%)
    all_to_all x9, blocking collectives, exchange(): return lax.all_to_all(blocks, axes, 0, 0, tiled=True)  126 us
    ppermute x9, starting transfers between devices, swap(): return lax.ppermute(value, axis, [(i, i ^ bits) for i in range(count)])  42.6 us
    all_to_all x5, starting transfers between devices, exchange(): return lax.all_to_all(blocks, axes, 0, 0, tiled=True)  22.9 us
    ppermute x9, waiting for transfers between devices, swap(): return lax.ppermute(value, axis, [(i, i ^ bits) for i in range(count)])  13.2 us
    pallas_call x1, Pallas kernels, per_device(): pl.pallas_call(final_kernel, in_specs=[vmem, vmem, hbm, hbm], out_specs=v...  5.69 us
  transfers between devices with their start and end apart: 14, of which 8 were waited for; matrix products, arithmetic and copies ran while one was open for 1% of the time, Pallas kernels for 7%

profile of v4, /device:TPU:24, one launch (start us, length us, event | category | flops | bytes accessed | tf_op | source)
XLA Modules:
  0.0 243.5 jit_solution(6141739709221247696)
XLA Ops:
  0.7 0.9 copy-done.3
  1.7 1.6 copy-done.5
  3.2 4.9 %setup.1 = (f32[8,384,512]{2,1,0:T(8,128)S(1)}, f32[8,1,384]{2,1,0:T(1,128)S(1)}, f32[8,384,512]{2,1,0:T(8,128)S(1)}) custom-call(s32[5]{0:T(128)S(1)} %stack.23.where_ref, bf16[384,256]{1,0:T(8,128)(2,1)S(1)} %copy-done.3, bf16[8,8,64,256]{3,2,1,0:T(8,128)(2,1)S(1)} %bitcast.27), custom_call_target="tpu_custom_call" | custom-call | flops 805306368 | bytes 6291456 | tf_op jit(solution)/shard_map/setup/pallas_call | solution.py:261
  8.1 30.6 %all_to_all.70.parts_ref = f32[8,1,384]{2,1,0:T(1,128)S(1)} all-to-all(f32[8,1,384]{2,1,0:T(1,128)S(1)} %get-tuple-element.13), channel_id=1, replica_groups=mesh['z'=8,'x'=4,'c'=2,'h'=2,'y'=4] {'h','y'}, dimensions={0} | all-to-all | bytes 24576 | tf_op jit(solution)/shard_map/all_to_all | solution.py:22
  38.7 0.8 columns.3
  39.6 9.4 %all_to_all.71.parts_ref = f32[8,1,512]{2,1,0:T(1,128)S(1)} all-to-all(f32[8,1,512]{2,1,0:T(1,128)S(1)} %columns.3), channel_id=1, replica_groups=mesh['z'=8,'x'=4,'c'=2,'h'=2,'y'=4] {'c','x'}, dimensions={0} | all-to-all | bytes 32768 | tf_op jit(solution)/shard_map/all_to_all | solution.py:22
  49.0 15.3 %all_to_all.72.parts_ref = f32[8,1,512]{2,1,0:T(1,128)S(1)} all-to-all(f32[8,1,512]{2,1,0:T(1,128)S(1)} %sums.3), channel_id=1, replica_groups=mesh['z'=8,'x'=4,'c'=2,'h'=2,'y'=4] {'z'}, dimensions={0} | all-to-all | bytes 32768 | tf_op jit(solution)/shard_map/all_to_all | solution.py:22
  64.3 7.6 %all_to_all.73.columns_ref = f32[8,1,512]{2,1,0:T(1,128)S(1)} all-to-all(f32[8,1,512]{2,1,0:T(1,128)S(1)} %inverse.3), channel_id=1, replica_groups=mesh['z'=8,'x'=4,'c'=2,'h'=2,'y'=4] {'c','x'}, dimensions={0} | all-to-all | bytes 32768 | tf_op jit(solution)/shard_map/all_to_all | solution.py:22
  72.0 0.8 rows.2
  72.7 17.3 %all_to_all.74.parts_ref = f32[8,1,384]{2,1,0:T(1,128)S(1)} all-to-all(f32[8,1,384]{2,1,0:T(1,128)S(1)} %rows.2), channel_id=1, replica_groups=mesh['z'=8,'x'=4,'c'=2,'h'=2,'y'=4] {'h','y'}, dimensions={0} | all-to-all | bytes 24576 | tf_op jit(solution)/shard_map/all_to_all | solution.py:22
  90.0 0.8 columns.4
  90.8 7.6 %all_to_all.75.parts_ref = f32[8,1,512]{2,1,0:T(1,128)S(1)} all-to-all(f32[8,1,512]{2,1,0:T(1,128)S(1)} %columns.4), channel_id=1, replica_groups=mesh['z'=8,'x'=4,'c'=2,'h'=2,'y'=4] {'c','x'}, dimensions={0} | all-to-all | bytes 32768 | tf_op jit(solution)/shard_map/all_to_all | solution.py:22
  98.5 12.9 %all_to_all.76.parts_ref = f32[8,1,512]{2,1,0:T(1,128)S(1)} all-to-all(f32[8,1,512]{2,1,0:T(1,128)S(1)} %sums.4), channel_id=1, replica_groups=mesh['z'=8,'x'=4,'c'=2,'h'=2,'y'=4] {'z'}, dimensions={0} | all-to-all | bytes 32768 | tf_op jit(solution)/shard_map/all_to_all | solution.py:22
  111.4 7.6 %all_to_all.77.columns_ref = f32[8,1,512]{2,1,0:T(1,128)S(1)} all-to-all(f32[8,1,512]{2,1,0:T(1,128)S(1)} %inverse.4), channel_id=1, replica_groups=mesh['z'=8,'x'=4,'c'=2,'h'=2,'y'=4] {'c','x'}, dimensions={0} | all-to-all | bytes 32768 | tf_op jit(solution)/shard_map/all_to_all | solution.py:22
  119.0 0.8 rows.3
  119.8 17.3 %all_to_all.78.parts_ref = f32[8,1,384]{2,1,0:T(1,128)S(1)} all-to-all(f32[8,1,384]{2,1,0:T(1,128)S(1)} %rows.3), channel_id=1, replica_groups=mesh['z'=8,'x'=4,'c'=2,'h'=2,'y'=4] {'h','y'}, dimensions={0} | all-to-all | bytes 24576 | tf_op jit(solution)/shard_map/all_to_all | solution.py:22
  137.1 2.9 %columns.5.after_ref = f32[8,1,512]{2,1,0:T(1,128)} custom-call(f32[8,1,384]{2,1,0:T(1,128)S(1)} %all_to_all.78.parts_ref, f32[8,384,512]{2,1,0:T(8,128)S(1)} %get-tuple-element.14.tile_ref), custom_call_target="tpu_custom_call" | custom-call | flops 3145728 | bytes 6291456 | tf_op jit(solution)/shard_map/columns/pallas_call | solution.py:290
  139.9 3.3 %all-to-all-start.9 = ((f32[8,1,512]{2,1,0:T(1,128)}), f32[8,1,512]{2,1,0:T(1,128)S(1)}, u32[]{:S(2)}, u32[]{:S(2)}) async-start(f32[8,1,512]{2,1,0:T(1,128)} %columns.5.after_ref), calls=%async_computation.9 | async-start | bytes 32768 | tf_op jit(solution)/shard_map/all_to_all | solution.py:22
  143.3 4.3 %targets_sent.1 = f32[4,256,512]{2,1,0:T(8,128)} custom-call(s32[5]{0:T(128)S(1)} %stack.23.where_ref, f32[8,1,384]{2,1,0:T(1,128)S(1)} %all_to_all.78.parts_ref, bf16[384,256]{1,0:T(8,128)(2,1)S(1)} %copy-done.4, f32[8,384,512]{2,1,0:T(8,128)} %copy-done, f32[8,1,512]{2,1,0:T(1,128)} %columns.5.after_ref), custom_call_target="tpu_custom_call" | custom-call | flops 402653184 | bytes 6291456 | tf_op jit(solution)/shard_map/targets_sent/pallas_call | solution.py:303
  147.7 2.3 collective-permute-start
  150.0 0.6 sums.5.after_ref
  150.6 3.3 %all-to-all-start.10 = ((f32[8,1,512]{2,1,0:T(1,128)}), f32[8,1,512]{2,1,0:T(1,128)S(1)}, u32[]{:S(2)}, u32[]{:S(2)}) async-start(f32[8,1,512]{2,1,0:T(1,128)} %sums.5.after_ref), calls=%async_computation.10 | async-start | bytes 32768 | tf_op jit(solution)/shard_map/all_to_all | solution.py:22
  154.1 4.5 %targets_kept.1 = (f32[2,128,512]{2,1,0:T(8,128)S(1)}, f32[2,128,512]{2,1,0:T(8,128)}, f32[2,128,512]{2,1,0:T(8,128)}, f32[2,128,512]{2,1,0:T(8,128)}) custom-call(s32[5]{0:T(128)S(1)} %stack.23.where_ref, f32[8,1,384]{2,1,0:T(1,128)S(1)} %all_to_all.78.parts_ref, bf16[384,256]{1,0:T(8,128)(2,1)S(1)} %copy-done.4, f32[8,384,512]{2,1,0:T(8,128)} %copy-done, ...), custom_call_target="tpu_custom_call" | custom-call | flops 402653184 | bytes 6291456 | tf_op jit(solution)/shard_map/targets_kept/pallas_call | solution.py:315
  158.6 5.0 %collective-permute-start.3 = (f32[2,128,512]{2,1,0:T(8,128)}, f32[2,128,512]{2,1,0:T(8,128)S(1)}, u32[]{:S(2)}, u32[]{:S(2)}) collective-permute-start(f32[2,128,512]{2,1,0:T(8,128)} %get-tuple-element.19), channel_id=1, source_target_pairs={{0,48},{16,32},{32,16},{48,0},{1,49},{17,33},{33,17},{49,1},{2,50}... | collective-permute-start | bytes 1572872 | tf_op jit(solution)/shard_map/ppermute | solution.py:343
  163.7 0.8 all-to-all-done.10.parts_ref
  164.4 0.6 inverse.5
  165.0 4.4 %all-to-all-start.11 = ((f32[8,1,512]{2,1,0:T(1,128)}), f32[8,1,512]{2,1,0:T(1,128)S(1)}, u32[]{:S(2)}, u32[]{:S(2)}) async-start(f32[8,1,512]{2,1,0:T(1,128)} %inverse.5), calls=%async_computation.11 | async-start | bytes 32768 | tf_op jit(solution)/shard_map/all_to_all | solution.py:22
  169.5 4.0 %collective-permute-start.1 = (f32[2,128,512]{2,1,0:T(8,128)S(1)}, f32[2,128,512]{2,1,0:T(8,128)S(1)}, u32[]{:S(2)}, u32[]{:S(2)}) collective-permute-start(f32[2,128,512]{2,1,0:T(8,128)S(1)} %get-tuple-element.17.refs_0_), channel_id=1, source_target_pairs={{0,16},{16,0},{32,48},{48,32},{1,17},{17,1},{33,49},{49,33},{2,18}... | collective-permute-start | bytes 1572872 | tf_op jit(solution)/shard_map/ppermute | solution.py:343
  173.5 2.8 %all-to-all-done.11.columns_ref = f32[8,1,512]{2,1,0:T(1,128)S(1)} async-done(((f32[8,1,512]{2,1,0:T(1,128)}), f32[8,1,512]{2,1,0:T(1,128)S(1)}, u32[]{:S(2)}, u32[]{:S(2)}) %all-to-all-start.11) | async-done | bytes 16416 | tf_op jit(solution)/shard_map/all_to_all | solution.py:22
  176.3 5.7 %final.1 = f32[4,104,256]{2,1,0:T(8,128)} custom-call(f32[8,1,384]{2,1,0:T(1,128)S(1)} %all_to_all.78.parts_ref, f32[8,1,512]{2,1,0:T(1,128)S(1)} %all-to-all-done.11.columns_ref, bf16[8,8,64,256]{3,2,1,0:T(8,128)(2,1)} %bitcast.26, f32[8,384,512]{2,1,0:T(8,128)} %copy-done), custom_call_target="tpu_custom_call" | custom-call | flops 5234491392 | bytes 6291456 | tf_op jit(solution)/shard_map/final/pallas_call | solution.py:377
  182.0 6.2 %all-to-all-start.12 = ((f32[4,104,256]{2,1,0:T(8,128)}), f32[4,104,256]{2,1,0:T(8,128)}, u32[]{:S(2)}, u32[]{:S(2)}) async-start(f32[4,104,256]{2,1,0:T(8,128)} %final.1), calls=%async_computation.12 | async-start | bytes 851968 | tf_op jit(solution)/shard_map/all_to_all | solution.py:22
  188.2 2.3 collective-permute-start.4
  190.7 4.4 %collective-permute-start.2 = (f32[128,512]{1,0:T(8,128)S(1)}, f32[128,512]{1,0:T(8,128)S(1)}, u32[]{:S(2)}, u32[]{:S(2)}) collective-permute-start(f32[128,512]{1,0:T(8,128)S(1)} %fusion.1), channel_id=1, source_target_pairs={{0,48},{16,32},{32,16},{48,0},{1,49},{17,33},{33,17},{49,1},{2,50}... | collective-permute-start | bytes 786440 | tf_op jit(solution)/shard_map/ppermute | solution.py:343
  195.2 1.0 reduce_sum.9.after_ref.kept_ref
  196.3 2.5 %collective-permute-start.7 = (f32[104,256]{1,0:T(8,128)S(1)}, f32[104,256]{1,0:T(8,128)S(1)}, u32[]{:S(2)}, u32[]{:S(2)}) collective-permute-start(f32[104,256]{1,0:T(8,128)S(1)} %reduce_sum.9.after_ref.kept_ref), channel_id=1, source_target_pairs={{0,4},{4,0},{1,5},{5,1},{2,6},{6,2},{3,7},{7,3},{8,12},{12,8},{9,1... | collective-permute-start | bytes 319496 | tf_op jit(solution)/shard_map/ppermute | solution.py:343
  198.8 2.8 %collective-permute-done.2.more_one_ref = f32[128,512]{1,0:T(8,128)S(1)} collective-permute-done((f32[128,512]{1,0:T(8,128)S(1)}, f32[128,512]{1,0:T(8,128)S(1)}, u32[]{:S(2)}, u32[]{:S(2)}) %collective-permute-start.2) | collective-permute-done | bytes 262176 | tf_op jit(solution)/shard_map/ppermute | solution.py:343
  201.5 0.8 turn.1
  202.3 3.4 %collective-permute-start.5 = (f32[4,64,256]{2,1,0:T(8,128)S(1)}, f32[4,64,256]{2,1,0:T(8,128)S(1)}, u32[]{:S(2)}, u32[]{:S(2)}) collective-permute-start(f32[4,64,256]{2,1,0:T(8,128)S(1)} %get-tuple-element.21), channel_id=1, source_target_pairs={{0,64},{64,0},{128,192},{192,128},{256,320},{320,256},{384,448},{4... | collective-permute-start | bytes 786440 | tf_op jit(solution)/shard_map/ppermute | solution.py:343
  205.8 0.7 multiply_bitcast_fusion
  206.5 5.3 %collective-permute-done.7.came_ref = f32[104,256]{1,0:T(8,128)S(1)} collective-permute-done((f32[104,256]{1,0:T(8,128)S(1)}, f32[104,256]{1,0:T(8,128)S(1)}, u32[]{:S(2)}, u32[]{:S(2)}) %collective-permute-start.7) | collective-permute-done | bytes 106528 | tf_op jit(solution)/shard_map/ppermute | solution.py:343
  211.8 0.8 join.1
  212.6 5.6 %all-to-all-start.13 = ((f32[4,96,256]{2,1,0:T(8,128)}), f32[4,96,256]{2,1,0:T(8,128)S(1)}, u32[]{:S(2)}, u32[]{:S(2)}) async-start(f32[4,96,256]{2,1,0:T(8,128)} %get-tuple-element.23), calls=%async_computation.13 | async-start | bytes 786432 | tf_op jit(solution)/shard_map/all_to_all | solution.py:22
  218.2 10.7 %collective-permute-start.6 = (f32[2,64,256]{2,1,0:T(8,128)S(1)}, f32[2,64,256]{2,1,0:T(8,128)S(1)}, u32[]{:S(2)}, u32[]{:S(2)}) collective-permute-start(f32[2,64,256]{2,1,0:T(8,128)S(1)} %get-tuple-element.24), channel_id=1, source_target_pairs={{0,128},{64,192},{128,0},{192,64},{256,384},{320,448},{384,256},{4... | collective-permute-start | bytes 393224 | tf_op jit(solution)/shard_map/ppermute | solution.py:343
  229.0 3.6 %collective-permute-done.6.came_ref = f32[2,64,256]{2,1,0:T(8,128)S(1)} collective-permute-done((f32[2,64,256]{2,1,0:T(8,128)S(1)}, f32[2,64,256]{2,1,0:T(8,128)S(1)}, u32[]{:S(2)}, u32[]{:S(2)}) %collective-permute-start.6) | collective-permute-done | bytes 131104 | tf_op jit(solution)/shard_map/ppermute | solution.py:343
  232.6 7.9 %collective-permute-start.8 = (f32[64,256]{1,0:T(8,128)S(1)}, f32[64,256]{1,0:T(8,128)S(1)}, u32[]{:S(2)}, u32[]{:S(2)}) collective-permute-start(f32[64,256]{1,0:T(8,128)S(1)} %slice_bitcast_fusion), channel_id=1, source_target_pairs={{0,256},{64,320},{128,384},{192,448},{256,0},{320,64},{384,128},{4... | collective-permute-start | bytes 196616 | tf_op jit(solution)/shard_map/ppermute | solution.py:343
  240.6 0.9 bitcast_divide_fusion
  241.4 1.4 collective-permute-done.8
  242.8 0.7 fusion.3
  (31 shorter events, 0.7 us)
Async XLA Ops:
  0.7 0.9 copy-start.3
  1.7 1.6 copy-start.5
  8.1 31.4 %copy-start = (f32[8,384,512]{2,1,0:T(8,128)}, f32[8,384,512]{2,1,0:T(8,128)S(1)}, u32[]{:S(2)}) copy-start(f32[8,384,512]{2,1,0:T(8,128)S(1)} %get-tuple-element.15.tile_ref) | copy-start | bytes 18874372
  137.1 6.2 %copy-start.4 = (bf16[384,256]{1,0:T(8,128)(2,1)S(1)}, bf16[384,256]{1,0:T(8,128)(2,1)}, u32[]{:S(2)}) copy-start(bf16[384,256]{1,0:T(8,128)(2,1)} %latents_ref.5) | copy-start | bytes 589828
  139.9 10.0 %all-to-all-start.9 = ((f32[8,1,512]{2,1,0:T(1,128)}), f32[8,1,512]{2,1,0:T(1,128)S(1)}, u32[]{:S(2)}, u32[]{:S(2)}) async-start(f32[8,1,512]{2,1,0:T(1,128)} %columns.5.after_ref), calls=%async_computation.9 | async-start | bytes 32768 | tf_op jit(solution)/shard_map/all_to_all | solution.py:22
  147.7 6.4 %collective-permute-start = (f32[4,256,512]{2,1,0:T(8,128)}, f32[4,256,512]{2,1,0:T(8,128)}, u32[]{:S(2)}, u32[]{:S(2)}) collective-permute-start(f32[4,256,512]{2,1,0:T(8,128)} %targets_sent.1), channel_id=1, source_target_pairs={{0,8},{8,0},{1,9},{9,1},{2,10},{10,2},{3,11},{11,3},{4,12},{12,4},... | collective-permute-start | bytes 6291464 | tf_op jit(solution)/shard_map/ppermute | solution.py:343
  150.6 13.8 %all-to-all-start.10 = ((f32[8,1,512]{2,1,0:T(1,128)}), f32[8,1,512]{2,1,0:T(1,128)S(1)}, u32[]{:S(2)}, u32[]{:S(2)}) async-start(f32[8,1,512]{2,1,0:T(1,128)} %sums.5.after_ref), calls=%async_computation.10 | async-start | bytes 32768 | tf_op jit(solution)/shard_map/all_to_all | solution.py:22
  158.6 29.5 %collective-permute-start.3 = (f32[2,128,512]{2,1,0:T(8,128)}, f32[2,128,512]{2,1,0:T(8,128)S(1)}, u32[]{:S(2)}, u32[]{:S(2)}) collective-permute-start(f32[2,128,512]{2,1,0:T(8,128)} %get-tuple-element.19), channel_id=1, source_target_pairs={{0,48},{16,32},{32,16},{48,0},{1,49},{17,33},{33,17},{49,1},{2,50}... | collective-permute-start | bytes 1572872 | tf_op jit(solution)/shard_map/ppermute | solution.py:343
  165.0 11.3 %all-to-all-start.11 = ((f32[8,1,512]{2,1,0:T(1,128)}), f32[8,1,512]{2,1,0:T(1,128)S(1)}, u32[]{:S(2)}, u32[]{:S(2)}) async-start(f32[8,1,512]{2,1,0:T(1,128)} %inverse.5), calls=%async_computation.11 | async-start | bytes 32768 | tf_op jit(solution)/shard_map/all_to_all | solution.py:22
  169.5 18.7 %copy-start.2 = (f32[2,128,512]{2,1,0:T(8,128)S(1)}, f32[2,128,512]{2,1,0:T(8,128)}, u32[]{:S(2)}) copy-start(f32[2,128,512]{2,1,0:T(8,128)} %get-tuple-element.18.own_two_ref) | copy-start | bytes 1572868
  169.5 21.1 %copy-start.1 = (f32[2,128,512]{2,1,0:T(8,128)S(1)}, f32[2,128,512]{2,1,0:T(8,128)}, u32[]{:S(2)}) copy-start(f32[2,128,512]{2,1,0:T(8,128)} %get-tuple-element.16.own_one_ref) | copy-start | bytes 1572868
  169.5 21.1 %collective-permute-start.1 = (f32[2,128,512]{2,1,0:T(8,128)S(1)}, f32[2,128,512]{2,1,0:T(8,128)S(1)}, u32[]{:S(2)}, u32[]{:S(2)}) collective-permute-start(f32[2,128,512]{2,1,0:T(8,128)S(1)} %get-tuple-element.17.refs_0_), channel_id=1, source_target_pairs={{0,16},{16,0},{32,48},{48,32},{1,17},{17,1},{33,49},{49,33},{2,18}... | collective-permute-start | bytes 1572872 | tf_op jit(solution)/shard_map/ppermute | solution.py:343
  182.0 13.2 %all-to-all-start.12 = ((f32[4,104,256]{2,1,0:T(8,128)}), f32[4,104,256]{2,1,0:T(8,128)}, u32[]{:S(2)}, u32[]{:S(2)}) async-start(f32[4,104,256]{2,1,0:T(8,128)} %final.1), calls=%async_computation.12 | async-start | bytes 851968 | tf_op jit(solution)/shard_map/all_to_all | solution.py:22
  188.2 10.5 %collective-permute-start.4 = (f32[128,512]{1,0:T(8,128)S(1)}, f32[128,512]{1,0:T(8,128)S(1)}, u32[]{:S(2)}, u32[]{:S(2)}) collective-permute-start(f32[128,512]{1,0:T(8,128)S(1)} %fusion), channel_id=1, source_target_pairs={{0,16},{16,0},{32,48},{48,32},{1,17},{17,1},{33,49},{49,33},{2,18}... | collective-permute-start | bytes 786440 | tf_op jit(solution)/shard_map/ppermute | solution.py:343
  190.7 10.9 %collective-permute-start.2 = (f32[128,512]{1,0:T(8,128)S(1)}, f32[128,512]{1,0:T(8,128)S(1)}, u32[]{:S(2)}, u32[]{:S(2)}) collective-permute-start(f32[128,512]{1,0:T(8,128)S(1)} %fusion.1), channel_id=1, source_target_pairs={{0,48},{16,32},{32,16},{48,0},{1,49},{17,33},{33,17},{49,1},{2,50}... | collective-permute-start | bytes 786440 | tf_op jit(solution)/shard_map/ppermute | solution.py:343
  196.3 15.5 %collective-permute-start.7 = (f32[104,256]{1,0:T(8,128)S(1)}, f32[104,256]{1,0:T(8,128)S(1)}, u32[]{:S(2)}, u32[]{:S(2)}) collective-permute-start(f32[104,256]{1,0:T(8,128)S(1)} %reduce_sum.9.after_ref.kept_ref), channel_id=1, source_target_pairs={{0,4},{4,0},{1,5},{5,1},{2,6},{6,2},{3,7},{7,3},{8,12},{12,8},{9,1... | collective-permute-start | bytes 319496 | tf_op jit(solution)/shard_map/ppermute | solution.py:343
  202.3 15.8 %collective-permute-start.5 = (f32[4,64,256]{2,1,0:T(8,128)S(1)}, f32[4,64,256]{2,1,0:T(8,128)S(1)}, u32[]{:S(2)}, u32[]{:S(2)}) collective-permute-start(f32[4,64,256]{2,1,0:T(8,128)S(1)} %get-tuple-element.21), channel_id=1, source_target_pairs={{0,64},{64,0},{128,192},{192,128},{256,320},{320,256},{384,448},{4... | collective-permute-start | bytes 786440 | tf_op jit(solution)/shard_map/ppermute | solution.py:343
  212.6 28.0 %all-to-all-start.13 = ((f32[4,96,256]{2,1,0:T(8,128)}), f32[4,96,256]{2,1,0:T(8,128)S(1)}, u32[]{:S(2)}, u32[]{:S(2)}) async-start(f32[4,96,256]{2,1,0:T(8,128)} %get-tuple-element.23), calls=%async_computation.13 | async-start | bytes 786432 | tf_op jit(solution)/shard_map/all_to_all | solution.py:22
  218.2 14.4 %collective-permute-start.6 = (f32[2,64,256]{2,1,0:T(8,128)S(1)}, f32[2,64,256]{2,1,0:T(8,128)S(1)}, u32[]{:S(2)}, u32[]{:S(2)}) collective-permute-start(f32[2,64,256]{2,1,0:T(8,128)S(1)} %get-tuple-element.24), channel_id=1, source_target_pairs={{0,128},{64,192},{128,0},{192,64},{256,384},{320,448},{384,256},{4... | collective-permute-start | bytes 393224 | tf_op jit(solution)/shard_map/ppermute | solution.py:343
  232.6 10.2 %collective-permute-start.8 = (f32[64,256]{1,0:T(8,128)S(1)}, f32[64,256]{1,0:T(8,128)S(1)}, u32[]{:S(2)}, u32[]{:S(2)}) collective-permute-start(f32[64,256]{1,0:T(8,128)S(1)} %slice_bitcast_fusion), channel_id=1, source_target_pairs={{0,256},{64,320},{128,384},{192,448},{256,0},{320,64},{384,128},{4... | collective-permute-start | bytes 196616 | tf_op jit(solution)/shard_map/ppermute | solution.py:343

commit v5 on v4

--- a/solution.py
+++ b/solution.py
@@ -113,7 +113,8 @@
         scale_ref[...] = row_scale_of(parts_ref)
 
     tile = tile_ref[...]
-    columns_ref[...] = jnp.sum(tile * widen(scale_ref[...], tile.shape[1]), axis=0, keepdims=True)
+    sums = jnp.sum(tile * widen(scale_ref[...], tile.shape[1]), axis=0, keepdims=True)
+    columns_ref[pl.program_id(0)] = sums
 
 
 def targets_part(tile, scale, latents):
@@ -169,7 +170,8 @@
     out_ref[...] = kept_ref[...] + came_ref[...]
 
 
-def join_kernel(kept_ref, came_ref, spread_ref, mass_ref):
+def join_kernel(kept_ref, came_ref, after_ref, spread_ref, mass_ref):
+    del after_ref
     total = kept_ref[...] + came_ref[...]
     group = spread_ref.shape[1]
     spread_ref[...] = jnp.broadcast_to(total[None, :group], spread_ref.shape)
@@ -291,7 +293,7 @@
             columns_kernel,
             grid=(BLOCKS,),
             in_specs=[rows_spec, tile_spec],
-            out_specs=columns_spec,
+            out_specs=whole(BLOCKS, 1, block),
             out_shape=columns_shape,
             scratch_shapes=[per_token],
             compiler_params=params(),
@@ -386,7 +388,7 @@
             pltpu.SemaphoreType.DMA((2 * BLOCKS,)),
         ],
         compiler_params=params(FETCHES),
-        cost_estimate=cost(13 * size * width, 4 * size),
+        cost_estimate=cost(12 * size * width, 4 * size),
         name="final",
     )(parts, col_scale, codes, far)
     packed = jnp.sum(exchange(packed, "y"), axis=0)
@@ -400,16 +402,16 @@
         cost_estimate=cost(3 * block * width, 12 * block * width),
         name="turn",
     )(where, own_one, one, more_one, own_two, two, more_two, packed)
+    near = near + swap(away, "z", Z, 1)
     numer, mass = pl.pallas_call(
         join_kernel,
-        in_specs=[vmem] * 2,
+        in_specs=[vmem] * 2 + [anywhere],
         out_specs=[vmem] * 2,
         out_shape=[f32(Y, group, width), f32(PAD, width)],
         compiler_params=params(),
         cost_estimate=cost(20000 * token_count * width, 8 * token_count * width),
         name="join",
-    )(packed, swap(packed, "h", H, 1))
-    near = near + swap(away, "z", Z, 1)
+    )(packed, swap(packed, "h", H, 1), near)
     near = add(near[:2], swap(near[2:], "z", Z, 2), mass)
     summed = near[0] + swap(near[1], "z", Z, 4)
     own = lax.dynamic_slice(mine, (0, 0, where[4]), (1, 1, share)).reshape(share)

time: 248 us -> 244 us (0.984)
  starting transfers between devices: 65.5 us -> 58.1 us
  waiting for transfers between devices: 16.9 us -> 24 us
    ppermute x9, waiting for transfers between devices: 13.2 us -> 20.4 us  [swap(): return lax.ppermute(value, axis, [(i, i ^ bits) for i in range(count)])]
    ppermute x9, starting transfers between devices: 42.6 us -> 36 us  [swap(): return lax.ppermute(value, axis, [(i, i ^ bits) for i in range(count)])]
  transfers between devices with their start and end apart: 14 -> 14, of which waited for: 8 -> 9; matrix products, arithmetic and copies ran while one was open for 1% -> 1% of each run, Pallas kernels for 7% -> 7%
where the time goes in v5:
time: 244 us; the launch traced here: 242 us
  blocking collectives  126 us (52%)
  starting transfers between devices  58.1 us (24%)
  Pallas kernels  26.9 us (11%)
  waiting for transfers between devices  24 us (10%)
  other arithmetic  3.49 us (1%)
  local copies, waits for them, and re-layouts  2.65 us (1%)
    all_to_all x9, blocking collectives, exchange(): return lax.all_to_all(blocks, axes, 0, 0, tiled=True)  126 us
    ppermute x9, starting transfers between devices, swap(): return lax.ppermute(value, axis, [(i, i ^ bits) for i in range(count)])  36 us
    all_to_all x5, starting transfers between devices, exchange(): return lax.all_to_all(blocks, axes, 0, 0, tiled=True)  22.1 us
    ppermute x9, waiting for transfers between devices, swap(): return lax.ppermute(value, axis, [(i, i ^ bits) for i in range(count)])  20.4 us
    pallas_call x1, Pallas kernels, per_device(): pl.pallas_call(final_kernel, in_specs=[vmem, vmem, hbm, hbm], out_specs=v...  5.69 us
  transfers between devices with their start and end apart: 14, of which 9 were waited for; matrix products, arithmetic and copies ran while one was open for 1% of the time, Pallas kernels for 7%

profile of v5, /device:TPU:24, one launch (start us, length us, event | category | flops | bytes accessed | tf_op | source)
XLA Modules:
  0.0 241.8 jit_solution(7951427721841398515)
XLA Ops:
  0.7 0.9 copy-done.3
  1.7 1.6 copy-done.5
  3.2 4.9 %setup.1 = (f32[8,384,512]{2,1,0:T(8,128)S(1)}, f32[8,1,384]{2,1,0:T(1,128)S(1)}, f32[8,384,512]{2,1,0:T(8,128)S(1)}) custom-call(s32[5]{0:T(128)S(1)} %stack.23.where_ref, bf16[384,256]{1,0:T(8,128)(2,1)S(1)} %copy-done.3, bf16[8,8,64,256]{3,2,1,0:T(8,128)(2,1)S(1)} %bitcast.27), custom_call_target="tpu_custom_call" | custom-call | flops 805306368 | bytes 6291456 | tf_op jit(solution)/shard_map/setup/pallas_call | solution.py:263
  8.1 30.6 %all_to_all.70.parts_ref = f32[8,1,384]{2,1,0:T(1,128)S(1)} all-to-all(f32[8,1,384]{2,1,0:T(1,128)S(1)} %get-tuple-element.13), channel_id=1, replica_groups=mesh['z'=8,'x'=4,'c'=2,'h'=2,'y'=4] {'h','y'}, dimensions={0} | all-to-all | bytes 24576 | tf_op jit(solution)/shard_map/all_to_all | solution.py:22
  38.7 0.8 columns.3
  39.6 9.4 %all_to_all.71.parts_ref = f32[8,1,512]{2,1,0:T(1,128)S(1)} all-to-all(f32[8,1,512]{2,1,0:T(1,128)S(1)} %columns.3), channel_id=1, replica_groups=mesh['z'=8,'x'=4,'c'=2,'h'=2,'y'=4] {'c','x'}, dimensions={0} | all-to-all | bytes 32768 | tf_op jit(solution)/shard_map/all_to_all | solution.py:22
  49.0 15.3 %all_to_all.72.parts_ref = f32[8,1,512]{2,1,0:T(1,128)S(1)} all-to-all(f32[8,1,512]{2,1,0:T(1,128)S(1)} %sums.3), channel_id=1, replica_groups=mesh['z'=8,'x'=4,'c'=2,'h'=2,'y'=4] {'z'}, dimensions={0} | all-to-all | bytes 32768 | tf_op jit(solution)/shard_map/all_to_all | solution.py:22
  64.3 7.6 %all_to_all.73.columns_ref = f32[8,1,512]{2,1,0:T(1,128)S(1)} all-to-all(f32[8,1,512]{2,1,0:T(1,128)S(1)} %inverse.3), channel_id=1, replica_groups=mesh['z'=8,'x'=4,'c'=2,'h'=2,'y'=4] {'c','x'}, dimensions={0} | all-to-all | bytes 32768 | tf_op jit(solution)/shard_map/all_to_all | solution.py:22
  72.0 0.8 rows.2
  72.7 17.3 %all_to_all.74.parts_ref = f32[8,1,384]{2,1,0:T(1,128)S(1)} all-to-all(f32[8,1,384]{2,1,0:T(1,128)S(1)} %rows.2), channel_id=1, replica_groups=mesh['z'=8,'x'=4,'c'=2,'h'=2,'y'=4] {'h','y'}, dimensions={0} | all-to-all | bytes 24576 | tf_op jit(solution)/shard_map/all_to_all | solution.py:22
  90.0 0.8 columns.4
  90.8 7.6 %all_to_all.75.parts_ref = f32[8,1,512]{2,1,0:T(1,128)S(1)} all-to-all(f32[8,1,512]{2,1,0:T(1,128)S(1)} %columns.4), channel_id=1, replica_groups=mesh['z'=8,'x'=4,'c'=2,'h'=2,'y'=4] {'c','x'}, dimensions={0} | all-to-all | bytes 32768 | tf_op jit(solution)/shard_map/all_to_all | solution.py:22
  98.5 12.9 %all_to_all.76.parts_ref = f32[8,1,512]{2,1,0:T(1,128)S(1)} all-to-all(f32[8,1,512]{2,1,0:T(1,128)S(1)} %sums.4), channel_id=1, replica_groups=mesh['z'=8,'x'=4,'c'=2,'h'=2,'y'=4] {'z'}, dimensions={0} | all-to-all | bytes 32768 | tf_op jit(solution)/shard_map/all_to_all | solution.py:22
  111.4 7.6 %all_to_all.77.columns_ref = f32[8,1,512]{2,1,0:T(1,128)S(1)} all-to-all(f32[8,1,512]{2,1,0:T(1,128)S(1)} %inverse.4), channel_id=1, replica_groups=mesh['z'=8,'x'=4,'c'=2,'h'=2,'y'=4] {'c','x'}, dimensions={0} | all-to-all | bytes 32768 | tf_op jit(solution)/shard_map/all_to_all | solution.py:22
  119.0 0.8 rows.3
  119.8 17.3 %all_to_all.78.parts_ref = f32[8,1,384]{2,1,0:T(1,128)S(1)} all-to-all(f32[8,1,384]{2,1,0:T(1,128)S(1)} %rows.3), channel_id=1, replica_groups=mesh['z'=8,'x'=4,'c'=2,'h'=2,'y'=4] {'h','y'}, dimensions={0} | all-to-all | bytes 24576 | tf_op jit(solution)/shard_map/all_to_all | solution.py:22
  137.1 1.4 columns.5.after_ref
  138.5 3.3 %all-to-all-start.9 = ((f32[8,1,512]{2,1,0:T(1,128)}), f32[8,1,512]{2,1,0:T(1,128)S(1)}, u32[]{:S(2)}, u32[]{:S(2)}) async-start(f32[8,1,512]{2,1,0:T(1,128)} %columns.5.after_ref), calls=%async_computation.9 | async-start | bytes 32768 | tf_op jit(solution)/shard_map/all_to_all | solution.py:22
  141.9 4.3 %targets_sent.1 = f32[4,256,512]{2,1,0:T(8,128)} custom-call(s32[5]{0:T(128)S(1)} %stack.23.where_ref, f32[8,1,384]{2,1,0:T(1,128)S(1)} %all_to_all.78.parts_ref, bf16[384,256]{1,0:T(8,128)(2,1)S(1)} %copy-done.4, f32[8,384,512]{2,1,0:T(8,128)} %copy-done, f32[8,1,512]{2,1,0:T(1,128)} %columns.5.after_ref), custom_call_target="tpu_custom_call" | custom-call | flops 402653184 | bytes 6291456 | tf_op jit(solution)/shard_map/targets_sent/pallas_call | solution.py:305
  146.2 2.3 collective-permute-start
  149.2 3.3 %all-to-all-start.10 = ((f32[8,1,512]{2,1,0:T(1,128)}), f32[8,1,512]{2,1,0:T(1,128)S(1)}, u32[]{:S(2)}, u32[]{:S(2)}) async-start(f32[8,1,512]{2,1,0:T(1,128)} %sums.5.after_ref), calls=%async_computation.10 | async-start | bytes 32768 | tf_op jit(solution)/shard_map/all_to_all | solution.py:22
  152.7 4.5 %targets_kept.1 = (f32[2,128,512]{2,1,0:T(8,128)S(1)}, f32[2,128,512]{2,1,0:T(8,128)}, f32[2,128,512]{2,1,0:T(8,128)}, f32[2,128,512]{2,1,0:T(8,128)}) custom-call(s32[5]{0:T(128)S(1)} %stack.23.where_ref, f32[8,1,384]{2,1,0:T(1,128)S(1)} %all_to_all.78.parts_ref, bf16[384,256]{1,0:T(8,128)(2,1)S(1)} %copy-done.4, f32[8,384,512]{2,1,0:T(8,128)} %copy-done, ...), custom_call_target="tpu_custom_call" | custom-call | flops 402653184 | bytes 6291456 | tf_op jit(solution)/shard_map/targets_kept/pallas_call | solution.py:317
  157.2 5.0 %collective-permute-start.3 = (f32[2,128,512]{2,1,0:T(8,128)}, f32[2,128,512]{2,1,0:T(8,128)S(1)}, u32[]{:S(2)}, u32[]{:S(2)}) collective-permute-start(f32[2,128,512]{2,1,0:T(8,128)} %get-tuple-element.19), channel_id=1, source_target_pairs={{0,48},{16,32},{32,16},{48,0},{1,49},{17,33},{33,17},{49,1},{2,50}... | collective-permute-start | bytes 1572872 | tf_op jit(solution)/shard_map/ppermute | solution.py:345
  162.2 0.8 all-to-all-done.10.parts_ref
  163.0 0.6 inverse.5
  163.6 4.4 %all-to-all-start.11 = ((f32[8,1,512]{2,1,0:T(1,128)}), f32[8,1,512]{2,1,0:T(1,128)S(1)}, u32[]{:S(2)}, u32[]{:S(2)}) async-start(f32[8,1,512]{2,1,0:T(1,128)} %inverse.5), calls=%async_computation.11 | async-start | bytes 32768 | tf_op jit(solution)/shard_map/all_to_all | solution.py:22
  168.1 4.0 %collective-permute-start.1 = (f32[2,128,512]{2,1,0:T(8,128)S(1)}, f32[2,128,512]{2,1,0:T(8,128)S(1)}, u32[]{:S(2)}, u32[]{:S(2)}) collective-permute-start(f32[2,128,512]{2,1,0:T(8,128)S(1)} %get-tuple-element.17.refs_0_), channel_id=1, source_target_pairs={{0,16},{16,0},{32,48},{48,32},{1,17},{17,1},{33,49},{49,33},{2,18}... | collective-permute-start | bytes 1572872 | tf_op jit(solution)/shard_map/ppermute | solution.py:345
  172.1 2.8 %all-to-all-done.11.columns_ref = f32[8,1,512]{2,1,0:T(1,128)S(1)} async-done(((f32[8,1,512]{2,1,0:T(1,128)}), f32[8,1,512]{2,1,0:T(1,128)S(1)}, u32[]{:S(2)}, u32[]{:S(2)}) %all-to-all-start.11) | async-done | bytes 16416 | tf_op jit(solution)/shard_map/all_to_all | solution.py:22
  174.9 5.7 %final.1 = f32[4,104,256]{2,1,0:T(8,128)} custom-call(f32[8,1,384]{2,1,0:T(1,128)S(1)} %all_to_all.78.parts_ref, f32[8,1,512]{2,1,0:T(1,128)S(1)} %all-to-all-done.11.columns_ref, bf16[8,8,64,256]{3,2,1,0:T(8,128)(2,1)} %bitcast.26, f32[8,384,512]{2,1,0:T(8,128)} %copy-done), custom_call_target="tpu_custom_call" | custom-call | flops 4831838208 | bytes 6291456 | tf_op jit(solution)/shard_map/final/pallas_call | solution.py:379
  180.6 6.2 %all-to-all-start.12 = ((f32[4,104,256]{2,1,0:T(8,128)}), f32[4,104,256]{2,1,0:T(8,128)}, u32[]{:S(2)}, u32[]{:S(2)}) async-start(f32[4,104,256]{2,1,0:T(8,128)} %final.1), calls=%async_computation.12 | async-start | bytes 851968 | tf_op jit(solution)/shard_map/all_to_all | solution.py:22
  186.8 2.4 collective-permute-start.4
  189.2 4.4 %collective-permute-start.2 = (f32[128,512]{1,0:T(8,128)S(1)}, f32[128,512]{1,0:T(8,128)S(1)}, u32[]{:S(2)}, u32[]{:S(2)}) collective-permute-start(f32[128,512]{1,0:T(8,128)S(1)} %fusion.1), channel_id=1, source_target_pairs={{0,48},{16,32},{32,16},{48,0},{1,49},{17,33},{33,17},{49,1},{2,50}... | collective-permute-start | bytes 786440 | tf_op jit(solution)/shard_map/ppermute | solution.py:345
  193.8 1.0 reduce_sum.9.after_ref.kept_ref
  194.8 1.9 collective-permute-done.4.more_two_ref
  196.7 3.4 %collective-permute-done.2.more_one_ref = f32[128,512]{1,0:T(8,128)S(1)} collective-permute-done((f32[128,512]{1,0:T(8,128)S(1)}, f32[128,512]{1,0:T(8,128)S(1)}, u32[]{:S(2)}, u32[]{:S(2)}) %collective-permute-start.2) | collective-permute-done | bytes 262176 | tf_op jit(solution)/shard_map/ppermute | solution.py:345
  200.1 0.8 turn.1
  200.9 3.4 %collective-permute-start.5 = (f32[4,64,256]{2,1,0:T(8,128)S(1)}, f32[4,64,256]{2,1,0:T(8,128)S(1)}, u32[]{:S(2)}, u32[]{:S(2)}) collective-permute-start(f32[4,64,256]{2,1,0:T(8,128)S(1)} %get-tuple-element.21), channel_id=1, source_target_pairs={{0,64},{64,0},{128,192},{192,128},{256,320},{320,256},{384,448},{4... | collective-permute-start | bytes 786440 | tf_op jit(solution)/shard_map/ppermute | solution.py:345
  204.3 0.7 multiply_bitcast_fusion
  205.1 2.5 %collective-permute-start.7 = (f32[104,256]{1,0:T(8,128)S(1)}, f32[104,256]{1,0:T(8,128)S(1)}, u32[]{:S(2)}, u32[]{:S(2)}) collective-permute-start(f32[104,256]{1,0:T(8,128)S(1)} %reduce_sum.9.after_ref.kept_ref), channel_id=1, source_target_pairs={{0,4},{4,0},{1,5},{5,1},{2,6},{6,2},{3,7},{7,3},{8,12},{12,8},{9,1... | collective-permute-start | bytes 319496 | tf_op jit(solution)/shard_map/ppermute | solution.py:345
  207.5 4.4 %collective-permute-done.5 = f32[4,64,256]{2,1,0:T(8,128)S(1)} collective-permute-done((f32[4,64,256]{2,1,0:T(8,128)S(1)}, f32[4,64,256]{2,1,0:T(8,128)S(1)}, u32[]{:S(2)}, u32[]{:S(2)}) %collective-permute-start.5) | collective-permute-done | bytes 262176 | tf_op jit(solution)/shard_map/ppermute | solution.py:345
  212.0 4.5 %collective-permute-start.6 = (f32[2,64,256]{2,1,0:T(8,128)S(1)}, f32[2,64,256]{2,1,0:T(8,128)S(1)}, u32[]{:S(2)}, u32[]{:S(2)}) collective-permute-start(f32[2,64,256]{2,1,0:T(8,128)S(1)} %get-tuple-element.24), channel_id=1, source_target_pairs={{0,128},{64,192},{128,0},{192,64},{256,384},{320,448},{384,256},{4... | collective-permute-start | bytes 393224 | tf_op jit(solution)/shard_map/ppermute | solution.py:345
  216.5 7.8 %collective-permute-done.7.came_ref = f32[104,256]{1,0:T(8,128)S(1)} collective-permute-done((f32[104,256]{1,0:T(8,128)S(1)}, f32[104,256]{1,0:T(8,128)S(1)}, u32[]{:S(2)}, u32[]{:S(2)}) %collective-permute-start.7) | collective-permute-done | bytes 106528 | tf_op jit(solution)/shard_map/ppermute | solution.py:345
  224.4 0.8 join.1
  225.2 4.8 %all-to-all-start.13 = ((f32[4,96,256]{2,1,0:T(8,128)}), f32[4,96,256]{2,1,0:T(8,128)S(1)}, u32[]{:S(2)}, u32[]{:S(2)}) async-start(f32[4,96,256]{2,1,0:T(8,128)} %get-tuple-element.23), calls=%async_computation.13 | async-start | bytes 786432 | tf_op jit(solution)/shard_map/all_to_all | solution.py:22
  230.0 7.5 %collective-permute-start.8 = (f32[64,256]{1,0:T(8,128)S(1)}, f32[64,256]{1,0:T(8,128)S(1)}, u32[]{:S(2)}, u32[]{:S(2)}) collective-permute-start(f32[64,256]{1,0:T(8,128)S(1)} %slice_bitcast_fusion), channel_id=1, source_target_pairs={{0,256},{64,320},{128,384},{192,448},{256,0},{320,64},{384,128},{4... | collective-permute-start | bytes 196616 | tf_op jit(solution)/shard_map/ppermute | solution.py:345
  237.5 2.7 %collective-permute-done.8 = f32[64,256]{1,0:T(8,128)S(1)} collective-permute-done((f32[64,256]{1,0:T(8,128)S(1)}, f32[64,256]{1,0:T(8,128)S(1)}, u32[]{:S(2)}, u32[]{:S(2)}) %collective-permute-start.8) | collective-permute-done | bytes 65568 | tf_op jit(solution)/shard_map/ppermute | solution.py:345
  240.2 0.7 fusion.3
  240.9 0.9 bitcast_divide_fusion
  (31 shorter events, 1.3 us)
Async XLA Ops:
  0.7 0.9 copy-start.3
  1.7 1.6 copy-start.5
  8.1 31.4 %copy-start = (f32[8,384,512]{2,1,0:T(8,128)}, f32[8,384,512]{2,1,0:T(8,128)S(1)}, u32[]{:S(2)}) copy-start(f32[8,384,512]{2,1,0:T(8,128)S(1)} %get-tuple-element.15.tile_ref) | copy-start | bytes 18874372
  137.1 4.8 %copy-start.4 = (bf16[384,256]{1,0:T(8,128)(2,1)S(1)}, bf16[384,256]{1,0:T(8,128)(2,1)}, u32[]{:S(2)}) copy-start(bf16[384,256]{1,0:T(8,128)(2,1)} %latents_ref.5) | copy-start | bytes 589828
  138.5 10.0 %all-to-all-start.9 = ((f32[8,1,512]{2,1,0:T(1,128)}), f32[8,1,512]{2,1,0:T(1,128)S(1)}, u32[]{:S(2)}, u32[]{:S(2)}) async-start(f32[8,1,512]{2,1,0:T(1,128)} %columns.5.after_ref), calls=%async_computation.9 | async-start | bytes 32768 | tf_op jit(solution)/shard_map/all_to_all | solution.py:22
  146.2 6.4 %collective-permute-start = (f32[4,256,512]{2,1,0:T(8,128)}, f32[4,256,512]{2,1,0:T(8,128)}, u32[]{:S(2)}, u32[]{:S(2)}) collective-permute-start(f32[4,256,512]{2,1,0:T(8,128)} %targets_sent.1), channel_id=1, source_target_pairs={{0,8},{8,0},{1,9},{9,1},{2,10},{10,2},{3,11},{11,3},{4,12},{12,4},... | collective-permute-start | bytes 6291464 | tf_op jit(solution)/shard_map/ppermute | solution.py:345
  149.2 13.8 %all-to-all-start.10 = ((f32[8,1,512]{2,1,0:T(1,128)}), f32[8,1,512]{2,1,0:T(1,128)S(1)}, u32[]{:S(2)}, u32[]{:S(2)}) async-start(f32[8,1,512]{2,1,0:T(1,128)} %sums.5.after_ref), calls=%async_computation.10 | async-start | bytes 32768 | tf_op jit(solution)/shard_map/all_to_all | solution.py:22
  157.2 29.5 %collective-permute-start.3 = (f32[2,128,512]{2,1,0:T(8,128)}, f32[2,128,512]{2,1,0:T(8,128)S(1)}, u32[]{:S(2)}, u32[]{:S(2)}) collective-permute-start(f32[2,128,512]{2,1,0:T(8,128)} %get-tuple-element.19), channel_id=1, source_target_pairs={{0,48},{16,32},{32,16},{48,0},{1,49},{17,33},{33,17},{49,1},{2,50}... | collective-permute-start | bytes 1572872 | tf_op jit(solution)/shard_map/ppermute | solution.py:345
  163.6 11.3 %all-to-all-start.11 = ((f32[8,1,512]{2,1,0:T(1,128)}), f32[8,1,512]{2,1,0:T(1,128)S(1)}, u32[]{:S(2)}, u32[]{:S(2)}) async-start(f32[8,1,512]{2,1,0:T(1,128)} %inverse.5), calls=%async_computation.11 | async-start | bytes 32768 | tf_op jit(solution)/shard_map/all_to_all | solution.py:22
  168.0 18.7 %copy-start.2 = (f32[2,128,512]{2,1,0:T(8,128)S(1)}, f32[2,128,512]{2,1,0:T(8,128)}, u32[]{:S(2)}) copy-start(f32[2,128,512]{2,1,0:T(8,128)} %get-tuple-element.18.own_two_ref) | copy-start | bytes 1572868
  168.1 21.1 %copy-start.1 = (f32[2,128,512]{2,1,0:T(8,128)S(1)}, f32[2,128,512]{2,1,0:T(8,128)}, u32[]{:S(2)}) copy-start(f32[2,128,512]{2,1,0:T(8,128)} %get-tuple-element.16.own_one_ref) | copy-start | bytes 1572868
  168.1 21.1 %collective-permute-start.1 = (f32[2,128,512]{2,1,0:T(8,128)S(1)}, f32[2,128,512]{2,1,0:T(8,128)S(1)}, u32[]{:S(2)}, u32[]{:S(2)}) collective-permute-start(f32[2,128,512]{2,1,0:T(8,128)S(1)} %get-tuple-element.17.refs_0_), channel_id=1, source_target_pairs={{0,16},{16,0},{32,48},{48,32},{1,17},{17,1},{33,49},{49,33},{2,18}... | collective-permute-start | bytes 1572872 | tf_op jit(solution)/shard_map/ppermute | solution.py:345
  180.6 13.2 %all-to-all-start.12 = ((f32[4,104,256]{2,1,0:T(8,128)}), f32[4,104,256]{2,1,0:T(8,128)}, u32[]{:S(2)}, u32[]{:S(2)}) async-start(f32[4,104,256]{2,1,0:T(8,128)} %final.1), calls=%async_computation.12 | async-start | bytes 851968 | tf_op jit(solution)/shard_map/all_to_all | solution.py:22
  186.8 9.9 %collective-permute-start.4 = (f32[128,512]{1,0:T(8,128)S(1)}, f32[128,512]{1,0:T(8,128)S(1)}, u32[]{:S(2)}, u32[]{:S(2)}) collective-permute-start(f32[128,512]{1,0:T(8,128)S(1)} %fusion), channel_id=1, source_target_pairs={{0,16},{16,0},{32,48},{48,32},{1,17},{17,1},{33,49},{49,33},{2,18}... | collective-permute-start | bytes 786440 | tf_op jit(solution)/shard_map/ppermute | solution.py:345
  189.2 10.9 %collective-permute-start.2 = (f32[128,512]{1,0:T(8,128)S(1)}, f32[128,512]{1,0:T(8,128)S(1)}, u32[]{:S(2)}, u32[]{:S(2)}) collective-permute-start(f32[128,512]{1,0:T(8,128)S(1)} %fusion.1), channel_id=1, source_target_pairs={{0,48},{16,32},{32,16},{48,0},{1,49},{17,33},{33,17},{49,1},{2,50}... | collective-permute-start | bytes 786440 | tf_op jit(solution)/shard_map/ppermute | solution.py:345
  200.9 11.0 %collective-permute-start.5 = (f32[4,64,256]{2,1,0:T(8,128)S(1)}, f32[4,64,256]{2,1,0:T(8,128)S(1)}, u32[]{:S(2)}, u32[]{:S(2)}) collective-permute-start(f32[4,64,256]{2,1,0:T(8,128)S(1)} %get-tuple-element.21), channel_id=1, source_target_pairs={{0,64},{64,0},{128,192},{192,128},{256,320},{320,256},{384,448},{4... | collective-permute-start | bytes 786440 | tf_op jit(solution)/shard_map/ppermute | solution.py:345
  205.1 19.3 %collective-permute-start.7 = (f32[104,256]{1,0:T(8,128)S(1)}, f32[104,256]{1,0:T(8,128)S(1)}, u32[]{:S(2)}, u32[]{:S(2)}) collective-permute-start(f32[104,256]{1,0:T(8,128)S(1)} %reduce_sum.9.after_ref.kept_ref), channel_id=1, source_target_pairs={{0,4},{4,0},{1,5},{5,1},{2,6},{6,2},{3,7},{7,3},{8,12},{12,8},{9,1... | collective-permute-start | bytes 319496 | tf_op jit(solution)/shard_map/ppermute | solution.py:345
  212.0 18.0 %collective-permute-start.6 = (f32[2,64,256]{2,1,0:T(8,128)S(1)}, f32[2,64,256]{2,1,0:T(8,128)S(1)}, u32[]{:S(2)}, u32[]{:S(2)}) collective-permute-start(f32[2,64,256]{2,1,0:T(8,128)S(1)} %get-tuple-element.24), channel_id=1, source_target_pairs={{0,128},{64,192},{128,0},{192,64},{256,384},{320,448},{384,256},{4... | collective-permute-start | bytes 393224 | tf_op jit(solution)/shard_map/ppermute | solution.py:345
  225.2 15.8 %all-to-all-start.13 = ((f32[4,96,256]{2,1,0:T(8,128)}), f32[4,96,256]{2,1,0:T(8,128)S(1)}, u32[]{:S(2)}, u32[]{:S(2)}) async-start(f32[4,96,256]{2,1,0:T(8,128)} %get-tuple-element.23), calls=%async_computation.13 | async-start | bytes 786432 | tf_op jit(solution)/shard_map/all_to_all | solution.py:22
  230.0 10.2 %collective-permute-start.8 = (f32[64,256]{1,0:T(8,128)S(1)}, f32[64,256]{1,0:T(8,128)S(1)}, u32[]{:S(2)}, u32[]{:S(2)}) collective-permute-start(f32[64,256]{1,0:T(8,128)S(1)} %slice_bitcast_fusion), channel_id=1, source_target_pairs={{0,256},{64,320},{128,384},{192,448},{256,0},{320,64},{384,128},{4... | collective-permute-start | bytes 196616 | tf_op jit(solution)/shard_map/ppermute | solution.py:345

commit v6 on v5

--- a/solution.py
+++ b/solution.py
@@ -53,18 +53,35 @@
     return (b % X) * C + b // X
 
 
-def fetch(pairs, sems):
-    copies = [pltpu.make_async_copy(source, target, sems.at[i]) for i, (source, target) in enumerate(pairs)]
-    for copy in copies:
-        copy.start()
-    return copies
+AHEAD = 3
+
+
+def fetch(steps, sems):
+    copies, count = [], 0
+    for pairs in steps:
+        copies.append([pltpu.make_async_copy(*pair, sems.at[count + i]) for i, pair in enumerate(pairs)])
+        count += len(pairs)
+
+    def start(step):
+        for copy in copies[step]:
+            copy.start()
+
+    def wait(step):
+        if step + AHEAD < len(copies):
+            start(step + AHEAD)
+        for copy in copies[step]:
+            copy.wait()
+
+    for step in range(min(AHEAD, len(copies))):
+        start(step)
+    return wait
 
 
 def setup_kernel(where_ref, latents_ref, codes_ref, tile_ref, rows_ref, far_ref, tokens_ref, held_ref, sems):
     del where_ref
-    pairs = [(codes_ref.at[:, place(b)], held_ref.at[b]) for b in range(BLOCKS)]
-    *copies, first = fetch(pairs + [(latents_ref, tokens_ref)], sems)
-    first.wait()
+    steps = [[(latents_ref, tokens_ref)]]
+    wait = fetch(steps + [[(codes_ref.at[:, place(b)], held_ref.at[b])] for b in range(BLOCKS)], sems)
+    wait(0)
     saves = []
     latents = tokens_ref[...]
     width = latents.shape[1]
@@ -74,7 +91,7 @@
     total = jnp.zeros(scale.shape, jnp.float32)
     across = (((1,), (1,)), ((), ()))
     for b in range(BLOCKS):
-        copies[b].wait()
+        wait(1 + b)
         codes = held_ref[b].reshape(-1, width)
         floats = codes.astype(jnp.float32)
         code_norm = lax.rsqrt(row_of(fold(floats * floats)) * (1.0 / width) + EPSILON)
@@ -124,35 +141,29 @@
 
 def targets_sent_kernel(where_ref, parts_ref, latents_ref, tile_ref, after_ref, out_ref, tiles_ref, sems):
     del after_ref
-    pairs = [(tile_ref.at[where_ref[3] * X + (where_ref[1] ^ s)], tiles_ref.at[s]) for s in range(X)]
-    copies = fetch(pairs, sems)
+    wait = fetch([[(tile_ref.at[where_ref[3] * X + (where_ref[1] ^ s)], tiles_ref.at[s])] for s in range(X)], sems)
     scale = row_scale_of(parts_ref)
     latents = latents_ref[...]
     for s in range(X):
-        copies[s].wait()
+        wait(s)
         out_ref[s] = targets_part(tiles_ref[s], scale, latents)
 
 
 def targets_kept_kernel(
-    where_ref, parts_ref, latents_ref, tile_ref, added_ref, after_ref,
-    one_ref, two_ref, own_one_ref, own_two_ref, tiles_ref, more_ref, sems,
+    where_ref, parts_ref, latents_ref, tile_ref, added_ref, after_ref, own_ref, one_ref, two_ref, three_ref, tiles_ref, more_ref, sems
 ):
     del after_ref
-    pairs = [(tile_ref.at[where_ref[0] * X + (where_ref[1] ^ s)], tiles_ref.at[s]) for s in range(X)]
-    pairs += [(added_ref.at[s], more_ref.at[s]) for s in range(X)]
-    copies = fetch([pairs[i] for s in range(X) for i in (s, s + X)], sems)
+    slots = (2, 1, 3, 0)
+    steps = [
+        [(tile_ref.at[where_ref[0] * X + (where_ref[1] ^ s)], tiles_ref.at[s]), (added_ref.at[s], more_ref.at[s])]
+        for s in slots
+    ]
+    wait = fetch(steps, sems)
     scale = row_scale_of(parts_ref)
     latents = latents_ref[...]
-    for s in range(X):
-        copies[2 * s].wait()
-        summed = targets_part(tiles_ref[s], scale, latents)
-        copies[2 * s + 1].wait()
-        summed += more_ref[s]
-        upper, lower = jnp.split(summed, 2, axis=0)
-        ref, index = ((own_one_ref, 0), (one_ref, 0), (one_ref, 1), (own_one_ref, 1))[s]
-        ref[index] = upper
-        ref, index = ((own_two_ref, 0), (own_two_ref, 1), (two_ref, 1), (two_ref, 0))[s]
-        ref[index] = lower
+    for step, s in enumerate(slots):
+        wait(step)
+        (own_ref, one_ref, two_ref, three_ref)[s][...] = targets_part(tiles_ref[s], scale, latents) + more_ref[s]
 
 
 def sum_kernel(parts_ref, *refs):
@@ -178,12 +189,9 @@
     mass_ref[...] = total[group:]
 
 
-def turn_kernel(where_ref, own_one_ref, one_ref, more_one_ref, own_two_ref, two_ref, more_two_ref, after_ref, *refs):
+def turn_kernel(where_ref, own_ref, one_ref, two_ref, three_ref, after_ref, send_ref, keep_ref, turned_ref):
     del after_ref
-    send_ref, keep_ref, turned_ref = refs
-    upper = own_one_ref[0] + one_ref[0] + more_one_ref[...]
-    lower = own_two_ref[0] + two_ref[0] + more_two_ref[...]
-    turned_ref[...] = jnp.concatenate([upper, lower], axis=0).T
+    turned_ref[...] = (own_ref[...] + one_ref[...] + two_ref[...] + three_ref[...]).T
     share = send_ref.shape[1]
     for i, slot in enumerate((0, 4, 2, 6)):
         for ref, s in ((keep_ref, slot), (send_ref, slot + 1)):
@@ -194,21 +202,18 @@
 def final_kernel(
     parts_ref, columns_ref, codes_ref, tile_ref, out_ref, held_ref, tiles_ref, numer_ref, sems
 ):
-    pairs = [
-        pair
-        for b in range(BLOCKS)
-        for pair in ((tile_ref.at[b], tiles_ref.at[b]), (codes_ref.at[:, place(b)], held_ref.at[b]))
+    steps = [
+        [(tile_ref.at[b], tiles_ref.at[b]), (codes_ref.at[:, place(b)], held_ref.at[b])] for b in range(BLOCKS)
     ]
-    copies = fetch(pairs, sems)
+    wait = fetch(steps, sems)
     tokens, width = numer_ref.shape
     scale = row_scale_of(parts_ref)
     total = jnp.zeros(scale.shape, jnp.float32)
     for b in range(BLOCKS):
-        copies[2 * b].wait()
+        wait(b)
         tile = tiles_ref[b]
         plan = (widen(scale, tile.shape[1]) * tile * columns_ref[b]).astype(jnp.bfloat16)
         total += fold(plan.astype(jnp.float32))
-        copies[2 * b + 1].wait()
         part = jnp.dot(plan, held_ref[b].reshape(-1, width), preferred_element_type=jnp.float32)
         numer_ref[...] = part if b == 0 else numer_ref[...] + part
     group = tokens // Y
@@ -318,7 +323,7 @@
             targets_kept_kernel,
             in_specs=[smem, vmem, vmem, hbm, hbm, anywhere],
             out_specs=[vmem] * 4,
-            out_shape=[f32(2, width // 2, block)] * 4,
+            out_shape=[f32(width, block)] * 4,
             scratch_shapes=[
                 tiles((X, token_count, block)),
                 tiles((X, width, block)),
@@ -370,10 +375,8 @@
         if not last:
             part = rows(col_scale)
 
-    one, two, own_one, own_two = kept
-    one, two = swap(one, "x", X, 1), swap(two, "x", X, 3)
-    more_one = swap(own_one[1] + one[1], "x", X, 3)
-    more_two = swap(own_two[1] + two[1], "x", X, 1)
+    own, *others = kept
+    others = [swap(other, "x", X, s) for s, other in enumerate(others, 1)]
 
     group = token_count // Y
     packed = pl.pallas_call(
@@ -388,20 +391,20 @@
             pltpu.SemaphoreType.DMA((2 * BLOCKS,)),
         ],
         compiler_params=params(FETCHES),
-        cost_estimate=cost(12 * size * width, 4 * size),
+        cost_estimate=cost(5 * size * width, 4 * size),
         name="final",
     )(parts, col_scale, codes, far)
     packed = jnp.sum(exchange(packed, "y"), axis=0)
     away, near = pl.pallas_call(
         turn_kernel,
-        in_specs=[smem] + [vmem] * 6 + [anywhere],
+        in_specs=[smem] + [vmem] * 4 + [anywhere],
         out_specs=[vmem] * 2,
         out_shape=[f32(Z // 2, share, width)] * 2,
         scratch_shapes=[pltpu.VMEM((block, width), jnp.float32)],
         compiler_params=params(16 << 20),
         cost_estimate=cost(3 * block * width, 12 * block * width),
         name="turn",
-    )(where, own_one, one, more_one, own_two, two, more_two, packed)
+    )(where, own, *others, packed)
     near = near + swap(away, "z", Z, 1)
     numer, mass = pl.pallas_call(
         join_kernel,
@@ -414,8 +417,8 @@
     )(packed, swap(packed, "h", H, 1), near)
     near = add(near[:2], swap(near[2:], "z", Z, 2), mass)
     summed = near[0] + swap(near[1], "z", Z, 4)
-    own = lax.dynamic_slice(mine, (0, 0, where[4]), (1, 1, share)).reshape(share)
-    targets = summed * (own * (total_codes / total_tokens))[:, None]
+    scale = lax.dynamic_slice(mine, (0, 0, where[4]), (1, 1, share)).reshape(share)
+    targets = summed * (scale * (total_codes / total_tokens))[:, None]
     mass = mass[:2].reshape(2 * width)[:token_count]
     rebuilt = exchange(numer, "y").reshape(token_count, width) / mass[:, None]
     return (targets, rebuilt)

time: 244 us -> 253 us (1.037)
  blocking collectives: 126 us -> 163 us
  starting transfers between devices: 58.1 us -> 45.2 us
  waiting for transfers between devices: 24 us -> 12.3 us
    all_to_all x9 -> x11, blocking collectives: 126 us -> 163 us  [exchange(): return lax.all_to_all(blocks, axes, 0, 0, tiled=True)]
    all_to_all x5 -> x3, starting transfers between devices: 22.1 us -> 12.2 us  [exchange(): return lax.all_to_all(blocks, axes, 0, 0, tiled=True)]
    ppermute x9 -> x8, waiting for transfers between devices: 20.4 us -> 12.3 us  [swap(): return lax.ppermute(value, axis, [(i, i ^ bits) for i in range(count)])]
    all_to_all x5 -> x3, waiting for transfers between devices: 3.69 us -> 0.01 us  [exchange(): return lax.all_to_all(blocks, axes, 0, 0, tiled=True)]
    ppermute x9 -> x8, starting transfers between devices: 36 us -> 33 us  [swap(): return lax.ppermute(value, axis, [(i, i ^ bits) for i in range(count)])]
  transfers between devices with their start and end apart: 14 -> 11, of which waited for: 9 -> 4; matrix products, arithmetic and copies ran while one was open for 1% -> 0% of each run, Pallas kernels for 7% -> 6%
where the time goes in v6:
time: 253 us; the launch traced here: 250 us
  blocking collectives  163 us (64%)
  starting transfers between devices  45.2 us (18%)
  Pallas kernels  24.5 us (10%)
  waiting for transfers between devices  12.3 us (5%)
  local copies, waits for them, and re-layouts  2.64 us (1%)
    all_to_all x11, blocking collectives, exchange(): return lax.all_to_all(blocks, axes, 0, 0, tiled=True)  163 us
    ppermute x8, starting transfers between devices, swap(): return lax.ppermute(value, axis, [(i, i ^ bits) for i in range(count)])  33 us
    ppermute x8, waiting for transfers between devices, swap(): return lax.ppermute(value, axis, [(i, i ^ bits) for i in range(count)])  12.3 us
    all_to_all x3, starting transfers between devices, exchange(): return lax.all_to_all(blocks, axes, 0, 0, tiled=True)  12.2 us
  transfers between devices with their start and end apart: 11, of which 4 were waited for; matrix products, arithmetic and copies ran while one was open for 0% of the time, Pallas kernels for 6%

profile of v6, /device:TPU:24, one launch (start us, length us, event | category | flops | bytes accessed | tf_op | source)
XLA Modules:
  0.0 250.4 jit_solution(6159748247596039003)
XLA Ops:
  0.6 0.1 stack.23.where_ref
  0.7 1.6 copy-done.1
  2.3 0.9 copy-done.2
  3.2 4.9 %setup.1 = (f32[8,384,512]{2,1,0:T(8,128)S(1)}, f32[8,1,384]{2,1,0:T(1,128)S(1)}, f32[8,384,512]{2,1,0:T(8,128)S(1)}) custom-call(s32[5]{0:T(128)S(1)} %stack.23.where_ref, bf16[384,256]{1,0:T(8,128)(2,1)S(1)} %copy-done.2, bf16[8,8,64,256]{3,2,1,0:T(8,128)(2,1)S(1)} %bitcast.23), custom_call_target="tpu_custom_call" | custom-call | flops 805306368 | bytes 6291456 | tf_op jit(solution)/shard_map/setup/pallas_call | solution.py:268
  8.1 30.6 %all_to_all.70.parts_ref = f32[8,1,384]{2,1,0:T(1,128)S(1)} all-to-all(f32[8,1,384]{2,1,0:T(1,128)S(1)} %get-tuple-element.13), channel_id=1, replica_groups=mesh['z'=8,'x'=4,'c'=2,'h'=2,'y'=4] {'h','y'}, dimensions={0} | all-to-all | bytes 24576 | tf_op jit(solution)/shard_map/all_to_all | solution.py:22
  38.7 0.8 columns.3
  39.6 9.4 %all_to_all.71.parts_ref = f32[8,1,512]{2,1,0:T(1,128)S(1)} all-to-all(f32[8,1,512]{2,1,0:T(1,128)S(1)} %columns.3), channel_id=1, replica_groups=mesh['z'=8,'x'=4,'c'=2,'h'=2,'y'=4] {'c','x'}, dimensions={0} | all-to-all | bytes 32768 | tf_op jit(solution)/shard_map/all_to_all | solution.py:22
  49.0 15.3 %all_to_all.72.parts_ref = f32[8,1,512]{2,1,0:T(1,128)S(1)} all-to-all(f32[8,1,512]{2,1,0:T(1,128)S(1)} %sums.3), channel_id=1, replica_groups=mesh['z'=8,'x'=4,'c'=2,'h'=2,'y'=4] {'z'}, dimensions={0} | all-to-all | bytes 32768 | tf_op jit(solution)/shard_map/all_to_all | solution.py:22
  64.3 7.6 %all_to_all.73.columns_ref = f32[8,1,512]{2,1,0:T(1,128)S(1)} all-to-all(f32[8,1,512]{2,1,0:T(1,128)S(1)} %inverse.3), channel_id=1, replica_groups=mesh['z'=8,'x'=4,'c'=2,'h'=2,'y'=4] {'c','x'}, dimensions={0} | all-to-all | bytes 32768 | tf_op jit(solution)/shard_map/all_to_all | solution.py:22
  72.0 0.8 rows.2
  72.7 17.3 %all_to_all.74.parts_ref = f32[8,1,384]{2,1,0:T(1,128)S(1)} all-to-all(f32[8,1,384]{2,1,0:T(1,128)S(1)} %rows.2), channel_id=1, replica_groups=mesh['z'=8,'x'=4,'c'=2,'h'=2,'y'=4] {'h','y'}, dimensions={0} | all-to-all | bytes 24576 | tf_op jit(solution)/shard_map/all_to_all | solution.py:22
  90.0 0.8 columns.4
  90.8 7.6 %all_to_all.75.parts_ref = f32[8,1,512]{2,1,0:T(1,128)S(1)} all-to-all(f32[8,1,512]{2,1,0:T(1,128)S(1)} %columns.4), channel_id=1, replica_groups=mesh['z'=8,'x'=4,'c'=2,'h'=2,'y'=4] {'c','x'}, dimensions={0} | all-to-all | bytes 32768 | tf_op jit(solution)/shard_map/all_to_all | solution.py:22
  98.5 12.9 %all_to_all.76.parts_ref = f32[8,1,512]{2,1,0:T(1,128)S(1)} all-to-all(f32[8,1,512]{2,1,0:T(1,128)S(1)} %sums.4), channel_id=1, replica_groups=mesh['z'=8,'x'=4,'c'=2,'h'=2,'y'=4] {'z'}, dimensions={0} | all-to-all | bytes 32768 | tf_op jit(solution)/shard_map/all_to_all | solution.py:22
  111.4 7.6 %all_to_all.77.columns_ref = f32[8,1,512]{2,1,0:T(1,128)S(1)} all-to-all(f32[8,1,512]{2,1,0:T(1,128)S(1)} %inverse.4), channel_id=1, replica_groups=mesh['z'=8,'x'=4,'c'=2,'h'=2,'y'=4] {'c','x'}, dimensions={0} | all-to-all | bytes 32768 | tf_op jit(solution)/shard_map/all_to_all | solution.py:22
  119.0 0.8 rows.3
  119.8 17.3 %all_to_all.78.parts_ref = f32[8,1,384]{2,1,0:T(1,128)S(1)} all-to-all(f32[8,1,384]{2,1,0:T(1,128)S(1)} %rows.3), channel_id=1, replica_groups=mesh['z'=8,'x'=4,'c'=2,'h'=2,'y'=4] {'h','y'}, dimensions={0} | all-to-all | bytes 24576 | tf_op jit(solution)/shard_map/all_to_all | solution.py:22
  137.1 1.4 columns.5.after_ref
  138.5 3.3 %all-to-all-start.9 = ((f32[8,1,512]{2,1,0:T(1,128)}), f32[8,1,512]{2,1,0:T(1,128)S(1)}, u32[]{:S(2)}, u32[]{:S(2)}) async-start(f32[8,1,512]{2,1,0:T(1,128)} %columns.5.after_ref), calls=%async_computation.9 | async-start | bytes 32768 | tf_op jit(solution)/shard_map/all_to_all | solution.py:22
  141.9 4.3 %targets_sent.1 = f32[4,256,512]{2,1,0:T(8,128)} custom-call(s32[5]{0:T(128)S(1)} %stack.23.where_ref, f32[8,1,384]{2,1,0:T(1,128)S(1)} %all_to_all.78.parts_ref, bf16[384,256]{1,0:T(8,128)(2,1)S(1)} %copy-done.3, f32[8,384,512]{2,1,0:T(8,128)} %copy-done, f32[8,1,512]{2,1,0:T(1,128)} %columns.5.after_ref), custom_call_target="tpu_custom_call" | custom-call | flops 402653184 | bytes 6291456 | tf_op jit(solution)/shard_map/targets_sent/pallas_call | solution.py:310
  146.2 2.3 collective-permute-start
  148.5 0.0 all-to-all-done.9.parts_ref
  148.6 0.6 sums.5.after_ref
  149.2 3.3 %all-to-all-start.10 = ((f32[8,1,512]{2,1,0:T(1,128)}), f32[8,1,512]{2,1,0:T(1,128)S(1)}, u32[]{:S(2)}, u32[]{:S(2)}) async-start(f32[8,1,512]{2,1,0:T(1,128)} %sums.5.after_ref), calls=%async_computation.10 | async-start | bytes 32768 | tf_op jit(solution)/shard_map/all_to_all | solution.py:22
  152.5 0.1 collective-permute-done.added_ref
  152.6 4.3 %targets_kept.1 = (f32[256,512]{1,0:T(8,128)S(1)}, f32[256,512]{1,0:T(8,128)}, f32[256,512]{1,0:T(8,128)}, f32[256,512]{1,0:T(8,128)}) custom-call(s32[5]{0:T(128)S(1)} %stack.23.where_ref, f32[8,1,384]{2,1,0:T(1,128)S(1)} %all_to_all.78.parts_ref, bf16[384,256]{1,0:T(8,128)(2,1)S(1)} %copy-done.3, f32[8,384,512]{2,1,0:T(8,128)} %copy-done, ...), custom_call_target="tpu_custom_call" | custom-call | flops 402653184 | bytes 6291456 | tf_op jit(solution)/shard_map/targets_kept/pallas_call | solution.py:322
  157.0 3.8 %collective-permute-start.1 = (f32[256,512]{1,0:T(8,128)}, f32[256,512]{1,0:T(8,128)S(1)}, u32[]{:S(2)}, u32[]{:S(2)}) collective-permute-start(f32[256,512]{1,0:T(8,128)} %get-tuple-element.17), channel_id=1, source_target_pairs={{0,16},{16,0},{32,48},{48,32},{1,17},{17,1},{33,49},{49,33},{2,18}... | collective-permute-start | bytes 1572872 | tf_op jit(solution)/shard_map/ppermute | solution.py:350
  160.7 4.6 %collective-permute-start.2 = (f32[256,512]{1,0:T(8,128)}, f32[256,512]{1,0:T(8,128)S(1)}, u32[]{:S(2)}, u32[]{:S(2)}) collective-permute-start(f32[256,512]{1,0:T(8,128)} %get-tuple-element.18), channel_id=1, source_target_pairs={{0,32},{16,48},{32,0},{48,16},{1,33},{17,49},{33,1},{49,17},{2,34}... | collective-permute-start | bytes 1572872 | tf_op jit(solution)/shard_map/ppermute | solution.py:350
  165.3 2.1 collective-permute-start.3
  167.4 0.0 all-to-all-done.10.parts_ref
  167.5 26.0 %all_to_all.79.columns_ref = f32[8,1,512]{2,1,0:T(1,128)S(1)} all-to-all(f32[8,1,512]{2,1,0:T(1,128)S(1)} %inverse.5), channel_id=1, replica_groups=mesh['z'=8,'x'=4,'c'=2,'h'=2,'y'=4] {'c','x'}, dimensions={0} | all-to-all | bytes 32768 | tf_op jit(solution)/shard_map/all_to_all | solution.py:22
  193.5 4.2 %final.1 = f32[4,104,256]{2,1,0:T(8,128)S(1)} custom-call(f32[8,1,384]{2,1,0:T(1,128)S(1)} %all_to_all.78.parts_ref, f32[8,1,512]{2,1,0:T(1,128)S(1)} %all_to_all.79.columns_ref, bf16[8,8,64,256]{3,2,1,0:T(8,128)(2,1)} %bitcast.22, f32[8,384,512]{2,1,0:T(8,128)} %copy-done), custom_call_target="tpu_custom_call" | custom-call | flops 2013265920 | bytes 6291456 | tf_op jit(solution)/shard_map/final/pallas_call | solution.py:382
  197.7 11.3 %all_to_all.80 = f32[4,104,256]{2,1,0:T(8,128)S(1)} all-to-all(f32[4,104,256]{2,1,0:T(8,128)S(1)} %final.1), channel_id=1, replica_groups=mesh['z'=8,'x'=4,'c'=2,'h'=2,'y'=4] {'y'}, dimensions={0} | all-to-all | bytes 851968 | tf_op jit(solution)/shard_map/all_to_all | solution.py:22
  209.0 0.0 collective-permute-done.1.one_ref
  209.0 0.0 collective-permute-done.2.two_ref
  209.1 0.8 turn.1
  209.8 3.4 %collective-permute-start.4 = (f32[4,64,256]{2,1,0:T(8,128)S(1)}, f32[4,64,256]{2,1,0:T(8,128)S(1)}, u32[]{:S(2)}, u32[]{:S(2)}) collective-permute-start(f32[4,64,256]{2,1,0:T(8,128)S(1)} %get-tuple-element.21), channel_id=1, source_target_pairs={{0,64},{64,0},{128,192},{192,128},{256,320},{320,256},{384,448},{4... | collective-permute-start | bytes 786440 | tf_op jit(solution)/shard_map/ppermute | solution.py:350
  213.3 0.1 multiply_bitcast_fusion
  213.3 2.5 collective-permute-start.6
  215.8 5.6 %collective-permute-done.4 = f32[4,64,256]{2,1,0:T(8,128)S(1)} collective-permute-done((f32[4,64,256]{2,1,0:T(8,128)S(1)}, f32[4,64,256]{2,1,0:T(8,128)S(1)}, u32[]{:S(2)}, u32[]{:S(2)}) %collective-permute-start.4) | collective-permute-done | bytes 262176 | tf_op jit(solution)/shard_map/ppermute | solution.py:350
  221.5 4.4 %collective-permute-start.5 = (f32[2,64,256]{2,1,0:T(8,128)S(1)}, f32[2,64,256]{2,1,0:T(8,128)S(1)}, u32[]{:S(2)}, u32[]{:S(2)}) collective-permute-start(f32[2,64,256]{2,1,0:T(8,128)S(1)} %get-tuple-element.24), channel_id=1, source_target_pairs={{0,128},{64,192},{128,0},{192,64},{256,384},{320,448},{384,256},{4... | collective-permute-start | bytes 393224 | tf_op jit(solution)/shard_map/ppermute | solution.py:350
  225.9 4.4 %collective-permute-done.6.came_ref = f32[104,256]{1,0:T(8,128)S(1)} collective-permute-done((f32[104,256]{1,0:T(8,128)S(1)}, f32[104,256]{1,0:T(8,128)S(1)}, u32[]{:S(2)}, u32[]{:S(2)}) %collective-permute-start.6) | collective-permute-done | bytes 106528 | tf_op jit(solution)/shard_map/ppermute | solution.py:350
  230.3 0.8 join.1
  231.1 5.5 %all-to-all-start.13 = ((f32[4,96,256]{2,1,0:T(8,128)}), f32[4,96,256]{2,1,0:T(8,128)S(1)}, u32[]{:S(2)}, u32[]{:S(2)}) async-start(f32[4,96,256]{2,1,0:T(8,128)} %get-tuple-element.23), calls=%async_computation.13 | async-start | bytes 786432 | tf_op jit(solution)/shard_map/all_to_all | solution.py:22
  236.6 9.9 %collective-permute-start.7 = (f32[64,256]{1,0:T(8,128)S(1)}, f32[64,256]{1,0:T(8,128)S(1)}, u32[]{:S(2)}, u32[]{:S(2)}) collective-permute-start(f32[64,256]{1,0:T(8,128)S(1)} %slice_bitcast_fusion), channel_id=1, source_target_pairs={{0,256},{64,320},{128,384},{192,448},{256,0},{320,64},{384,128},{4... | collective-permute-start | bytes 196616 | tf_op jit(solution)/shard_map/ppermute | solution.py:350
  246.6 2.2 collective-permute-done.7
  248.8 0.7 fusion.1
  249.5 0.9 bitcast_divide_fusion
  (21 shorter events, 0.3 us)
Async XLA Ops:
  0.7 1.6 copy-start.1
  2.3 0.9 copy-start.2
  8.1 31.4 %copy-start = (f32[8,384,512]{2,1,0:T(8,128)}, f32[8,384,512]{2,1,0:T(8,128)S(1)}, u32[]{:S(2)}) copy-start(f32[8,384,512]{2,1,0:T(8,128)S(1)} %get-tuple-element.15.tile_ref) | copy-start | bytes 18874372
  137.1 4.8 %copy-start.3 = (bf16[384,256]{1,0:T(8,128)(2,1)S(1)}, bf16[384,256]{1,0:T(8,128)(2,1)}, u32[]{:S(2)}) copy-start(bf16[384,256]{1,0:T(8,128)(2,1)} %latents_ref.5) | copy-start | bytes 589828
  138.5 10.0 %all-to-all-start.9 = ((f32[8,1,512]{2,1,0:T(1,128)}), f32[8,1,512]{2,1,0:T(1,128)S(1)}, u32[]{:S(2)}, u32[]{:S(2)}) async-start(f32[8,1,512]{2,1,0:T(1,128)} %columns.5.after_ref), calls=%async_computation.9 | async-start | bytes 32768 | tf_op jit(solution)/shard_map/all_to_all | solution.py:22
  146.2 6.4 %collective-permute-start = (f32[4,256,512]{2,1,0:T(8,128)}, f32[4,256,512]{2,1,0:T(8,128)}, u32[]{:S(2)}, u32[]{:S(2)}) collective-permute-start(f32[4,256,512]{2,1,0:T(8,128)} %targets_sent.1), channel_id=1, source_target_pairs={{0,8},{8,0},{1,9},{9,1},{2,10},{10,2},{3,11},{11,3},{4,12},{12,4},... | collective-permute-start | bytes 6291464 | tf_op jit(solution)/shard_map/ppermute | solution.py:350
  149.2 18.2 %all-to-all-start.10 = ((f32[8,1,512]{2,1,0:T(1,128)}), f32[8,1,512]{2,1,0:T(1,128)S(1)}, u32[]{:S(2)}, u32[]{:S(2)}) async-start(f32[8,1,512]{2,1,0:T(1,128)} %sums.5.after_ref), calls=%async_computation.10 | async-start | bytes 32768 | tf_op jit(solution)/shard_map/all_to_all | solution.py:22
  157.0 52.1 %collective-permute-start.1 = (f32[256,512]{1,0:T(8,128)}, f32[256,512]{1,0:T(8,128)S(1)}, u32[]{:S(2)}, u32[]{:S(2)}) collective-permute-start(f32[256,512]{1,0:T(8,128)} %get-tuple-element.17), channel_id=1, source_target_pairs={{0,16},{16,0},{32,48},{48,32},{1,17},{17,1},{33,49},{49,33},{2,18}... | collective-permute-start | bytes 1572872 | tf_op jit(solution)/shard_map/ppermute | solution.py:350
  160.7 48.3 %collective-permute-start.2 = (f32[256,512]{1,0:T(8,128)}, f32[256,512]{1,0:T(8,128)S(1)}, u32[]{:S(2)}, u32[]{:S(2)}) collective-permute-start(f32[256,512]{1,0:T(8,128)} %get-tuple-element.18), channel_id=1, source_target_pairs={{0,32},{16,48},{32,0},{48,16},{1,33},{17,49},{33,1},{49,17},{2,34}... | collective-permute-start | bytes 1572872 | tf_op jit(solution)/shard_map/ppermute | solution.py:350
  165.3 43.7 %collective-permute-start.3 = (f32[256,512]{1,0:T(8,128)}, f32[256,512]{1,0:T(8,128)S(1)}, u32[]{:S(2)}, u32[]{:S(2)}) collective-permute-start(f32[256,512]{1,0:T(8,128)} %get-tuple-element.19), channel_id=1, source_target_pairs={{0,48},{16,32},{32,16},{48,0},{1,49},{17,33},{33,17},{49,1},{2,50}... | collective-permute-start | bytes 1572872 | tf_op jit(solution)/shard_map/ppermute | solution.py:350
  209.8 11.6 %collective-permute-start.4 = (f32[4,64,256]{2,1,0:T(8,128)S(1)}, f32[4,64,256]{2,1,0:T(8,128)S(1)}, u32[]{:S(2)}, u32[]{:S(2)}) collective-permute-start(f32[4,64,256]{2,1,0:T(8,128)S(1)} %get-tuple-element.21), channel_id=1, source_target_pairs={{0,64},{64,0},{128,192},{192,128},{256,320},{320,256},{384,448},{4... | collective-permute-start | bytes 786440 | tf_op jit(solution)/shard_map/ppermute | solution.py:350
  213.3 17.0 %collective-permute-start.6 = (f32[104,256]{1,0:T(8,128)S(1)}, f32[104,256]{1,0:T(8,128)S(1)}, u32[]{:S(2)}, u32[]{:S(2)}) collective-permute-start(f32[104,256]{1,0:T(8,128)S(1)} %reduce_sum.9.after_ref.kept_ref), channel_id=1, source_target_pairs={{0,4},{4,0},{1,5},{5,1},{2,6},{6,2},{3,7},{7,3},{8,12},{12,8},{9,1... | collective-permute-start | bytes 319496 | tf_op jit(solution)/shard_map/ppermute | solution.py:350
  221.5 15.1 %collective-permute-start.5 = (f32[2,64,256]{2,1,0:T(8,128)S(1)}, f32[2,64,256]{2,1,0:T(8,128)S(1)}, u32[]{:S(2)}, u32[]{:S(2)}) collective-permute-start(f32[2,64,256]{2,1,0:T(8,128)S(1)} %get-tuple-element.24), channel_id=1, source_target_pairs={{0,128},{64,192},{128,0},{192,64},{256,384},{320,448},{384,256},{4... | collective-permute-start | bytes 393224 | tf_op jit(solution)/shard_map/ppermute | solution.py:350
  231.1 18.4 %all-to-all-start.13 = ((f32[4,96,256]{2,1,0:T(8,128)}), f32[4,96,256]{2,1,0:T(8,128)S(1)}, u32[]{:S(2)}, u32[]{:S(2)}) async-start(f32[4,96,256]{2,1,0:T(8,128)} %get-tuple-element.23), calls=%async_computation.13 | async-start | bytes 786432 | tf_op jit(solution)/shard_map/all_to_all | solution.py:22
  236.6 12.2 %collective-permute-start.7 = (f32[64,256]{1,0:T(8,128)S(1)}, f32[64,256]{1,0:T(8,128)S(1)}, u32[]{:S(2)}, u32[]{:S(2)}) collective-permute-start(f32[64,256]{1,0:T(8,128)S(1)} %slice_bitcast_fusion), channel_id=1, source_target_pairs={{0,256},{64,320},{128,384},{192,448},{256,0},{320,64},{384,128},{4... | collective-permute-start | bytes 196616 | tf_op jit(solution)/shard_map/ppermute | solution.py:350

commit v7 on v6

--- a/solution.py
+++ b/solution.py
@@ -150,20 +150,25 @@
 
 
 def targets_kept_kernel(
-    where_ref, parts_ref, latents_ref, tile_ref, added_ref, after_ref, own_ref, one_ref, two_ref, three_ref, tiles_ref, more_ref, sems
+    where_ref, parts_ref, latents_ref, tile_ref, added_ref, after_ref,
+    one_ref, two_ref, own_one_ref, own_two_ref, tiles_ref, more_ref, sems,
 ):
     del after_ref
-    slots = (2, 1, 3, 0)
     steps = [
         [(tile_ref.at[where_ref[0] * X + (where_ref[1] ^ s)], tiles_ref.at[s]), (added_ref.at[s], more_ref.at[s])]
-        for s in slots
+        for s in range(X)
     ]
     wait = fetch(steps, sems)
     scale = row_scale_of(parts_ref)
     latents = latents_ref[...]
-    for step, s in enumerate(slots):
-        wait(step)
-        (own_ref, one_ref, two_ref, three_ref)[s][...] = targets_part(tiles_ref[s], scale, latents) + more_ref[s]
+    for s in range(X):
+        wait(s)
+        summed = targets_part(tiles_ref[s], scale, latents) + more_ref[s]
+        upper, lower = jnp.split(summed, 2, axis=0)
+        ref, index = ((own_one_ref, 0), (one_ref, 0), (one_ref, 1), (own_one_ref, 1))[s]
+        ref[index] = upper
+        ref, index = ((own_two_ref, 0), (own_two_ref, 1), (two_ref, 1), (two_ref, 0))[s]
+        ref[index] = lower
 
 
 def sum_kernel(parts_ref, *refs):
@@ -189,9 +194,12 @@
     mass_ref[...] = total[group:]
 
 
-def turn_kernel(where_ref, own_ref, one_ref, two_ref, three_ref, after_ref, send_ref, keep_ref, turned_ref):
+def turn_kernel(where_ref, own_one_ref, one_ref, more_one_ref, own_two_ref, two_ref, more_two_ref, after_ref, *refs):
     del after_ref
-    turned_ref[...] = (own_ref[...] + one_ref[...] + two_ref[...] + three_ref[...]).T
+    send_ref, keep_ref, turned_ref = refs
+    upper = own_one_ref[0] + one_ref[0] + more_one_ref[...]
+    lower = own_two_ref[0] + two_ref[0] + more_two_ref[...]
+    turned_ref[...] = jnp.concatenate([upper, lower], axis=0).T
     share = send_ref.shape[1]
     for i, slot in enumerate((0, 4, 2, 6)):
         for ref, s in ((keep_ref, slot), (send_ref, slot + 1)):
@@ -323,7 +331,7 @@
             targets_kept_kernel,
             in_specs=[smem, vmem, vmem, hbm, hbm, anywhere],
             out_specs=[vmem] * 4,
-            out_shape=[f32(width, block)] * 4,
+            out_shape=[f32(2, width // 2, block)] * 4,
             scratch_shapes=[
                 tiles((X, token_count, block)),
                 tiles((X, width, block)),
@@ -375,8 +383,10 @@
         if not last:
             part = rows(col_scale)
 
-    own, *others = kept
-    others = [swap(other, "x", X, s) for s, other in enumerate(others, 1)]
+    one, two, own_one, own_two = kept
+    one, two = swap(one, "x", X, 1), swap(two, "x", X, 3)
+    more_one = swap(own_one[1] + one[1], "x", X, 3)
+    more_two = swap(own_two[1] + two[1], "x", X, 1)
 
     group = token_count // Y
     packed = pl.pallas_call(
@@ -391,20 +401,20 @@
             pltpu.SemaphoreType.DMA((2 * BLOCKS,)),
         ],
         compiler_params=params(FETCHES),
-        cost_estimate=cost(5 * size * width, 4 * size),
+        cost_estimate=cost(12 * size * width, 4 * size),
         name="final",
     )(parts, col_scale, codes, far)
     packed = jnp.sum(exchange(packed, "y"), axis=0)
     away, near = pl.pallas_call(
         turn_kernel,
-        in_specs=[smem] + [vmem] * 4 + [anywhere],
+        in_specs=[smem] + [vmem] * 6 + [anywhere],
         out_specs=[vmem] * 2,
         out_shape=[f32(Z // 2, share, width)] * 2,
         scratch_shapes=[pltpu.VMEM((block, width), jnp.float32)],
         compiler_params=params(16 << 20),
         cost_estimate=cost(3 * block * width, 12 * block * width),
         name="turn",
-    )(where, own, *others, packed)
+    )(where, own_one, one, more_one, own_two, two, more_two, packed)
     near = near + swap(away, "z", Z, 1)
     numer, mass = pl.pallas_call(
         join_kernel,
@@ -417,8 +427,8 @@
     )(packed, swap(packed, "h", H, 1), near)
     near = add(near[:2], swap(near[2:], "z", Z, 2), mass)
     summed = near[0] + swap(near[1], "z", Z, 4)
-    scale = lax.dynamic_slice(mine, (0, 0, where[4]), (1, 1, share)).reshape(share)
-    targets = summed * (scale * (total_codes / total_tokens))[:, None]
+    own = lax.dynamic_slice(mine, (0, 0, where[4]), (1, 1, share)).reshape(share)
+    targets = summed * (own * (total_codes / total_tokens))[:, None]
     mass = mass[:2].reshape(2 * width)[:token_count]
     rebuilt = exchange(numer, "y").reshape(token_count, width) / mass[:, None]
     return (targets, rebuilt)

time: 253 us -> 243 us (0.960)
  blocking collectives: 163 us -> 126 us
  starting transfers between devices: 45.2 us -> 58 us
  waiting for transfers between devices: 12.3 us -> 24.1 us
    all_to_all x11 -> x9, blocking collectives: 163 us -> 126 us  [exchange(): return lax.all_to_all(blocks, axes, 0, 0, tiled=True)]
    all_to_all x3 -> x5, starting transfers between devices: 12.2 us -> 22.1 us  [exchange(): return lax.all_to_all(blocks, axes, 0, 0, tiled=True)]
    ppermute x8 -> x9, waiting for transfers between devices: 12.3 us -> 20.4 us  [swap(): return lax.ppermute(value, axis, [(i, i ^ bits) for i in range(count)])]
    all_to_all x3 -> x5, waiting for transfers between devices: 0.01 us -> 3.69 us  [exchange(): return lax.all_to_all(blocks, axes, 0, 0, tiled=True)]
    ppermute x8 -> x9, starting transfers between devices: 33 us -> 36 us  [swap(): return lax.ppermute(value, axis, [(i, i ^ bits) for i in range(count)])]
  transfers between devices with their start and end apart: 11 -> 14, of which waited for: 4 -> 9; matrix products, arithmetic and copies ran while one was open for 0% -> 1% of each run, Pallas kernels for 6% -> 7%
where the time goes in v7:
time: 243 us; the launch traced here: 241 us
  blocking collectives  126 us (52%)
  starting transfers between devices  58 us (24%)
  Pallas kernels  26.2 us (11%)
  waiting for transfers between devices  24.1 us (10%)
  other arithmetic  3.49 us (1%)
  local copies, waits for them, and re-layouts  2.65 us (1%)
    all_to_all x9, blocking collectives, exchange(): return lax.all_to_all(blocks, axes, 0, 0, tiled=True)  126 us
    ppermute x9, starting transfers between devices, swap(): return lax.ppermute(value, axis, [(i, i ^ bits) for i in range(count)])  36 us
    all_to_all x5, starting transfers between devices, exchange(): return lax.all_to_all(blocks, axes, 0, 0, tiled=True)  22.1 us
    ppermute x9, waiting for transfers between devices, swap(): return lax.ppermute(value, axis, [(i, i ^ bits) for i in range(count)])  20.4 us
    pallas_call x1, Pallas kernels, per_device(): pl.pallas_call(final_kernel, in_specs=[vmem, vmem, hbm, hbm], out_specs=v...  4.92 us
    pallas_call x1, Pallas kernels, per_device(): pl.pallas_call(setup_kernel, in_specs=[smem, hbm, hbm], out_specs=[vmem,...  4.88 us
  transfers between devices with their start and end apart: 14, of which 9 were waited for; matrix products, arithmetic and copies ran while one was open for 1% of the time, Pallas kernels for 7%

profile of v7, /device:TPU:24, one launch (start us, length us, event | category | flops | bytes accessed | tf_op | source)
XLA Modules:
  0.0 241.1 jit_solution(15996455766075020872)
XLA Ops:
  0.7 0.9 copy-done.3
  1.7 1.6 copy-done.5
  3.2 4.9 %setup.1 = (f32[8,384,512]{2,1,0:T(8,128)S(1)}, f32[8,1,384]{2,1,0:T(1,128)S(1)}, f32[8,384,512]{2,1,0:T(8,128)S(1)}) custom-call(s32[5]{0:T(128)S(1)} %stack.23.where_ref, bf16[384,256]{1,0:T(8,128)(2,1)S(1)} %copy-done.3, bf16[8,8,64,256]{3,2,1,0:T(8,128)(2,1)S(1)} %bitcast.27), custom_call_target="tpu_custom_call" | custom-call | flops 805306368 | bytes 6291456 | tf_op jit(solution)/shard_map/setup/pallas_call | solution.py:276
  8.1 30.6 %all_to_all.70.parts_ref = f32[8,1,384]{2,1,0:T(1,128)S(1)} all-to-all(f32[8,1,384]{2,1,0:T(1,128)S(1)} %get-tuple-element.13), channel_id=1, replica_groups=mesh['z'=8,'x'=4,'c'=2,'h'=2,'y'=4] {'h','y'}, dimensions={0} | all-to-all | bytes 24576 | tf_op jit(solution)/shard_map/all_to_all | solution.py:22
  38.7 0.8 columns.3
  39.6 9.4 %all_to_all.71.parts_ref = f32[8,1,512]{2,1,0:T(1,128)S(1)} all-to-all(f32[8,1,512]{2,1,0:T(1,128)S(1)} %columns.3), channel_id=1, replica_groups=mesh['z'=8,'x'=4,'c'=2,'h'=2,'y'=4] {'c','x'}, dimensions={0} | all-to-all | bytes 32768 | tf_op jit(solution)/shard_map/all_to_all | solution.py:22
  49.0 15.3 %all_to_all.72.parts_ref = f32[8,1,512]{2,1,0:T(1,128)S(1)} all-to-all(f32[8,1,512]{2,1,0:T(1,128)S(1)} %sums.3), channel_id=1, replica_groups=mesh['z'=8,'x'=4,'c'=2,'h'=2,'y'=4] {'z'}, dimensions={0} | all-to-all | bytes 32768 | tf_op jit(solution)/shard_map/all_to_all | solution.py:22
  64.3 7.6 %all_to_all.73.columns_ref = f32[8,1,512]{2,1,0:T(1,128)S(1)} all-to-all(f32[8,1,512]{2,1,0:T(1,128)S(1)} %inverse.3), channel_id=1, replica_groups=mesh['z'=8,'x'=4,'c'=2,'h'=2,'y'=4] {'c','x'}, dimensions={0} | all-to-all | bytes 32768 | tf_op jit(solution)/shard_map/all_to_all | solution.py:22
  72.0 0.8 rows.2
  72.7 17.3 %all_to_all.74.parts_ref = f32[8,1,384]{2,1,0:T(1,128)S(1)} all-to-all(f32[8,1,384]{2,1,0:T(1,128)S(1)} %rows.2), channel_id=1, replica_groups=mesh['z'=8,'x'=4,'c'=2,'h'=2,'y'=4] {'h','y'}, dimensions={0} | all-to-all | bytes 24576 | tf_op jit(solution)/shard_map/all_to_all | solution.py:22
  90.0 0.8 columns.4
  90.8 7.6 %all_to_all.75.parts_ref = f32[8,1,512]{2,1,0:T(1,128)S(1)} all-to-all(f32[8,1,512]{2,1,0:T(1,128)S(1)} %columns.4), channel_id=1, replica_groups=mesh['z'=8,'x'=4,'c'=2,'h'=2,'y'=4] {'c','x'}, dimensions={0} | all-to-all | bytes 32768 | tf_op jit(solution)/shard_map/all_to_all | solution.py:22
  98.5 12.9 %all_to_all.76.parts_ref = f32[8,1,512]{2,1,0:T(1,128)S(1)} all-to-all(f32[8,1,512]{2,1,0:T(1,128)S(1)} %sums.4), channel_id=1, replica_groups=mesh['z'=8,'x'=4,'c'=2,'h'=2,'y'=4] {'z'}, dimensions={0} | all-to-all | bytes 32768 | tf_op jit(solution)/shard_map/all_to_all | solution.py:22
  111.4 7.6 %all_to_all.77.columns_ref = f32[8,1,512]{2,1,0:T(1,128)S(1)} all-to-all(f32[8,1,512]{2,1,0:T(1,128)S(1)} %inverse.4), channel_id=1, replica_groups=mesh['z'=8,'x'=4,'c'=2,'h'=2,'y'=4] {'c','x'}, dimensions={0} | all-to-all | bytes 32768 | tf_op jit(solution)/shard_map/all_to_all | solution.py:22
  119.0 0.8 rows.3
  119.8 17.3 %all_to_all.78.parts_ref = f32[8,1,384]{2,1,0:T(1,128)S(1)} all-to-all(f32[8,1,384]{2,1,0:T(1,128)S(1)} %rows.3), channel_id=1, replica_groups=mesh['z'=8,'x'=4,'c'=2,'h'=2,'y'=4] {'h','y'}, dimensions={0} | all-to-all | bytes 24576 | tf_op jit(solution)/shard_map/all_to_all | solution.py:22
  137.1 1.4 columns.5.after_ref
  138.5 3.3 %all-to-all-start.9 = ((f32[8,1,512]{2,1,0:T(1,128)}), f32[8,1,512]{2,1,0:T(1,128)S(1)}, u32[]{:S(2)}, u32[]{:S(2)}) async-start(f32[8,1,512]{2,1,0:T(1,128)} %columns.5.after_ref), calls=%async_computation.9 | async-start | bytes 32768 | tf_op jit(solution)/shard_map/all_to_all | solution.py:22
  141.9 4.3 %targets_sent.1 = f32[4,256,512]{2,1,0:T(8,128)} custom-call(s32[5]{0:T(128)S(1)} %stack.23.where_ref, f32[8,1,384]{2,1,0:T(1,128)S(1)} %all_to_all.78.parts_ref, bf16[384,256]{1,0:T(8,128)(2,1)S(1)} %copy-done.4, f32[8,384,512]{2,1,0:T(8,128)} %copy-done, f32[8,1,512]{2,1,0:T(1,128)} %columns.5.after_ref), custom_call_target="tpu_custom_call" | custom-call | flops 402653184 | bytes 6291456 | tf_op jit(solution)/shard_map/targets_sent/pallas_call | solution.py:318
  146.2 2.3 collective-permute-start
  149.2 3.3 %all-to-all-start.10 = ((f32[8,1,512]{2,1,0:T(1,128)}), f32[8,1,512]{2,1,0:T(1,128)S(1)}, u32[]{:S(2)}, u32[]{:S(2)}) async-start(f32[8,1,512]{2,1,0:T(1,128)} %sums.5.after_ref), calls=%async_computation.10 | async-start | bytes 32768 | tf_op jit(solution)/shard_map/all_to_all | solution.py:22
  152.6 4.5 %targets_kept.1 = (f32[2,128,512]{2,1,0:T(8,128)S(1)}, f32[2,128,512]{2,1,0:T(8,128)}, f32[2,128,512]{2,1,0:T(8,128)}, f32[2,128,512]{2,1,0:T(8,128)}) custom-call(s32[5]{0:T(128)S(1)} %stack.23.where_ref, f32[8,1,384]{2,1,0:T(1,128)S(1)} %all_to_all.78.parts_ref, bf16[384,256]{1,0:T(8,128)(2,1)S(1)} %copy-done.4, f32[8,384,512]{2,1,0:T(8,128)} %copy-done, ...), custom_call_target="tpu_custom_call" | custom-call | flops 402653184 | bytes 6291456 | tf_op jit(solution)/shard_map/targets_kept/pallas_call | solution.py:330
  157.2 5.0 %collective-permute-start.3 = (f32[2,128,512]{2,1,0:T(8,128)}, f32[2,128,512]{2,1,0:T(8,128)S(1)}, u32[]{:S(2)}, u32[]{:S(2)}) collective-permute-start(f32[2,128,512]{2,1,0:T(8,128)} %get-tuple-element.19), channel_id=1, source_target_pairs={{0,48},{16,32},{32,16},{48,0},{1,49},{17,33},{33,17},{49,1},{2,50}... | collective-permute-start | bytes 1572872 | tf_op jit(solution)/shard_map/ppermute | solution.py:358
  162.2 0.7 all-to-all-done.10.parts_ref
  163.0 0.6 inverse.5
  163.6 4.4 %all-to-all-start.11 = ((f32[8,1,512]{2,1,0:T(1,128)}), f32[8,1,512]{2,1,0:T(1,128)S(1)}, u32[]{:S(2)}, u32[]{:S(2)}) async-start(f32[8,1,512]{2,1,0:T(1,128)} %inverse.5), calls=%async_computation.11 | async-start | bytes 32768 | tf_op jit(solution)/shard_map/all_to_all | solution.py:22
  168.1 4.0 %collective-permute-start.1 = (f32[2,128,512]{2,1,0:T(8,128)S(1)}, f32[2,128,512]{2,1,0:T(8,128)S(1)}, u32[]{:S(2)}, u32[]{:S(2)}) collective-permute-start(f32[2,128,512]{2,1,0:T(8,128)S(1)} %get-tuple-element.17.refs_0_), channel_id=1, source_target_pairs={{0,16},{16,0},{32,48},{48,32},{1,17},{17,1},{33,49},{49,33},{2,18}... | collective-permute-start | bytes 1572872 | tf_op jit(solution)/shard_map/ppermute | solution.py:358
  172.1 2.8 %all-to-all-done.11.columns_ref = f32[8,1,512]{2,1,0:T(1,128)S(1)} async-done(((f32[8,1,512]{2,1,0:T(1,128)}), f32[8,1,512]{2,1,0:T(1,128)S(1)}, u32[]{:S(2)}, u32[]{:S(2)}) %all-to-all-start.11) | async-done | bytes 16416 | tf_op jit(solution)/shard_map/all_to_all | solution.py:22
  174.9 4.9 %final.1 = f32[4,104,256]{2,1,0:T(8,128)} custom-call(f32[8,1,384]{2,1,0:T(1,128)S(1)} %all_to_all.78.parts_ref, f32[8,1,512]{2,1,0:T(1,128)S(1)} %all-to-all-done.11.columns_ref, bf16[8,8,64,256]{3,2,1,0:T(8,128)(2,1)} %bitcast.26, f32[8,384,512]{2,1,0:T(8,128)} %copy-done), custom_call_target="tpu_custom_call" | custom-call | flops 4831838208 | bytes 6291456 | tf_op jit(solution)/shard_map/final/pallas_call | solution.py:392
  179.8 6.2 %all-to-all-start.12 = ((f32[4,104,256]{2,1,0:T(8,128)}), f32[4,104,256]{2,1,0:T(8,128)}, u32[]{:S(2)}, u32[]{:S(2)}) async-start(f32[4,104,256]{2,1,0:T(8,128)} %final.1), calls=%async_computation.12 | async-start | bytes 851968 | tf_op jit(solution)/shard_map/all_to_all | solution.py:22
  186.0 2.4 collective-permute-start.4
  188.5 4.4 %collective-permute-start.2 = (f32[128,512]{1,0:T(8,128)S(1)}, f32[128,512]{1,0:T(8,128)S(1)}, u32[]{:S(2)}, u32[]{:S(2)}) collective-permute-start(f32[128,512]{1,0:T(8,128)S(1)} %fusion.1), channel_id=1, source_target_pairs={{0,48},{16,32},{32,16},{48,0},{1,49},{17,33},{33,17},{49,1},{2,50}... | collective-permute-start | bytes 786440 | tf_op jit(solution)/shard_map/ppermute | solution.py:358
  193.0 1.0 reduce_sum.9.after_ref.kept_ref
  194.1 1.9 collective-permute-done.4.more_two_ref
  196.0 3.4 %collective-permute-done.2.more_one_ref = f32[128,512]{1,0:T(8,128)S(1)} collective-permute-done((f32[128,512]{1,0:T(8,128)S(1)}, f32[128,512]{1,0:T(8,128)S(1)}, u32[]{:S(2)}, u32[]{:S(2)}) %collective-permute-start.2) | collective-permute-done | bytes 262176 | tf_op jit(solution)/shard_map/ppermute | solution.py:358
  199.3 0.8 turn.1
  200.1 3.4 %collective-permute-start.5 = (f32[4,64,256]{2,1,0:T(8,128)S(1)}, f32[4,64,256]{2,1,0:T(8,128)S(1)}, u32[]{:S(2)}, u32[]{:S(2)}) collective-permute-start(f32[4,64,256]{2,1,0:T(8,128)S(1)} %get-tuple-element.21), channel_id=1, source_target_pairs={{0,64},{64,0},{128,192},{192,128},{256,320},{320,256},{384,448},{4... | collective-permute-start | bytes 786440 | tf_op jit(solution)/shard_map/ppermute | solution.py:358
  203.6 0.7 multiply_bitcast_fusion
  204.3 2.5 %collective-permute-start.7 = (f32[104,256]{1,0:T(8,128)S(1)}, f32[104,256]{1,0:T(8,128)S(1)}, u32[]{:S(2)}, u32[]{:S(2)}) collective-permute-start(f32[104,256]{1,0:T(8,128)S(1)} %reduce_sum.9.after_ref.kept_ref), channel_id=1, source_target_pairs={{0,4},{4,0},{1,5},{5,1},{2,6},{6,2},{3,7},{7,3},{8,12},{12,8},{9,1... | collective-permute-start | bytes 319496 | tf_op jit(solution)/shard_map/ppermute | solution.py:358
  206.8 4.4 %collective-permute-done.5 = f32[4,64,256]{2,1,0:T(8,128)S(1)} collective-permute-done((f32[4,64,256]{2,1,0:T(8,128)S(1)}, f32[4,64,256]{2,1,0:T(8,128)S(1)}, u32[]{:S(2)}, u32[]{:S(2)}) %collective-permute-start.5) | collective-permute-done | bytes 262176 | tf_op jit(solution)/shard_map/ppermute | solution.py:358
  211.2 4.5 %collective-permute-start.6 = (f32[2,64,256]{2,1,0:T(8,128)S(1)}, f32[2,64,256]{2,1,0:T(8,128)S(1)}, u32[]{:S(2)}, u32[]{:S(2)}) collective-permute-start(f32[2,64,256]{2,1,0:T(8,128)S(1)} %get-tuple-element.24), channel_id=1, source_target_pairs={{0,128},{64,192},{128,0},{192,64},{256,384},{320,448},{384,256},{4... | collective-permute-start | bytes 393224 | tf_op jit(solution)/shard_map/ppermute | solution.py:358
  215.8 7.9 %collective-permute-done.7.came_ref = f32[104,256]{1,0:T(8,128)S(1)} collective-permute-done((f32[104,256]{1,0:T(8,128)S(1)}, f32[104,256]{1,0:T(8,128)S(1)}, u32[]{:S(2)}, u32[]{:S(2)}) %collective-permute-start.7) | collective-permute-done | bytes 106528 | tf_op jit(solution)/shard_map/ppermute | solution.py:358
  223.7 0.8 join.1
  224.4 4.8 %all-to-all-start.13 = ((f32[4,96,256]{2,1,0:T(8,128)}), f32[4,96,256]{2,1,0:T(8,128)S(1)}, u32[]{:S(2)}, u32[]{:S(2)}) async-start(f32[4,96,256]{2,1,0:T(8,128)} %get-tuple-element.23), calls=%async_computation.13 | async-start | bytes 786432 | tf_op jit(solution)/shard_map/all_to_all | solution.py:22
  229.3 7.4 %collective-permute-start.8 = (f32[64,256]{1,0:T(8,128)S(1)}, f32[64,256]{1,0:T(8,128)S(1)}, u32[]{:S(2)}, u32[]{:S(2)}) collective-permute-start(f32[64,256]{1,0:T(8,128)S(1)} %slice_bitcast_fusion), channel_id=1, source_target_pairs={{0,256},{64,320},{128,384},{192,448},{256,0},{320,64},{384,128},{4... | collective-permute-start | bytes 196616 | tf_op jit(solution)/shard_map/ppermute | solution.py:358
  236.7 2.7 %collective-permute-done.8 = f32[64,256]{1,0:T(8,128)S(1)} collective-permute-done((f32[64,256]{1,0:T(8,128)S(1)}, f32[64,256]{1,0:T(8,128)S(1)}, u32[]{:S(2)}, u32[]{:S(2)}) %collective-permute-start.8) | collective-permute-done | bytes 65568 | tf_op jit(solution)/shard_map/ppermute | solution.py:358
  239.5 0.7 fusion.3
  240.2 0.9 bitcast_divide_fusion
  (31 shorter events, 1.3 us)
Async XLA Ops:
  0.7 0.9 copy-start.3
  1.7 1.6 copy-start.5
  8.1 31.4 %copy-start = (f32[8,384,512]{2,1,0:T(8,128)}, f32[8,384,512]{2,1,0:T(8,128)S(1)}, u32[]{:S(2)}) copy-start(f32[8,384,512]{2,1,0:T(8,128)S(1)} %get-tuple-element.15.tile_ref) | copy-start | bytes 18874372
  137.1 4.8 %copy-start.4 = (bf16[384,256]{1,0:T(8,128)(2,1)S(1)}, bf16[384,256]{1,0:T(8,128)(2,1)}, u32[]{:S(2)}) copy-start(bf16[384,256]{1,0:T(8,128)(2,1)} %latents_ref.5) | copy-start | bytes 589828
  138.5 10.0 %all-to-all-start.9 = ((f32[8,1,512]{2,1,0:T(1,128)}), f32[8,1,512]{2,1,0:T(1,128)S(1)}, u32[]{:S(2)}, u32[]{:S(2)}) async-start(f32[8,1,512]{2,1,0:T(1,128)} %columns.5.after_ref), calls=%async_computation.9 | async-start | bytes 32768 | tf_op jit(solution)/shard_map/all_to_all | solution.py:22
  146.2 6.4 %collective-permute-start = (f32[4,256,512]{2,1,0:T(8,128)}, f32[4,256,512]{2,1,0:T(8,128)}, u32[]{:S(2)}, u32[]{:S(2)}) collective-permute-start(f32[4,256,512]{2,1,0:T(8,128)} %targets_sent.1), channel_id=1, source_target_pairs={{0,8},{8,0},{1,9},{9,1},{2,10},{10,2},{3,11},{11,3},{4,12},{12,4},... | collective-permute-start | bytes 6291464 | tf_op jit(solution)/shard_map/ppermute | solution.py:358
  149.2 13.8 %all-to-all-start.10 = ((f32[8,1,512]{2,1,0:T(1,128)}), f32[8,1,512]{2,1,0:T(1,128)S(1)}, u32[]{:S(2)}, u32[]{:S(2)}) async-start(f32[8,1,512]{2,1,0:T(1,128)} %sums.5.after_ref), calls=%async_computation.10 | async-start | bytes 32768 | tf_op jit(solution)/shard_map/all_to_all | solution.py:22
  157.2 28.8 %collective-permute-start.3 = (f32[2,128,512]{2,1,0:T(8,128)}, f32[2,128,512]{2,1,0:T(8,128)S(1)}, u32[]{:S(2)}, u32[]{:S(2)}) collective-permute-start(f32[2,128,512]{2,1,0:T(8,128)} %get-tuple-element.19), channel_id=1, source_target_pairs={{0,48},{16,32},{32,16},{48,0},{1,49},{17,33},{33,17},{49,1},{2,50}... | collective-permute-start | bytes 1572872 | tf_op jit(solution)/shard_map/ppermute | solution.py:358
  163.6 11.3 %all-to-all-start.11 = ((f32[8,1,512]{2,1,0:T(1,128)}), f32[8,1,512]{2,1,0:T(1,128)S(1)}, u32[]{:S(2)}, u32[]{:S(2)}) async-start(f32[8,1,512]{2,1,0:T(1,128)} %inverse.5), calls=%async_computation.11 | async-start | bytes 32768 | tf_op jit(solution)/shard_map/all_to_all | solution.py:22
  168.0 17.9 %copy-start.2 = (f32[2,128,512]{2,1,0:T(8,128)S(1)}, f32[2,128,512]{2,1,0:T(8,128)}, u32[]{:S(2)}) copy-start(f32[2,128,512]{2,1,0:T(8,128)} %get-tuple-element.18.own_two_ref) | copy-start | bytes 1572868
  168.0 20.4 %copy-start.1 = (f32[2,128,512]{2,1,0:T(8,128)S(1)}, f32[2,128,512]{2,1,0:T(8,128)}, u32[]{:S(2)}) copy-start(f32[2,128,512]{2,1,0:T(8,128)} %get-tuple-element.16.own_one_ref) | copy-start | bytes 1572868
  168.1 20.3 %collective-permute-start.1 = (f32[2,128,512]{2,1,0:T(8,128)S(1)}, f32[2,128,512]{2,1,0:T(8,128)S(1)}, u32[]{:S(2)}, u32[]{:S(2)}) collective-permute-start(f32[2,128,512]{2,1,0:T(8,128)S(1)} %get-tuple-element.17.refs_0_), channel_id=1, source_target_pairs={{0,16},{16,0},{32,48},{48,32},{1,17},{17,1},{33,49},{49,33},{2,18}... | collective-permute-start | bytes 1572872 | tf_op jit(solution)/shard_map/ppermute | solution.py:358
  179.8 13.2 %all-to-all-start.12 = ((f32[4,104,256]{2,1,0:T(8,128)}), f32[4,104,256]{2,1,0:T(8,128)}, u32[]{:S(2)}, u32[]{:S(2)}) async-start(f32[4,104,256]{2,1,0:T(8,128)} %final.1), calls=%async_computation.12 | async-start | bytes 851968 | tf_op jit(solution)/shard_map/all_to_all | solution.py:22
  186.0 9.9 %collective-permute-start.4 = (f32[128,512]{1,0:T(8,128)S(1)}, f32[128,512]{1,0:T(8,128)S(1)}, u32[]{:S(2)}, u32[]{:S(2)}) collective-permute-start(f32[128,512]{1,0:T(8,128)S(1)} %fusion), channel_id=1, source_target_pairs={{0,16},{16,0},{32,48},{48,32},{1,17},{17,1},{33,49},{49,33},{2,18}... | collective-permute-start | bytes 786440 | tf_op jit(solution)/shard_map/ppermute | solution.py:358
  188.5 10.9 %collective-permute-start.2 = (f32[128,512]{1,0:T(8,128)S(1)}, f32[128,512]{1,0:T(8,128)S(1)}, u32[]{:S(2)}, u32[]{:S(2)}) collective-permute-start(f32[128,512]{1,0:T(8,128)S(1)} %fusion.1), channel_id=1, source_target_pairs={{0,48},{16,32},{32,16},{48,0},{1,49},{17,33},{33,17},{49,1},{2,50}... | collective-permute-start | bytes 786440 | tf_op jit(solution)/shard_map/ppermute | solution.py:358
  200.1 11.0 %collective-permute-start.5 = (f32[4,64,256]{2,1,0:T(8,128)S(1)}, f32[4,64,256]{2,1,0:T(8,128)S(1)}, u32[]{:S(2)}, u32[]{:S(2)}) collective-permute-start(f32[4,64,256]{2,1,0:T(8,128)S(1)} %get-tuple-element.21), channel_id=1, source_target_pairs={{0,64},{64,0},{128,192},{192,128},{256,320},{320,256},{384,448},{4... | collective-permute-start | bytes 786440 | tf_op jit(solution)/shard_map/ppermute | solution.py:358
  204.3 19.4 %collective-permute-start.7 = (f32[104,256]{1,0:T(8,128)S(1)}, f32[104,256]{1,0:T(8,128)S(1)}, u32[]{:S(2)}, u32[]{:S(2)}) collective-permute-start(f32[104,256]{1,0:T(8,128)S(1)} %reduce_sum.9.after_ref.kept_ref), channel_id=1, source_target_pairs={{0,4},{4,0},{1,5},{5,1},{2,6},{6,2},{3,7},{7,3},{8,12},{12,8},{9,1... | collective-permute-start | bytes 319496 | tf_op jit(solution)/shard_map/ppermute | solution.py:358
  211.2 18.0 %collective-permute-start.6 = (f32[2,64,256]{2,1,0:T(8,128)S(1)}, f32[2,64,256]{2,1,0:T(8,128)S(1)}, u32[]{:S(2)}, u32[]{:S(2)}) collective-permute-start(f32[2,64,256]{2,1,0:T(8,128)S(1)} %get-tuple-element.24), channel_id=1, source_target_pairs={{0,128},{64,192},{128,0},{192,64},{256,384},{320,448},{384,256},{4... | collective-permute-start | bytes 393224 | tf_op jit(solution)/shard_map/ppermute | solution.py:358
  224.4 15.7 %all-to-all-start.13 = ((f32[4,96,256]{2,1,0:T(8,128)}), f32[4,96,256]{2,1,0:T(8,128)S(1)}, u32[]{:S(2)}, u32[]{:S(2)}) async-start(f32[4,96,256]{2,1,0:T(8,128)} %get-tuple-element.23), calls=%async_computation.13 | async-start | bytes 786432 | tf_op jit(solution)/shard_map/all_to_all | solution.py:22
  229.3 10.2 %collective-permute-start.8 = (f32[64,256]{1,0:T(8,128)S(1)}, f32[64,256]{1,0:T(8,128)S(1)}, u32[]{:S(2)}, u32[]{:S(2)}) collective-permute-start(f32[64,256]{1,0:T(8,128)S(1)} %slice_bitcast_fusion), channel_id=1, source_target_pairs={{0,256},{64,320},{128,384},{192,448},{256,0},{320,64},{384,128},{4... | collective-permute-start | bytes 196616 | tf_op jit(solution)/shard_map/ppermute | solution.py:358

commit v8 on v7

--- a/solution.py
+++ b/solution.py
@@ -176,6 +176,11 @@
     out_ref[...] = jnp.broadcast_to(jnp.sum(parts_ref[...], axis=0, keepdims=True), out_ref.shape)
 
 
+def gather_kernel(parts_ref, after_ref, out_ref):
+    del after_ref
+    out_ref[...] = jnp.sum(parts_ref[...], axis=0)
+
+
 def inverse_kernel(factor, parts_ref, *refs):
     out_ref = refs[-1]
     out_ref[...] = jnp.broadcast_to(factor / jnp.sum(parts_ref[...], axis=0, keepdims=True), out_ref.shape)
@@ -194,8 +199,7 @@
     mass_ref[...] = total[group:]
 
 
-def turn_kernel(where_ref, own_one_ref, one_ref, more_one_ref, own_two_ref, two_ref, more_two_ref, after_ref, *refs):
-    del after_ref
+def turn_kernel(where_ref, own_one_ref, one_ref, more_one_ref, own_two_ref, two_ref, more_two_ref, *refs):
     send_ref, keep_ref, turned_ref = refs
     upper = own_one_ref[0] + one_ref[0] + more_one_ref[...]
     lower = own_two_ref[0] + two_ref[0] + more_two_ref[...]
@@ -208,8 +212,10 @@
 
 
 def final_kernel(
-    parts_ref, columns_ref, codes_ref, tile_ref, out_ref, held_ref, tiles_ref, numer_ref, sems
+    parts_ref, columns_ref, codes_ref, tile_ref, more_one_ref, more_two_ref,
+    out_ref, held_ref, tiles_ref, numer_ref, sems,
 ):
+    del more_one_ref, more_two_ref
     steps = [
         [(tile_ref.at[b], tiles_ref.at[b]), (codes_ref.at[:, place(b)], held_ref.at[b])] for b in range(BLOCKS)
     ]
@@ -378,20 +384,19 @@
         if last:
             kept = targets_kept(parts, swap(sent, "c", C, 1), sums)
         after = (kept[0],) if last else ()
-        mine = small(inverse, "inverse", BLOCKS, 1, exchange(sums, "z"), *after)
+        mine = small(inverse, "inverse", BLOCKS, 2_000_000 if last else 1, exchange(sums, "z"), *after)
         col_scale = exchange(mine, ("c", "x"))
         if not last:
             part = rows(col_scale)
 
     one, two, own_one, own_two = kept
     one, two = swap(one, "x", X, 1), swap(two, "x", X, 3)
-    more_one = swap(own_one[1] + one[1], "x", X, 3)
-    more_two = swap(own_two[1] + two[1], "x", X, 1)
+    more_one, more_two = own_one[1] + one[1], own_two[1] + two[1]
 
     group = token_count // Y
     packed = pl.pallas_call(
         final_kernel,
-        in_specs=[vmem, vmem, hbm, hbm],
+        in_specs=[vmem, vmem, hbm, hbm, anywhere, anywhere],
         out_specs=vmem,
         out_shape=f32(Y, group + PAD, width),
         scratch_shapes=[
@@ -403,18 +408,27 @@
         compiler_params=params(FETCHES),
         cost_estimate=cost(12 * size * width, 4 * size),
         name="final",
-    )(parts, col_scale, codes, far)
-    packed = jnp.sum(exchange(packed, "y"), axis=0)
+    )(parts, col_scale, codes, far, more_one, more_two)
+    more_one, more_two = swap(more_one, "x", X, 3), swap(more_two, "x", X, 1)
     away, near = pl.pallas_call(
         turn_kernel,
-        in_specs=[smem] + [vmem] * 6 + [anywhere],
+        in_specs=[smem] + [vmem] * 6,
         out_specs=[vmem] * 2,
         out_shape=[f32(Z // 2, share, width)] * 2,
         scratch_shapes=[pltpu.VMEM((block, width), jnp.float32)],
         compiler_params=params(16 << 20),
         cost_estimate=cost(3 * block * width, 12 * block * width),
         name="turn",
-    )(where, own_one, one, more_one, own_two, two, more_two, packed)
+    )(where, own_one, one, more_one, own_two, two, more_two)
+    packed = pl.pallas_call(
+        gather_kernel,
+        in_specs=[vmem, anywhere],
+        out_specs=vmem,
+        out_shape=f32(group + PAD, width),
+        compiler_params=params(),
+        cost_estimate=cost(packed.size, 4 * packed.size),
+        name="gathered",
+    )(exchange(packed, "y"), away)
     near = near + swap(away, "z", Z, 1)
     numer, mass = pl.pallas_call(
         join_kernel,

time: 243 us -> 237 us (0.975)
  starting transfers between devices: 58 us -> 54.3 us
    all_to_all x5, waiting for transfers between devices: 3.69 us -> 0.32 us  [exchange(): return lax.all_to_all(blocks, axes, 0, 0, tiled=True)]
    pallas_call x2 -> x3, Pallas kernels: 5.7 us -> 6.16 us  [the longest x1 4.95 us: per_device(): pl.pallas_call(final_kernel, in_specs=[vmem, vmem, hbm, hbm, anywhere, an...]
  transfers between devices with their start and end apart: 14 -> 14, of which waited for: 9 -> 6; matrix products, arithmetic and copies ran while one was open for 1% -> 1% of each run, Pallas kernels for 7% -> 7%
where the time goes in v8:
time: 237 us; the launch traced here: 236 us
  blocking collectives  126 us (53%)
  starting transfers between devices  54.3 us (23%)
  Pallas kernels  26.6 us (11%)
  waiting for transfers between devices  21.9 us (9%)
  local copies, waits for them, and re-layouts  4.04 us (2%)
  other arithmetic  2.43 us (1%)
    all_to_all x9, blocking collectives, exchange(): return lax.all_to_all(blocks, axes, 0, 0, tiled=True)  126 us
    ppermute x9, starting transfers between devices, swap(): return lax.ppermute(value, axis, [(i, i ^ bits) for i in range(count)])  34.1 us
    ppermute x9, waiting for transfers between devices, swap(): return lax.ppermute(value, axis, [(i, i ^ bits) for i in range(count)])  21.6 us
    all_to_all x5, starting transfers between devices, exchange(): return lax.all_to_all(blocks, axes, 0, 0, tiled=True)  20.2 us
    pallas_call x1, Pallas kernels, per_device(): pl.pallas_call(final_kernel, in_specs=[vmem, vmem, hbm, hbm, anywhere, an...  4.95 us
    pallas_call x1, Pallas kernels, per_device(): pl.pallas_call(setup_kernel, in_specs=[smem, hbm, hbm], out_specs=[vmem,...  4.88 us
  transfers between devices with their start and end apart: 14, of which 6 were waited for; matrix products, arithmetic and copies ran while one was open for 1% of the time, Pallas kernels for 7%

profile of v8, /device:TPU:24, one launch (start us, length us, event | category | flops | bytes accessed | tf_op | source)
XLA Modules:
  0.0 235.8 jit_solution(10264905137132401246)
XLA Ops:
  0.7 0.9 copy-done.3
  1.7 1.6 copy-done.5
  3.2 4.9 %setup.1 = (f32[8,384,512]{2,1,0:T(8,128)S(1)}, f32[8,1,384]{2,1,0:T(1,128)S(1)}, f32[8,384,512]{2,1,0:T(8,128)S(1)}) custom-call(s32[5]{0:T(128)S(1)} %stack.23.where_ref, bf16[384,256]{1,0:T(8,128)(2,1)S(1)} %copy-done.3, bf16[8,8,64,256]{3,2,1,0:T(8,128)(2,1)S(1)} %bitcast.27), custom_call_target="tpu_custom_call" | custom-call | flops 805306368 | bytes 6291456 | tf_op jit(solution)/shard_map/setup/pallas_call | solution.py:282
  8.1 30.6 %all_to_all.70.parts_ref = f32[8,1,384]{2,1,0:T(1,128)S(1)} all-to-all(f32[8,1,384]{2,1,0:T(1,128)S(1)} %get-tuple-element.13), channel_id=1, replica_groups=mesh['z'=8,'x'=4,'c'=2,'h'=2,'y'=4] {'h','y'}, dimensions={0} | all-to-all | bytes 24576 | tf_op jit(solution)/shard_map/all_to_all | solution.py:22
  38.7 0.8 columns.3
  39.6 9.4 %all_to_all.71.parts_ref = f32[8,1,512]{2,1,0:T(1,128)S(1)} all-to-all(f32[8,1,512]{2,1,0:T(1,128)S(1)} %columns.3), channel_id=1, replica_groups=mesh['z'=8,'x'=4,'c'=2,'h'=2,'y'=4] {'c','x'}, dimensions={0} | all-to-all | bytes 32768 | tf_op jit(solution)/shard_map/all_to_all | solution.py:22
  49.0 15.3 %all_to_all.72.parts_ref = f32[8,1,512]{2,1,0:T(1,128)S(1)} all-to-all(f32[8,1,512]{2,1,0:T(1,128)S(1)} %sums.3), channel_id=1, replica_groups=mesh['z'=8,'x'=4,'c'=2,'h'=2,'y'=4] {'z'}, dimensions={0} | all-to-all | bytes 32768 | tf_op jit(solution)/shard_map/all_to_all | solution.py:22
  64.3 7.6 %all_to_all.73.columns_ref = f32[8,1,512]{2,1,0:T(1,128)S(1)} all-to-all(f32[8,1,512]{2,1,0:T(1,128)S(1)} %inverse.3), channel_id=1, replica_groups=mesh['z'=8,'x'=4,'c'=2,'h'=2,'y'=4] {'c','x'}, dimensions={0} | all-to-all | bytes 32768 | tf_op jit(solution)/shard_map/all_to_all | solution.py:22
  72.0 0.8 rows.2
  72.7 17.3 %all_to_all.74.parts_ref = f32[8,1,384]{2,1,0:T(1,128)S(1)} all-to-all(f32[8,1,384]{2,1,0:T(1,128)S(1)} %rows.2), channel_id=1, replica_groups=mesh['z'=8,'x'=4,'c'=2,'h'=2,'y'=4] {'h','y'}, dimensions={0} | all-to-all | bytes 24576 | tf_op jit(solution)/shard_map/all_to_all | solution.py:22
  90.0 0.8 columns.4
  90.8 7.6 %all_to_all.75.parts_ref = f32[8,1,512]{2,1,0:T(1,128)S(1)} all-to-all(f32[8,1,512]{2,1,0:T(1,128)S(1)} %columns.4), channel_id=1, replica_groups=mesh['z'=8,'x'=4,'c'=2,'h'=2,'y'=4] {'c','x'}, dimensions={0} | all-to-all | bytes 32768 | tf_op jit(solution)/shard_map/all_to_all | solution.py:22
  98.5 12.9 %all_to_all.76.parts_ref = f32[8,1,512]{2,1,0:T(1,128)S(1)} all-to-all(f32[8,1,512]{2,1,0:T(1,128)S(1)} %sums.4), channel_id=1, replica_groups=mesh['z'=8,'x'=4,'c'=2,'h'=2,'y'=4] {'z'}, dimensions={0} | all-to-all | bytes 32768 | tf_op jit(solution)/shard_map/all_to_all | solution.py:22
  111.4 7.6 %all_to_all.77.columns_ref = f32[8,1,512]{2,1,0:T(1,128)S(1)} all-to-all(f32[8,1,512]{2,1,0:T(1,128)S(1)} %inverse.4), channel_id=1, replica_groups=mesh['z'=8,'x'=4,'c'=2,'h'=2,'y'=4] {'c','x'}, dimensions={0} | all-to-all | bytes 32768 | tf_op jit(solution)/shard_map/all_to_all | solution.py:22
  119.1 0.8 rows.3
  119.8 17.3 %all_to_all.78.parts_ref = f32[8,1,384]{2,1,0:T(1,128)S(1)} all-to-all(f32[8,1,384]{2,1,0:T(1,128)S(1)} %rows.3), channel_id=1, replica_groups=mesh['z'=8,'x'=4,'c'=2,'h'=2,'y'=4] {'h','y'}, dimensions={0} | all-to-all | bytes 24576 | tf_op jit(solution)/shard_map/all_to_all | solution.py:22
  137.1 1.4 columns.5.after_ref
  138.5 3.3 %all-to-all-start.9 = ((f32[8,1,512]{2,1,0:T(1,128)}), f32[8,1,512]{2,1,0:T(1,128)S(1)}, u32[]{:S(2)}, u32[]{:S(2)}) async-start(f32[8,1,512]{2,1,0:T(1,128)} %columns.5.after_ref), calls=%async_computation.9 | async-start | bytes 32768 | tf_op jit(solution)/shard_map/all_to_all | solution.py:22
  141.9 4.3 %targets_sent.1 = f32[4,256,512]{2,1,0:T(8,128)} custom-call(s32[5]{0:T(128)S(1)} %stack.23.where_ref, f32[8,1,384]{2,1,0:T(1,128)S(1)} %all_to_all.78.parts_ref, bf16[384,256]{1,0:T(8,128)(2,1)S(1)} %copy-done.4, f32[8,384,512]{2,1,0:T(8,128)} %copy-done, f32[8,1,512]{2,1,0:T(1,128)} %columns.5.after_ref), custom_call_target="tpu_custom_call" | custom-call | flops 402653184 | bytes 6291456 | tf_op jit(solution)/shard_map/targets_sent/pallas_call | solution.py:324
  146.2 2.3 collective-permute-start
  148.6 0.6 sums.5.after_ref
  149.2 3.3 %all-to-all-start.10 = ((f32[8,1,512]{2,1,0:T(1,128)}), f32[8,1,512]{2,1,0:T(1,128)S(1)}, u32[]{:S(2)}, u32[]{:S(2)}) async-start(f32[8,1,512]{2,1,0:T(1,128)} %sums.5.after_ref), calls=%async_computation.10 | async-start | bytes 32768 | tf_op jit(solution)/shard_map/all_to_all | solution.py:22
  152.6 1.4 copy-done.6
  154.0 4.5 %targets_kept.1 = (f32[2,128,512]{2,1,0:T(8,128)}, f32[2,128,512]{2,1,0:T(8,128)}, f32[2,128,512]{2,1,0:T(8,128)}, f32[2,128,512]{2,1,0:T(8,128)}) custom-call(s32[5]{0:T(128)S(1)} %stack.23.where_ref, f32[8,1,384]{2,1,0:T(1,128)S(1)} %all_to_all.78.parts_ref, bf16[384,256]{1,0:T(8,128)(2,1)S(1)} %copy-done.4, f32[8,384,512]{2,1,0:T(8,128)} %copy-done, ...), custom_call_target="tpu_custom_call" | custom-call | flops 402653184 | bytes 6291456 | tf_op jit(solution)/shard_map/targets_kept/pallas_call | solution.py:336
  158.4 5.0 %collective-permute-start.3 = (f32[2,128,512]{2,1,0:T(8,128)}, f32[2,128,512]{2,1,0:T(8,128)S(1)}, u32[]{:S(2)}, u32[]{:S(2)}) collective-permute-start(f32[2,128,512]{2,1,0:T(8,128)} %get-tuple-element.19), channel_id=1, source_target_pairs={{0,48},{16,32},{32,16},{48,0},{1,49},{17,33},{33,17},{49,1},{2,50}... | collective-permute-start | bytes 1572872 | tf_op jit(solution)/shard_map/ppermute | solution.py:364
  163.4 2.3 collective-permute-start.1
  165.7 0.6 inverse.5
  166.4 3.3 %all-to-all-start.11 = ((f32[8,1,512]{2,1,0:T(1,128)}), f32[8,1,512]{2,1,0:T(1,128)S(1)}, u32[]{:S(2)}, u32[]{:S(2)}) async-start(f32[8,1,512]{2,1,0:T(1,128)} %inverse.5), calls=%async_computation.11 | async-start | bytes 32768 | tf_op jit(solution)/shard_map/all_to_all | solution.py:22
  169.7 6.2 %collective-permute-done.3.two_ref = f32[2,128,512]{2,1,0:T(8,128)S(1)} collective-permute-done((f32[2,128,512]{2,1,0:T(8,128)}, f32[2,128,512]{2,1,0:T(8,128)S(1)}, u32[]{:S(2)}, u32[]{:S(2)}) %collective-permute-start.3) | collective-permute-done | bytes 524320 | tf_op jit(solution)/shard_map/ppermute | solution.py:364
  176.0 2.3 collective-permute-start.4
  178.4 1.1 collective-permute-done.1.one_ref
  179.5 3.3 %collective-permute-start.2 = (f32[128,512]{1,0:T(8,128)S(1)}, f32[128,512]{1,0:T(8,128)}, u32[]{:S(2)}, u32[]{:S(2)}) collective-permute-start(f32[128,512]{1,0:T(8,128)S(1)} %fusion.1.more_one_ref), channel_id=1, source_target_pairs={{0,48},{16,32},{32,16},{48,0},{1,49},{17,33},{33,17},{49,1},{2,50}... | collective-permute-start | bytes 786440 | tf_op jit(solution)/shard_map/ppermute | solution.py:364
  182.8 4.9 %final.1 = f32[4,104,256]{2,1,0:T(8,128)} custom-call(f32[8,1,384]{2,1,0:T(1,128)S(1)} %all_to_all.78.parts_ref, f32[8,1,512]{2,1,0:T(1,128)S(1)} %all-to-all-done.11.columns_ref, bf16[8,8,64,256]{3,2,1,0:T(8,128)(2,1)} %bitcast.26, f32[8,384,512]{2,1,0:T(8,128)} %copy-done, f32[128,512]{1,0:T(8,128)S(1)} %fusion.1.more_one_ref, f32[128,512]{1,0:T(8,128)S(1)} %fusion.more_two_ref), custom_call_target="tpu_custom_call" | custom-call | flops 4831838208 | bytes 6291456 | tf_op jit(solution)/shard_map/final/pallas_call | solution.py:397
  187.8 5.5 %all-to-all-start.12 = ((f32[4,104,256]{2,1,0:T(8,128)}), f32[4,104,256]{2,1,0:T(8,128)S(1)}, u32[]{:S(2)}, u32[]{:S(2)}) async-start(f32[4,104,256]{2,1,0:T(8,128)} %final.1), calls=%async_computation.12 | async-start | bytes 851968 | tf_op jit(solution)/shard_map/all_to_all | solution.py:22
  193.3 1.2 turn.1
  194.5 3.5 %collective-permute-start.5 = (f32[4,64,256]{2,1,0:T(8,128)S(1)}, f32[4,64,256]{2,1,0:T(8,128)S(1)}, u32[]{:S(2)}, u32[]{:S(2)}) collective-permute-start(f32[4,64,256]{2,1,0:T(8,128)S(1)} %get-tuple-element.21.after_ref), channel_id=1, source_target_pairs={{0,64},{64,0},{128,192},{192,128},{256,320},{320,256},{384,448},{4... | collective-permute-start | bytes 786440 | tf_op jit(solution)/shard_map/ppermute | solution.py:364
  198.0 0.7 multiply_bitcast_fusion
  198.8 0.3 all-to-all-done.12.parts_ref
  199.1 2.5 %collective-permute-start.7 = (f32[104,256]{1,0:T(8,128)S(1)}, f32[104,256]{1,0:T(8,128)S(1)}, u32[]{:S(2)}, u32[]{:S(2)}) collective-permute-start(f32[104,256]{1,0:T(8,128)S(1)} %gathered.1.kept_ref), channel_id=1, source_target_pairs={{0,4},{4,0},{1,5},{5,1},{2,6},{6,2},{3,7},{7,3},{8,12},{12,8},{9,1... | collective-permute-start | bytes 319496 | tf_op jit(solution)/shard_map/ppermute | solution.py:364
  201.6 4.0 %collective-permute-done.5 = f32[4,64,256]{2,1,0:T(8,128)S(1)} collective-permute-done((f32[4,64,256]{2,1,0:T(8,128)S(1)}, f32[4,64,256]{2,1,0:T(8,128)S(1)}, u32[]{:S(2)}, u32[]{:S(2)}) %collective-permute-start.5) | collective-permute-done | bytes 262176 | tf_op jit(solution)/shard_map/ppermute | solution.py:364
  205.7 4.5 %collective-permute-start.6 = (f32[2,64,256]{2,1,0:T(8,128)S(1)}, f32[2,64,256]{2,1,0:T(8,128)S(1)}, u32[]{:S(2)}, u32[]{:S(2)}) collective-permute-start(f32[2,64,256]{2,1,0:T(8,128)S(1)} %get-tuple-element.24), channel_id=1, source_target_pairs={{0,128},{64,192},{128,0},{192,64},{256,384},{320,448},{384,256},{4... | collective-permute-start | bytes 393224 | tf_op jit(solution)/shard_map/ppermute | solution.py:364
  210.2 8.0 %collective-permute-done.7.came_ref = f32[104,256]{1,0:T(8,128)S(1)} collective-permute-done((f32[104,256]{1,0:T(8,128)S(1)}, f32[104,256]{1,0:T(8,128)S(1)}, u32[]{:S(2)}, u32[]{:S(2)}) %collective-permute-start.7) | collective-permute-done | bytes 106528 | tf_op jit(solution)/shard_map/ppermute | solution.py:364
  218.2 0.8 join.1
  219.0 4.7 %all-to-all-start.13 = ((f32[4,96,256]{2,1,0:T(8,128)}), f32[4,96,256]{2,1,0:T(8,128)S(1)}, u32[]{:S(2)}, u32[]{:S(2)}) async-start(f32[4,96,256]{2,1,0:T(8,128)} %get-tuple-element.23), calls=%async_computation.13 | async-start | bytes 786432 | tf_op jit(solution)/shard_map/all_to_all | solution.py:22
  223.7 8.3 %collective-permute-start.8 = (f32[64,256]{1,0:T(8,128)S(1)}, f32[64,256]{1,0:T(8,128)S(1)}, u32[]{:S(2)}, u32[]{:S(2)}) collective-permute-start(f32[64,256]{1,0:T(8,128)S(1)} %slice_bitcast_fusion), channel_id=1, source_target_pairs={{0,256},{64,320},{128,384},{192,448},{256,0},{320,64},{384,128},{4... | collective-permute-start | bytes 196616 | tf_op jit(solution)/shard_map/ppermute | solution.py:364
  232.0 2.2 collective-permute-done.8
  234.3 0.7 fusion.3
  235.0 0.9 bitcast_divide_fusion
  (33 shorter events, 0.4 us)
Async XLA Ops:
  0.7 0.9 copy-start.3
  1.7 1.6 copy-start.5
  8.1 31.4 %copy-start = (f32[8,384,512]{2,1,0:T(8,128)}, f32[8,384,512]{2,1,0:T(8,128)S(1)}, u32[]{:S(2)}) copy-start(f32[8,384,512]{2,1,0:T(8,128)S(1)} %get-tuple-element.15.tile_ref) | copy-start | bytes 18874372
  137.1 4.8 %copy-start.4 = (bf16[384,256]{1,0:T(8,128)(2,1)S(1)}, bf16[384,256]{1,0:T(8,128)(2,1)}, u32[]{:S(2)}) copy-start(bf16[384,256]{1,0:T(8,128)(2,1)} %latents_ref.5) | copy-start | bytes 589828
  138.5 10.0 %all-to-all-start.9 = ((f32[8,1,512]{2,1,0:T(1,128)}), f32[8,1,512]{2,1,0:T(1,128)S(1)}, u32[]{:S(2)}, u32[]{:S(2)}) async-start(f32[8,1,512]{2,1,0:T(1,128)} %columns.5.after_ref), calls=%async_computation.9 | async-start | bytes 32768 | tf_op jit(solution)/shard_map/all_to_all | solution.py:22
  146.2 6.3 %collective-permute-start = (f32[4,256,512]{2,1,0:T(8,128)}, f32[4,256,512]{2,1,0:T(8,128)S(1)}, u32[]{:S(2)}, u32[]{:S(2)}) collective-permute-start(f32[4,256,512]{2,1,0:T(8,128)} %targets_sent.1), channel_id=1, source_target_pairs={{0,8},{8,0},{1,9},{9,1},{2,10},{10,2},{3,11},{11,3},{4,12},{12,4},... | collective-permute-start | bytes 6291464 | tf_op jit(solution)/shard_map/ppermute | solution.py:364
  149.2 16.5 %all-to-all-start.10 = ((f32[8,1,512]{2,1,0:T(1,128)}), f32[8,1,512]{2,1,0:T(1,128)S(1)}, u32[]{:S(2)}, u32[]{:S(2)}) async-start(f32[8,1,512]{2,1,0:T(1,128)} %sums.5.after_ref), calls=%async_computation.10 | async-start | bytes 32768 | tf_op jit(solution)/shard_map/all_to_all | solution.py:22
  152.6 1.4 copy-start.6
  158.4 17.5 %collective-permute-start.3 = (f32[2,128,512]{2,1,0:T(8,128)}, f32[2,128,512]{2,1,0:T(8,128)S(1)}, u32[]{:S(2)}, u32[]{:S(2)}) collective-permute-start(f32[2,128,512]{2,1,0:T(8,128)} %get-tuple-element.19), channel_id=1, source_target_pairs={{0,48},{16,32},{32,16},{48,0},{1,49},{17,33},{33,17},{49,1},{2,50}... | collective-permute-start | bytes 1572872 | tf_op jit(solution)/shard_map/ppermute | solution.py:364
  163.4 12.6 %copy-start.2 = (f32[2,128,512]{2,1,0:T(8,128)S(1)}, f32[2,128,512]{2,1,0:T(8,128)}, u32[]{:S(2)}) copy-start(f32[2,128,512]{2,1,0:T(8,128)} %get-tuple-element.18.own_two_ref) | copy-start | bytes 1572868
  163.4 16.0 %copy-start.1 = (f32[2,128,512]{2,1,0:T(8,128)S(1)}, f32[2,128,512]{2,1,0:T(8,128)}, u32[]{:S(2)}) copy-start(f32[2,128,512]{2,1,0:T(8,128)} %get-tuple-element.16.own_one_ref) | copy-start | bytes 1572868
  163.4 16.0 %collective-permute-start.1 = (f32[2,128,512]{2,1,0:T(8,128)}, f32[2,128,512]{2,1,0:T(8,128)S(1)}, u32[]{:S(2)}, u32[]{:S(2)}) collective-permute-start(f32[2,128,512]{2,1,0:T(8,128)} %get-tuple-element.17.refs_0_), channel_id=1, source_target_pairs={{0,16},{16,0},{32,48},{48,32},{1,17},{17,1},{33,49},{49,33},{2,18}... | collective-permute-start | bytes 1572872 | tf_op jit(solution)/shard_map/ppermute | solution.py:364
  166.4 16.4 %all-to-all-start.11 = ((f32[8,1,512]{2,1,0:T(1,128)}), f32[8,1,512]{2,1,0:T(1,128)S(1)}, u32[]{:S(2)}, u32[]{:S(2)}) async-start(f32[8,1,512]{2,1,0:T(1,128)} %inverse.5), calls=%async_computation.11 | async-start | bytes 32768 | tf_op jit(solution)/shard_map/all_to_all | solution.py:22
  176.0 17.3 %collective-permute-start.4 = (f32[128,512]{1,0:T(8,128)S(1)}, f32[128,512]{1,0:T(8,128)S(1)}, u32[]{:S(2)}, u32[]{:S(2)}) collective-permute-start(f32[128,512]{1,0:T(8,128)S(1)} %fusion.more_two_ref), channel_id=1, source_target_pairs={{0,16},{16,0},{32,48},{48,32},{1,17},{17,1},{33,49},{49,33},{2,18}... | collective-permute-start | bytes 786440 | tf_op jit(solution)/shard_map/ppermute | solution.py:364
  179.5 13.8 %collective-permute-start.2 = (f32[128,512]{1,0:T(8,128)S(1)}, f32[128,512]{1,0:T(8,128)}, u32[]{:S(2)}, u32[]{:S(2)}) collective-permute-start(f32[128,512]{1,0:T(8,128)S(1)} %fusion.1.more_one_ref), channel_id=1, source_target_pairs={{0,48},{16,32},{32,16},{48,0},{1,49},{17,33},{33,17},{49,1},{2,50}... | collective-permute-start | bytes 786440 | tf_op jit(solution)/shard_map/ppermute | solution.py:364
  187.8 11.3 %all-to-all-start.12 = ((f32[4,104,256]{2,1,0:T(8,128)}), f32[4,104,256]{2,1,0:T(8,128)S(1)}, u32[]{:S(2)}, u32[]{:S(2)}) async-start(f32[4,104,256]{2,1,0:T(8,128)} %final.1), calls=%async_computation.12 | async-start | bytes 851968 | tf_op jit(solution)/shard_map/all_to_all | solution.py:22
  194.5 11.1 %collective-permute-start.5 = (f32[4,64,256]{2,1,0:T(8,128)S(1)}, f32[4,64,256]{2,1,0:T(8,128)S(1)}, u32[]{:S(2)}, u32[]{:S(2)}) collective-permute-start(f32[4,64,256]{2,1,0:T(8,128)S(1)} %get-tuple-element.21.after_ref), channel_id=1, source_target_pairs={{0,64},{64,0},{128,192},{192,128},{256,320},{320,256},{384,448},{4... | collective-permute-start | bytes 786440 | tf_op jit(solution)/shard_map/ppermute | solution.py:364
  199.1 19.1 %collective-permute-start.7 = (f32[104,256]{1,0:T(8,128)S(1)}, f32[104,256]{1,0:T(8,128)S(1)}, u32[]{:S(2)}, u32[]{:S(2)}) collective-permute-start(f32[104,256]{1,0:T(8,128)S(1)} %gathered.1.kept_ref), channel_id=1, source_target_pairs={{0,4},{4,0},{1,5},{5,1},{2,6},{6,2},{3,7},{7,3},{8,12},{12,8},{9,1... | collective-permute-start | bytes 319496 | tf_op jit(solution)/shard_map/ppermute | solution.py:364
  205.7 18.0 %collective-permute-start.6 = (f32[2,64,256]{2,1,0:T(8,128)S(1)}, f32[2,64,256]{2,1,0:T(8,128)S(1)}, u32[]{:S(2)}, u32[]{:S(2)}) collective-permute-start(f32[2,64,256]{2,1,0:T(8,128)S(1)} %get-tuple-element.24), channel_id=1, source_target_pairs={{0,128},{64,192},{128,0},{192,64},{256,384},{320,448},{384,256},{4... | collective-permute-start | bytes 393224 | tf_op jit(solution)/shard_map/ppermute | solution.py:364
  219.0 16.0 %all-to-all-start.13 = ((f32[4,96,256]{2,1,0:T(8,128)}), f32[4,96,256]{2,1,0:T(8,128)S(1)}, u32[]{:S(2)}, u32[]{:S(2)}) async-start(f32[4,96,256]{2,1,0:T(8,128)} %get-tuple-element.23), calls=%async_computation.13 | async-start | bytes 786432 | tf_op jit(solution)/shard_map/all_to_all | solution.py:22
  223.7 10.6 %collective-permute-start.8 = (f32[64,256]{1,0:T(8,128)S(1)}, f32[64,256]{1,0:T(8,128)S(1)}, u32[]{:S(2)}, u32[]{:S(2)}) collective-permute-start(f32[64,256]{1,0:T(8,128)S(1)} %slice_bitcast_fusion), channel_id=1, source_target_pairs={{0,256},{64,320},{128,384},{192,448},{256,0},{320,64},{384,128},{4... | collective-permute-start | bytes 196616 | tf_op jit(solution)/shard_map/ppermute | solution.py:364

commit v9 on v8

--- a/solution.py
+++ b/solution.py
@@ -24,6 +24,7 @@
 
 FETCHES = 55_500_000
 FETCHES_BESIDE_TILE = 40_000_000
+FETCHES_BESIDE_SUMS = 53_000_000
 
 
 def params(limit=8 << 20):
@@ -139,19 +140,30 @@
     return lax.dot_general(latents, weighted, (((0,), (0,)), ((), ())), preferred_element_type=jnp.float32)
 
 
-def targets_sent_kernel(where_ref, parts_ref, latents_ref, tile_ref, after_ref, out_ref, tiles_ref, sems):
+def leave(pieces, sems, first):
+    copies = [pltpu.make_async_copy(*piece, sems.at[first + i]) for i, piece in enumerate(pieces)]
+    for copy in copies:
+        copy.start()
+    return copies
+
+
+def targets_sent_kernel(where_ref, parts_ref, latents_ref, tile_ref, after_ref, out_ref, tiles_ref, done_ref, sems):
     del after_ref
     wait = fetch([[(tile_ref.at[where_ref[3] * X + (where_ref[1] ^ s)], tiles_ref.at[s])] for s in range(X)], sems)
     scale = row_scale_of(parts_ref)
     latents = latents_ref[...]
+    copies = []
     for s in range(X):
         wait(s)
-        out_ref[s] = targets_part(tiles_ref[s], scale, latents)
+        done_ref[s] = targets_part(tiles_ref[s], scale, latents)
+        copies += leave([(done_ref.at[s], out_ref.at[s])], sems, X + s)
+    for copy in copies:
+        copy.wait()
 
 
 def targets_kept_kernel(
     where_ref, parts_ref, latents_ref, tile_ref, added_ref, after_ref,
-    one_ref, two_ref, own_one_ref, own_two_ref, tiles_ref, more_ref, sems,
+    one_ref, two_ref, own_one_ref, own_two_ref, tiles_ref, more_ref, done_ref, sems,
 ):
     del after_ref
     steps = [
@@ -161,14 +173,17 @@
     wait = fetch(steps, sems)
     scale = row_scale_of(parts_ref)
     latents = latents_ref[...]
+    half = latents.shape[1] // 2
+    uppers = (own_one_ref.at[0], one_ref.at[0], one_ref.at[1], own_one_ref.at[1])
+    lowers = (own_two_ref.at[0], own_two_ref.at[1], two_ref.at[1], two_ref.at[0])
+    copies = []
     for s in range(X):
         wait(s)
-        summed = targets_part(tiles_ref[s], scale, latents) + more_ref[s]
-        upper, lower = jnp.split(summed, 2, axis=0)
-        ref, index = ((own_one_ref, 0), (one_ref, 0), (one_ref, 1), (own_one_ref, 1))[s]
-        ref[index] = upper
-        ref, index = ((own_two_ref, 0), (own_two_ref, 1), (two_ref, 1), (two_ref, 0))[s]
-        ref[index] = lower
+        done_ref[s] = targets_part(tiles_ref[s], scale, latents) + more_ref[s]
+        pieces = [(done_ref.at[s, :half], uppers[s]), (done_ref.at[s, half:], lowers[s])]
+        copies += leave(pieces, sems, 2 * X + 2 * s)
+    for copy in copies:
+        copy.wait()
 
 
 def sum_kernel(parts_ref, *refs):
@@ -184,11 +199,6 @@
 def inverse_kernel(factor, parts_ref, *refs):
     out_ref = refs[-1]
     out_ref[...] = jnp.broadcast_to(factor / jnp.sum(parts_ref[...], axis=0, keepdims=True), out_ref.shape)
-
-
-def add_kernel(kept_ref, came_ref, after_ref, out_ref):
-    del after_ref
-    out_ref[...] = kept_ref[...] + came_ref[...]
 
 
 def join_kernel(kept_ref, came_ref, after_ref, spread_ref, mass_ref):
@@ -324,26 +334,31 @@
         return pl.pallas_call(
             targets_sent_kernel,
             in_specs=[smem, vmem, vmem, hbm, anywhere],
-            out_specs=vmem,
+            out_specs=hbm,
             out_shape=f32(X, width, block),
-            scratch_shapes=[tiles((X, token_count, block)), pltpu.SemaphoreType.DMA((X,))],
-            compiler_params=params(FETCHES),
-            cost_estimate=cost(size * width, 4 * size),
-            name="targets_sent",
-        )(where, parts, latents, far, after)
-
-    def targets_kept(parts, added, after):
-        return pl.pallas_call(
-            targets_kept_kernel,
-            in_specs=[smem, vmem, vmem, hbm, hbm, anywhere],
-            out_specs=[vmem] * 4,
-            out_shape=[f32(2, width // 2, block)] * 4,
             scratch_shapes=[
                 tiles((X, token_count, block)),
                 tiles((X, width, block)),
                 pltpu.SemaphoreType.DMA((2 * X,)),
             ],
             compiler_params=params(FETCHES),
+            cost_estimate=cost(size * width, 4 * size),
+            name="targets_sent",
+        )(where, parts, latents, far, after)
+
+    def targets_kept(parts, added, after):
+        return pl.pallas_call(
+            targets_kept_kernel,
+            in_specs=[smem, vmem, vmem, hbm, anywhere, anywhere],
+            out_specs=[hbm] * 4,
+            out_shape=[f32(2, width // 2, block)] * 4,
+            scratch_shapes=[
+                tiles((X, token_count, block)),
+                tiles((X, width, block)),
+                tiles((X, width, block)),
+                pltpu.SemaphoreType.DMA((4 * X,)),
+            ],
+            compiler_params=params(FETCHES_BESIDE_SUMS),
             cost_estimate=cost(size * width, 4 * size),
             name="targets_kept",
         )(where, parts, latents, far, added, after)
@@ -362,17 +377,6 @@
     inverse = functools.partial(inverse_kernel, total_tokens / total_codes)
     def swap(value, axis, count, bits):
         return lax.ppermute(value, axis, [(i, i ^ bits) for i in range(count)])
-
-    def add(kept, came, after):
-        return pl.pallas_call(
-            add_kernel,
-            in_specs=[vmem] * 2 + [anywhere],
-            out_specs=vmem,
-            out_shape=f32(*kept.shape),
-            compiler_params=params(),
-            cost_estimate=cost(kept.size, 12 * kept.size),
-            name="add",
-        )(kept, came, after)
 
     for sweep_index in range(ITERS):
         last = sweep_index == ITERS - 1
@@ -439,7 +443,7 @@
         cost_estimate=cost(20000 * token_count * width, 8 * token_count * width),
         name="join",
     )(packed, swap(packed, "h", H, 1), near)
-    near = add(near[:2], swap(near[2:], "z", Z, 2), mass)
+    near = near[:2] + swap(near[2:], "z", Z, 2)
     summed = near[0] + swap(near[1], "z", Z, 4)
     own = lax.dynamic_slice(mine, (0, 0, where[4]), (1, 1, share)).reshape(share)
     targets = summed * (own * (total_codes / total_tokens))[:, None]

time: 237 us -> 235 us (level)
    ppermute x9, waiting for transfers between devices: 21.6 us -> 18.5 us  [swap(): return lax.ppermute(value, axis, [(i, i ^ bits) for i in range(count)])]
  transfers between devices with their start and end apart: 14 -> 14, of which waited for: 6 -> 7; matrix products, arithmetic and copies ran while one was open for 1% -> 1% of each run, Pallas kernels for 7% -> 7%
where the time goes in v9:
time: 235 us; the launch traced here: 233 us
  blocking collectives  126 us (54%)
  starting transfers between devices  56.4 us (24%)
  Pallas kernels  25.3 us (11%)
  waiting for transfers between devices  19.7 us (8%)
  local copies, waits for them, and re-layouts  2.63 us (1%)
  other arithmetic  2.43 us (1%)
    all_to_all x9, blocking collectives, exchange(): return lax.all_to_all(blocks, axes, 0, 0, tiled=True)  126 us
    ppermute x9, starting transfers between devices, swap(): return lax.ppermute(value, axis, [(i, i ^ bits) for i in range(count)])  35.9 us
    all_to_all x5, starting transfers between devices, exchange(): return lax.all_to_all(blocks, axes, 0, 0, tiled=True)  20.5 us
    ppermute x9, waiting for transfers between devices, swap(): return lax.ppermute(value, axis, [(i, i ^ bits) for i in range(count)])  18.5 us
    pallas_call x1, Pallas kernels, per_device(): pl.pallas_call(final_kernel, in_specs=[vmem, vmem, hbm, hbm, anywhere, an...  4.93 us
    pallas_call x1, Pallas kernels, per_device(): pl.pallas_call(setup_kernel, in_specs=[smem, hbm, hbm], out_specs=[vmem,...  4.88 us
  transfers between devices with their start and end apart: 14, of which 7 were waited for; matrix products, arithmetic and copies ran while one was open for 1% of the time, Pallas kernels for 7%

profile of v9, /device:TPU:24, one launch (start us, length us, event | category | flops | bytes accessed | tf_op | source)
XLA Modules:
  0.0 233.0 jit_solution(14938353114264759319)
XLA Ops:
  0.7 0.9 copy-done.1
  1.7 1.6 copy-done.3
  3.2 4.9 %setup.1 = (f32[8,384,512]{2,1,0:T(8,128)S(1)}, f32[8,1,384]{2,1,0:T(1,128)S(1)}, f32[8,384,512]{2,1,0:T(8,128)S(1)}) custom-call(s32[5]{0:T(128)S(1)} %stack.23.where_ref, bf16[384,256]{1,0:T(8,128)(2,1)S(1)} %copy-done.1, bf16[8,8,64,256]{3,2,1,0:T(8,128)(2,1)S(1)} %bitcast.27), custom_call_target="tpu_custom_call" | custom-call | flops 805306368 | bytes 6291456 | tf_op jit(solution)/shard_map/setup/pallas_call | solution.py:292
  8.1 30.6 %all_to_all.70.parts_ref = f32[8,1,384]{2,1,0:T(1,128)S(1)} all-to-all(f32[8,1,384]{2,1,0:T(1,128)S(1)} %get-tuple-element.13), channel_id=1, replica_groups=mesh['z'=8,'x'=4,'c'=2,'h'=2,'y'=4] {'h','y'}, dimensions={0} | all-to-all | bytes 24576 | tf_op jit(solution)/shard_map/all_to_all | solution.py:22
  38.7 0.8 columns.3
  39.6 9.4 %all_to_all.71.parts_ref = f32[8,1,512]{2,1,0:T(1,128)S(1)} all-to-all(f32[8,1,512]{2,1,0:T(1,128)S(1)} %columns.3), channel_id=1, replica_groups=mesh['z'=8,'x'=4,'c'=2,'h'=2,'y'=4] {'c','x'}, dimensions={0} | all-to-all | bytes 32768 | tf_op jit(solution)/shard_map/all_to_all | solution.py:22
  49.0 15.3 %all_to_all.72.parts_ref = f32[8,1,512]{2,1,0:T(1,128)S(1)} all-to-all(f32[8,1,512]{2,1,0:T(1,128)S(1)} %sums.3), channel_id=1, replica_groups=mesh['z'=8,'x'=4,'c'=2,'h'=2,'y'=4] {'z'}, dimensions={0} | all-to-all | bytes 32768 | tf_op jit(solution)/shard_map/all_to_all | solution.py:22
  64.3 7.6 %all_to_all.73.columns_ref = f32[8,1,512]{2,1,0:T(1,128)S(1)} all-to-all(f32[8,1,512]{2,1,0:T(1,128)S(1)} %inverse.3), channel_id=1, replica_groups=mesh['z'=8,'x'=4,'c'=2,'h'=2,'y'=4] {'c','x'}, dimensions={0} | all-to-all | bytes 32768 | tf_op jit(solution)/shard_map/all_to_all | solution.py:22
  72.0 0.8 rows.2
  72.7 17.3 %all_to_all.74.parts_ref = f32[8,1,384]{2,1,0:T(1,128)S(1)} all-to-all(f32[8,1,384]{2,1,0:T(1,128)S(1)} %rows.2), channel_id=1, replica_groups=mesh['z'=8,'x'=4,'c'=2,'h'=2,'y'=4] {'h','y'}, dimensions={0} | all-to-all | bytes 24576 | tf_op jit(solution)/shard_map/all_to_all | solution.py:22
  90.0 0.8 columns.4
  90.8 7.6 %all_to_all.75.parts_ref = f32[8,1,512]{2,1,0:T(1,128)S(1)} all-to-all(f32[8,1,512]{2,1,0:T(1,128)S(1)} %columns.4), channel_id=1, replica_groups=mesh['z'=8,'x'=4,'c'=2,'h'=2,'y'=4] {'c','x'}, dimensions={0} | all-to-all | bytes 32768 | tf_op jit(solution)/shard_map/all_to_all | solution.py:22
  98.5 12.9 %all_to_all.76.parts_ref = f32[8,1,512]{2,1,0:T(1,128)S(1)} all-to-all(f32[8,1,512]{2,1,0:T(1,128)S(1)} %sums.4), channel_id=1, replica_groups=mesh['z'=8,'x'=4,'c'=2,'h'=2,'y'=4] {'z'}, dimensions={0} | all-to-all | bytes 32768 | tf_op jit(solution)/shard_map/all_to_all | solution.py:22
  111.4 7.6 %all_to_all.77.columns_ref = f32[8,1,512]{2,1,0:T(1,128)S(1)} all-to-all(f32[8,1,512]{2,1,0:T(1,128)S(1)} %inverse.4), channel_id=1, replica_groups=mesh['z'=8,'x'=4,'c'=2,'h'=2,'y'=4] {'c','x'}, dimensions={0} | all-to-all | bytes 32768 | tf_op jit(solution)/shard_map/all_to_all | solution.py:22
  119.0 0.8 rows.3
  119.8 17.3 %all_to_all.78.parts_ref = f32[8,1,384]{2,1,0:T(1,128)S(1)} all-to-all(f32[8,1,384]{2,1,0:T(1,128)S(1)} %rows.3), channel_id=1, replica_groups=mesh['z'=8,'x'=4,'c'=2,'h'=2,'y'=4] {'h','y'}, dimensions={0} | all-to-all | bytes 24576 | tf_op jit(solution)/shard_map/all_to_all | solution.py:22
  137.1 1.4 columns.5.after_ref
  138.5 3.3 %all-to-all-start.9 = ((f32[8,1,512]{2,1,0:T(1,128)}), f32[8,1,512]{2,1,0:T(1,128)S(1)}, u32[]{:S(2)}, u32[]{:S(2)}) async-start(f32[8,1,512]{2,1,0:T(1,128)} %columns.5.after_ref), calls=%async_computation.9 | async-start | bytes 32768 | tf_op jit(solution)/shard_map/all_to_all | solution.py:22
  141.9 3.8 %targets_sent.1 = f32[4,256,512]{2,1,0:T(8,128)} custom-call(s32[5]{0:T(128)S(1)} %stack.23.where_ref, f32[8,1,384]{2,1,0:T(1,128)S(1)} %all_to_all.78.parts_ref, bf16[384,256]{1,0:T(8,128)(2,1)S(1)} %copy-done.2, f32[8,384,512]{2,1,0:T(8,128)} %copy-done, f32[8,1,512]{2,1,0:T(1,128)} %columns.5.after_ref), custom_call_target="tpu_custom_call" | custom-call | flops 402653184 | bytes 6291456 | tf_op jit(solution)/shard_map/targets_sent/pallas_call | solution.py:334
  145.7 2.3 collective-permute-start
  148.0 0.6 sums.5.after_ref
  148.7 3.3 %all-to-all-start.10 = ((f32[8,1,512]{2,1,0:T(1,128)}), f32[8,1,512]{2,1,0:T(1,128)S(1)}, u32[]{:S(2)}, u32[]{:S(2)}) async-start(f32[8,1,512]{2,1,0:T(1,128)} %sums.5.after_ref), calls=%async_computation.10 | async-start | bytes 32768 | tf_op jit(solution)/shard_map/all_to_all | solution.py:22
  152.0 0.1 collective-permute-done.added_ref
  152.1 3.8 %targets_kept.1 = (f32[2,128,512]{2,1,0:T(8,128)}, f32[2,128,512]{2,1,0:T(8,128)S(1)}, f32[2,128,512]{2,1,0:T(8,128)S(1)}, f32[2,128,512]{2,1,0:T(8,128)S(1)}) custom-call(s32[5]{0:T(128)S(1)} %stack.23.where_ref, f32[8,1,384]{2,1,0:T(1,128)S(1)} %all_to_all.78.parts_ref, bf16[384,256]{1,0:T(8,128)(2,1)S(1)} %copy-done.2, f32[8,384,512]{2,1,0:T(8,128)} %copy-done, ...), custom_call_target="tpu_custom_call" | custom-call | flops 402653184 | bytes 6291456 | tf_op jit(solution)/shard_map/targets_kept/pallas_call | solution.py:350
  155.9 5.0 %collective-permute-start.3 = (f32[2,128,512]{2,1,0:T(8,128)S(1)}, f32[2,128,512]{2,1,0:T(8,128)S(1)}, u32[]{:S(2)}, u32[]{:S(2)}) collective-permute-start(f32[2,128,512]{2,1,0:T(8,128)S(1)} %get-tuple-element.19), channel_id=1, source_target_pairs={{0,48},{16,32},{32,16},{48,0},{1,49},{17,33},{33,17},{49,1},{2,50}... | collective-permute-start | bytes 1572872 | tf_op jit(solution)/shard_map/ppermute | solution.py:379
  160.9 2.2 collective-permute-start.1
  163.1 0.6 inverse.5
  163.7 3.8 %all-to-all-start.11 = ((f32[8,1,512]{2,1,0:T(1,128)}), f32[8,1,512]{2,1,0:T(1,128)S(1)}, u32[]{:S(2)}, u32[]{:S(2)}) async-start(f32[8,1,512]{2,1,0:T(1,128)} %inverse.5), calls=%async_computation.11 | async-start | bytes 32768 | tf_op jit(solution)/shard_map/all_to_all | solution.py:22
  167.5 5.8 %collective-permute-done.3.two_ref = f32[2,128,512]{2,1,0:T(8,128)S(1)} collective-permute-done((f32[2,128,512]{2,1,0:T(8,128)S(1)}, f32[2,128,512]{2,1,0:T(8,128)S(1)}, u32[]{:S(2)}, u32[]{:S(2)}) %collective-permute-start.3) | collective-permute-done | bytes 524320 | tf_op jit(solution)/shard_map/ppermute | solution.py:379
  173.3 2.4 %collective-permute-start.4 = (f32[128,512]{1,0:T(8,128)S(1)}, f32[128,512]{1,0:T(8,128)S(1)}, u32[]{:S(2)}, u32[]{:S(2)}) collective-permute-start(f32[128,512]{1,0:T(8,128)S(1)} %fusion.more_two_ref), channel_id=1, source_target_pairs={{0,16},{16,0},{32,48},{48,32},{1,17},{17,1},{33,49},{49,33},{2,18}... | collective-permute-start | bytes 786440 | tf_op jit(solution)/shard_map/ppermute | solution.py:379
  175.7 1.2 collective-permute-done.1.one_ref
  176.9 3.2 %collective-permute-start.2 = (f32[128,512]{1,0:T(8,128)S(1)}, f32[128,512]{1,0:T(8,128)}, u32[]{:S(2)}, u32[]{:S(2)}) collective-permute-start(f32[128,512]{1,0:T(8,128)S(1)} %fusion.1.more_one_ref), channel_id=1, source_target_pairs={{0,48},{16,32},{32,16},{48,0},{1,49},{17,33},{33,17},{49,1},{2,50}... | collective-permute-start | bytes 786440 | tf_op jit(solution)/shard_map/ppermute | solution.py:379
  180.1 4.9 %final.1 = f32[4,104,256]{2,1,0:T(8,128)} custom-call(f32[8,1,384]{2,1,0:T(1,128)S(1)} %all_to_all.78.parts_ref, f32[8,1,512]{2,1,0:T(1,128)S(1)} %all-to-all-done.11.columns_ref, bf16[8,8,64,256]{3,2,1,0:T(8,128)(2,1)} %bitcast.26, f32[8,384,512]{2,1,0:T(8,128)} %copy-done, f32[128,512]{1,0:T(8,128)S(1)} %fusion.1.more_one_ref, f32[128,512]{1,0:T(8,128)S(1)} %fusion.more_two_ref), custom_call_target="tpu_custom_call" | custom-call | flops 4831838208 | bytes 6291456 | tf_op jit(solution)/shard_map/final/pallas_call | solution.py:401
  185.0 5.5 %all-to-all-start.12 = ((f32[4,104,256]{2,1,0:T(8,128)}), f32[4,104,256]{2,1,0:T(8,128)S(1)}, u32[]{:S(2)}, u32[]{:S(2)}) async-start(f32[4,104,256]{2,1,0:T(8,128)} %final.1), calls=%async_computation.12 | async-start | bytes 851968 | tf_op jit(solution)/shard_map/all_to_all | solution.py:22
  190.6 1.2 turn.1
  191.8 3.4 %collective-permute-start.5 = (f32[4,64,256]{2,1,0:T(8,128)S(1)}, f32[4,64,256]{2,1,0:T(8,128)S(1)}, u32[]{:S(2)}, u32[]{:S(2)}) collective-permute-start(f32[4,64,256]{2,1,0:T(8,128)S(1)} %get-tuple-element.21.after_ref), channel_id=1, source_target_pairs={{0,64},{64,0},{128,192},{192,128},{256,320},{320,256},{384,448},{4... | collective-permute-start | bytes 786440 | tf_op jit(solution)/shard_map/ppermute | solution.py:379
  195.2 1.2 all-to-all-done.12.parts_ref
  196.4 2.5 %collective-permute-start.8 = (f32[104,256]{1,0:T(8,128)S(1)}, f32[104,256]{1,0:T(8,128)S(1)}, u32[]{:S(2)}, u32[]{:S(2)}) collective-permute-start(f32[104,256]{1,0:T(8,128)S(1)} %gathered.1.kept_ref), channel_id=1, source_target_pairs={{0,4},{4,0},{1,5},{5,1},{2,6},{6,2},{3,7},{7,3},{8,12},{12,8},{9,1... | collective-permute-start | bytes 319496 | tf_op jit(solution)/shard_map/ppermute | solution.py:379
  198.9 0.7 multiply_bitcast_fusion
  199.6 3.3 %collective-permute-done.5 = f32[4,64,256]{2,1,0:T(8,128)S(1)} collective-permute-done((f32[4,64,256]{2,1,0:T(8,128)S(1)}, f32[4,64,256]{2,1,0:T(8,128)S(1)}, u32[]{:S(2)}, u32[]{:S(2)}) %collective-permute-start.5) | collective-permute-done | bytes 262176 | tf_op jit(solution)/shard_map/ppermute | solution.py:379
  202.9 4.4 %collective-permute-start.6 = (f32[2,64,256]{2,1,0:T(8,128)S(1)}, f32[2,64,256]{2,1,0:T(8,128)S(1)}, u32[]{:S(2)}, u32[]{:S(2)}) collective-permute-start(f32[2,64,256]{2,1,0:T(8,128)S(1)} %slice.43), channel_id=1, source_target_pairs={{0,128},{64,192},{128,0},{192,64},{256,384},{320,448},{384,256},{4... | collective-permute-start | bytes 393224 | tf_op jit(solution)/shard_map/ppermute | solution.py:379
  207.3 6.0 %collective-permute-done.8.came_ref = f32[104,256]{1,0:T(8,128)S(1)} collective-permute-done((f32[104,256]{1,0:T(8,128)S(1)}, f32[104,256]{1,0:T(8,128)S(1)}, u32[]{:S(2)}, u32[]{:S(2)}) %collective-permute-start.8) | collective-permute-done | bytes 106528 | tf_op jit(solution)/shard_map/ppermute | solution.py:379
  213.3 0.8 join.1
  214.1 4.5 %all-to-all-start.13 = ((f32[4,96,256]{2,1,0:T(8,128)}), f32[4,96,256]{2,1,0:T(8,128)S(1)}, u32[]{:S(2)}, u32[]{:S(2)}) async-start(f32[4,96,256]{2,1,0:T(8,128)} %get-tuple-element.22), calls=%async_computation.13 | async-start | bytes 786432 | tf_op jit(solution)/shard_map/all_to_all | solution.py:22
  218.6 10.6 %collective-permute-start.7 = (f32[64,256]{1,0:T(8,128)S(1)}, f32[64,256]{1,0:T(8,128)S(1)}, u32[]{:S(2)}, u32[]{:S(2)}) collective-permute-start(f32[64,256]{1,0:T(8,128)S(1)} %slice_bitcast_fusion), channel_id=1, source_target_pairs={{0,256},{64,320},{128,384},{192,448},{256,0},{320,64},{384,128},{4... | collective-permute-start | bytes 196616 | tf_op jit(solution)/shard_map/ppermute | solution.py:379
  229.2 2.2 collective-permute-done.7
  231.4 0.7 fusion.3
  232.1 0.9 bitcast_divide_fusion
  (27 shorter events, 0.4 us)
Async XLA Ops:
  0.7 0.9 copy-start.1
  1.7 1.6 copy-start.3
  8.1 31.4 %copy-start = (f32[8,384,512]{2,1,0:T(8,128)}, f32[8,384,512]{2,1,0:T(8,128)S(1)}, u32[]{:S(2)}) copy-start(f32[8,384,512]{2,1,0:T(8,128)S(1)} %get-tuple-element.15.tile_ref) | copy-start | bytes 18874372
  137.1 4.8 %copy-start.2 = (bf16[384,256]{1,0:T(8,128)(2,1)S(1)}, bf16[384,256]{1,0:T(8,128)(2,1)}, u32[]{:S(2)}) copy-start(bf16[384,256]{1,0:T(8,128)(2,1)} %latents_ref.5) | copy-start | bytes 589828
  138.5 9.5 %all-to-all-start.9 = ((f32[8,1,512]{2,1,0:T(1,128)}), f32[8,1,512]{2,1,0:T(1,128)S(1)}, u32[]{:S(2)}, u32[]{:S(2)}) async-start(f32[8,1,512]{2,1,0:T(1,128)} %columns.5.after_ref), calls=%async_computation.9 | async-start | bytes 32768 | tf_op jit(solution)/shard_map/all_to_all | solution.py:22
  145.7 6.4 %collective-permute-start = (f32[4,256,512]{2,1,0:T(8,128)}, f32[4,256,512]{2,1,0:T(8,128)}, u32[]{:S(2)}, u32[]{:S(2)}) collective-permute-start(f32[4,256,512]{2,1,0:T(8,128)} %targets_sent.1), channel_id=1, source_target_pairs={{0,8},{8,0},{1,9},{9,1},{2,10},{10,2},{3,11},{11,3},{4,12},{12,4},... | collective-permute-start | bytes 6291464 | tf_op jit(solution)/shard_map/ppermute | solution.py:379
  148.7 14.4 %all-to-all-start.10 = ((f32[8,1,512]{2,1,0:T(1,128)}), f32[8,1,512]{2,1,0:T(1,128)S(1)}, u32[]{:S(2)}, u32[]{:S(2)}) async-start(f32[8,1,512]{2,1,0:T(1,128)} %sums.5.after_ref), calls=%async_computation.10 | async-start | bytes 32768 | tf_op jit(solution)/shard_map/all_to_all | solution.py:22
  155.9 17.3 %collective-permute-start.3 = (f32[2,128,512]{2,1,0:T(8,128)S(1)}, f32[2,128,512]{2,1,0:T(8,128)S(1)}, u32[]{:S(2)}, u32[]{:S(2)}) collective-permute-start(f32[2,128,512]{2,1,0:T(8,128)S(1)} %get-tuple-element.19), channel_id=1, source_target_pairs={{0,48},{16,32},{32,16},{48,0},{1,49},{17,33},{33,17},{49,1},{2,50}... | collective-permute-start | bytes 1572872 | tf_op jit(solution)/shard_map/ppermute | solution.py:379
  160.9 15.9 %collective-permute-start.1 = (f32[2,128,512]{2,1,0:T(8,128)}, f32[2,128,512]{2,1,0:T(8,128)S(1)}, u32[]{:S(2)}, u32[]{:S(2)}) collective-permute-start(f32[2,128,512]{2,1,0:T(8,128)} %get-tuple-element.17.refs_0_), channel_id=1, source_target_pairs={{0,16},{16,0},{32,48},{48,32},{1,17},{17,1},{33,49},{49,33},{2,18}... | collective-permute-start | bytes 1572872 | tf_op jit(solution)/shard_map/ppermute | solution.py:379
  163.7 16.4 %all-to-all-start.11 = ((f32[8,1,512]{2,1,0:T(1,128)}), f32[8,1,512]{2,1,0:T(1,128)S(1)}, u32[]{:S(2)}, u32[]{:S(2)}) async-start(f32[8,1,512]{2,1,0:T(1,128)} %inverse.5), calls=%async_computation.11 | async-start | bytes 32768 | tf_op jit(solution)/shard_map/all_to_all | solution.py:22
  173.3 17.2 %collective-permute-start.4 = (f32[128,512]{1,0:T(8,128)S(1)}, f32[128,512]{1,0:T(8,128)S(1)}, u32[]{:S(2)}, u32[]{:S(2)}) collective-permute-start(f32[128,512]{1,0:T(8,128)S(1)} %fusion.more_two_ref), channel_id=1, source_target_pairs={{0,16},{16,0},{32,48},{48,32},{1,17},{17,1},{33,49},{49,33},{2,18}... | collective-permute-start | bytes 786440 | tf_op jit(solution)/shard_map/ppermute | solution.py:379
  176.9 13.7 %collective-permute-start.2 = (f32[128,512]{1,0:T(8,128)S(1)}, f32[128,512]{1,0:T(8,128)}, u32[]{:S(2)}, u32[]{:S(2)}) collective-permute-start(f32[128,512]{1,0:T(8,128)S(1)} %fusion.1.more_one_ref), channel_id=1, source_target_pairs={{0,48},{16,32},{32,16},{48,0},{1,49},{17,33},{33,17},{49,1},{2,50}... | collective-permute-start | bytes 786440 | tf_op jit(solution)/shard_map/ppermute | solution.py:379
  185.0 11.3 %all-to-all-start.12 = ((f32[4,104,256]{2,1,0:T(8,128)}), f32[4,104,256]{2,1,0:T(8,128)S(1)}, u32[]{:S(2)}, u32[]{:S(2)}) async-start(f32[4,104,256]{2,1,0:T(8,128)} %final.1), calls=%async_computation.12 | async-start | bytes 851968 | tf_op jit(solution)/shard_map/all_to_all | solution.py:22
  191.8 11.1 %collective-permute-start.5 = (f32[4,64,256]{2,1,0:T(8,128)S(1)}, f32[4,64,256]{2,1,0:T(8,128)S(1)}, u32[]{:S(2)}, u32[]{:S(2)}) collective-permute-start(f32[4,64,256]{2,1,0:T(8,128)S(1)} %get-tuple-element.21.after_ref), channel_id=1, source_target_pairs={{0,64},{64,0},{128,192},{192,128},{256,320},{320,256},{384,448},{4... | collective-permute-start | bytes 786440 | tf_op jit(solution)/shard_map/ppermute | solution.py:379
  196.4 16.9 %collective-permute-start.8 = (f32[104,256]{1,0:T(8,128)S(1)}, f32[104,256]{1,0:T(8,128)S(1)}, u32[]{:S(2)}, u32[]{:S(2)}) collective-permute-start(f32[104,256]{1,0:T(8,128)S(1)} %gathered.1.kept_ref), channel_id=1, source_target_pairs={{0,4},{4,0},{1,5},{5,1},{2,6},{6,2},{3,7},{7,3},{8,12},{12,8},{9,1... | collective-permute-start | bytes 319496 | tf_op jit(solution)/shard_map/ppermute | solution.py:379
  202.9 15.6 %collective-permute-start.6 = (f32[2,64,256]{2,1,0:T(8,128)S(1)}, f32[2,64,256]{2,1,0:T(8,128)S(1)}, u32[]{:S(2)}, u32[]{:S(2)}) collective-permute-start(f32[2,64,256]{2,1,0:T(8,128)S(1)} %slice.43), channel_id=1, source_target_pairs={{0,128},{64,192},{128,0},{192,64},{256,384},{320,448},{384,256},{4... | collective-permute-start | bytes 393224 | tf_op jit(solution)/shard_map/ppermute | solution.py:379
  214.1 18.1 %all-to-all-start.13 = ((f32[4,96,256]{2,1,0:T(8,128)}), f32[4,96,256]{2,1,0:T(8,128)S(1)}, u32[]{:S(2)}, u32[]{:S(2)}) async-start(f32[4,96,256]{2,1,0:T(8,128)} %get-tuple-element.22), calls=%async_computation.13 | async-start | bytes 786432 | tf_op jit(solution)/shard_map/all_to_all | solution.py:22
  218.6 12.8 %collective-permute-start.7 = (f32[64,256]{1,0:T(8,128)S(1)}, f32[64,256]{1,0:T(8,128)S(1)}, u32[]{:S(2)}, u32[]{:S(2)}) collective-permute-start(f32[64,256]{1,0:T(8,128)S(1)} %slice_bitcast_fusion), channel_id=1, source_target_pairs={{0,256},{64,320},{128,384},{192,448},{256,0},{320,64},{384,128},{4... | collective-permute-start | bytes 196616 | tf_op jit(solution)/shard_map/ppermute | solution.py:379

commit v10 on v9

--- a/solution.py
+++ b/solution.py
@@ -23,7 +23,6 @@
 
 
 FETCHES = 55_500_000
-FETCHES_BESIDE_TILE = 40_000_000
 FETCHES_BESIDE_SUMS = 53_000_000
 
 
@@ -78,13 +77,9 @@
     return wait
 
 
-def setup_kernel(where_ref, latents_ref, codes_ref, tile_ref, rows_ref, far_ref, tokens_ref, held_ref, sems):
+def setup_kernel(where_ref, latents_ref, codes_ref, tile_ref, rows_ref):
     del where_ref
-    steps = [[(latents_ref, tokens_ref)]]
-    wait = fetch(steps + [[(codes_ref.at[:, place(b)], held_ref.at[b])] for b in range(BLOCKS)], sems)
-    wait(0)
-    saves = []
-    latents = tokens_ref[...]
+    latents = latents_ref[...]
     width = latents.shape[1]
     floats = latents.astype(jnp.float32)
     mean = jnp.sum(floats * floats, axis=1, keepdims=True) * (1.0 / width)
@@ -92,19 +87,14 @@
     total = jnp.zeros(scale.shape, jnp.float32)
     across = (((1,), (1,)), ((), ()))
     for b in range(BLOCKS):
-        wait(1 + b)
-        codes = held_ref[b].reshape(-1, width)
+        codes = codes_ref[:, place(b)].reshape(-1, width)
         floats = codes.astype(jnp.float32)
         code_norm = lax.rsqrt(row_of(fold(floats * floats)) * (1.0 / width) + EPSILON)
         inner = lax.dot_general(latents, codes, across, preferred_element_type=jnp.float32)
         tile = jnp.exp(inner * widen(scale, codes.shape[0]) * code_norm)
         tile_ref[b] = tile
-        saves.append(pltpu.make_async_copy(tile_ref.at[b], far_ref.at[b], sems.at[BLOCKS + 1 + b]))
-        saves[b].start()
         total += fold(tile)
     rows_ref[...] = jnp.broadcast_to(row_of(total)[None], rows_ref.shape)
-    for save in saves:
-        save.wait()
 
 
 def rows_kernel(columns_ref, tile_ref, rows_ref, total_ref):
@@ -289,17 +279,12 @@
     core, x, z = (lax.axis_index(axis) for axis in ("c", "x", "z"))
     where = jnp.stack([core, x, z, 1 - core, z * share])
 
-    tile, part, far = pl.pallas_call(
+    tile, part = pl.pallas_call(
         setup_kernel,
-        in_specs=[smem, hbm, hbm],
-        out_specs=[vmem, vmem, hbm],
-        out_shape=[f32(BLOCKS, token_count, block), rows_shape, f32(BLOCKS, token_count, block)],
-        scratch_shapes=[
-            pltpu.VMEM((token_count, width), jnp.bfloat16),
-            held,
-            pltpu.SemaphoreType.DMA((2 * BLOCKS + 1,)),
-        ],
-        compiler_params=params(FETCHES_BESIDE_TILE),
+        in_specs=[smem, vmem, vmem],
+        out_specs=[vmem, vmem],
+        out_shape=[f32(BLOCKS, token_count, block), rows_shape],
+        compiler_params=params(40_000_000),
         cost_estimate=cost(2 * size * width, 4 * size, size),
         name="setup",
     )(where, latents, codes)
@@ -344,7 +329,7 @@
             compiler_params=params(FETCHES),
             cost_estimate=cost(size * width, 4 * size),
             name="targets_sent",
-        )(where, parts, latents, far, after)
+        )(where, parts, latents, tile, after)
 
     def targets_kept(parts, added, after):
         return pl.pallas_call(
@@ -361,7 +346,7 @@
             compiler_params=params(FETCHES_BESIDE_SUMS),
             cost_estimate=cost(size * width, 4 * size),
             name="targets_kept",
-        )(where, parts, latents, far, added, after)
+        )(where, parts, latents, tile, added, after)
 
     def small(kernel, name, count, weight, parts, *after):
         return pl.pallas_call(
@@ -412,7 +397,7 @@
         compiler_params=params(FETCHES),
         cost_estimate=cost(12 * size * width, 4 * size),
         name="final",
-    )(parts, col_scale, codes, far, more_one, more_two)
+    )(parts, col_scale, codes, tile, more_one, more_two)
     more_one, more_two = swap(more_one, "x", X, 3), swap(more_two, "x", X, 1)
     away, near = pl.pallas_call(
         turn_kernel,

time: 235 us -> 233 us (level)
  no operation moved by 1% of the time
where the time goes in v10:
time: 233 us; the launch traced here: 231 us
  blocking collectives  126 us (54%)
  starting transfers between devices  56.3 us (24%)
  Pallas kernels  23.2 us (10%)
  waiting for transfers between devices  19.7 us (8%)
  local copies, waits for them, and re-layouts  2.63 us (1%)
  other arithmetic  2.43 us (1%)
    all_to_all x9, blocking collectives, exchange(): return lax.all_to_all(blocks, axes, 0, 0, tiled=True)  126 us
    ppermute x9, starting transfers between devices, swap(): return lax.ppermute(value, axis, [(i, i ^ bits) for i in range(count)])  35.9 us
    all_to_all x5, starting transfers between devices, exchange(): return lax.all_to_all(blocks, axes, 0, 0, tiled=True)  20.5 us
    ppermute x9, waiting for transfers between devices, swap(): return lax.ppermute(value, axis, [(i, i ^ bits) for i in range(count)])  18.5 us
    pallas_call x1, Pallas kernels, per_device(): pl.pallas_call(final_kernel, in_specs=[vmem, vmem, hbm, hbm, anywhere, an...  4.93 us
  transfers between devices with their start and end apart: 14, of which 7 were waited for; matrix products, arithmetic and copies ran while one was open for 1% of the time, Pallas kernels for 7%

profile of v10, /device:TPU:24, one launch (start us, length us, event | category | flops | bytes accessed | tf_op | source)
XLA Modules:
  0.0 230.9 jit_solution(11428075085293565844)
XLA Ops:
  0.7 0.9 copy-done.1
  1.7 1.6 copy-done.3
  3.2 2.8 %setup.1 = (f32[8,384,512]{2,1,0:T(8,128)S(1)}, f32[8,1,384]{2,1,0:T(1,128)S(1)}) custom-call(s32[5]{0:T(128)S(1)} %stack.23.where_ref, bf16[384,256]{1,0:T(8,128)(2,1)S(1)} %copy-done.1, bf16[8,8,64,256]{3,2,1,0:T(8,128)(2,1)S(1)} %bitcast.27), custom_call_target="tpu_custom_call" | custom-call | flops 805306368 | bytes 6291456 | tf_op jit(solution)/shard_map/setup/pallas_call | solution.py:282
  6.0 30.6 %all_to_all.70.parts_ref = f32[8,1,384]{2,1,0:T(1,128)S(1)} all-to-all(f32[8,1,384]{2,1,0:T(1,128)S(1)} %get-tuple-element.12), channel_id=1, replica_groups=mesh['z'=8,'x'=4,'c'=2,'h'=2,'y'=4] {'h','y'}, dimensions={0} | all-to-all | bytes 24576 | tf_op jit(solution)/shard_map/all_to_all | solution.py:22
  36.6 0.8 columns.3
  37.4 9.4 %all_to_all.71.parts_ref = f32[8,1,512]{2,1,0:T(1,128)S(1)} all-to-all(f32[8,1,512]{2,1,0:T(1,128)S(1)} %columns.3), channel_id=1, replica_groups=mesh['z'=8,'x'=4,'c'=2,'h'=2,'y'=4] {'c','x'}, dimensions={0} | all-to-all | bytes 32768 | tf_op jit(solution)/shard_map/all_to_all | solution.py:22
  46.9 15.3 %all_to_all.72.parts_ref = f32[8,1,512]{2,1,0:T(1,128)S(1)} all-to-all(f32[8,1,512]{2,1,0:T(1,128)S(1)} %sums.3), channel_id=1, replica_groups=mesh['z'=8,'x'=4,'c'=2,'h'=2,'y'=4] {'z'}, dimensions={0} | all-to-all | bytes 32768 | tf_op jit(solution)/shard_map/all_to_all | solution.py:22
  62.2 7.6 %all_to_all.73.columns_ref = f32[8,1,512]{2,1,0:T(1,128)S(1)} all-to-all(f32[8,1,512]{2,1,0:T(1,128)S(1)} %inverse.3), channel_id=1, replica_groups=mesh['z'=8,'x'=4,'c'=2,'h'=2,'y'=4] {'c','x'}, dimensions={0} | all-to-all | bytes 32768 | tf_op jit(solution)/shard_map/all_to_all | solution.py:22
  69.9 0.8 rows.2
  70.6 17.3 %all_to_all.74.parts_ref = f32[8,1,384]{2,1,0:T(1,128)S(1)} all-to-all(f32[8,1,384]{2,1,0:T(1,128)S(1)} %rows.2), channel_id=1, replica_groups=mesh['z'=8,'x'=4,'c'=2,'h'=2,'y'=4] {'h','y'}, dimensions={0} | all-to-all | bytes 24576 | tf_op jit(solution)/shard_map/all_to_all | solution.py:22
  87.9 0.8 columns.4
  88.7 7.6 %all_to_all.75.parts_ref = f32[8,1,512]{2,1,0:T(1,128)S(1)} all-to-all(f32[8,1,512]{2,1,0:T(1,128)S(1)} %columns.4), channel_id=1, replica_groups=mesh['z'=8,'x'=4,'c'=2,'h'=2,'y'=4] {'c','x'}, dimensions={0} | all-to-all | bytes 32768 | tf_op jit(solution)/shard_map/all_to_all | solution.py:22
  96.4 12.9 %all_to_all.76.parts_ref = f32[8,1,512]{2,1,0:T(1,128)S(1)} all-to-all(f32[8,1,512]{2,1,0:T(1,128)S(1)} %sums.4), channel_id=1, replica_groups=mesh['z'=8,'x'=4,'c'=2,'h'=2,'y'=4] {'z'}, dimensions={0} | all-to-all | bytes 32768 | tf_op jit(solution)/shard_map/all_to_all | solution.py:22
  109.3 7.6 %all_to_all.77.columns_ref = f32[8,1,512]{2,1,0:T(1,128)S(1)} all-to-all(f32[8,1,512]{2,1,0:T(1,128)S(1)} %inverse.4), channel_id=1, replica_groups=mesh['z'=8,'x'=4,'c'=2,'h'=2,'y'=4] {'c','x'}, dimensions={0} | all-to-all | bytes 32768 | tf_op jit(solution)/shard_map/all_to_all | solution.py:22
  116.9 0.8 rows.3
  117.7 17.3 %all_to_all.78.parts_ref = f32[8,1,384]{2,1,0:T(1,128)S(1)} all-to-all(f32[8,1,384]{2,1,0:T(1,128)S(1)} %rows.3), channel_id=1, replica_groups=mesh['z'=8,'x'=4,'c'=2,'h'=2,'y'=4] {'h','y'}, dimensions={0} | all-to-all | bytes 24576 | tf_op jit(solution)/shard_map/all_to_all | solution.py:22
  135.0 1.4 columns.5.after_ref
  136.4 3.3 %all-to-all-start.9 = ((f32[8,1,512]{2,1,0:T(1,128)}), f32[8,1,512]{2,1,0:T(1,128)S(1)}, u32[]{:S(2)}, u32[]{:S(2)}) async-start(f32[8,1,512]{2,1,0:T(1,128)} %columns.5.after_ref), calls=%async_computation.9 | async-start | bytes 32768 | tf_op jit(solution)/shard_map/all_to_all | solution.py:22
  139.8 3.8 %targets_sent.1 = f32[4,256,512]{2,1,0:T(8,128)} custom-call(s32[5]{0:T(128)S(1)} %stack.23.where_ref, f32[8,1,384]{2,1,0:T(1,128)S(1)} %all_to_all.78.parts_ref, bf16[384,256]{1,0:T(8,128)(2,1)S(1)} %copy-done.2, f32[8,384,512]{2,1,0:T(8,128)} %copy-done, f32[8,1,512]{2,1,0:T(1,128)} %columns.5.after_ref), custom_call_target="tpu_custom_call" | custom-call | flops 402653184 | bytes 6291456 | tf_op jit(solution)/shard_map/targets_sent/pallas_call | solution.py:319
  143.6 2.3 %collective-permute-start = (f32[4,256,512]{2,1,0:T(8,128)}, f32[4,256,512]{2,1,0:T(8,128)}, u32[]{:S(2)}, u32[]{:S(2)}) collective-permute-start(f32[4,256,512]{2,1,0:T(8,128)} %targets_sent.1), channel_id=1, source_target_pairs={{0,8},{8,0},{1,9},{9,1},{2,10},{10,2},{3,11},{11,3},{4,12},{12,4},... | collective-permute-start | bytes 6291464 | tf_op jit(solution)/shard_map/ppermute | solution.py:364
  145.9 0.6 sums.5.after_ref
  146.6 3.3 %all-to-all-start.10 = ((f32[8,1,512]{2,1,0:T(1,128)}), f32[8,1,512]{2,1,0:T(1,128)S(1)}, u32[]{:S(2)}, u32[]{:S(2)}) async-start(f32[8,1,512]{2,1,0:T(1,128)} %sums.5.after_ref), calls=%async_computation.10 | async-start | bytes 32768 | tf_op jit(solution)/shard_map/all_to_all | solution.py:22
  149.9 0.1 collective-permute-done.added_ref
  150.0 3.8 %targets_kept.1 = (f32[2,128,512]{2,1,0:T(8,128)}, f32[2,128,512]{2,1,0:T(8,128)S(1)}, f32[2,128,512]{2,1,0:T(8,128)S(1)}, f32[2,128,512]{2,1,0:T(8,128)S(1)}) custom-call(s32[5]{0:T(128)S(1)} %stack.23.where_ref, f32[8,1,384]{2,1,0:T(1,128)S(1)} %all_to_all.78.parts_ref, bf16[384,256]{1,0:T(8,128)(2,1)S(1)} %copy-done.2, f32[8,384,512]{2,1,0:T(8,128)} %copy-done, ...), custom_call_target="tpu_custom_call" | custom-call | flops 402653184 | bytes 6291456 | tf_op jit(solution)/shard_map/targets_kept/pallas_call | solution.py:335
  153.8 5.0 %collective-permute-start.3 = (f32[2,128,512]{2,1,0:T(8,128)S(1)}, f32[2,128,512]{2,1,0:T(8,128)S(1)}, u32[]{:S(2)}, u32[]{:S(2)}) collective-permute-start(f32[2,128,512]{2,1,0:T(8,128)S(1)} %get-tuple-element.17), channel_id=1, source_target_pairs={{0,48},{16,32},{32,16},{48,0},{1,49},{17,33},{33,17},{49,1},{2,50}... | collective-permute-start | bytes 1572872 | tf_op jit(solution)/shard_map/ppermute | solution.py:364
  158.8 2.2 collective-permute-start.1
  161.0 0.6 inverse.5
  161.6 3.8 %all-to-all-start.11 = ((f32[8,1,512]{2,1,0:T(1,128)}), f32[8,1,512]{2,1,0:T(1,128)S(1)}, u32[]{:S(2)}, u32[]{:S(2)}) async-start(f32[8,1,512]{2,1,0:T(1,128)} %inverse.5), calls=%async_computation.11 | async-start | bytes 32768 | tf_op jit(solution)/shard_map/all_to_all | solution.py:22
  165.4 5.8 %collective-permute-done.3.two_ref = f32[2,128,512]{2,1,0:T(8,128)S(1)} collective-permute-done((f32[2,128,512]{2,1,0:T(8,128)S(1)}, f32[2,128,512]{2,1,0:T(8,128)S(1)}, u32[]{:S(2)}, u32[]{:S(2)}) %collective-permute-start.3) | collective-permute-done | bytes 524320 | tf_op jit(solution)/shard_map/ppermute | solution.py:364
  171.2 2.4 %collective-permute-start.4 = (f32[128,512]{1,0:T(8,128)S(1)}, f32[128,512]{1,0:T(8,128)S(1)}, u32[]{:S(2)}, u32[]{:S(2)}) collective-permute-start(f32[128,512]{1,0:T(8,128)S(1)} %fusion.more_two_ref), channel_id=1, source_target_pairs={{0,16},{16,0},{32,48},{48,32},{1,17},{17,1},{33,49},{49,33},{2,18}... | collective-permute-start | bytes 786440 | tf_op jit(solution)/shard_map/ppermute | solution.py:364
  173.6 1.2 collective-permute-done.1.one_ref
  174.8 3.2 %collective-permute-start.2 = (f32[128,512]{1,0:T(8,128)S(1)}, f32[128,512]{1,0:T(8,128)}, u32[]{:S(2)}, u32[]{:S(2)}) collective-permute-start(f32[128,512]{1,0:T(8,128)S(1)} %fusion.1.more_one_ref), channel_id=1, source_target_pairs={{0,48},{16,32},{32,16},{48,0},{1,49},{17,33},{33,17},{49,1},{2,50}... | collective-permute-start | bytes 786440 | tf_op jit(solution)/shard_map/ppermute | solution.py:364
  178.0 4.9 %final.1 = f32[4,104,256]{2,1,0:T(8,128)} custom-call(f32[8,1,384]{2,1,0:T(1,128)S(1)} %all_to_all.78.parts_ref, f32[8,1,512]{2,1,0:T(1,128)S(1)} %all-to-all-done.11.columns_ref, bf16[8,8,64,256]{3,2,1,0:T(8,128)(2,1)} %bitcast.26, f32[8,384,512]{2,1,0:T(8,128)} %copy-done, f32[128,512]{1,0:T(8,128)S(1)} %fusion.1.more_one_ref, f32[128,512]{1,0:T(8,128)S(1)} %fusion.more_two_ref), custom_call_target="tpu_custom_call" | custom-call | flops 4831838208 | bytes 6291456 | tf_op jit(solution)/shard_map/final/pallas_call | solution.py:386
  182.9 5.5 %all-to-all-start.12 = ((f32[4,104,256]{2,1,0:T(8,128)}), f32[4,104,256]{2,1,0:T(8,128)S(1)}, u32[]{:S(2)}, u32[]{:S(2)}) async-start(f32[4,104,256]{2,1,0:T(8,128)} %final.1), calls=%async_computation.12 | async-start | bytes 851968 | tf_op jit(solution)/shard_map/all_to_all | solution.py:22
  188.5 1.2 turn.1
  189.7 3.4 %collective-permute-start.5 = (f32[4,64,256]{2,1,0:T(8,128)S(1)}, f32[4,64,256]{2,1,0:T(8,128)S(1)}, u32[]{:S(2)}, u32[]{:S(2)}) collective-permute-start(f32[4,64,256]{2,1,0:T(8,128)S(1)} %get-tuple-element.19.after_ref), channel_id=1, source_target_pairs={{0,64},{64,0},{128,192},{192,128},{256,320},{320,256},{384,448},{4... | collective-permute-start | bytes 786440 | tf_op jit(solution)/shard_map/ppermute | solution.py:364
  193.1 1.2 all-to-all-done.12.parts_ref
  194.3 2.5 %collective-permute-start.8 = (f32[104,256]{1,0:T(8,128)S(1)}, f32[104,256]{1,0:T(8,128)S(1)}, u32[]{:S(2)}, u32[]{:S(2)}) collective-permute-start(f32[104,256]{1,0:T(8,128)S(1)} %gathered.1.kept_ref), channel_id=1, source_target_pairs={{0,4},{4,0},{1,5},{5,1},{2,6},{6,2},{3,7},{7,3},{8,12},{12,8},{9,1... | collective-permute-start | bytes 319496 | tf_op jit(solution)/shard_map/ppermute | solution.py:364
  196.8 0.7 multiply_bitcast_fusion
  197.5 3.3 %collective-permute-done.5 = f32[4,64,256]{2,1,0:T(8,128)S(1)} collective-permute-done((f32[4,64,256]{2,1,0:T(8,128)S(1)}, f32[4,64,256]{2,1,0:T(8,128)S(1)}, u32[]{:S(2)}, u32[]{:S(2)}) %collective-permute-start.5) | collective-permute-done | bytes 262176 | tf_op jit(solution)/shard_map/ppermute | solution.py:364
  200.8 4.4 %collective-permute-start.6 = (f32[2,64,256]{2,1,0:T(8,128)S(1)}, f32[2,64,256]{2,1,0:T(8,128)S(1)}, u32[]{:S(2)}, u32[]{:S(2)}) collective-permute-start(f32[2,64,256]{2,1,0:T(8,128)S(1)} %slice.43), channel_id=1, source_target_pairs={{0,128},{64,192},{128,0},{192,64},{256,384},{320,448},{384,256},{4... | collective-permute-start | bytes 393224 | tf_op jit(solution)/shard_map/ppermute | solution.py:364
  205.2 6.0 %collective-permute-done.8.came_ref = f32[104,256]{1,0:T(8,128)S(1)} collective-permute-done((f32[104,256]{1,0:T(8,128)S(1)}, f32[104,256]{1,0:T(8,128)S(1)}, u32[]{:S(2)}, u32[]{:S(2)}) %collective-permute-start.8) | collective-permute-done | bytes 106528 | tf_op jit(solution)/shard_map/ppermute | solution.py:364
  211.2 0.8 join.1
  212.0 4.5 %all-to-all-start.13 = ((f32[4,96,256]{2,1,0:T(8,128)}), f32[4,96,256]{2,1,0:T(8,128)S(1)}, u32[]{:S(2)}, u32[]{:S(2)}) async-start(f32[4,96,256]{2,1,0:T(8,128)} %get-tuple-element.20), calls=%async_computation.13 | async-start | bytes 786432 | tf_op jit(solution)/shard_map/all_to_all | solution.py:22
  216.5 10.6 %collective-permute-start.7 = (f32[64,256]{1,0:T(8,128)S(1)}, f32[64,256]{1,0:T(8,128)S(1)}, u32[]{:S(2)}, u32[]{:S(2)}) collective-permute-start(f32[64,256]{1,0:T(8,128)S(1)} %slice_bitcast_fusion), channel_id=1, source_target_pairs={{0,256},{64,320},{128,384},{192,448},{256,0},{320,64},{384,128},{4... | collective-permute-start | bytes 196616 | tf_op jit(solution)/shard_map/ppermute | solution.py:364
  227.1 2.2 collective-permute-done.7
  229.3 0.7 fusion.3
  230.0 0.9 bitcast_divide_fusion
  (27 shorter events, 0.4 us)
Async XLA Ops:
  0.7 0.9 copy-start.1
  1.7 1.6 copy-start.3
  6.0 129.0 %copy-start = (f32[8,384,512]{2,1,0:T(8,128)}, f32[8,384,512]{2,1,0:T(8,128)S(1)}, u32[]{:S(2)}) copy-start(f32[8,384,512]{2,1,0:T(8,128)S(1)} %get-tuple-element.13.tile_ref) | copy-start | bytes 18874372
  135.0 4.8 %copy-start.2 = (bf16[384,256]{1,0:T(8,128)(2,1)S(1)}, bf16[384,256]{1,0:T(8,128)(2,1)}, u32[]{:S(2)}) copy-start(bf16[384,256]{1,0:T(8,128)(2,1)} %latents_ref.5) | copy-start | bytes 589828
  136.4 9.5 %all-to-all-start.9 = ((f32[8,1,512]{2,1,0:T(1,128)}), f32[8,1,512]{2,1,0:T(1,128)S(1)}, u32[]{:S(2)}, u32[]{:S(2)}) async-start(f32[8,1,512]{2,1,0:T(1,128)} %columns.5.after_ref), calls=%async_computation.9 | async-start | bytes 32768 | tf_op jit(solution)/shard_map/all_to_all | solution.py:22
  143.6 6.4 %collective-permute-start = (f32[4,256,512]{2,1,0:T(8,128)}, f32[4,256,512]{2,1,0:T(8,128)}, u32[]{:S(2)}, u32[]{:S(2)}) collective-permute-start(f32[4,256,512]{2,1,0:T(8,128)} %targets_sent.1), channel_id=1, source_target_pairs={{0,8},{8,0},{1,9},{9,1},{2,10},{10,2},{3,11},{11,3},{4,12},{12,4},... | collective-permute-start | bytes 6291464 | tf_op jit(solution)/shard_map/ppermute | solution.py:364
  146.6 14.4 %all-to-all-start.10 = ((f32[8,1,512]{2,1,0:T(1,128)}), f32[8,1,512]{2,1,0:T(1,128)S(1)}, u32[]{:S(2)}, u32[]{:S(2)}) async-start(f32[8,1,512]{2,1,0:T(1,128)} %sums.5.after_ref), calls=%async_computation.10 | async-start | bytes 32768 | tf_op jit(solution)/shard_map/all_to_all | solution.py:22
  153.8 17.4 %collective-permute-start.3 = (f32[2,128,512]{2,1,0:T(8,128)S(1)}, f32[2,128,512]{2,1,0:T(8,128)S(1)}, u32[]{:S(2)}, u32[]{:S(2)}) collective-permute-start(f32[2,128,512]{2,1,0:T(8,128)S(1)} %get-tuple-element.17), channel_id=1, source_target_pairs={{0,48},{16,32},{32,16},{48,0},{1,49},{17,33},{33,17},{49,1},{2,50}... | collective-permute-start | bytes 1572872 | tf_op jit(solution)/shard_map/ppermute | solution.py:364
  158.8 15.9 %collective-permute-start.1 = (f32[2,128,512]{2,1,0:T(8,128)}, f32[2,128,512]{2,1,0:T(8,128)S(1)}, u32[]{:S(2)}, u32[]{:S(2)}) collective-permute-start(f32[2,128,512]{2,1,0:T(8,128)} %get-tuple-element.15.refs_0_), channel_id=1, source_target_pairs={{0,16},{16,0},{32,48},{48,32},{1,17},{17,1},{33,49},{49,33},{2,18}... | collective-permute-start | bytes 1572872 | tf_op jit(solution)/shard_map/ppermute | solution.py:364
  161.6 16.4 %all-to-all-start.11 = ((f32[8,1,512]{2,1,0:T(1,128)}), f32[8,1,512]{2,1,0:T(1,128)S(1)}, u32[]{:S(2)}, u32[]{:S(2)}) async-start(f32[8,1,512]{2,1,0:T(1,128)} %inverse.5), calls=%async_computation.11 | async-start | bytes 32768 | tf_op jit(solution)/shard_map/all_to_all | solution.py:22
  171.2 17.2 %collective-permute-start.4 = (f32[128,512]{1,0:T(8,128)S(1)}, f32[128,512]{1,0:T(8,128)S(1)}, u32[]{:S(2)}, u32[]{:S(2)}) collective-permute-start(f32[128,512]{1,0:T(8,128)S(1)} %fusion.more_two_ref), channel_id=1, source_target_pairs={{0,16},{16,0},{32,48},{48,32},{1,17},{17,1},{33,49},{49,33},{2,18}... | collective-permute-start | bytes 786440 | tf_op jit(solution)/shard_map/ppermute | solution.py:364
  174.8 13.7 %collective-permute-start.2 = (f32[128,512]{1,0:T(8,128)S(1)}, f32[128,512]{1,0:T(8,128)}, u32[]{:S(2)}, u32[]{:S(2)}) collective-permute-start(f32[128,512]{1,0:T(8,128)S(1)} %fusion.1.more_one_ref), channel_id=1, source_target_pairs={{0,48},{16,32},{32,16},{48,0},{1,49},{17,33},{33,17},{49,1},{2,50}... | collective-permute-start | bytes 786440 | tf_op jit(solution)/shard_map/ppermute | solution.py:364
  182.9 11.3 %all-to-all-start.12 = ((f32[4,104,256]{2,1,0:T(8,128)}), f32[4,104,256]{2,1,0:T(8,128)S(1)}, u32[]{:S(2)}, u32[]{:S(2)}) async-start(f32[4,104,256]{2,1,0:T(8,128)} %final.1), calls=%async_computation.12 | async-start | bytes 851968 | tf_op jit(solution)/shard_map/all_to_all | solution.py:22
  189.7 11.1 %collective-permute-start.5 = (f32[4,64,256]{2,1,0:T(8,128)S(1)}, f32[4,64,256]{2,1,0:T(8,128)S(1)}, u32[]{:S(2)}, u32[]{:S(2)}) collective-permute-start(f32[4,64,256]{2,1,0:T(8,128)S(1)} %get-tuple-element.19.after_ref), channel_id=1, source_target_pairs={{0,64},{64,0},{128,192},{192,128},{256,320},{320,256},{384,448},{4... | collective-permute-start | bytes 786440 | tf_op jit(solution)/shard_map/ppermute | solution.py:364
  194.3 16.9 %collective-permute-start.8 = (f32[104,256]{1,0:T(8,128)S(1)}, f32[104,256]{1,0:T(8,128)S(1)}, u32[]{:S(2)}, u32[]{:S(2)}) collective-permute-start(f32[104,256]{1,0:T(8,128)S(1)} %gathered.1.kept_ref), channel_id=1, source_target_pairs={{0,4},{4,0},{1,5},{5,1},{2,6},{6,2},{3,7},{7,3},{8,12},{12,8},{9,1... | collective-permute-start | bytes 319496 | tf_op jit(solution)/shard_map/ppermute | solution.py:364
  200.8 15.7 %collective-permute-start.6 = (f32[2,64,256]{2,1,0:T(8,128)S(1)}, f32[2,64,256]{2,1,0:T(8,128)S(1)}, u32[]{:S(2)}, u32[]{:S(2)}) collective-permute-start(f32[2,64,256]{2,1,0:T(8,128)S(1)} %slice.43), channel_id=1, source_target_pairs={{0,128},{64,192},{128,0},{192,64},{256,384},{320,448},{384,256},{4... | collective-permute-start | bytes 393224 | tf_op jit(solution)/shard_map/ppermute | solution.py:364
  212.0 18.0 %all-to-all-start.13 = ((f32[4,96,256]{2,1,0:T(8,128)}), f32[4,96,256]{2,1,0:T(8,128)S(1)}, u32[]{:S(2)}, u32[]{:S(2)}) async-start(f32[4,96,256]{2,1,0:T(8,128)} %get-tuple-element.20), calls=%async_computation.13 | async-start | bytes 786432 | tf_op jit(solution)/shard_map/all_to_all | solution.py:22
  216.5 12.8 %collective-permute-start.7 = (f32[64,256]{1,0:T(8,128)S(1)}, f32[64,256]{1,0:T(8,128)S(1)}, u32[]{:S(2)}, u32[]{:S(2)}) collective-permute-start(f32[64,256]{1,0:T(8,128)S(1)} %slice_bitcast_fusion), channel_id=1, source_target_pairs={{0,256},{64,320},{128,384},{192,448},{256,0},{320,64},{384,128},{4... | collective-permute-start | bytes 196616 | tf_op jit(solution)/shard_map/ppermute | solution.py:364

commit v11 on v10

--- a/solution.py
+++ b/solution.py
@@ -153,25 +153,23 @@
 
 def targets_kept_kernel(
     where_ref, parts_ref, latents_ref, tile_ref, added_ref, after_ref,
-    one_ref, two_ref, own_one_ref, own_two_ref, tiles_ref, more_ref, done_ref, sems,
+    own_ref, one_ref, two_ref, three_ref, tiles_ref, more_ref, done_ref, sems,
 ):
     del after_ref
+    slots = (1, 3, 2, 0)
     steps = [
         [(tile_ref.at[where_ref[0] * X + (where_ref[1] ^ s)], tiles_ref.at[s]), (added_ref.at[s], more_ref.at[s])]
-        for s in range(X)
+        for s in slots
     ]
     wait = fetch(steps, sems)
     scale = row_scale_of(parts_ref)
     latents = latents_ref[...]
-    half = latents.shape[1] // 2
-    uppers = (own_one_ref.at[0], one_ref.at[0], one_ref.at[1], own_one_ref.at[1])
-    lowers = (own_two_ref.at[0], own_two_ref.at[1], two_ref.at[1], two_ref.at[0])
+    outs = (own_ref, one_ref, two_ref, three_ref)
     copies = []
-    for s in range(X):
-        wait(s)
+    for step, s in enumerate(slots):
+        wait(step)
         done_ref[s] = targets_part(tiles_ref[s], scale, latents) + more_ref[s]
-        pieces = [(done_ref.at[s, :half], uppers[s]), (done_ref.at[s, half:], lowers[s])]
-        copies += leave(pieces, sems, 2 * X + 2 * s)
+        copies += leave([(done_ref.at[s], outs[s])], sems, 2 * X + s)
     for copy in copies:
         copy.wait()
 
@@ -199,11 +197,12 @@
     mass_ref[...] = total[group:]
 
 
-def turn_kernel(where_ref, own_one_ref, one_ref, more_one_ref, own_two_ref, two_ref, more_two_ref, *refs):
-    send_ref, keep_ref, turned_ref = refs
-    upper = own_one_ref[0] + one_ref[0] + more_one_ref[...]
-    lower = own_two_ref[0] + two_ref[0] + more_two_ref[...]
-    turned_ref[...] = jnp.concatenate([upper, lower], axis=0).T
+def near_kernel(own_ref, one_ref, three_ref, out_ref):
+    out_ref[...] = own_ref[...] + one_ref[...] + three_ref[...]
+
+
+def turn_kernel(where_ref, near_ref, two_ref, send_ref, keep_ref, turned_ref):
+    turned_ref[...] = (near_ref[...] + two_ref[...]).T
     share = send_ref.shape[1]
     for i, slot in enumerate((0, 4, 2, 6)):
         for ref, s in ((keep_ref, slot), (send_ref, slot + 1)):
@@ -212,10 +211,8 @@
 
 
 def final_kernel(
-    parts_ref, columns_ref, codes_ref, tile_ref, more_one_ref, more_two_ref,
-    out_ref, held_ref, tiles_ref, numer_ref, sems,
+    parts_ref, columns_ref, codes_ref, tile_ref, out_ref, held_ref, tiles_ref, numer_ref, sems
 ):
-    del more_one_ref, more_two_ref
     steps = [
         [(tile_ref.at[b], tiles_ref.at[b]), (codes_ref.at[:, place(b)], held_ref.at[b])] for b in range(BLOCKS)
     ]
@@ -336,12 +333,12 @@
             targets_kept_kernel,
             in_specs=[smem, vmem, vmem, hbm, anywhere, anywhere],
             out_specs=[hbm] * 4,
-            out_shape=[f32(2, width // 2, block)] * 4,
+            out_shape=[f32(width, block)] * 4,
             scratch_shapes=[
                 tiles((X, token_count, block)),
                 tiles((X, width, block)),
                 tiles((X, width, block)),
-                pltpu.SemaphoreType.DMA((4 * X,)),
+                pltpu.SemaphoreType.DMA((3 * X,)),
             ],
             compiler_params=params(FETCHES_BESIDE_SUMS),
             cost_estimate=cost(size * width, 4 * size),
@@ -378,14 +375,13 @@
         if not last:
             part = rows(col_scale)
 
-    one, two, own_one, own_two = kept
-    one, two = swap(one, "x", X, 1), swap(two, "x", X, 3)
-    more_one, more_two = own_one[1] + one[1], own_two[1] + two[1]
+    own, *others = kept
+    one, two, three = (swap(other, "x", X, s) for s, other in enumerate(others, 1))
 
     group = token_count // Y
     packed = pl.pallas_call(
         final_kernel,
-        in_specs=[vmem, vmem, hbm, hbm, anywhere, anywhere],
+        in_specs=[vmem, vmem, hbm, hbm],
         out_specs=vmem,
         out_shape=f32(Y, group + PAD, width),
         scratch_shapes=[
@@ -397,18 +393,26 @@
         compiler_params=params(FETCHES),
         cost_estimate=cost(12 * size * width, 4 * size),
         name="final",
-    )(parts, col_scale, codes, tile, more_one, more_two)
-    more_one, more_two = swap(more_one, "x", X, 3), swap(more_two, "x", X, 1)
+    )(parts, col_scale, codes, tile)
+    chips = pl.pallas_call(
+        near_kernel,
+        in_specs=[vmem] * 3,
+        out_specs=vmem,
+        out_shape=f32(width, block),
+        compiler_params=params(),
+        cost_estimate=cost(80_000 * width * block, 12 * width * block),
+        name="chips",
+    )(own, one, three)
     away, near = pl.pallas_call(
         turn_kernel,
-        in_specs=[smem] + [vmem] * 6,
+        in_specs=[smem] + [vmem] * 2,
         out_specs=[vmem] * 2,
         out_shape=[f32(Z // 2, share, width)] * 2,
         scratch_shapes=[pltpu.VMEM((block, width), jnp.float32)],
         compiler_params=params(16 << 20),
         cost_estimate=cost(3 * block * width, 12 * block * width),
         name="turn",
-    )(where, own_one, one, more_one, own_two, two, more_two)
+    )(where, chips, two)
     packed = pl.pallas_call(
         gather_kernel,
         in_specs=[vmem, anywhere],
@@ -430,8 +434,8 @@
     )(packed, swap(packed, "h", H, 1), near)
     near = near[:2] + swap(near[2:], "z", Z, 2)
     summed = near[0] + swap(near[1], "z", Z, 4)
-    own = lax.dynamic_slice(mine, (0, 0, where[4]), (1, 1, share)).reshape(share)
-    targets = summed * (own * (total_codes / total_tokens))[:, None]
+    scale = lax.dynamic_slice(mine, (0, 0, where[4]), (1, 1, share)).reshape(share)
+    targets = summed * (scale * (total_codes / total_tokens))[:, None]
     mass = mass[:2].reshape(2 * width)[:token_count]
     rebuilt = exchange(numer, "y").reshape(token_count, width) / mass[:, None]
     return (targets, rebuilt)

time: 233 us -> 243 us (1.043)
  waiting for transfers between devices: 19.7 us -> 26 us
  starting transfers between devices: 56.3 us -> 58.8 us
    all_to_all x5, waiting for transfers between devices: 1.19 us -> 16.3 us  [exchange(): return lax.all_to_all(blocks, axes, 0, 0, tiled=True)]
    ppermute x9 -> x8, waiting for transfers between devices: 18.5 us -> 9.68 us  [swap(): return lax.ppermute(value, axis, [(i, i ^ bits) for i in range(count)])]
    ppermute x9 -> x8, starting transfers between devices: 35.9 us -> 38.4 us  [swap(): return lax.ppermute(value, axis, [(i, i ^ bits) for i in range(count)])]
    pallas_call x2 -> x3, Pallas kernels: 6.12 us -> 6.83 us  [the longest x1 4.93 us: per_device(): pl.pallas_call(final_kernel, in_specs=[vmem, vmem, hbm, hbm], out_specs=v...]
  transfers between devices with their start and end apart: 14 -> 13, of which waited for: 7 -> 6; matrix products, arithmetic and copies ran while one was open for 1% -> 1% of each run, Pallas kernels for 7% -> 7%
where the time goes in v11:
time: 243 us; the launch traced here: 240 us
  blocking collectives  126 us (52%)
  starting transfers between devices  58.8 us (24%)
  waiting for transfers between devices  26 us (11%)
  Pallas kernels  23.6 us (10%)
  local copies, waits for them, and re-layouts  2.63 us (1%)
    all_to_all x9, blocking collectives, exchange(): return lax.all_to_all(blocks, axes, 0, 0, tiled=True)  126 us
    ppermute x8, starting transfers between devices, swap(): return lax.ppermute(value, axis, [(i, i ^ bits) for i in range(count)])  38.4 us
    all_to_all x5, starting transfers between devices, exchange(): return lax.all_to_all(blocks, axes, 0, 0, tiled=True)  20.5 us
    all_to_all x5, waiting for transfers between devices, exchange(): return lax.all_to_all(blocks, axes, 0, 0, tiled=True)  16.3 us
    ppermute x8, waiting for transfers between devices, swap(): return lax.ppermute(value, axis, [(i, i ^ bits) for i in range(count)])  9.68 us
    pallas_call x1, Pallas kernels, per_device(): pl.pallas_call(final_kernel, in_specs=[vmem, vmem, hbm, hbm], out_specs=v...  4.93 us
  transfers between devices with their start and end apart: 13, of which 6 were waited for; matrix products, arithmetic and copies ran while one was open for 1% of the time, Pallas kernels for 7%

profile of v11, /device:TPU:24, one launch (start us, length us, event | category | flops | bytes accessed | tf_op | source)
XLA Modules:
  0.0 240.0 jit_solution(13706440939426644432)
XLA Ops:
  0.6 0.1 stack.23.where_ref
  0.7 0.9 copy-done.1
  1.7 1.6 copy-done.3
  3.2 2.8 %setup.1 = (f32[8,384,512]{2,1,0:T(8,128)S(1)}, f32[8,1,384]{2,1,0:T(1,128)S(1)}) custom-call(s32[5]{0:T(128)S(1)} %stack.23.where_ref, bf16[384,256]{1,0:T(8,128)(2,1)S(1)} %copy-done.1, bf16[8,8,64,256]{3,2,1,0:T(8,128)(2,1)S(1)} %bitcast.23), custom_call_target="tpu_custom_call" | custom-call | flops 805306368 | bytes 6291456 | tf_op jit(solution)/shard_map/setup/pallas_call | solution.py:279
  6.0 30.6 %all_to_all.70.parts_ref = f32[8,1,384]{2,1,0:T(1,128)S(1)} all-to-all(f32[8,1,384]{2,1,0:T(1,128)S(1)} %get-tuple-element.12), channel_id=1, replica_groups=mesh['z'=8,'x'=4,'c'=2,'h'=2,'y'=4] {'h','y'}, dimensions={0} | all-to-all | bytes 24576 | tf_op jit(solution)/shard_map/all_to_all | solution.py:22
  36.6 0.8 columns.3
  37.4 9.4 %all_to_all.71.parts_ref = f32[8,1,512]{2,1,0:T(1,128)S(1)} all-to-all(f32[8,1,512]{2,1,0:T(1,128)S(1)} %columns.3), channel_id=1, replica_groups=mesh['z'=8,'x'=4,'c'=2,'h'=2,'y'=4] {'c','x'}, dimensions={0} | all-to-all | bytes 32768 | tf_op jit(solution)/shard_map/all_to_all | solution.py:22
  46.9 15.3 %all_to_all.72.parts_ref = f32[8,1,512]{2,1,0:T(1,128)S(1)} all-to-all(f32[8,1,512]{2,1,0:T(1,128)S(1)} %sums.3), channel_id=1, replica_groups=mesh['z'=8,'x'=4,'c'=2,'h'=2,'y'=4] {'z'}, dimensions={0} | all-to-all | bytes 32768 | tf_op jit(solution)/shard_map/all_to_all | solution.py:22
  62.2 7.6 %all_to_all.73.columns_ref = f32[8,1,512]{2,1,0:T(1,128)S(1)} all-to-all(f32[8,1,512]{2,1,0:T(1,128)S(1)} %inverse.3), channel_id=1, replica_groups=mesh['z'=8,'x'=4,'c'=2,'h'=2,'y'=4] {'c','x'}, dimensions={0} | all-to-all | bytes 32768 | tf_op jit(solution)/shard_map/all_to_all | solution.py:22
  69.9 0.8 rows.2
  70.6 17.3 %all_to_all.74.parts_ref = f32[8,1,384]{2,1,0:T(1,128)S(1)} all-to-all(f32[8,1,384]{2,1,0:T(1,128)S(1)} %rows.2), channel_id=1, replica_groups=mesh['z'=8,'x'=4,'c'=2,'h'=2,'y'=4] {'h','y'}, dimensions={0} | all-to-all | bytes 24576 | tf_op jit(solution)/shard_map/all_to_all | solution.py:22
  87.9 0.8 columns.4
  88.7 7.6 %all_to_all.75.parts_ref = f32[8,1,512]{2,1,0:T(1,128)S(1)} all-to-all(f32[8,1,512]{2,1,0:T(1,128)S(1)} %columns.4), channel_id=1, replica_groups=mesh['z'=8,'x'=4,'c'=2,'h'=2,'y'=4] {'c','x'}, dimensions={0} | all-to-all | bytes 32768 | tf_op jit(solution)/shard_map/all_to_all | solution.py:22
  96.4 12.9 %all_to_all.76.parts_ref = f32[8,1,512]{2,1,0:T(1,128)S(1)} all-to-all(f32[8,1,512]{2,1,0:T(1,128)S(1)} %sums.4), channel_id=1, replica_groups=mesh['z'=8,'x'=4,'c'=2,'h'=2,'y'=4] {'z'}, dimensions={0} | all-to-all | bytes 32768 | tf_op jit(solution)/shard_map/all_to_all | solution.py:22
  109.3 7.6 %all_to_all.77.columns_ref = f32[8,1,512]{2,1,0:T(1,128)S(1)} all-to-all(f32[8,1,512]{2,1,0:T(1,128)S(1)} %inverse.4), channel_id=1, replica_groups=mesh['z'=8,'x'=4,'c'=2,'h'=2,'y'=4] {'c','x'}, dimensions={0} | all-to-all | bytes 32768 | tf_op jit(solution)/shard_map/all_to_all | solution.py:22
  116.9 0.8 rows.3
  117.7 17.3 %all_to_all.78.parts_ref = f32[8,1,384]{2,1,0:T(1,128)S(1)} all-to-all(f32[8,1,384]{2,1,0:T(1,128)S(1)} %rows.3), channel_id=1, replica_groups=mesh['z'=8,'x'=4,'c'=2,'h'=2,'y'=4] {'h','y'}, dimensions={0} | all-to-all | bytes 24576 | tf_op jit(solution)/shard_map/all_to_all | solution.py:22
  135.0 1.4 columns.5.after_ref
  136.4 3.3 %all-to-all-start.9 = ((f32[8,1,512]{2,1,0:T(1,128)}), f32[8,1,512]{2,1,0:T(1,128)S(1)}, u32[]{:S(2)}, u32[]{:S(2)}) async-start(f32[8,1,512]{2,1,0:T(1,128)} %columns.5.after_ref), calls=%async_computation.9 | async-start | bytes 32768 | tf_op jit(solution)/shard_map/all_to_all | solution.py:22
  139.8 3.8 %targets_sent.1 = f32[4,256,512]{2,1,0:T(8,128)} custom-call(s32[5]{0:T(128)S(1)} %stack.23.where_ref, f32[8,1,384]{2,1,0:T(1,128)S(1)} %all_to_all.78.parts_ref, bf16[384,256]{1,0:T(8,128)(2,1)S(1)} %copy-done.2, f32[8,384,512]{2,1,0:T(8,128)} %copy-done, f32[8,1,512]{2,1,0:T(1,128)} %columns.5.after_ref), custom_call_target="tpu_custom_call" | custom-call | flops 402653184 | bytes 6291456 | tf_op jit(solution)/shard_map/targets_sent/pallas_call | solution.py:316
  143.6 2.3 collective-permute-start
  145.9 0.6 sums.5.after_ref
  146.5 3.3 %all-to-all-start.10 = ((f32[8,1,512]{2,1,0:T(1,128)}), f32[8,1,512]{2,1,0:T(1,128)S(1)}, u32[]{:S(2)}, u32[]{:S(2)}) async-start(f32[8,1,512]{2,1,0:T(1,128)} %sums.5.after_ref), calls=%async_computation.10 | async-start | bytes 32768 | tf_op jit(solution)/shard_map/all_to_all | solution.py:22
  149.9 0.1 collective-permute-done.added_ref
  150.0 3.5 %targets_kept.1 = (f32[256,512]{1,0:T(8,128)S(1)}, f32[256,512]{1,0:T(8,128)}, f32[256,512]{1,0:T(8,128)S(1)}, f32[256,512]{1,0:T(8,128)S(1)}) custom-call(s32[5]{0:T(128)S(1)} %stack.23.where_ref, f32[8,1,384]{2,1,0:T(1,128)S(1)} %all_to_all.78.parts_ref, bf16[384,256]{1,0:T(8,128)(2,1)S(1)} %copy-done.2, f32[8,384,512]{2,1,0:T(8,128)} %copy-done, ...), custom_call_target="tpu_custom_call" | custom-call | flops 402653184 | bytes 6291456 | tf_op jit(solution)/shard_map/targets_kept/pallas_call | solution.py:332
  153.5 3.8 %collective-permute-start.1 = (f32[256,512]{1,0:T(8,128)}, f32[256,512]{1,0:T(8,128)S(1)}, u32[]{:S(2)}, u32[]{:S(2)}) collective-permute-start(f32[256,512]{1,0:T(8,128)} %get-tuple-element.15), channel_id=1, source_target_pairs={{0,16},{16,0},{32,48},{48,32},{1,17},{17,1},{33,49},{49,33},{2,18}... | collective-permute-start | bytes 1572872 | tf_op jit(solution)/shard_map/ppermute | solution.py:361
  157.3 4.0 %collective-permute-start.2 = (f32[256,512]{1,0:T(8,128)S(1)}, f32[256,512]{1,0:T(8,128)}, u32[]{:S(2)}, u32[]{:S(2)}) collective-permute-start(f32[256,512]{1,0:T(8,128)S(1)} %get-tuple-element.16), channel_id=1, source_target_pairs={{0,48},{16,32},{32,16},{48,0},{1,49},{17,33},{33,17},{49,1},{2,50}... | collective-permute-start | bytes 1572872 | tf_op jit(solution)/shard_map/ppermute | solution.py:361
  161.3 0.6 inverse.5
  161.9 3.5 %all-to-all-start.11 = ((f32[8,1,512]{2,1,0:T(1,128)}), f32[8,1,512]{2,1,0:T(1,128)S(1)}, u32[]{:S(2)}, u32[]{:S(2)}) async-start(f32[8,1,512]{2,1,0:T(1,128)} %inverse.5), calls=%async_computation.11 | async-start | bytes 32768 | tf_op jit(solution)/shard_map/all_to_all | solution.py:22
  165.4 5.4 %collective-permute-start.3 = (f32[256,512]{1,0:T(8,128)S(1)}, f32[256,512]{1,0:T(8,128)S(1)}, u32[]{:S(2)}, u32[]{:S(2)}) collective-permute-start(f32[256,512]{1,0:T(8,128)S(1)} %get-tuple-element.17), channel_id=1, source_target_pairs={{0,32},{16,48},{32,0},{48,16},{1,33},{17,49},{33,1},{49,17},{2,34}... | collective-permute-start | bytes 1572872 | tf_op jit(solution)/shard_map/ppermute | solution.py:361
  170.8 14.7 %all-to-all-done.11.columns_ref = f32[8,1,512]{2,1,0:T(1,128)S(1)} async-done(((f32[8,1,512]{2,1,0:T(1,128)}), f32[8,1,512]{2,1,0:T(1,128)S(1)}, u32[]{:S(2)}, u32[]{:S(2)}) %all-to-all-start.11) | async-done | bytes 16416 | tf_op jit(solution)/shard_map/all_to_all | solution.py:22
  185.6 4.9 %final.1 = f32[4,104,256]{2,1,0:T(8,128)} custom-call(f32[8,1,384]{2,1,0:T(1,128)S(1)} %all_to_all.78.parts_ref, f32[8,1,512]{2,1,0:T(1,128)S(1)} %all-to-all-done.11.columns_ref, bf16[8,8,64,256]{3,2,1,0:T(8,128)(2,1)} %bitcast.22, f32[8,384,512]{2,1,0:T(8,128)} %copy-done), custom_call_target="tpu_custom_call" | custom-call | flops 4831838208 | bytes 6291456 | tf_op jit(solution)/shard_map/final/pallas_call | solution.py:382
  190.5 5.5 %all-to-all-start.12 = ((f32[4,104,256]{2,1,0:T(8,128)}), f32[4,104,256]{2,1,0:T(8,128)S(1)}, u32[]{:S(2)}, u32[]{:S(2)}) async-start(f32[4,104,256]{2,1,0:T(8,128)} %final.1), calls=%async_computation.12 | async-start | bytes 851968 | tf_op jit(solution)/shard_map/all_to_all | solution.py:22
  196.0 1.1 chips.1.near_ref
  197.1 0.8 turn.1
  197.9 3.4 %collective-permute-start.4 = (f32[4,64,256]{2,1,0:T(8,128)S(1)}, f32[4,64,256]{2,1,0:T(8,128)S(1)}, u32[]{:S(2)}, u32[]{:S(2)}) collective-permute-start(f32[4,64,256]{2,1,0:T(8,128)S(1)} %get-tuple-element.19.after_ref), channel_id=1, source_target_pairs={{0,64},{64,0},{128,192},{192,128},{256,320},{320,256},{384,448},{4... | collective-permute-start | bytes 786440 | tf_op jit(solution)/shard_map/ppermute | solution.py:361
  201.3 1.6 all-to-all-done.12.parts_ref
  202.9 2.5 %collective-permute-start.7 = (f32[104,256]{1,0:T(8,128)S(1)}, f32[104,256]{1,0:T(8,128)S(1)}, u32[]{:S(2)}, u32[]{:S(2)}) collective-permute-start(f32[104,256]{1,0:T(8,128)S(1)} %gathered.1.kept_ref), channel_id=1, source_target_pairs={{0,4},{4,0},{1,5},{5,1},{2,6},{6,2},{3,7},{7,3},{8,12},{12,8},{9,1... | collective-permute-start | bytes 319496 | tf_op jit(solution)/shard_map/ppermute | solution.py:361
  205.4 0.7 multiply_bitcast_fusion
  206.2 3.0 %collective-permute-done.4 = f32[4,64,256]{2,1,0:T(8,128)S(1)} collective-permute-done((f32[4,64,256]{2,1,0:T(8,128)S(1)}, f32[4,64,256]{2,1,0:T(8,128)S(1)}, u32[]{:S(2)}, u32[]{:S(2)}) %collective-permute-start.4) | collective-permute-done | bytes 262176 | tf_op jit(solution)/shard_map/ppermute | solution.py:361
  209.2 5.4 %collective-permute-start.5 = (f32[2,64,256]{2,1,0:T(8,128)S(1)}, f32[2,64,256]{2,1,0:T(8,128)S(1)}, u32[]{:S(2)}, u32[]{:S(2)}) collective-permute-start(f32[2,64,256]{2,1,0:T(8,128)S(1)} %slice.25), channel_id=1, source_target_pairs={{0,128},{64,192},{128,0},{192,64},{256,384},{320,448},{384,256},{4... | collective-permute-start | bytes 393224 | tf_op jit(solution)/shard_map/ppermute | solution.py:361
  214.7 4.4 %collective-permute-done.7.came_ref = f32[104,256]{1,0:T(8,128)S(1)} collective-permute-done((f32[104,256]{1,0:T(8,128)S(1)}, f32[104,256]{1,0:T(8,128)S(1)}, u32[]{:S(2)}, u32[]{:S(2)}) %collective-permute-start.7) | collective-permute-done | bytes 106528 | tf_op jit(solution)/shard_map/ppermute | solution.py:361
  219.0 0.8 join.1
  219.8 4.8 %all-to-all-start.13 = ((f32[4,96,256]{2,1,0:T(8,128)}), f32[4,96,256]{2,1,0:T(8,128)S(1)}, u32[]{:S(2)}, u32[]{:S(2)}) async-start(f32[4,96,256]{2,1,0:T(8,128)} %get-tuple-element.20), calls=%async_computation.13 | async-start | bytes 786432 | tf_op jit(solution)/shard_map/all_to_all | solution.py:22
  224.6 11.5 %collective-permute-start.6 = (f32[64,256]{1,0:T(8,128)S(1)}, f32[64,256]{1,0:T(8,128)S(1)}, u32[]{:S(2)}, u32[]{:S(2)}) collective-permute-start(f32[64,256]{1,0:T(8,128)S(1)} %slice_bitcast_fusion), channel_id=1, source_target_pairs={{0,256},{64,320},{128,384},{192,448},{256,0},{320,64},{384,128},{4... | collective-permute-start | bytes 196616 | tf_op jit(solution)/shard_map/ppermute | solution.py:361
  236.2 2.2 collective-permute-done.6
  238.4 0.7 fusion.1
  239.1 0.9 bitcast_divide_fusion
  (24 shorter events, 0.2 us)
Async XLA Ops:
  0.7 0.9 copy-start.1
  1.7 1.6 copy-start.3
  6.0 129.0 %copy-start = (f32[8,384,512]{2,1,0:T(8,128)}, f32[8,384,512]{2,1,0:T(8,128)S(1)}, u32[]{:S(2)}) copy-start(f32[8,384,512]{2,1,0:T(8,128)S(1)} %get-tuple-element.13.tile_ref) | copy-start | bytes 18874372
  135.0 4.8 %copy-start.2 = (bf16[384,256]{1,0:T(8,128)(2,1)S(1)}, bf16[384,256]{1,0:T(8,128)(2,1)}, u32[]{:S(2)}) copy-start(bf16[384,256]{1,0:T(8,128)(2,1)} %latents_ref.5) | copy-start | bytes 589828
  136.4 9.5 %all-to-all-start.9 = ((f32[8,1,512]{2,1,0:T(1,128)}), f32[8,1,512]{2,1,0:T(1,128)S(1)}, u32[]{:S(2)}, u32[]{:S(2)}) async-start(f32[8,1,512]{2,1,0:T(1,128)} %columns.5.after_ref), calls=%async_computation.9 | async-start | bytes 32768 | tf_op jit(solution)/shard_map/all_to_all | solution.py:22
  143.6 6.4 %collective-permute-start = (f32[4,256,512]{2,1,0:T(8,128)}, f32[4,256,512]{2,1,0:T(8,128)}, u32[]{:S(2)}, u32[]{:S(2)}) collective-permute-start(f32[4,256,512]{2,1,0:T(8,128)} %targets_sent.1), channel_id=1, source_target_pairs={{0,8},{8,0},{1,9},{9,1},{2,10},{10,2},{3,11},{11,3},{4,12},{12,4},... | collective-permute-start | bytes 6291464 | tf_op jit(solution)/shard_map/ppermute | solution.py:361
  146.5 14.7 %all-to-all-start.10 = ((f32[8,1,512]{2,1,0:T(1,128)}), f32[8,1,512]{2,1,0:T(1,128)S(1)}, u32[]{:S(2)}, u32[]{:S(2)}) async-start(f32[8,1,512]{2,1,0:T(1,128)} %sums.5.after_ref), calls=%async_computation.10 | async-start | bytes 32768 | tf_op jit(solution)/shard_map/all_to_all | solution.py:22
  153.5 42.5 %collective-permute-start.1 = (f32[256,512]{1,0:T(8,128)}, f32[256,512]{1,0:T(8,128)S(1)}, u32[]{:S(2)}, u32[]{:S(2)}) collective-permute-start(f32[256,512]{1,0:T(8,128)} %get-tuple-element.15), channel_id=1, source_target_pairs={{0,16},{16,0},{32,48},{48,32},{1,17},{17,1},{33,49},{49,33},{2,18}... | collective-permute-start | bytes 1572872 | tf_op jit(solution)/shard_map/ppermute | solution.py:361
  157.3 38.7 %collective-permute-start.2 = (f32[256,512]{1,0:T(8,128)S(1)}, f32[256,512]{1,0:T(8,128)}, u32[]{:S(2)}, u32[]{:S(2)}) collective-permute-start(f32[256,512]{1,0:T(8,128)S(1)} %get-tuple-element.16), channel_id=1, source_target_pairs={{0,48},{16,32},{32,16},{48,0},{1,49},{17,33},{33,17},{49,1},{2,50}... | collective-permute-start | bytes 1572872 | tf_op jit(solution)/shard_map/ppermute | solution.py:361
  161.9 23.6 %all-to-all-start.11 = ((f32[8,1,512]{2,1,0:T(1,128)}), f32[8,1,512]{2,1,0:T(1,128)S(1)}, u32[]{:S(2)}, u32[]{:S(2)}) async-start(f32[8,1,512]{2,1,0:T(1,128)} %inverse.5), calls=%async_computation.11 | async-start | bytes 32768 | tf_op jit(solution)/shard_map/all_to_all | solution.py:22
  165.4 31.7 %collective-permute-start.3 = (f32[256,512]{1,0:T(8,128)S(1)}, f32[256,512]{1,0:T(8,128)S(1)}, u32[]{:S(2)}, u32[]{:S(2)}) collective-permute-start(f32[256,512]{1,0:T(8,128)S(1)} %get-tuple-element.17), channel_id=1, source_target_pairs={{0,32},{16,48},{32,0},{48,16},{1,33},{17,49},{33,1},{49,17},{2,34}... | collective-permute-start | bytes 1572872 | tf_op jit(solution)/shard_map/ppermute | solution.py:361
  190.5 12.4 %all-to-all-start.12 = ((f32[4,104,256]{2,1,0:T(8,128)}), f32[4,104,256]{2,1,0:T(8,128)S(1)}, u32[]{:S(2)}, u32[]{:S(2)}) async-start(f32[4,104,256]{2,1,0:T(8,128)} %final.1), calls=%async_computation.12 | async-start | bytes 851968 | tf_op jit(solution)/shard_map/all_to_all | solution.py:22
  197.9 11.2 %collective-permute-start.4 = (f32[4,64,256]{2,1,0:T(8,128)S(1)}, f32[4,64,256]{2,1,0:T(8,128)S(1)}, u32[]{:S(2)}, u32[]{:S(2)}) collective-permute-start(f32[4,64,256]{2,1,0:T(8,128)S(1)} %get-tuple-element.19.after_ref), channel_id=1, source_target_pairs={{0,64},{64,0},{128,192},{192,128},{256,320},{320,256},{384,448},{4... | collective-permute-start | bytes 786440 | tf_op jit(solution)/shard_map/ppermute | solution.py:361
  202.9 16.1 %collective-permute-start.7 = (f32[104,256]{1,0:T(8,128)S(1)}, f32[104,256]{1,0:T(8,128)S(1)}, u32[]{:S(2)}, u32[]{:S(2)}) collective-permute-start(f32[104,256]{1,0:T(8,128)S(1)} %gathered.1.kept_ref), channel_id=1, source_target_pairs={{0,4},{4,0},{1,5},{5,1},{2,6},{6,2},{3,7},{7,3},{8,12},{12,8},{9,1... | collective-permute-start | bytes 319496 | tf_op jit(solution)/shard_map/ppermute | solution.py:361
  209.2 15.4 %collective-permute-start.5 = (f32[2,64,256]{2,1,0:T(8,128)S(1)}, f32[2,64,256]{2,1,0:T(8,128)S(1)}, u32[]{:S(2)}, u32[]{:S(2)}) collective-permute-start(f32[2,64,256]{2,1,0:T(8,128)S(1)} %slice.25), channel_id=1, source_target_pairs={{0,128},{64,192},{128,0},{192,64},{256,384},{320,448},{384,256},{4... | collective-permute-start | bytes 393224 | tf_op jit(solution)/shard_map/ppermute | solution.py:361
  219.8 19.3 %all-to-all-start.13 = ((f32[4,96,256]{2,1,0:T(8,128)}), f32[4,96,256]{2,1,0:T(8,128)S(1)}, u32[]{:S(2)}, u32[]{:S(2)}) async-start(f32[4,96,256]{2,1,0:T(8,128)} %get-tuple-element.20), calls=%async_computation.13 | async-start | bytes 786432 | tf_op jit(solution)/shard_map/all_to_all | solution.py:22
  224.6 13.8 %collective-permute-start.6 = (f32[64,256]{1,0:T(8,128)S(1)}, f32[64,256]{1,0:T(8,128)S(1)}, u32[]{:S(2)}, u32[]{:S(2)}) collective-permute-start(f32[64,256]{1,0:T(8,128)S(1)} %slice_bitcast_fusion), channel_id=1, source_target_pairs={{0,256},{64,320},{128,384},{192,448},{256,0},{320,64},{384,128},{4... | collective-permute-start | bytes 196616 | tf_op jit(solution)/shard_map/ppermute | solution.py:361

commit v12 on v10

--- a/solution.py
+++ b/solution.py
@@ -97,32 +97,22 @@
     rows_ref[...] = jnp.broadcast_to(row_of(total)[None], rows_ref.shape)
 
 
-def rows_kernel(columns_ref, tile_ref, rows_ref, total_ref):
-    step = pl.program_id(0)
-
-    @pl.when(step == 0)
-    def _():
-        total_ref[...] = jnp.zeros_like(total_ref)
-
-    total_ref[...] += fold(tile_ref[...] * columns_ref[...])
-
-    @pl.when(step == pl.num_programs(0) - 1)
-    def _():
-        rows_ref[...] = jnp.broadcast_to(row_of(total_ref[...])[None], rows_ref.shape)
+def rows_kernel(columns_ref, tile_ref, rows_ref):
+    total = fold(tile_ref[0] * columns_ref[0])
+    for b in range(1, BLOCKS):
+        total += fold(tile_ref[b] * columns_ref[b])
+    rows_ref[...] = jnp.broadcast_to(row_of(total)[None], rows_ref.shape)
 
 
 def row_scale_of(parts_ref):
     return column_of(1.0 / jnp.sum(parts_ref[...], axis=0))
 
 
-def columns_kernel(parts_ref, tile_ref, columns_ref, scale_ref):
-    @pl.when(pl.program_id(0) == 0)
-    def _():
-        scale_ref[...] = row_scale_of(parts_ref)
-
-    tile = tile_ref[...]
-    sums = jnp.sum(tile * widen(scale_ref[...], tile.shape[1]), axis=0, keepdims=True)
-    columns_ref[pl.program_id(0)] = sums
+def columns_kernel(parts_ref, tile_ref, columns_ref):
+    scale = row_scale_of(parts_ref)
+    for b in range(BLOCKS):
+        tile = tile_ref[b]
+        columns_ref[b] = jnp.sum(tile * widen(scale, tile.shape[1]), axis=0, keepdims=True)
 
 
 def targets_part(tile, scale, latents):
@@ -245,10 +235,6 @@
     return jax.ShapeDtypeStruct(shape, jnp.float32)
 
 
-def whole(*shape):
-    return pl.BlockSpec(shape, lambda *_: (0,) * len(shape))
-
-
 def cost(flops, moved, exps=0):
     return pl.CostEstimate(flops=flops, bytes_accessed=moved, transcendentals=exps)
 
@@ -263,14 +249,10 @@
     size = token_count * code_count
 
     codes = codebook.reshape(Z, X * C, share, width)
-    tile_spec = pl.BlockSpec((None, token_count, block), lambda b: (b, 0, 0))
-    rows_spec = whole(H * Y, 1, token_count)
-    columns_spec = pl.BlockSpec((None, 1, block), lambda b: (b, 0, 0))
     vmem = pl.BlockSpec(memory_space=pltpu.VMEM)
     smem = pl.BlockSpec(memory_space=pltpu.SMEM)
     hbm = pl.BlockSpec(memory_space=pltpu.HBM)
     anywhere = pl.BlockSpec(memory_space=pl.ANY)
-    per_token = pltpu.VMEM((token_count, LANES), jnp.float32)
     held = pltpu.VMEM((BLOCKS, Z, share, width), jnp.bfloat16)
     tiles = functools.partial(pltpu.VMEM, dtype=jnp.float32)
     rows_shape = f32(H * Y, 1, token_count)
@@ -289,31 +271,22 @@
         name="setup",
     )(where, latents, codes)
 
-    def rows(columns):
+    def sweep(kernel, name, given, shape):
         return pl.pallas_call(
-            rows_kernel,
-            grid=(BLOCKS,),
-            in_specs=[columns_spec, tile_spec],
-            out_specs=rows_spec,
-            out_shape=rows_shape,
-            scratch_shapes=[per_token],
+            kernel,
+            in_specs=[vmem, vmem],
+            out_specs=vmem,
+            out_shape=shape,
             compiler_params=params(),
             cost_estimate=cost(2 * size, 4 * size),
-            name="rows",
-        )(columns, tile)
+            name=name,
+        )(given, tile)
+
+    def rows(columns):
+        return sweep(rows_kernel, "rows", columns, rows_shape)
 
     def columns(parts):
-        return pl.pallas_call(
-            columns_kernel,
-            grid=(BLOCKS,),
-            in_specs=[rows_spec, tile_spec],
-            out_specs=whole(BLOCKS, 1, block),
-            out_shape=columns_shape,
-            scratch_shapes=[per_token],
-            compiler_params=params(),
-            cost_estimate=cost(2 * size, 4 * size),
-            name="columns",
-        )(parts, tile)
+        return sweep(columns_kernel, "columns", parts, columns_shape)
 
     def targets_sent(parts, after):
         return pl.pallas_call(

time: 233 us -> 232 us (level)
  no operation moved by 1% of the time
where the time goes in v12:
time: 232 us; the launch traced here: 230 us
  blocking collectives  126 us (54%)
  starting transfers between devices  56.3 us (24%)
  Pallas kernels  22.2 us (10%)
  waiting for transfers between devices  19.7 us (8%)
  local copies, waits for them, and re-layouts  2.63 us (1%)
  other arithmetic  2.43 us (1%)
    all_to_all x9, blocking collectives, exchange(): return lax.all_to_all(blocks, axes, 0, 0, tiled=True)  126 us
    ppermute x9, starting transfers between devices, swap(): return lax.ppermute(value, axis, [(i, i ^ bits) for i in range(count)])  35.9 us
    all_to_all x5, starting transfers between devices, exchange(): return lax.all_to_all(blocks, axes, 0, 0, tiled=True)  20.5 us
    ppermute x9, waiting for transfers between devices, swap(): return lax.ppermute(value, axis, [(i, i ^ bits) for i in range(count)])  18.5 us
    pallas_call x1, Pallas kernels, per_device(): pl.pallas_call(final_kernel, in_specs=[vmem, vmem, hbm, hbm, anywhere, an...  4.93 us
  transfers between devices with their start and end apart: 14, of which 7 were waited for; matrix products, arithmetic and copies ran while one was open for 1% of the time, Pallas kernels for 7%

profile of v12, /device:TPU:24, one launch (start us, length us, event | category | flops | bytes accessed | tf_op | source)
XLA Modules:
  0.0 229.8 jit_solution(8448603773930865191)
XLA Ops:
  0.7 0.9 copy-done.1
  1.7 1.6 copy-done.3
  3.2 2.8 %setup.1 = (f32[8,384,512]{2,1,0:T(8,128)S(1)}, f32[8,1,384]{2,1,0:T(1,128)S(1)}) custom-call(s32[5]{0:T(128)S(1)} %stack.23.where_ref, bf16[384,256]{1,0:T(8,128)(2,1)S(1)} %copy-done.1, bf16[8,8,64,256]{3,2,1,0:T(8,128)(2,1)S(1)} %bitcast.27), custom_call_target="tpu_custom_call" | custom-call | flops 805306368 | bytes 6291456 | tf_op jit(solution)/shard_map/setup/pallas_call | solution.py:264
  6.0 30.6 %all_to_all.70.parts_ref = f32[8,1,384]{2,1,0:T(1,128)S(1)} all-to-all(f32[8,1,384]{2,1,0:T(1,128)S(1)} %get-tuple-element.12), channel_id=1, replica_groups=mesh['z'=8,'x'=4,'c'=2,'h'=2,'y'=4] {'h','y'}, dimensions={0} | all-to-all | bytes 24576 | tf_op jit(solution)/shard_map/all_to_all | solution.py:22
  36.6 0.7 columns.3
  37.3 9.4 %all_to_all.71.parts_ref = f32[8,1,512]{2,1,0:T(1,128)S(1)} all-to-all(f32[8,1,512]{2,1,0:T(1,128)S(1)} %columns.3), channel_id=1, replica_groups=mesh['z'=8,'x'=4,'c'=2,'h'=2,'y'=4] {'c','x'}, dimensions={0} | all-to-all | bytes 32768 | tf_op jit(solution)/shard_map/all_to_all | solution.py:22
  46.7 15.3 %all_to_all.72.parts_ref = f32[8,1,512]{2,1,0:T(1,128)S(1)} all-to-all(f32[8,1,512]{2,1,0:T(1,128)S(1)} %sums.3), channel_id=1, replica_groups=mesh['z'=8,'x'=4,'c'=2,'h'=2,'y'=4] {'z'}, dimensions={0} | all-to-all | bytes 32768 | tf_op jit(solution)/shard_map/all_to_all | solution.py:22
  62.1 7.6 %all_to_all.73.columns_ref = f32[8,1,512]{2,1,0:T(1,128)S(1)} all-to-all(f32[8,1,512]{2,1,0:T(1,128)S(1)} %inverse.3), channel_id=1, replica_groups=mesh['z'=8,'x'=4,'c'=2,'h'=2,'y'=4] {'c','x'}, dimensions={0} | all-to-all | bytes 32768 | tf_op jit(solution)/shard_map/all_to_all | solution.py:22
  69.7 0.5 rows.2
  70.2 17.3 %all_to_all.74.parts_ref = f32[8,1,384]{2,1,0:T(1,128)S(1)} all-to-all(f32[8,1,384]{2,1,0:T(1,128)S(1)} %rows.2), channel_id=1, replica_groups=mesh['z'=8,'x'=4,'c'=2,'h'=2,'y'=4] {'h','y'}, dimensions={0} | all-to-all | bytes 24576 | tf_op jit(solution)/shard_map/all_to_all | solution.py:22
  87.5 0.7 columns.4
  88.2 7.6 %all_to_all.75.parts_ref = f32[8,1,512]{2,1,0:T(1,128)S(1)} all-to-all(f32[8,1,512]{2,1,0:T(1,128)S(1)} %columns.4), channel_id=1, replica_groups=mesh['z'=8,'x'=4,'c'=2,'h'=2,'y'=4] {'c','x'}, dimensions={0} | all-to-all | bytes 32768 | tf_op jit(solution)/shard_map/all_to_all | solution.py:22
  95.8 12.9 %all_to_all.76.parts_ref = f32[8,1,512]{2,1,0:T(1,128)S(1)} all-to-all(f32[8,1,512]{2,1,0:T(1,128)S(1)} %sums.4), channel_id=1, replica_groups=mesh['z'=8,'x'=4,'c'=2,'h'=2,'y'=4] {'z'}, dimensions={0} | all-to-all | bytes 32768 | tf_op jit(solution)/shard_map/all_to_all | solution.py:22
  108.7 7.6 %all_to_all.77.columns_ref = f32[8,1,512]{2,1,0:T(1,128)S(1)} all-to-all(f32[8,1,512]{2,1,0:T(1,128)S(1)} %inverse.4), channel_id=1, replica_groups=mesh['z'=8,'x'=4,'c'=2,'h'=2,'y'=4] {'c','x'}, dimensions={0} | all-to-all | bytes 32768 | tf_op jit(solution)/shard_map/all_to_all | solution.py:22
  116.4 0.5 rows.3
  116.9 17.3 %all_to_all.78.parts_ref = f32[8,1,384]{2,1,0:T(1,128)S(1)} all-to-all(f32[8,1,384]{2,1,0:T(1,128)S(1)} %rows.3), channel_id=1, replica_groups=mesh['z'=8,'x'=4,'c'=2,'h'=2,'y'=4] {'h','y'}, dimensions={0} | all-to-all | bytes 24576 | tf_op jit(solution)/shard_map/all_to_all | solution.py:22
  134.2 1.2 columns.5.after_ref
  135.4 3.3 %all-to-all-start.9 = ((f32[8,1,512]{2,1,0:T(1,128)}), f32[8,1,512]{2,1,0:T(1,128)S(1)}, u32[]{:S(2)}, u32[]{:S(2)}) async-start(f32[8,1,512]{2,1,0:T(1,128)} %columns.5.after_ref), calls=%async_computation.9 | async-start | bytes 32768 | tf_op jit(solution)/shard_map/all_to_all | solution.py:22
  138.7 3.8 %targets_sent.1 = f32[4,256,512]{2,1,0:T(8,128)} custom-call(s32[5]{0:T(128)S(1)} %stack.23.where_ref, f32[8,1,384]{2,1,0:T(1,128)S(1)} %all_to_all.78.parts_ref, bf16[384,256]{1,0:T(8,128)(2,1)S(1)} %copy-done.2, f32[8,384,512]{2,1,0:T(8,128)} %copy-done, f32[8,1,512]{2,1,0:T(1,128)} %columns.5.after_ref), custom_call_target="tpu_custom_call" | custom-call | flops 402653184 | bytes 6291456 | tf_op jit(solution)/shard_map/targets_sent/pallas_call | solution.py:292
  142.5 2.3 %collective-permute-start = (f32[4,256,512]{2,1,0:T(8,128)}, f32[4,256,512]{2,1,0:T(8,128)}, u32[]{:S(2)}, u32[]{:S(2)}) collective-permute-start(f32[4,256,512]{2,1,0:T(8,128)} %targets_sent.1), channel_id=1, source_target_pairs={{0,8},{8,0},{1,9},{9,1},{2,10},{10,2},{3,11},{11,3},{4,12},{12,4},... | collective-permute-start | bytes 6291464 | tf_op jit(solution)/shard_map/ppermute | solution.py:337
  144.9 0.6 sums.5.after_ref
  145.5 3.3 %all-to-all-start.10 = ((f32[8,1,512]{2,1,0:T(1,128)}), f32[8,1,512]{2,1,0:T(1,128)S(1)}, u32[]{:S(2)}, u32[]{:S(2)}) async-start(f32[8,1,512]{2,1,0:T(1,128)} %sums.5.after_ref), calls=%async_computation.10 | async-start | bytes 32768 | tf_op jit(solution)/shard_map/all_to_all | solution.py:22
  148.9 0.1 collective-permute-done.added_ref
  149.0 3.8 %targets_kept.1 = (f32[2,128,512]{2,1,0:T(8,128)}, f32[2,128,512]{2,1,0:T(8,128)S(1)}, f32[2,128,512]{2,1,0:T(8,128)S(1)}, f32[2,128,512]{2,1,0:T(8,128)S(1)}) custom-call(s32[5]{0:T(128)S(1)} %stack.23.where_ref, f32[8,1,384]{2,1,0:T(1,128)S(1)} %all_to_all.78.parts_ref, bf16[384,256]{1,0:T(8,128)(2,1)S(1)} %copy-done.2, f32[8,384,512]{2,1,0:T(8,128)} %copy-done, ...), custom_call_target="tpu_custom_call" | custom-call | flops 402653184 | bytes 6291456 | tf_op jit(solution)/shard_map/targets_kept/pallas_call | solution.py:308
  152.8 5.0 %collective-permute-start.3 = (f32[2,128,512]{2,1,0:T(8,128)S(1)}, f32[2,128,512]{2,1,0:T(8,128)S(1)}, u32[]{:S(2)}, u32[]{:S(2)}) collective-permute-start(f32[2,128,512]{2,1,0:T(8,128)S(1)} %get-tuple-element.17), channel_id=1, source_target_pairs={{0,48},{16,32},{32,16},{48,0},{1,49},{17,33},{33,17},{49,1},{2,50}... | collective-permute-start | bytes 1572872 | tf_op jit(solution)/shard_map/ppermute | solution.py:337
  157.8 2.2 collective-permute-start.1
  160.0 0.6 inverse.5
  160.6 3.8 %all-to-all-start.11 = ((f32[8,1,512]{2,1,0:T(1,128)}), f32[8,1,512]{2,1,0:T(1,128)S(1)}, u32[]{:S(2)}, u32[]{:S(2)}) async-start(f32[8,1,512]{2,1,0:T(1,128)} %inverse.5), calls=%async_computation.11 | async-start | bytes 32768 | tf_op jit(solution)/shard_map/all_to_all | solution.py:22
  164.4 5.8 %collective-permute-done.3.two_ref = f32[2,128,512]{2,1,0:T(8,128)S(1)} collective-permute-done((f32[2,128,512]{2,1,0:T(8,128)S(1)}, f32[2,128,512]{2,1,0:T(8,128)S(1)}, u32[]{:S(2)}, u32[]{:S(2)}) %collective-permute-start.3) | collective-permute-done | bytes 524320 | tf_op jit(solution)/shard_map/ppermute | solution.py:337
  170.2 2.4 %collective-permute-start.4 = (f32[128,512]{1,0:T(8,128)S(1)}, f32[128,512]{1,0:T(8,128)S(1)}, u32[]{:S(2)}, u32[]{:S(2)}) collective-permute-start(f32[128,512]{1,0:T(8,128)S(1)} %fusion.more_two_ref), channel_id=1, source_target_pairs={{0,16},{16,0},{32,48},{48,32},{1,17},{17,1},{33,49},{49,33},{2,18}... | collective-permute-start | bytes 786440 | tf_op jit(solution)/shard_map/ppermute | solution.py:337
  172.5 1.2 collective-permute-done.1.one_ref
  173.7 3.2 %collective-permute-start.2 = (f32[128,512]{1,0:T(8,128)S(1)}, f32[128,512]{1,0:T(8,128)}, u32[]{:S(2)}, u32[]{:S(2)}) collective-permute-start(f32[128,512]{1,0:T(8,128)S(1)} %fusion.1.more_one_ref), channel_id=1, source_target_pairs={{0,48},{16,32},{32,16},{48,0},{1,49},{17,33},{33,17},{49,1},{2,50}... | collective-permute-start | bytes 786440 | tf_op jit(solution)/shard_map/ppermute | solution.py:337
  177.0 4.9 %final.1 = f32[4,104,256]{2,1,0:T(8,128)} custom-call(f32[8,1,384]{2,1,0:T(1,128)S(1)} %all_to_all.78.parts_ref, f32[8,1,512]{2,1,0:T(1,128)S(1)} %all-to-all-done.11.columns_ref, bf16[8,8,64,256]{3,2,1,0:T(8,128)(2,1)} %bitcast.26, f32[8,384,512]{2,1,0:T(8,128)} %copy-done, f32[128,512]{1,0:T(8,128)S(1)} %fusion.1.more_one_ref, f32[128,512]{1,0:T(8,128)S(1)} %fusion.more_two_ref), custom_call_target="tpu_custom_call" | custom-call | flops 4831838208 | bytes 6291456 | tf_op jit(solution)/shard_map/final/pallas_call | solution.py:359
  181.9 5.5 %all-to-all-start.12 = ((f32[4,104,256]{2,1,0:T(8,128)}), f32[4,104,256]{2,1,0:T(8,128)S(1)}, u32[]{:S(2)}, u32[]{:S(2)}) async-start(f32[4,104,256]{2,1,0:T(8,128)} %final.1), calls=%async_computation.12 | async-start | bytes 851968 | tf_op jit(solution)/shard_map/all_to_all | solution.py:22
  187.4 1.2 turn.1
  188.6 3.4 %collective-permute-start.5 = (f32[4,64,256]{2,1,0:T(8,128)S(1)}, f32[4,64,256]{2,1,0:T(8,128)S(1)}, u32[]{:S(2)}, u32[]{:S(2)}) collective-permute-start(f32[4,64,256]{2,1,0:T(8,128)S(1)} %get-tuple-element.19.after_ref), channel_id=1, source_target_pairs={{0,64},{64,0},{128,192},{192,128},{256,320},{320,256},{384,448},{4... | collective-permute-start | bytes 786440 | tf_op jit(solution)/shard_map/ppermute | solution.py:337
  192.0 1.2 all-to-all-done.12.parts_ref
  193.2 2.5 %collective-permute-start.8 = (f32[104,256]{1,0:T(8,128)S(1)}, f32[104,256]{1,0:T(8,128)S(1)}, u32[]{:S(2)}, u32[]{:S(2)}) collective-permute-start(f32[104,256]{1,0:T(8,128)S(1)} %gathered.1.kept_ref), channel_id=1, source_target_pairs={{0,4},{4,0},{1,5},{5,1},{2,6},{6,2},{3,7},{7,3},{8,12},{12,8},{9,1... | collective-permute-start | bytes 319496 | tf_op jit(solution)/shard_map/ppermute | solution.py:337
  195.7 0.7 multiply_bitcast_fusion
  196.5 3.3 %collective-permute-done.5 = f32[4,64,256]{2,1,0:T(8,128)S(1)} collective-permute-done((f32[4,64,256]{2,1,0:T(8,128)S(1)}, f32[4,64,256]{2,1,0:T(8,128)S(1)}, u32[]{:S(2)}, u32[]{:S(2)}) %collective-permute-start.5) | collective-permute-done | bytes 262176 | tf_op jit(solution)/shard_map/ppermute | solution.py:337
  199.8 4.4 %collective-permute-start.6 = (f32[2,64,256]{2,1,0:T(8,128)S(1)}, f32[2,64,256]{2,1,0:T(8,128)S(1)}, u32[]{:S(2)}, u32[]{:S(2)}) collective-permute-start(f32[2,64,256]{2,1,0:T(8,128)S(1)} %slice.43), channel_id=1, source_target_pairs={{0,128},{64,192},{128,0},{192,64},{256,384},{320,448},{384,256},{4... | collective-permute-start | bytes 393224 | tf_op jit(solution)/shard_map/ppermute | solution.py:337
  204.2 6.0 %collective-permute-done.8.came_ref = f32[104,256]{1,0:T(8,128)S(1)} collective-permute-done((f32[104,256]{1,0:T(8,128)S(1)}, f32[104,256]{1,0:T(8,128)S(1)}, u32[]{:S(2)}, u32[]{:S(2)}) %collective-permute-start.8) | collective-permute-done | bytes 106528 | tf_op jit(solution)/shard_map/ppermute | solution.py:337
  210.2 0.8 join.1
  210.9 4.5 %all-to-all-start.13 = ((f32[4,96,256]{2,1,0:T(8,128)}), f32[4,96,256]{2,1,0:T(8,128)S(1)}, u32[]{:S(2)}, u32[]{:S(2)}) async-start(f32[4,96,256]{2,1,0:T(8,128)} %get-tuple-element.20), calls=%async_computation.13 | async-start | bytes 786432 | tf_op jit(solution)/shard_map/all_to_all | solution.py:22
  215.5 10.5 %collective-permute-start.7 = (f32[64,256]{1,0:T(8,128)S(1)}, f32[64,256]{1,0:T(8,128)S(1)}, u32[]{:S(2)}, u32[]{:S(2)}) collective-permute-start(f32[64,256]{1,0:T(8,128)S(1)} %slice_bitcast_fusion), channel_id=1, source_target_pairs={{0,256},{64,320},{128,384},{192,448},{256,0},{320,64},{384,128},{4... | collective-permute-start | bytes 196616 | tf_op jit(solution)/shard_map/ppermute | solution.py:337
  226.1 2.2 collective-permute-done.7
  228.3 0.7 fusion.3
  229.0 0.9 bitcast_divide_fusion
  (27 shorter events, 0.4 us)
Async XLA Ops:
  0.7 0.9 copy-start.1
  1.7 1.6 copy-start.3
  6.0 128.1 %copy-start = (f32[8,384,512]{2,1,0:T(8,128)}, f32[8,384,512]{2,1,0:T(8,128)S(1)}, u32[]{:S(2)}) copy-start(f32[8,384,512]{2,1,0:T(8,128)S(1)} %get-tuple-element.13.tile_ref) | copy-start | bytes 18874372
  134.1 4.6 %copy-start.2 = (bf16[384,256]{1,0:T(8,128)(2,1)S(1)}, bf16[384,256]{1,0:T(8,128)(2,1)}, u32[]{:S(2)}) copy-start(bf16[384,256]{1,0:T(8,128)(2,1)} %latents_ref.5) | copy-start | bytes 589828
  135.4 9.5 %all-to-all-start.9 = ((f32[8,1,512]{2,1,0:T(1,128)}), f32[8,1,512]{2,1,0:T(1,128)S(1)}, u32[]{:S(2)}, u32[]{:S(2)}) async-start(f32[8,1,512]{2,1,0:T(1,128)} %columns.5.after_ref), calls=%async_computation.9 | async-start | bytes 32768 | tf_op jit(solution)/shard_map/all_to_all | solution.py:22
  142.5 6.4 %collective-permute-start = (f32[4,256,512]{2,1,0:T(8,128)}, f32[4,256,512]{2,1,0:T(8,128)}, u32[]{:S(2)}, u32[]{:S(2)}) collective-permute-start(f32[4,256,512]{2,1,0:T(8,128)} %targets_sent.1), channel_id=1, source_target_pairs={{0,8},{8,0},{1,9},{9,1},{2,10},{10,2},{3,11},{11,3},{4,12},{12,4},... | collective-permute-start | bytes 6291464 | tf_op jit(solution)/shard_map/ppermute | solution.py:337
  145.5 14.4 %all-to-all-start.10 = ((f32[8,1,512]{2,1,0:T(1,128)}), f32[8,1,512]{2,1,0:T(1,128)S(1)}, u32[]{:S(2)}, u32[]{:S(2)}) async-start(f32[8,1,512]{2,1,0:T(1,128)} %sums.5.after_ref), calls=%async_computation.10 | async-start | bytes 32768 | tf_op jit(solution)/shard_map/all_to_all | solution.py:22
  152.8 17.3 %collective-permute-start.3 = (f32[2,128,512]{2,1,0:T(8,128)S(1)}, f32[2,128,512]{2,1,0:T(8,128)S(1)}, u32[]{:S(2)}, u32[]{:S(2)}) collective-permute-start(f32[2,128,512]{2,1,0:T(8,128)S(1)} %get-tuple-element.17), channel_id=1, source_target_pairs={{0,48},{16,32},{32,16},{48,0},{1,49},{17,33},{33,17},{49,1},{2,50}... | collective-permute-start | bytes 1572872 | tf_op jit(solution)/shard_map/ppermute | solution.py:337
  157.8 15.9 %collective-permute-start.1 = (f32[2,128,512]{2,1,0:T(8,128)}, f32[2,128,512]{2,1,0:T(8,128)S(1)}, u32[]{:S(2)}, u32[]{:S(2)}) collective-permute-start(f32[2,128,512]{2,1,0:T(8,128)} %get-tuple-element.15.refs_0_), channel_id=1, source_target_pairs={{0,16},{16,0},{32,48},{48,32},{1,17},{17,1},{33,49},{49,33},{2,18}... | collective-permute-start | bytes 1572872 | tf_op jit(solution)/shard_map/ppermute | solution.py:337
  160.6 16.4 %all-to-all-start.11 = ((f32[8,1,512]{2,1,0:T(1,128)}), f32[8,1,512]{2,1,0:T(1,128)S(1)}, u32[]{:S(2)}, u32[]{:S(2)}) async-start(f32[8,1,512]{2,1,0:T(1,128)} %inverse.5), calls=%async_computation.11 | async-start | bytes 32768 | tf_op jit(solution)/shard_map/all_to_all | solution.py:22
  170.2 17.2 %collective-permute-start.4 = (f32[128,512]{1,0:T(8,128)S(1)}, f32[128,512]{1,0:T(8,128)S(1)}, u32[]{:S(2)}, u32[]{:S(2)}) collective-permute-start(f32[128,512]{1,0:T(8,128)S(1)} %fusion.more_two_ref), channel_id=1, source_target_pairs={{0,16},{16,0},{32,48},{48,32},{1,17},{17,1},{33,49},{49,33},{2,18}... | collective-permute-start | bytes 786440 | tf_op jit(solution)/shard_map/ppermute | solution.py:337
  173.7 13.7 %collective-permute-start.2 = (f32[128,512]{1,0:T(8,128)S(1)}, f32[128,512]{1,0:T(8,128)}, u32[]{:S(2)}, u32[]{:S(2)}) collective-permute-start(f32[128,512]{1,0:T(8,128)S(1)} %fusion.1.more_one_ref), channel_id=1, source_target_pairs={{0,48},{16,32},{32,16},{48,0},{1,49},{17,33},{33,17},{49,1},{2,50}... | collective-permute-start | bytes 786440 | tf_op jit(solution)/shard_map/ppermute | solution.py:337
  181.9 11.3 %all-to-all-start.12 = ((f32[4,104,256]{2,1,0:T(8,128)}), f32[4,104,256]{2,1,0:T(8,128)S(1)}, u32[]{:S(2)}, u32[]{:S(2)}) async-start(f32[4,104,256]{2,1,0:T(8,128)} %final.1), calls=%async_computation.12 | async-start | bytes 851968 | tf_op jit(solution)/shard_map/all_to_all | solution.py:22
  188.6 11.1 %collective-permute-start.5 = (f32[4,64,256]{2,1,0:T(8,128)S(1)}, f32[4,64,256]{2,1,0:T(8,128)S(1)}, u32[]{:S(2)}, u32[]{:S(2)}) collective-permute-start(f32[4,64,256]{2,1,0:T(8,128)S(1)} %get-tuple-element.19.after_ref), channel_id=1, source_target_pairs={{0,64},{64,0},{128,192},{192,128},{256,320},{320,256},{384,448},{4... | collective-permute-start | bytes 786440 | tf_op jit(solution)/shard_map/ppermute | solution.py:337
  193.2 16.9 %collective-permute-start.8 = (f32[104,256]{1,0:T(8,128)S(1)}, f32[104,256]{1,0:T(8,128)S(1)}, u32[]{:S(2)}, u32[]{:S(2)}) collective-permute-start(f32[104,256]{1,0:T(8,128)S(1)} %gathered.1.kept_ref), channel_id=1, source_target_pairs={{0,4},{4,0},{1,5},{5,1},{2,6},{6,2},{3,7},{7,3},{8,12},{12,8},{9,1... | collective-permute-start | bytes 319496 | tf_op jit(solution)/shard_map/ppermute | solution.py:337
  199.8 15.7 %collective-permute-start.6 = (f32[2,64,256]{2,1,0:T(8,128)S(1)}, f32[2,64,256]{2,1,0:T(8,128)S(1)}, u32[]{:S(2)}, u32[]{:S(2)}) collective-permute-start(f32[2,64,256]{2,1,0:T(8,128)S(1)} %slice.43), channel_id=1, source_target_pairs={{0,128},{64,192},{128,0},{192,64},{256,384},{320,448},{384,256},{4... | collective-permute-start | bytes 393224 | tf_op jit(solution)/shard_map/ppermute | solution.py:337
  210.9 18.0 %all-to-all-start.13 = ((f32[4,96,256]{2,1,0:T(8,128)}), f32[4,96,256]{2,1,0:T(8,128)S(1)}, u32[]{:S(2)}, u32[]{:S(2)}) async-start(f32[4,96,256]{2,1,0:T(8,128)} %get-tuple-element.20), calls=%async_computation.13 | async-start | bytes 786432 | tf_op jit(solution)/shard_map/all_to_all | solution.py:22
  215.5 12.8 %collective-permute-start.7 = (f32[64,256]{1,0:T(8,128)S(1)}, f32[64,256]{1,0:T(8,128)S(1)}, u32[]{:S(2)}, u32[]{:S(2)}) collective-permute-start(f32[64,256]{1,0:T(8,128)S(1)} %slice_bitcast_fusion), channel_id=1, source_target_pairs={{0,256},{64,320},{128,384},{192,448},{256,0},{320,64},{384,128},{4... | collective-permute-start | bytes 196616 | tf_op jit(solution)/shard_map/ppermute | solution.py:337

commit v13 on v12

--- a/solution.py
+++ b/solution.py
@@ -179,6 +179,10 @@
 def inverse_kernel(factor, parts_ref, *refs):
     out_ref = refs[-1]
     out_ref[...] = jnp.broadcast_to(factor / jnp.sum(parts_ref[...], axis=0, keepdims=True), out_ref.shape)
+
+
+def kept_kernel(near_ref, out_ref):
+    out_ref[...] = near_ref[...]
 
 
 def join_kernel(kept_ref, came_ref, after_ref, spread_ref, mass_ref):
@@ -392,16 +396,25 @@
         name="gathered",
     )(exchange(packed, "y"), away)
     near = near + swap(away, "z", Z, 1)
+    came = swap(near[2:], "z", Z, 2)
+    near = pl.pallas_call(
+        kept_kernel,
+        in_specs=[vmem],
+        out_specs=vmem,
+        out_shape=f32(2, share, width),
+        compiler_params=params(),
+        cost_estimate=cost(400_000 * share * width, 16 * share * width),
+        name="kept",
+    )(near[:2]) + came
     numer, mass = pl.pallas_call(
         join_kernel,
         in_specs=[vmem] * 2 + [anywhere],
         out_specs=[vmem] * 2,
         out_shape=[f32(Y, group, width), f32(PAD, width)],
         compiler_params=params(),
-        cost_estimate=cost(20000 * token_count * width, 8 * token_count * width),
+        cost_estimate=cost(400_000 * token_count * width, 8 * token_count * width),
         name="join",
     )(packed, swap(packed, "h", H, 1), near)
-    near = near[:2] + swap(near[2:], "z", Z, 2)
     summed = near[0] + swap(near[1], "z", Z, 4)
     own = lax.dynamic_slice(mine, (0, 0, where[4]), (1, 1, share)).reshape(share)
     targets = summed * (own * (total_codes / total_tokens))[:, None]

time: 232 us -> 233 us (level)
  waiting for transfers between devices: 19.7 us -> 24.7 us
  starting transfers between devices: 56.3 us -> 53.3 us
    ppermute x9, waiting for transfers between devices: 18.5 us -> 24.3 us  [swap(): return lax.ppermute(value, axis, [(i, i ^ bits) for i in range(count)])]
    ppermute x9, starting transfers between devices: 35.9 us -> 32.7 us  [swap(): return lax.ppermute(value, axis, [(i, i ^ bits) for i in range(count)])]
  transfers between devices with their start and end apart: 14 -> 14, of which waited for: 7 -> 7; matrix products, arithmetic and copies ran while one was open for 1% -> 1% of each run, Pallas kernels for 7% -> 6%
where the time goes in v13:
time: 233 us; the launch traced here: 232 us
  blocking collectives  126 us (54%)
  starting transfers between devices  53.3 us (23%)
  waiting for transfers between devices  24.7 us (11%)
  Pallas kernels  22.2 us (10%)
  local copies, waits for them, and re-layouts  2.64 us (1%)
  other arithmetic  2.43 us (1%)
    all_to_all x9, blocking collectives, exchange(): return lax.all_to_all(blocks, axes, 0, 0, tiled=True)  126 us
    ppermute x9, starting transfers between devices, swap(): return lax.ppermute(value, axis, [(i, i ^ bits) for i in range(count)])  32.7 us
    ppermute x9, waiting for transfers between devices, swap(): return lax.ppermute(value, axis, [(i, i ^ bits) for i in range(count)])  24.3 us
    all_to_all x5, starting transfers between devices, exchange(): return lax.all_to_all(blocks, axes, 0, 0, tiled=True)  20.6 us
    pallas_call x1, Pallas kernels, per_device(): pl.pallas_call(final_kernel, in_specs=[vmem, vmem, hbm, hbm, anywhere, an...  4.92 us
  transfers between devices with their start and end apart: 14, of which 7 were waited for; matrix products, arithmetic and copies ran while one was open for 1% of the time, Pallas kernels for 6%

profile of v13, /device:TPU:24, one launch (start us, length us, event | category | flops | bytes accessed | tf_op | source)
XLA Modules:
  0.0 231.8 jit_solution(11594012510345390638)
XLA Ops:
  0.7 0.9 copy-done.1
  1.7 1.6 copy-done.3
  3.2 2.8 %setup.1 = (f32[8,384,512]{2,1,0:T(8,128)S(1)}, f32[8,1,384]{2,1,0:T(1,128)S(1)}) custom-call(s32[5]{0:T(128)S(1)} %stack.23.where_ref, bf16[384,256]{1,0:T(8,128)(2,1)S(1)} %copy-done.1, bf16[8,8,64,256]{3,2,1,0:T(8,128)(2,1)S(1)} %bitcast.27), custom_call_target="tpu_custom_call" | custom-call | flops 805306368 | bytes 6291456 | tf_op jit(solution)/shard_map/setup/pallas_call | solution.py:268
  6.0 30.6 %all_to_all.70.parts_ref = f32[8,1,384]{2,1,0:T(1,128)S(1)} all-to-all(f32[8,1,384]{2,1,0:T(1,128)S(1)} %get-tuple-element.12), channel_id=1, replica_groups=mesh['z'=8,'x'=4,'c'=2,'h'=2,'y'=4] {'h','y'}, dimensions={0} | all-to-all | bytes 24576 | tf_op jit(solution)/shard_map/all_to_all | solution.py:22
  36.6 0.7 columns.3
  37.3 9.4 %all_to_all.71.parts_ref = f32[8,1,512]{2,1,0:T(1,128)S(1)} all-to-all(f32[8,1,512]{2,1,0:T(1,128)S(1)} %columns.3), channel_id=1, replica_groups=mesh['z'=8,'x'=4,'c'=2,'h'=2,'y'=4] {'c','x'}, dimensions={0} | all-to-all | bytes 32768 | tf_op jit(solution)/shard_map/all_to_all | solution.py:22
  46.7 15.3 %all_to_all.72.parts_ref = f32[8,1,512]{2,1,0:T(1,128)S(1)} all-to-all(f32[8,1,512]{2,1,0:T(1,128)S(1)} %sums.3), channel_id=1, replica_groups=mesh['z'=8,'x'=4,'c'=2,'h'=2,'y'=4] {'z'}, dimensions={0} | all-to-all | bytes 32768 | tf_op jit(solution)/shard_map/all_to_all | solution.py:22
  62.1 7.6 %all_to_all.73.columns_ref = f32[8,1,512]{2,1,0:T(1,128)S(1)} all-to-all(f32[8,1,512]{2,1,0:T(1,128)S(1)} %inverse.3), channel_id=1, replica_groups=mesh['z'=8,'x'=4,'c'=2,'h'=2,'y'=4] {'c','x'}, dimensions={0} | all-to-all | bytes 32768 | tf_op jit(solution)/shard_map/all_to_all | solution.py:22
  69.7 0.5 rows.2
  70.2 17.3 %all_to_all.74.parts_ref = f32[8,1,384]{2,1,0:T(1,128)S(1)} all-to-all(f32[8,1,384]{2,1,0:T(1,128)S(1)} %rows.2), channel_id=1, replica_groups=mesh['z'=8,'x'=4,'c'=2,'h'=2,'y'=4] {'h','y'}, dimensions={0} | all-to-all | bytes 24576 | tf_op jit(solution)/shard_map/all_to_all | solution.py:22
  87.5 0.7 columns.4
  88.2 7.6 %all_to_all.75.parts_ref = f32[8,1,512]{2,1,0:T(1,128)S(1)} all-to-all(f32[8,1,512]{2,1,0:T(1,128)S(1)} %columns.4), channel_id=1, replica_groups=mesh['z'=8,'x'=4,'c'=2,'h'=2,'y'=4] {'c','x'}, dimensions={0} | all-to-all | bytes 32768 | tf_op jit(solution)/shard_map/all_to_all | solution.py:22
  95.8 12.9 %all_to_all.76.parts_ref = f32[8,1,512]{2,1,0:T(1,128)S(1)} all-to-all(f32[8,1,512]{2,1,0:T(1,128)S(1)} %sums.4), channel_id=1, replica_groups=mesh['z'=8,'x'=4,'c'=2,'h'=2,'y'=4] {'z'}, dimensions={0} | all-to-all | bytes 32768 | tf_op jit(solution)/shard_map/all_to_all | solution.py:22
  108.7 7.6 %all_to_all.77.columns_ref = f32[8,1,512]{2,1,0:T(1,128)S(1)} all-to-all(f32[8,1,512]{2,1,0:T(1,128)S(1)} %inverse.4), channel_id=1, replica_groups=mesh['z'=8,'x'=4,'c'=2,'h'=2,'y'=4] {'c','x'}, dimensions={0} | all-to-all | bytes 32768 | tf_op jit(solution)/shard_map/all_to_all | solution.py:22
  116.4 0.5 rows.3
  116.9 17.3 %all_to_all.78.parts_ref = f32[8,1,384]{2,1,0:T(1,128)S(1)} all-to-all(f32[8,1,384]{2,1,0:T(1,128)S(1)} %rows.3), channel_id=1, replica_groups=mesh['z'=8,'x'=4,'c'=2,'h'=2,'y'=4] {'h','y'}, dimensions={0} | all-to-all | bytes 24576 | tf_op jit(solution)/shard_map/all_to_all | solution.py:22
  134.2 1.2 columns.5.after_ref
  135.4 3.3 %all-to-all-start.9 = ((f32[8,1,512]{2,1,0:T(1,128)}), f32[8,1,512]{2,1,0:T(1,128)S(1)}, u32[]{:S(2)}, u32[]{:S(2)}) async-start(f32[8,1,512]{2,1,0:T(1,128)} %columns.5.after_ref), calls=%async_computation.9 | async-start | bytes 32768 | tf_op jit(solution)/shard_map/all_to_all | solution.py:22
  138.7 3.8 %targets_sent.1 = f32[4,256,512]{2,1,0:T(8,128)} custom-call(s32[5]{0:T(128)S(1)} %stack.23.where_ref, f32[8,1,384]{2,1,0:T(1,128)S(1)} %all_to_all.78.parts_ref, bf16[384,256]{1,0:T(8,128)(2,1)S(1)} %copy-done.2, f32[8,384,512]{2,1,0:T(8,128)} %copy-done, f32[8,1,512]{2,1,0:T(1,128)} %columns.5.after_ref), custom_call_target="tpu_custom_call" | custom-call | flops 402653184 | bytes 6291456 | tf_op jit(solution)/shard_map/targets_sent/pallas_call | solution.py:296
  142.5 2.3 %collective-permute-start = (f32[4,256,512]{2,1,0:T(8,128)}, f32[4,256,512]{2,1,0:T(8,128)}, u32[]{:S(2)}, u32[]{:S(2)}) collective-permute-start(f32[4,256,512]{2,1,0:T(8,128)} %targets_sent.1), channel_id=1, source_target_pairs={{0,8},{8,0},{1,9},{9,1},{2,10},{10,2},{3,11},{11,3},{4,12},{12,4},... | collective-permute-start | bytes 6291464 | tf_op jit(solution)/shard_map/ppermute | solution.py:341
  144.9 0.6 sums.5.after_ref
  145.5 3.3 %all-to-all-start.10 = ((f32[8,1,512]{2,1,0:T(1,128)}), f32[8,1,512]{2,1,0:T(1,128)S(1)}, u32[]{:S(2)}, u32[]{:S(2)}) async-start(f32[8,1,512]{2,1,0:T(1,128)} %sums.5.after_ref), calls=%async_computation.10 | async-start | bytes 32768 | tf_op jit(solution)/shard_map/all_to_all | solution.py:22
  148.8 0.1 collective-permute-done.added_ref
  149.0 3.8 %targets_kept.1 = (f32[2,128,512]{2,1,0:T(8,128)}, f32[2,128,512]{2,1,0:T(8,128)S(1)}, f32[2,128,512]{2,1,0:T(8,128)S(1)}, f32[2,128,512]{2,1,0:T(8,128)S(1)}) custom-call(s32[5]{0:T(128)S(1)} %stack.23.where_ref, f32[8,1,384]{2,1,0:T(1,128)S(1)} %all_to_all.78.parts_ref, bf16[384,256]{1,0:T(8,128)(2,1)S(1)} %copy-done.2, f32[8,384,512]{2,1,0:T(8,128)} %copy-done, ...), custom_call_target="tpu_custom_call" | custom-call | flops 402653184 | bytes 6291456 | tf_op jit(solution)/shard_map/targets_kept/pallas_call | solution.py:312
  152.8 5.0 %collective-permute-start.3 = (f32[2,128,512]{2,1,0:T(8,128)S(1)}, f32[2,128,512]{2,1,0:T(8,128)S(1)}, u32[]{:S(2)}, u32[]{:S(2)}) collective-permute-start(f32[2,128,512]{2,1,0:T(8,128)S(1)} %get-tuple-element.17), channel_id=1, source_target_pairs={{0,48},{16,32},{32,16},{48,0},{1,49},{17,33},{33,17},{49,1},{2,50}... | collective-permute-start | bytes 1572872 | tf_op jit(solution)/shard_map/ppermute | solution.py:341
  157.8 2.2 collective-permute-start.1
  159.9 0.6 inverse.5
  160.6 3.8 %all-to-all-start.11 = ((f32[8,1,512]{2,1,0:T(1,128)}), f32[8,1,512]{2,1,0:T(1,128)S(1)}, u32[]{:S(2)}, u32[]{:S(2)}) async-start(f32[8,1,512]{2,1,0:T(1,128)} %inverse.5), calls=%async_computation.11 | async-start | bytes 32768 | tf_op jit(solution)/shard_map/all_to_all | solution.py:22
  164.4 5.8 %collective-permute-done.3.two_ref = f32[2,128,512]{2,1,0:T(8,128)S(1)} collective-permute-done((f32[2,128,512]{2,1,0:T(8,128)S(1)}, f32[2,128,512]{2,1,0:T(8,128)S(1)}, u32[]{:S(2)}, u32[]{:S(2)}) %collective-permute-start.3) | collective-permute-done | bytes 524320 | tf_op jit(solution)/shard_map/ppermute | solution.py:341
  170.1 2.4 %collective-permute-start.4 = (f32[128,512]{1,0:T(8,128)S(1)}, f32[128,512]{1,0:T(8,128)S(1)}, u32[]{:S(2)}, u32[]{:S(2)}) collective-permute-start(f32[128,512]{1,0:T(8,128)S(1)} %fusion.more_two_ref), channel_id=1, source_target_pairs={{0,16},{16,0},{32,48},{48,32},{1,17},{17,1},{33,49},{49,33},{2,18}... | collective-permute-start | bytes 786440 | tf_op jit(solution)/shard_map/ppermute | solution.py:341
  172.5 1.2 collective-permute-done.1.one_ref
  173.7 3.2 %collective-permute-start.2 = (f32[128,512]{1,0:T(8,128)S(1)}, f32[128,512]{1,0:T(8,128)}, u32[]{:S(2)}, u32[]{:S(2)}) collective-permute-start(f32[128,512]{1,0:T(8,128)S(1)} %fusion.1.more_one_ref), channel_id=1, source_target_pairs={{0,48},{16,32},{32,16},{48,0},{1,49},{17,33},{33,17},{49,1},{2,50}... | collective-permute-start | bytes 786440 | tf_op jit(solution)/shard_map/ppermute | solution.py:341
  176.9 4.9 %final.1 = f32[4,104,256]{2,1,0:T(8,128)} custom-call(f32[8,1,384]{2,1,0:T(1,128)S(1)} %all_to_all.78.parts_ref, f32[8,1,512]{2,1,0:T(1,128)S(1)} %all-to-all-done.11.columns_ref, bf16[8,8,64,256]{3,2,1,0:T(8,128)(2,1)} %bitcast.26, f32[8,384,512]{2,1,0:T(8,128)} %copy-done, f32[128,512]{1,0:T(8,128)S(1)} %fusion.1.more_one_ref, f32[128,512]{1,0:T(8,128)S(1)} %fusion.more_two_ref), custom_call_target="tpu_custom_call" | custom-call | flops 4831838208 | bytes 6291456 | tf_op jit(solution)/shard_map/final/pallas_call | solution.py:363
  181.9 5.5 %all-to-all-start.12 = ((f32[4,104,256]{2,1,0:T(8,128)}), f32[4,104,256]{2,1,0:T(8,128)S(1)}, u32[]{:S(2)}, u32[]{:S(2)}) async-start(f32[4,104,256]{2,1,0:T(8,128)} %final.1), calls=%async_computation.12 | async-start | bytes 851968 | tf_op jit(solution)/shard_map/all_to_all | solution.py:22
  187.4 1.2 turn.1
  188.6 3.4 %collective-permute-start.5 = (f32[4,64,256]{2,1,0:T(8,128)S(1)}, f32[4,64,256]{2,1,0:T(8,128)S(1)}, u32[]{:S(2)}, u32[]{:S(2)}) collective-permute-start(f32[4,64,256]{2,1,0:T(8,128)S(1)} %get-tuple-element.19.after_ref), channel_id=1, source_target_pairs={{0,64},{64,0},{128,192},{192,128},{256,320},{320,256},{384,448},{4... | collective-permute-start | bytes 786440 | tf_op jit(solution)/shard_map/ppermute | solution.py:341
  192.0 0.7 multiply_bitcast_fusion
  192.7 0.4 all-to-all-done.12.parts_ref
  193.2 2.5 %collective-permute-start.8 = (f32[104,256]{1,0:T(8,128)S(1)}, f32[104,256]{1,0:T(8,128)S(1)}, u32[]{:S(2)}, u32[]{:S(2)}) collective-permute-start(f32[104,256]{1,0:T(8,128)S(1)} %gathered.1.kept_ref), channel_id=1, source_target_pairs={{0,4},{4,0},{1,5},{5,1},{2,6},{6,2},{3,7},{7,3},{8,12},{12,8},{9,1... | collective-permute-start | bytes 319496 | tf_op jit(solution)/shard_map/ppermute | solution.py:341
  195.7 4.0 %collective-permute-done.5 = f32[4,64,256]{2,1,0:T(8,128)S(1)} collective-permute-done((f32[4,64,256]{2,1,0:T(8,128)S(1)}, f32[4,64,256]{2,1,0:T(8,128)S(1)}, u32[]{:S(2)}, u32[]{:S(2)}) %collective-permute-start.5) | collective-permute-done | bytes 262176 | tf_op jit(solution)/shard_map/ppermute | solution.py:341
  199.8 4.4 %collective-permute-start.6 = (f32[2,64,256]{2,1,0:T(8,128)S(1)}, f32[2,64,256]{2,1,0:T(8,128)S(1)}, u32[]{:S(2)}, u32[]{:S(2)}) collective-permute-start(f32[2,64,256]{2,1,0:T(8,128)S(1)} %get-tuple-element.22), channel_id=1, source_target_pairs={{0,128},{64,192},{128,0},{192,64},{256,384},{320,448},{384,256},{4... | collective-permute-start | bytes 393224 | tf_op jit(solution)/shard_map/ppermute | solution.py:341
  204.2 9.8 %collective-permute-done.6 = f32[2,64,256]{2,1,0:T(8,128)S(1)} collective-permute-done((f32[2,64,256]{2,1,0:T(8,128)S(1)}, f32[2,64,256]{2,1,0:T(8,128)S(1)}, u32[]{:S(2)}, u32[]{:S(2)}) %collective-permute-start.6) | collective-permute-done | bytes 131104 | tf_op jit(solution)/shard_map/ppermute | solution.py:341
  214.1 0.8 join.1
  214.9 4.7 %all-to-all-start.13 = ((f32[4,96,256]{2,1,0:T(8,128)}), f32[4,96,256]{2,1,0:T(8,128)S(1)}, u32[]{:S(2)}, u32[]{:S(2)}) async-start(f32[4,96,256]{2,1,0:T(8,128)} %get-tuple-element.20), calls=%async_computation.13 | async-start | bytes 786432 | tf_op jit(solution)/shard_map/all_to_all | solution.py:22
  219.5 7.3 %collective-permute-start.7 = (f32[64,256]{1,0:T(8,128)S(1)}, f32[64,256]{1,0:T(8,128)S(1)}, u32[]{:S(2)}, u32[]{:S(2)}) collective-permute-start(f32[64,256]{1,0:T(8,128)S(1)} %slice_bitcast_fusion), channel_id=1, source_target_pairs={{0,256},{64,320},{128,384},{192,448},{256,0},{320,64},{384,128},{4... | collective-permute-start | bytes 196616 | tf_op jit(solution)/shard_map/ppermute | solution.py:341
  226.9 3.4 %collective-permute-done.7 = f32[64,256]{1,0:T(8,128)S(1)} collective-permute-done((f32[64,256]{1,0:T(8,128)S(1)}, f32[64,256]{1,0:T(8,128)S(1)}, u32[]{:S(2)}, u32[]{:S(2)}) %collective-permute-start.7) | collective-permute-done | bytes 65568 | tf_op jit(solution)/shard_map/ppermute | solution.py:341
  230.3 0.7 fusion.3
  231.0 0.9 bitcast_divide_fusion
  (28 shorter events, 0.4 us)
Async XLA Ops:
  0.7 0.9 copy-start.1
  1.7 1.6 copy-start.3
  6.0 128.1 %copy-start = (f32[8,384,512]{2,1,0:T(8,128)}, f32[8,384,512]{2,1,0:T(8,128)S(1)}, u32[]{:S(2)}) copy-start(f32[8,384,512]{2,1,0:T(8,128)S(1)} %get-tuple-element.13.tile_ref) | copy-start | bytes 18874372
  134.1 4.6 %copy-start.2 = (bf16[384,256]{1,0:T(8,128)(2,1)S(1)}, bf16[384,256]{1,0:T(8,128)(2,1)}, u32[]{:S(2)}) copy-start(bf16[384,256]{1,0:T(8,128)(2,1)} %latents_ref.5) | copy-start | bytes 589828
  135.4 9.5 %all-to-all-start.9 = ((f32[8,1,512]{2,1,0:T(1,128)}), f32[8,1,512]{2,1,0:T(1,128)S(1)}, u32[]{:S(2)}, u32[]{:S(2)}) async-start(f32[8,1,512]{2,1,0:T(1,128)} %columns.5.after_ref), calls=%async_computation.9 | async-start | bytes 32768 | tf_op jit(solution)/shard_map/all_to_all | solution.py:22
  142.5 6.4 %collective-permute-start = (f32[4,256,512]{2,1,0:T(8,128)}, f32[4,256,512]{2,1,0:T(8,128)}, u32[]{:S(2)}, u32[]{:S(2)}) collective-permute-start(f32[4,256,512]{2,1,0:T(8,128)} %targets_sent.1), channel_id=1, source_target_pairs={{0,8},{8,0},{1,9},{9,1},{2,10},{10,2},{3,11},{11,3},{4,12},{12,4},... | collective-permute-start | bytes 6291464 | tf_op jit(solution)/shard_map/ppermute | solution.py:341
  145.5 14.4 %all-to-all-start.10 = ((f32[8,1,512]{2,1,0:T(1,128)}), f32[8,1,512]{2,1,0:T(1,128)S(1)}, u32[]{:S(2)}, u32[]{:S(2)}) async-start(f32[8,1,512]{2,1,0:T(1,128)} %sums.5.after_ref), calls=%async_computation.10 | async-start | bytes 32768 | tf_op jit(solution)/shard_map/all_to_all | solution.py:22
  152.8 17.3 %collective-permute-start.3 = (f32[2,128,512]{2,1,0:T(8,128)S(1)}, f32[2,128,512]{2,1,0:T(8,128)S(1)}, u32[]{:S(2)}, u32[]{:S(2)}) collective-permute-start(f32[2,128,512]{2,1,0:T(8,128)S(1)} %get-tuple-element.17), channel_id=1, source_target_pairs={{0,48},{16,32},{32,16},{48,0},{1,49},{17,33},{33,17},{49,1},{2,50}... | collective-permute-start | bytes 1572872 | tf_op jit(solution)/shard_map/ppermute | solution.py:341
  157.8 15.9 %collective-permute-start.1 = (f32[2,128,512]{2,1,0:T(8,128)}, f32[2,128,512]{2,1,0:T(8,128)S(1)}, u32[]{:S(2)}, u32[]{:S(2)}) collective-permute-start(f32[2,128,512]{2,1,0:T(8,128)} %get-tuple-element.15.refs_0_), channel_id=1, source_target_pairs={{0,16},{16,0},{32,48},{48,32},{1,17},{17,1},{33,49},{49,33},{2,18}... | collective-permute-start | bytes 1572872 | tf_op jit(solution)/shard_map/ppermute | solution.py:341
  160.6 16.4 %all-to-all-start.11 = ((f32[8,1,512]{2,1,0:T(1,128)}), f32[8,1,512]{2,1,0:T(1,128)S(1)}, u32[]{:S(2)}, u32[]{:S(2)}) async-start(f32[8,1,512]{2,1,0:T(1,128)} %inverse.5), calls=%async_computation.11 | async-start | bytes 32768 | tf_op jit(solution)/shard_map/all_to_all | solution.py:22
  170.1 17.2 %collective-permute-start.4 = (f32[128,512]{1,0:T(8,128)S(1)}, f32[128,512]{1,0:T(8,128)S(1)}, u32[]{:S(2)}, u32[]{:S(2)}) collective-permute-start(f32[128,512]{1,0:T(8,128)S(1)} %fusion.more_two_ref), channel_id=1, source_target_pairs={{0,16},{16,0},{32,48},{48,32},{1,17},{17,1},{33,49},{49,33},{2,18}... | collective-permute-start | bytes 786440 | tf_op jit(solution)/shard_map/ppermute | solution.py:341
  173.7 13.7 %collective-permute-start.2 = (f32[128,512]{1,0:T(8,128)S(1)}, f32[128,512]{1,0:T(8,128)}, u32[]{:S(2)}, u32[]{:S(2)}) collective-permute-start(f32[128,512]{1,0:T(8,128)S(1)} %fusion.1.more_one_ref), channel_id=1, source_target_pairs={{0,48},{16,32},{32,16},{48,0},{1,49},{17,33},{33,17},{49,1},{2,50}... | collective-permute-start | bytes 786440 | tf_op jit(solution)/shard_map/ppermute | solution.py:341
  181.9 11.3 %all-to-all-start.12 = ((f32[4,104,256]{2,1,0:T(8,128)}), f32[4,104,256]{2,1,0:T(8,128)S(1)}, u32[]{:S(2)}, u32[]{:S(2)}) async-start(f32[4,104,256]{2,1,0:T(8,128)} %final.1), calls=%async_computation.12 | async-start | bytes 851968 | tf_op jit(solution)/shard_map/all_to_all | solution.py:22
  188.6 11.1 %collective-permute-start.5 = (f32[4,64,256]{2,1,0:T(8,128)S(1)}, f32[4,64,256]{2,1,0:T(8,128)S(1)}, u32[]{:S(2)}, u32[]{:S(2)}) collective-permute-start(f32[4,64,256]{2,1,0:T(8,128)S(1)} %get-tuple-element.19.after_ref), channel_id=1, source_target_pairs={{0,64},{64,0},{128,192},{192,128},{256,320},{320,256},{384,448},{4... | collective-permute-start | bytes 786440 | tf_op jit(solution)/shard_map/ppermute | solution.py:341
  193.2 20.9 %collective-permute-start.8 = (f32[104,256]{1,0:T(8,128)S(1)}, f32[104,256]{1,0:T(8,128)S(1)}, u32[]{:S(2)}, u32[]{:S(2)}) collective-permute-start(f32[104,256]{1,0:T(8,128)S(1)} %gathered.1.kept_ref), channel_id=1, source_target_pairs={{0,4},{4,0},{1,5},{5,1},{2,6},{6,2},{3,7},{7,3},{8,12},{12,8},{9,1... | collective-permute-start | bytes 319496 | tf_op jit(solution)/shard_map/ppermute | solution.py:341
  199.8 14.3 %collective-permute-start.6 = (f32[2,64,256]{2,1,0:T(8,128)S(1)}, f32[2,64,256]{2,1,0:T(8,128)S(1)}, u32[]{:S(2)}, u32[]{:S(2)}) collective-permute-start(f32[2,64,256]{2,1,0:T(8,128)S(1)} %get-tuple-element.22), channel_id=1, source_target_pairs={{0,128},{64,192},{128,0},{192,64},{256,384},{320,448},{384,256},{4... | collective-permute-start | bytes 393224 | tf_op jit(solution)/shard_map/ppermute | solution.py:341
  214.9 16.1 %all-to-all-start.13 = ((f32[4,96,256]{2,1,0:T(8,128)}), f32[4,96,256]{2,1,0:T(8,128)S(1)}, u32[]{:S(2)}, u32[]{:S(2)}) async-start(f32[4,96,256]{2,1,0:T(8,128)} %get-tuple-element.20), calls=%async_computation.13 | async-start | bytes 786432 | tf_op jit(solution)/shard_map/all_to_all | solution.py:22
  219.5 10.8 %collective-permute-start.7 = (f32[64,256]{1,0:T(8,128)S(1)}, f32[64,256]{1,0:T(8,128)S(1)}, u32[]{:S(2)}, u32[]{:S(2)}) collective-permute-start(f32[64,256]{1,0:T(8,128)S(1)} %slice_bitcast_fusion), channel_id=1, source_target_pairs={{0,256},{64,320},{128,384},{192,448},{256,0},{320,64},{384,128},{4... | collective-permute-start | bytes 196616 | tf_op jit(solution)/shard_map/ppermute | solution.py:341

commit v14 on v12

--- a/solution.py
+++ b/solution.py
@@ -53,7 +53,7 @@
     return (b % X) * C + b // X
 
 
-AHEAD = 3
+AHEAD = 2
 
 
 def fetch(steps, sems):

time: 232 us -> 234 us (level)
  transfers between devices with their start and end apart: 14 -> 14, of which waited for: 7 -> 7; matrix products, arithmetic and copies ran while one was open for 1% -> 1% of each run, Pallas kernels for 7% -> 8%
where the time goes in v14:
time: 234 us; the launch traced here: 232 us
  blocking collectives  126 us (54%)
  starting transfers between devices  56 us (24%)
  Pallas kernels  24.3 us (10%)
  waiting for transfers between devices  20.1 us (9%)
  local copies, waits for them, and re-layouts  2.63 us (1%)
  other arithmetic  2.43 us (1%)
    all_to_all x9, blocking collectives, exchange(): return lax.all_to_all(blocks, axes, 0, 0, tiled=True)  126 us
    ppermute x9, starting transfers between devices, swap(): return lax.ppermute(value, axis, [(i, i ^ bits) for i in range(count)])  35.9 us
    all_to_all x5, starting transfers between devices, exchange(): return lax.all_to_all(blocks, axes, 0, 0, tiled=True)  20.1 us
    ppermute x9, waiting for transfers between devices, swap(): return lax.ppermute(value, axis, [(i, i ^ bits) for i in range(count)])  18.9 us
    pallas_call x1, Pallas kernels, per_device(): pl.pallas_call(final_kernel, in_specs=[vmem, vmem, hbm, hbm, anywhere, an...  5.71 us
    pallas_call x1, Pallas kernels, targets_sent(): pl.pallas_call(targets_sent_kernel, in_specs=[smem, vmem, vmem, hbm, anyw...  4.76 us
  transfers between devices with their start and end apart: 14, of which 7 were waited for; matrix products, arithmetic and copies ran while one was open for 1% of the time, Pallas kernels for 8%

profile of v14, /device:TPU:24, one launch (start us, length us, event | category | flops | bytes accessed | tf_op | source)
XLA Modules:
  0.0 231.9 jit_solution(9493683729461951730)
XLA Ops:
  0.7 0.9 copy-done.1
  1.7 1.6 copy-done.3
  3.2 2.8 %setup.1 = (f32[8,384,512]{2,1,0:T(8,128)S(1)}, f32[8,1,384]{2,1,0:T(1,128)S(1)}) custom-call(s32[5]{0:T(128)S(1)} %stack.23.where_ref, bf16[384,256]{1,0:T(8,128)(2,1)S(1)} %copy-done.1, bf16[8,8,64,256]{3,2,1,0:T(8,128)(2,1)S(1)} %bitcast.27), custom_call_target="tpu_custom_call" | custom-call | flops 805306368 | bytes 6291456 | tf_op jit(solution)/shard_map/setup/pallas_call | solution.py:264
  6.0 30.6 %all_to_all.70.parts_ref = f32[8,1,384]{2,1,0:T(1,128)S(1)} all-to-all(f32[8,1,384]{2,1,0:T(1,128)S(1)} %get-tuple-element.12), channel_id=1, replica_groups=mesh['z'=8,'x'=4,'c'=2,'h'=2,'y'=4] {'h','y'}, dimensions={0} | all-to-all | bytes 24576 | tf_op jit(solution)/shard_map/all_to_all | solution.py:22
  36.6 0.7 columns.3
  37.3 9.4 %all_to_all.71.parts_ref = f32[8,1,512]{2,1,0:T(1,128)S(1)} all-to-all(f32[8,1,512]{2,1,0:T(1,128)S(1)} %columns.3), channel_id=1, replica_groups=mesh['z'=8,'x'=4,'c'=2,'h'=2,'y'=4] {'c','x'}, dimensions={0} | all-to-all | bytes 32768 | tf_op jit(solution)/shard_map/all_to_all | solution.py:22
  46.7 15.3 %all_to_all.72.parts_ref = f32[8,1,512]{2,1,0:T(1,128)S(1)} all-to-all(f32[8,1,512]{2,1,0:T(1,128)S(1)} %sums.3), channel_id=1, replica_groups=mesh['z'=8,'x'=4,'c'=2,'h'=2,'y'=4] {'z'}, dimensions={0} | all-to-all | bytes 32768 | tf_op jit(solution)/shard_map/all_to_all | solution.py:22
  62.1 7.6 %all_to_all.73.columns_ref = f32[8,1,512]{2,1,0:T(1,128)S(1)} all-to-all(f32[8,1,512]{2,1,0:T(1,128)S(1)} %inverse.3), channel_id=1, replica_groups=mesh['z'=8,'x'=4,'c'=2,'h'=2,'y'=4] {'c','x'}, dimensions={0} | all-to-all | bytes 32768 | tf_op jit(solution)/shard_map/all_to_all | solution.py:22
  69.7 0.5 rows.2
  70.2 17.3 %all_to_all.74.parts_ref = f32[8,1,384]{2,1,0:T(1,128)S(1)} all-to-all(f32[8,1,384]{2,1,0:T(1,128)S(1)} %rows.2), channel_id=1, replica_groups=mesh['z'=8,'x'=4,'c'=2,'h'=2,'y'=4] {'h','y'}, dimensions={0} | all-to-all | bytes 24576 | tf_op jit(solution)/shard_map/all_to_all | solution.py:22
  87.5 0.7 columns.4
  88.2 7.6 %all_to_all.75.parts_ref = f32[8,1,512]{2,1,0:T(1,128)S(1)} all-to-all(f32[8,1,512]{2,1,0:T(1,128)S(1)} %columns.4), channel_id=1, replica_groups=mesh['z'=8,'x'=4,'c'=2,'h'=2,'y'=4] {'c','x'}, dimensions={0} | all-to-all | bytes 32768 | tf_op jit(solution)/shard_map/all_to_all | solution.py:22
  95.8 12.9 %all_to_all.76.parts_ref = f32[8,1,512]{2,1,0:T(1,128)S(1)} all-to-all(f32[8,1,512]{2,1,0:T(1,128)S(1)} %sums.4), channel_id=1, replica_groups=mesh['z'=8,'x'=4,'c'=2,'h'=2,'y'=4] {'z'}, dimensions={0} | all-to-all | bytes 32768 | tf_op jit(solution)/shard_map/all_to_all | solution.py:22
  108.7 7.6 %all_to_all.77.columns_ref = f32[8,1,512]{2,1,0:T(1,128)S(1)} all-to-all(f32[8,1,512]{2,1,0:T(1,128)S(1)} %inverse.4), channel_id=1, replica_groups=mesh['z'=8,'x'=4,'c'=2,'h'=2,'y'=4] {'c','x'}, dimensions={0} | all-to-all | bytes 32768 | tf_op jit(solution)/shard_map/all_to_all | solution.py:22
  116.4 0.5 rows.3
  116.9 17.3 %all_to_all.78.parts_ref = f32[8,1,384]{2,1,0:T(1,128)S(1)} all-to-all(f32[8,1,384]{2,1,0:T(1,128)S(1)} %rows.3), channel_id=1, replica_groups=mesh['z'=8,'x'=4,'c'=2,'h'=2,'y'=4] {'h','y'}, dimensions={0} | all-to-all | bytes 24576 | tf_op jit(solution)/shard_map/all_to_all | solution.py:22
  134.2 1.2 columns.5.after_ref
  135.4 3.3 %all-to-all-start.9 = ((f32[8,1,512]{2,1,0:T(1,128)}), f32[8,1,512]{2,1,0:T(1,128)S(1)}, u32[]{:S(2)}, u32[]{:S(2)}) async-start(f32[8,1,512]{2,1,0:T(1,128)} %columns.5.after_ref), calls=%async_computation.9 | async-start | bytes 32768 | tf_op jit(solution)/shard_map/all_to_all | solution.py:22
  138.7 4.8 %targets_sent.1 = f32[4,256,512]{2,1,0:T(8,128)} custom-call(s32[5]{0:T(128)S(1)} %stack.23.where_ref, f32[8,1,384]{2,1,0:T(1,128)S(1)} %all_to_all.78.parts_ref, bf16[384,256]{1,0:T(8,128)(2,1)S(1)} %copy-done.2, f32[8,384,512]{2,1,0:T(8,128)} %copy-done, f32[8,1,512]{2,1,0:T(1,128)} %columns.5.after_ref), custom_call_target="tpu_custom_call" | custom-call | flops 402653184 | bytes 6291456 | tf_op jit(solution)/shard_map/targets_sent/pallas_call | solution.py:292
  143.5 2.3 %collective-permute-start = (f32[4,256,512]{2,1,0:T(8,128)}, f32[4,256,512]{2,1,0:T(8,128)}, u32[]{:S(2)}, u32[]{:S(2)}) collective-permute-start(f32[4,256,512]{2,1,0:T(8,128)} %targets_sent.1), channel_id=1, source_target_pairs={{0,8},{8,0},{1,9},{9,1},{2,10},{10,2},{3,11},{11,3},{4,12},{12,4},... | collective-permute-start | bytes 6291464 | tf_op jit(solution)/shard_map/ppermute | solution.py:337
  145.8 0.6 sums.5.after_ref
  146.5 3.3 %all-to-all-start.10 = ((f32[8,1,512]{2,1,0:T(1,128)}), f32[8,1,512]{2,1,0:T(1,128)S(1)}, u32[]{:S(2)}, u32[]{:S(2)}) async-start(f32[8,1,512]{2,1,0:T(1,128)} %sums.5.after_ref), calls=%async_computation.10 | async-start | bytes 32768 | tf_op jit(solution)/shard_map/all_to_all | solution.py:22
  149.8 0.1 collective-permute-done.added_ref
  149.9 4.2 %targets_kept.1 = (f32[2,128,512]{2,1,0:T(8,128)}, f32[2,128,512]{2,1,0:T(8,128)S(1)}, f32[2,128,512]{2,1,0:T(8,128)S(1)}, f32[2,128,512]{2,1,0:T(8,128)S(1)}) custom-call(s32[5]{0:T(128)S(1)} %stack.23.where_ref, f32[8,1,384]{2,1,0:T(1,128)S(1)} %all_to_all.78.parts_ref, bf16[384,256]{1,0:T(8,128)(2,1)S(1)} %copy-done.2, f32[8,384,512]{2,1,0:T(8,128)} %copy-done, ...), custom_call_target="tpu_custom_call" | custom-call | flops 402653184 | bytes 6291456 | tf_op jit(solution)/shard_map/targets_kept/pallas_call | solution.py:308
  154.1 5.0 %collective-permute-start.3 = (f32[2,128,512]{2,1,0:T(8,128)S(1)}, f32[2,128,512]{2,1,0:T(8,128)S(1)}, u32[]{:S(2)}, u32[]{:S(2)}) collective-permute-start(f32[2,128,512]{2,1,0:T(8,128)S(1)} %get-tuple-element.17), channel_id=1, source_target_pairs={{0,48},{16,32},{32,16},{48,0},{1,49},{17,33},{33,17},{49,1},{2,50}... | collective-permute-start | bytes 1572872 | tf_op jit(solution)/shard_map/ppermute | solution.py:337
  159.1 2.2 collective-permute-start.1
  161.3 0.6 inverse.5
  161.9 3.4 %all-to-all-start.11 = ((f32[8,1,512]{2,1,0:T(1,128)}), f32[8,1,512]{2,1,0:T(1,128)S(1)}, u32[]{:S(2)}, u32[]{:S(2)}) async-start(f32[8,1,512]{2,1,0:T(1,128)} %inverse.5), calls=%async_computation.11 | async-start | bytes 32768 | tf_op jit(solution)/shard_map/all_to_all | solution.py:22
  165.3 6.1 %collective-permute-done.3.two_ref = f32[2,128,512]{2,1,0:T(8,128)S(1)} collective-permute-done((f32[2,128,512]{2,1,0:T(8,128)S(1)}, f32[2,128,512]{2,1,0:T(8,128)S(1)}, u32[]{:S(2)}, u32[]{:S(2)}) %collective-permute-start.3) | collective-permute-done | bytes 524320 | tf_op jit(solution)/shard_map/ppermute | solution.py:337
  171.5 2.3 %collective-permute-start.4 = (f32[128,512]{1,0:T(8,128)S(1)}, f32[128,512]{1,0:T(8,128)S(1)}, u32[]{:S(2)}, u32[]{:S(2)}) collective-permute-start(f32[128,512]{1,0:T(8,128)S(1)} %fusion.more_two_ref), channel_id=1, source_target_pairs={{0,16},{16,0},{32,48},{48,32},{1,17},{17,1},{33,49},{49,33},{2,18}... | collective-permute-start | bytes 786440 | tf_op jit(solution)/shard_map/ppermute | solution.py:337
  173.8 1.2 collective-permute-done.1.one_ref
  175.0 3.2 %collective-permute-start.2 = (f32[128,512]{1,0:T(8,128)S(1)}, f32[128,512]{1,0:T(8,128)}, u32[]{:S(2)}, u32[]{:S(2)}) collective-permute-start(f32[128,512]{1,0:T(8,128)S(1)} %fusion.1.more_one_ref), channel_id=1, source_target_pairs={{0,48},{16,32},{32,16},{48,0},{1,49},{17,33},{33,17},{49,1},{2,50}... | collective-permute-start | bytes 786440 | tf_op jit(solution)/shard_map/ppermute | solution.py:337
  178.3 5.7 %final.1 = f32[4,104,256]{2,1,0:T(8,128)} custom-call(f32[8,1,384]{2,1,0:T(1,128)S(1)} %all_to_all.78.parts_ref, f32[8,1,512]{2,1,0:T(1,128)S(1)} %all-to-all-done.11.columns_ref, bf16[8,8,64,256]{3,2,1,0:T(8,128)(2,1)} %bitcast.26, f32[8,384,512]{2,1,0:T(8,128)} %copy-done, f32[128,512]{1,0:T(8,128)S(1)} %fusion.1.more_one_ref, f32[128,512]{1,0:T(8,128)S(1)} %fusion.more_two_ref), custom_call_target="tpu_custom_call" | custom-call | flops 4831838208 | bytes 6291456 | tf_op jit(solution)/shard_map/final/pallas_call | solution.py:359
  184.0 5.5 %all-to-all-start.12 = ((f32[4,104,256]{2,1,0:T(8,128)}), f32[4,104,256]{2,1,0:T(8,128)S(1)}, u32[]{:S(2)}, u32[]{:S(2)}) async-start(f32[4,104,256]{2,1,0:T(8,128)} %final.1), calls=%async_computation.12 | async-start | bytes 851968 | tf_op jit(solution)/shard_map/all_to_all | solution.py:22
  189.5 1.2 turn.1
  190.7 3.4 %collective-permute-start.5 = (f32[4,64,256]{2,1,0:T(8,128)S(1)}, f32[4,64,256]{2,1,0:T(8,128)S(1)}, u32[]{:S(2)}, u32[]{:S(2)}) collective-permute-start(f32[4,64,256]{2,1,0:T(8,128)S(1)} %get-tuple-element.19.after_ref), channel_id=1, source_target_pairs={{0,64},{64,0},{128,192},{192,128},{256,320},{320,256},{384,448},{4... | collective-permute-start | bytes 786440 | tf_op jit(solution)/shard_map/ppermute | solution.py:337
  194.1 1.2 all-to-all-done.12.parts_ref
  195.3 2.5 %collective-permute-start.8 = (f32[104,256]{1,0:T(8,128)S(1)}, f32[104,256]{1,0:T(8,128)S(1)}, u32[]{:S(2)}, u32[]{:S(2)}) collective-permute-start(f32[104,256]{1,0:T(8,128)S(1)} %gathered.1.kept_ref), channel_id=1, source_target_pairs={{0,4},{4,0},{1,5},{5,1},{2,6},{6,2},{3,7},{7,3},{8,12},{12,8},{9,1... | collective-permute-start | bytes 319496 | tf_op jit(solution)/shard_map/ppermute | solution.py:337
  197.8 0.7 multiply_bitcast_fusion
  198.6 3.3 %collective-permute-done.5 = f32[4,64,256]{2,1,0:T(8,128)S(1)} collective-permute-done((f32[4,64,256]{2,1,0:T(8,128)S(1)}, f32[4,64,256]{2,1,0:T(8,128)S(1)}, u32[]{:S(2)}, u32[]{:S(2)}) %collective-permute-start.5) | collective-permute-done | bytes 262176 | tf_op jit(solution)/shard_map/ppermute | solution.py:337
  201.9 4.4 %collective-permute-start.6 = (f32[2,64,256]{2,1,0:T(8,128)S(1)}, f32[2,64,256]{2,1,0:T(8,128)S(1)}, u32[]{:S(2)}, u32[]{:S(2)}) collective-permute-start(f32[2,64,256]{2,1,0:T(8,128)S(1)} %slice.43), channel_id=1, source_target_pairs={{0,128},{64,192},{128,0},{192,64},{256,384},{320,448},{384,256},{4... | collective-permute-start | bytes 393224 | tf_op jit(solution)/shard_map/ppermute | solution.py:337
  206.3 6.0 %collective-permute-done.8.came_ref = f32[104,256]{1,0:T(8,128)S(1)} collective-permute-done((f32[104,256]{1,0:T(8,128)S(1)}, f32[104,256]{1,0:T(8,128)S(1)}, u32[]{:S(2)}, u32[]{:S(2)}) %collective-permute-start.8) | collective-permute-done | bytes 106528 | tf_op jit(solution)/shard_map/ppermute | solution.py:337
  212.3 0.8 join.1
  213.0 4.5 %all-to-all-start.13 = ((f32[4,96,256]{2,1,0:T(8,128)}), f32[4,96,256]{2,1,0:T(8,128)S(1)}, u32[]{:S(2)}, u32[]{:S(2)}) async-start(f32[4,96,256]{2,1,0:T(8,128)} %get-tuple-element.20), calls=%async_computation.13 | async-start | bytes 786432 | tf_op jit(solution)/shard_map/all_to_all | solution.py:22
  217.6 10.5 %collective-permute-start.7 = (f32[64,256]{1,0:T(8,128)S(1)}, f32[64,256]{1,0:T(8,128)S(1)}, u32[]{:S(2)}, u32[]{:S(2)}) collective-permute-start(f32[64,256]{1,0:T(8,128)S(1)} %slice_bitcast_fusion), channel_id=1, source_target_pairs={{0,256},{64,320},{128,384},{192,448},{256,0},{320,64},{384,128},{4... | collective-permute-start | bytes 196616 | tf_op jit(solution)/shard_map/ppermute | solution.py:337
  228.1 2.2 collective-permute-done.7
  230.4 0.7 fusion.3
  231.1 0.9 bitcast_divide_fusion
  (27 shorter events, 0.4 us)
Async XLA Ops:
  0.7 0.9 copy-start.1
  1.7 1.6 copy-start.3
  6.0 128.1 %copy-start = (f32[8,384,512]{2,1,0:T(8,128)}, f32[8,384,512]{2,1,0:T(8,128)S(1)}, u32[]{:S(2)}) copy-start(f32[8,384,512]{2,1,0:T(8,128)S(1)} %get-tuple-element.13.tile_ref) | copy-start | bytes 18874372
  134.1 4.6 %copy-start.2 = (bf16[384,256]{1,0:T(8,128)(2,1)S(1)}, bf16[384,256]{1,0:T(8,128)(2,1)}, u32[]{:S(2)}) copy-start(bf16[384,256]{1,0:T(8,128)(2,1)} %latents_ref.5) | copy-start | bytes 589828
  135.4 10.5 %all-to-all-start.9 = ((f32[8,1,512]{2,1,0:T(1,128)}), f32[8,1,512]{2,1,0:T(1,128)S(1)}, u32[]{:S(2)}, u32[]{:S(2)}) async-start(f32[8,1,512]{2,1,0:T(1,128)} %columns.5.after_ref), calls=%async_computation.9 | async-start | bytes 32768 | tf_op jit(solution)/shard_map/all_to_all | solution.py:22
  143.5 6.4 %collective-permute-start = (f32[4,256,512]{2,1,0:T(8,128)}, f32[4,256,512]{2,1,0:T(8,128)}, u32[]{:S(2)}, u32[]{:S(2)}) collective-permute-start(f32[4,256,512]{2,1,0:T(8,128)} %targets_sent.1), channel_id=1, source_target_pairs={{0,8},{8,0},{1,9},{9,1},{2,10},{10,2},{3,11},{11,3},{4,12},{12,4},... | collective-permute-start | bytes 6291464 | tf_op jit(solution)/shard_map/ppermute | solution.py:337
  146.5 14.8 %all-to-all-start.10 = ((f32[8,1,512]{2,1,0:T(1,128)}), f32[8,1,512]{2,1,0:T(1,128)S(1)}, u32[]{:S(2)}, u32[]{:S(2)}) async-start(f32[8,1,512]{2,1,0:T(1,128)} %sums.5.after_ref), calls=%async_computation.10 | async-start | bytes 32768 | tf_op jit(solution)/shard_map/all_to_all | solution.py:22
  154.1 17.4 %collective-permute-start.3 = (f32[2,128,512]{2,1,0:T(8,128)S(1)}, f32[2,128,512]{2,1,0:T(8,128)S(1)}, u32[]{:S(2)}, u32[]{:S(2)}) collective-permute-start(f32[2,128,512]{2,1,0:T(8,128)S(1)} %get-tuple-element.17), channel_id=1, source_target_pairs={{0,48},{16,32},{32,16},{48,0},{1,49},{17,33},{33,17},{49,1},{2,50}... | collective-permute-start | bytes 1572872 | tf_op jit(solution)/shard_map/ppermute | solution.py:337
  159.1 15.9 %collective-permute-start.1 = (f32[2,128,512]{2,1,0:T(8,128)}, f32[2,128,512]{2,1,0:T(8,128)S(1)}, u32[]{:S(2)}, u32[]{:S(2)}) collective-permute-start(f32[2,128,512]{2,1,0:T(8,128)} %get-tuple-element.15.refs_0_), channel_id=1, source_target_pairs={{0,16},{16,0},{32,48},{48,32},{1,17},{17,1},{33,49},{49,33},{2,18}... | collective-permute-start | bytes 1572872 | tf_op jit(solution)/shard_map/ppermute | solution.py:337
  161.9 16.4 %all-to-all-start.11 = ((f32[8,1,512]{2,1,0:T(1,128)}), f32[8,1,512]{2,1,0:T(1,128)S(1)}, u32[]{:S(2)}, u32[]{:S(2)}) async-start(f32[8,1,512]{2,1,0:T(1,128)} %inverse.5), calls=%async_computation.11 | async-start | bytes 32768 | tf_op jit(solution)/shard_map/all_to_all | solution.py:22
  171.5 18.0 %collective-permute-start.4 = (f32[128,512]{1,0:T(8,128)S(1)}, f32[128,512]{1,0:T(8,128)S(1)}, u32[]{:S(2)}, u32[]{:S(2)}) collective-permute-start(f32[128,512]{1,0:T(8,128)S(1)} %fusion.more_two_ref), channel_id=1, source_target_pairs={{0,16},{16,0},{32,48},{48,32},{1,17},{17,1},{33,49},{49,33},{2,18}... | collective-permute-start | bytes 786440 | tf_op jit(solution)/shard_map/ppermute | solution.py:337
  175.0 14.5 %collective-permute-start.2 = (f32[128,512]{1,0:T(8,128)S(1)}, f32[128,512]{1,0:T(8,128)}, u32[]{:S(2)}, u32[]{:S(2)}) collective-permute-start(f32[128,512]{1,0:T(8,128)S(1)} %fusion.1.more_one_ref), channel_id=1, source_target_pairs={{0,48},{16,32},{32,16},{48,0},{1,49},{17,33},{33,17},{49,1},{2,50}... | collective-permute-start | bytes 786440 | tf_op jit(solution)/shard_map/ppermute | solution.py:337
  184.0 11.3 %all-to-all-start.12 = ((f32[4,104,256]{2,1,0:T(8,128)}), f32[4,104,256]{2,1,0:T(8,128)S(1)}, u32[]{:S(2)}, u32[]{:S(2)}) async-start(f32[4,104,256]{2,1,0:T(8,128)} %final.1), calls=%async_computation.12 | async-start | bytes 851968 | tf_op jit(solution)/shard_map/all_to_all | solution.py:22
  190.7 11.1 %collective-permute-start.5 = (f32[4,64,256]{2,1,0:T(8,128)S(1)}, f32[4,64,256]{2,1,0:T(8,128)S(1)}, u32[]{:S(2)}, u32[]{:S(2)}) collective-permute-start(f32[4,64,256]{2,1,0:T(8,128)S(1)} %get-tuple-element.19.after_ref), channel_id=1, source_target_pairs={{0,64},{64,0},{128,192},{192,128},{256,320},{320,256},{384,448},{4... | collective-permute-start | bytes 786440 | tf_op jit(solution)/shard_map/ppermute | solution.py:337
  195.3 16.9 %collective-permute-start.8 = (f32[104,256]{1,0:T(8,128)S(1)}, f32[104,256]{1,0:T(8,128)S(1)}, u32[]{:S(2)}, u32[]{:S(2)}) collective-permute-start(f32[104,256]{1,0:T(8,128)S(1)} %gathered.1.kept_ref), channel_id=1, source_target_pairs={{0,4},{4,0},{1,5},{5,1},{2,6},{6,2},{3,7},{7,3},{8,12},{12,8},{9,1... | collective-permute-start | bytes 319496 | tf_op jit(solution)/shard_map/ppermute | solution.py:337
  201.9 15.7 %collective-permute-start.6 = (f32[2,64,256]{2,1,0:T(8,128)S(1)}, f32[2,64,256]{2,1,0:T(8,128)S(1)}, u32[]{:S(2)}, u32[]{:S(2)}) collective-permute-start(f32[2,64,256]{2,1,0:T(8,128)S(1)} %slice.43), channel_id=1, source_target_pairs={{0,128},{64,192},{128,0},{192,64},{256,384},{320,448},{384,256},{4... | collective-permute-start | bytes 393224 | tf_op jit(solution)/shard_map/ppermute | solution.py:337
  213.0 18.0 %all-to-all-start.13 = ((f32[4,96,256]{2,1,0:T(8,128)}), f32[4,96,256]{2,1,0:T(8,128)S(1)}, u32[]{:S(2)}, u32[]{:S(2)}) async-start(f32[4,96,256]{2,1,0:T(8,128)} %get-tuple-element.20), calls=%async_computation.13 | async-start | bytes 786432 | tf_op jit(solution)/shard_map/all_to_all | solution.py:22
  217.6 12.8 %collective-permute-start.7 = (f32[64,256]{1,0:T(8,128)S(1)}, f32[64,256]{1,0:T(8,128)S(1)}, u32[]{:S(2)}, u32[]{:S(2)}) collective-permute-start(f32[64,256]{1,0:T(8,128)S(1)} %slice_bitcast_fusion), channel_id=1, source_target_pairs={{0,256},{64,320},{128,384},{192,448},{256,0},{320,64},{384,128},{4... | collective-permute-start | bytes 196616 | tf_op jit(solution)/shard_map/ppermute | solution.py:337
